TPU v7x, 32 devices: a whole 2x2x4 slice. The times are simulated.
32 devices in a mesh: resp: 8 (over z, x), head: 4 (over y, core).
Axes of the slice: x: 2, y: 2, z: 4, core: 2. Of those that a mesh axis runs over, the one named last changes fastest.
Arguments:
- queries: bfloat16 [2048, 8192], P('resp', 'head'), may hold values from -240 to 240
- d_out: bfloat16 [2048, 8192], P('resp', 'head'), may hold values from -24 to 24
- prefix_keys: bfloat16 [128, 1024], P('resp', 'head'), may hold values from -17 to 17
- prefix_values: bfloat16 [128, 1024], P('resp', 'head'), may hold values from -6 to 6
- k_weight: bfloat16 [8192, 1024], P(None, 'head'), may hold values from -0.0625 to 0.0625
- v_weight: bfloat16 [8192, 1024], P(None, 'head'), may hold values from -0.0625 to 0.0625
- lengths: int32 [8], P('resp'), may hold values from 1 to 256, as said below
Outputs:
- prefix_dk: bfloat16 [128, 1024], P('resp', 'head')
- prefix_dv: bfloat16 [128, 1024], P('resp', 'head')
- input_grad: bfloat16 [128, 8192], P('resp', 'head')
Inputs may be any that keep to these rules, and one draw needn't show every extreme that they name: `lengths`: every response has at least one live token and one response has exactly 256.
All inputs are finite; a program needn't handle non-finite values.
Results may differ from a plain program's by a relative error of at most 0.015.
Values may be sent and summed in bfloat16 or wider, within the bound.
No kernel may reach another device: no remote copies, remote signals or barrier semaphores. Data moves between devices by JAX's collectives and lax.ppermute only.
A program may use at most 128 MiB of HBM per device.

v0:
```python
import jax
import jax.numpy as jnp
from jax import lax
from jax.sharding import PartitionSpec as P

HD = 128
LEN = 256


def body(queries, d_out, prefix_keys, prefix_values, k_weight, v_weight, lengths):
    scale = HD ** (-0.5)
    rows = queries.shape[0]
    kv_local = prefix_keys.shape[1] // HD
    group = queries.shape[1] // HD // kv_local
    count_resp = lengths.shape[0]
    position = jnp.arange(rows, dtype=jnp.int32) % LEN
    owner = jnp.arange(rows, dtype=jnp.int32) // LEN
    live = jnp.any(
        (owner[:, None] == jnp.arange(count_resp, dtype=jnp.int32)[None, :])
        & (position[:, None] < lengths[None, :]),
        axis=1,
    )
    masked = jnp.where(live[:, None], d_out, jnp.zeros_like(d_out))
    query_heads = queries.reshape(rows, kv_local, group, HD)
    grad_heads = masked.reshape(rows, kv_local, group, HD)
    key_all, value_all = (
        lax.all_gather(prefix_keys, "resp", axis=0, tiled=True),
        lax.all_gather(prefix_values, "resp", axis=0, tiled=True),
    )
    keys = key_all.reshape(-1, kv_local, HD)
    values = value_all.reshape(-1, kv_local, HD)
    scores = (
        jnp.einsum("tkgd,skd->tkgs", query_heads, keys, preferred_element_type=jnp.float32) * scale
    )
    dprobs = jnp.einsum("tkgd,skd->tkgs", grad_heads, values, preferred_element_type=jnp.float32)
    top = jnp.full((rows, kv_local, group), -jnp.inf, jnp.float32)
    total = jnp.zeros((rows, kv_local, group), jnp.float32)
    weighted = jnp.zeros((rows, kv_local, group), jnp.float32)
    new_top = jnp.max(scores, axis=-1)
    factor = jnp.exp(top - new_top)
    expo = jnp.exp(scores - new_top[..., None])
    top, total, weighted = (
        new_top,
        total * factor + jnp.sum(expo, axis=-1),
        weighted * factor + jnp.sum(expo * dprobs, axis=-1),
    )
    lse = top + jnp.log(total)
    delta = weighted / total
    count = key_all.shape[0]
    keys = key_all.reshape(count, kv_local, HD)
    values = value_all.reshape(count, kv_local, HD)
    scores = (
        jnp.einsum("tkgd,skd->tkgs", query_heads, keys, preferred_element_type=jnp.float32) * scale
    )
    probs = jnp.exp(scores - lse[..., None])
    probs_low = probs.astype(jnp.bfloat16)
    grad_v = jnp.einsum("tkgs,tkgd->skd", probs_low, grad_heads, preferred_element_type=jnp.float32)
    dprobs = jnp.einsum("tkgd,skd->tkgs", grad_heads, values, preferred_element_type=jnp.float32)
    dscores = (probs * (dprobs - delta[..., None]) * scale).astype(jnp.bfloat16)
    grad_k = jnp.einsum("tkgs,tkgd->skd", dscores, query_heads, preferred_element_type=jnp.float32)
    shares = lax.psum_scatter(
        jnp.concatenate(
            [grad_k.reshape(count, kv_local * HD), grad_v.reshape(count, kv_local * HD)], axis=1
        ),
        "resp",
        scatter_dimension=0,
        tiled=True,
    )
    width = kv_local * HD
    dk_low = shares[:, :width].astype(jnp.bfloat16)
    dv_low = shares[:, width:].astype(jnp.bfloat16)
    partial_input = jnp.einsum("pc,dc->pd", dk_low, k_weight, preferred_element_type=jnp.float32)
    partial_input = partial_input + jnp.einsum(
        "pc,dc->pd", dv_low, v_weight, preferred_element_type=jnp.float32
    )
    input_grad = lax.psum_scatter(
        partial_input.astype(jnp.bfloat16), "head", scatter_dimension=1, tiled=True
    )
    return (dk_low, dv_low, input_grad)


def solution(mesh):
    placed = (
        P("resp", "head"),
        P("resp", "head"),
        P("resp", "head"),
        P("resp", "head"),
        P(None, "head"),
        P(None, "head"),
        P("resp"),
    )
    return jax.shard_map(
        body,
        mesh=mesh,
        in_specs=placed,
        out_specs=(P("resp", "head"), P("resp", "head"), P("resp", "head")),
        check_vma=False,
    )
```

profile of v0, /device:TPU:0, one launch (start us, length us, event | category | flops | bytes accessed | tf_op | source)
XLA Modules:
  0.0 181.7 jit_solution(17252900632570347614)
XLA Ops:
  7.2 0.0 reduce-scatter.3.cloned.1.call-start
  7.9 32.5 %all_gather.6 = bf16[128,256]{1,0:T(8,128)(2,1)S(1)} all-gather(bf16[16,256]{1,0:T(8,128)(2,1)} %param.9), channel_id=1, replica_groups=mesh['resp'=8,'head'=4] {'resp'}, dimensions={0}, use_global_device_ids=true | all-gather | bytes 73728 | tf_op jit(solution)/shard_map/all_gather | solution.py:27
  40.4 0.1 copy.30
  40.5 30.7 %all_gather.7 = bf16[128,256]{1,0:T(8,128)(2,1)S(1)} all-gather(bf16[16,256]{1,0:T(8,128)(2,1)} %param.10), channel_id=1, replica_groups=mesh['resp'=8,'head'=4] {'resp'}, dimensions={0}, use_global_device_ids=true | all-gather | bytes 73728 | tf_op jit(solution)/shard_map/all_gather | solution.py:28
  71.2 0.1 copy.33
  71.3 0.0 copy-start.2
  71.3 1.5 select_bitcast_fusion
  72.8 1.2 copy.50
  74.0 0.0 copy-done.2
  74.0 0.5 copy.49
  74.5 0.0 copy-start.1
  74.6 0.5 bitcast_reduce_fusion
  75.1 0.7 copy-done.1
  75.8 2.0 %fusion.1 = (f32[256,2,8]{0,2,1:T(8,128)S(1)}, f32[256,2,8]{0,2,1:T(8,128)S(1)}, f32[2,256,8,128]{1,3,2,0:T(8,128)}) fusion(f32[2,128,256,8]{2,1,3,0:T(8,128)S(1)} %get-tuple-element.10, f32[256,2,8]{0,2,1:T(8,128)S(1)} %get-tuple-element.9, bf16[128,2,128,1]{0,2,3,1:T(8,128)(2,1)S(1)} %bitcast.73, bf16[256,2,8,128]{3,2,1,0:T(8,128)(2,1)S(1)} %bitcast.70), kind=kOutput, calls=%fused_computation.4 | convolution fusion | flops 136306688 | bytes 5357568 | tf_op jit(solution)/shard_map/tkgd,skd->tkgs/dot_general | solution.py:58
  77.8 1.3 fusion.7
  79.1 2.7 %copy.38 = bf16[256,2,8,128]{3,2,1,0:T(8,128)(2,1)} copy(bf16[256,2,8,128]{0,3,2,1:T(8,128)(2,1)} %fusion.7) | data formatting | bytes 2097152 | tf_op jit(solution)/shard_map/convert_element_type | solution.py:56
  81.7 2.0 %fusion.18 = f32[2,128,128,1]{2,1,0,3:T(8,128)S(1)} fusion(bf16[256,2,8,128]{3,2,1,0:T(8,128)(2,1)} %bitcast.69, bf16[256,2,8,128]{3,2,1,0:T(8,128)(2,1)} %copy.38), kind=kOutput, calls=%fused_computation.35 | convolution fusion | flops 134217728 | bytes 2228224 | tf_op jit(solution)/shard_map/tkgs,tkgd->skd/dot_general | solution.py:57
  83.8 0.1 copy.40
  83.9 2.3 %fusion.11 = f32[2,128,128,1]{1,2,3,0:T(8,128)S(1)} fusion(bf16[256,2,8,128]{0,3,2,1:T(8,128)(2,1)S(1)} %bitcast.68, f32[2,256,8,128]{1,3,2,0:T(8,128)} %get-tuple-element.11, f32[2,128,256,8]{2,1,3,0:T(8,128)S(1)} %get-tuple-element.10, f32[256,2,8]{0,2,1:T(8,128)S(1)} %get-tuple-element.5, f32[256,2,8]{0,2,1:T(8,128)S(1)} %get-tuple-element.6), kind=kOutput, calls=%fused_computation.19 | convolution fusion | flops 136839168 | bytes 5406720 | tf_op jit(solution)/shard_map/tkgs,tkgd->skd/dot_general | solution.py:60
  86.2 0.1 copy.39
  86.3 0.7 pad_maximum_fusion
  87.0 0.0 reduce-scatter.3.cloned.1.call-update
  87.0 0.0 reduce-scatter.5.cloned.1.call-start
  87.1 62.2 %reduce-scatter.3.cloned.1.call-done = f32[16,512]{1,0:T(8,128)} async-done(((f32[128,512]{1,0:T(8,128)}), f32[16,512]{1,0:T(8,128)}) %reduce-scatter.3.cloned.1.call-update) | async-done | bytes 32784 | tf_op jit(solution)/shard_map/reduce_scatter | solution.py:61
  149.3 0.8 convert.4
  150.0 0.0 copy-start.4
  150.0 0.0 copy-start.3
  150.0 0.0 copy-start
  150.1 3.5 %fusion.19 = f32[16,8192]{1,0:T(8,128)S(1)} fusion(bf16[16,256]{1,0:T(8,128)(2,1)S(1)} %get-tuple-element.8, bf16[8192,256]{1,0:T(8,128)(2,1)} %param.11), kind=kOutput, calls=%fused_computation.36 | convolution fusion | flops 67108864 | bytes 4726784 | tf_op jit(solution)/shard_map/pc,dc->pd/dot_general | solution.py:72
  153.6 0.0 copy-done.4
  153.6 0.0 copy-done.3
  153.6 0.0 copy-done
  153.6 1.9 %fusion = bf16[16,8192]{1,0:T(8,128)(2,1)} fusion(f32[16,8192]{1,0:T(8,128)S(1)} %fusion.19, bf16[16,256]{1,0:T(8,128)(2,1)S(1)} %get-tuple-element.7, bf16[8192,256]{1,0:T(8,128)(2,1)S(1)} %copy-done), kind=kOutput, calls=%fused_computation.1 | convolution fusion | flops 67371008 | bytes 4988928 | tf_op jit(solution)/shard_map/pc,dc->pd/dot_general | solution.py:73
  155.5 0.0 reduce-scatter.5.cloned.1.call-update
  155.5 19.3 %reduce-scatter.5.cloned.1.call-done = bf16[16,2048]{1,0:T(8,128)(2,1)} async-done(((bf16[16,8192]{1,0:T(8,128)(2,1)}), bf16[16,2048]{1,0:T(8,128)(2,1)}) %reduce-scatter.5.cloned.1.call-update) | async-done | bytes 65552 | tf_op jit(solution)/shard_map/reduce_scatter | solution.py:76
  (3 shorter events, 0.0 us)
Async XLA Ops:
  7.2 142.1 %reduce-scatter.3.cloned.1.call-start = ((), (), s32[]{:S(2)}) async-start(), calls=%async_computation.2 | async-start | bytes 294912 | tf_op jit(solution)/shard_map/reduce_scatter | solution.py:61
  71.3 2.7 %copy-start.2 = (bf16[256,2048]{1,0:T(8,128)(2,1)S(1)}, bf16[256,2048]{1,0:T(8,128)(2,1)}, u32[]{:S(2)}) copy-start(bf16[256,2048]{1,0:T(8,128)(2,1)} %param.7) | copy-start | bytes 3145732
  74.5 1.2 copy-start.1
  87.0 87.8 %reduce-scatter.5.cloned.1.call-start = ((), (), s32[]{:S(2)}) async-start(), calls=%async_computation.3 | async-start | bytes 327680 | tf_op jit(solution)/shard_map/reduce_scatter | solution.py:76
  150.0 3.6 %copy-start.4 = (bf16[16,256]{1,0:T(8,128)(2,1)}, bf16[16,256]{1,0:T(8,128)(2,1)S(1)}, u32[]{:S(2)}) copy-start(bf16[16,256]{1,0:T(8,128)(2,1)S(1)} %get-tuple-element.8) | copy-start | bytes 24580
  150.0 3.6 %copy-start.3 = (bf16[16,256]{1,0:T(8,128)(2,1)}, bf16[16,256]{1,0:T(8,128)(2,1)S(1)}, u32[]{:S(2)}) copy-start(bf16[16,256]{1,0:T(8,128)(2,1)S(1)} %get-tuple-element.7) | copy-start | bytes 24580
  150.0 3.6 %copy-start = (bf16[8192,256]{1,0:T(8,128)(2,1)S(1)}, bf16[8192,256]{1,0:T(8,128)(2,1)}, u32[]{:S(2)}) copy-start(bf16[8192,256]{1,0:T(8,128)(2,1)} %param.12) | copy-start | bytes 12582916
Sparse Core Ops, SparseCore 0:
  87.2 62.0 reduce-scatter.2
  155.7 19.1 reduce-scatter.4
where the time goes:
time: 182 us
  waiting for transfers between devices  81.5 us (45%)
  blocking collectives  63.2 us (35%)
  between operations  14.8 us (8%)
  matrix products  12.3 us (7%)
  local copies, waits for them, and re-layouts  5.58 us (3%)
  other arithmetic  4.23 us (2%)
    reduce_scatter x1, waiting for transfers between devices, body(): lax.psum_scatter(jnp.concatenate([grad_k.reshape(count, kv_local * HD), g...  62.2 us
    all_gather x1, blocking collectives, body(): lax.all_gather(prefix_keys, 'resp', axis=0, tiled=True)  32.5 us
    all_gather x1, blocking collectives, body(): lax.all_gather(prefix_values, 'resp', axis=0, tiled=True)  30.7 us
    reduce_scatter x1, waiting for transfers between devices, body(): lax.psum_scatter(partial_input.astype(jnp.bfloat16), 'head', scatter_dime...  19.3 us
  transfers between devices with their start and end apart: 2, of which 2 were waited for; matrix products, arithmetic and copies ran while one was open for 0% of the time, Pallas kernels for 0%

commit v1 on v0

v1 whole, which is shorter than its diff:
```python
import functools

import jax
import jax.numpy as jnp
from jax import lax
from jax.experimental import pallas as pl
from jax.experimental.pallas import tpu as pltpu
from jax.sharding import PartitionSpec as P

HD = 128
LEN = 256
NT = (((1,), (1,)), ((), ()))


def attention_kernel(lengths_ref, q_ref, g_ref, kv_ref, out_ref):
    scale = HD ** (-0.5)
    tokens, both = kv_ref.shape
    width = both // 2
    kv_local = width // HD
    group = q_ref.shape[1] // HD // kv_local
    for part in range(q_ref.shape[0] // LEN):
        rows = pl.ds(part * LEN, LEN)
        live = lax.broadcasted_iota(jnp.int32, (1, LEN), 1) < lengths_ref[part]
        for k in range(kv_local):
            key_cols = pl.ds(k * HD, HD)
            value_cols = pl.ds(width + k * HD, HD)
            keys = kv_ref[:, key_cols]
            values = kv_ref[:, value_cols]
            grad_k = jnp.zeros((tokens, HD), jnp.float32)
            grad_v = jnp.zeros((tokens, HD), jnp.float32)
            for h in range(group):
                cols = pl.ds((k * group + h) * HD, HD)
                q = q_ref[rows, cols]
                g = g_ref[rows, cols]
                scores = lax.dot_general(keys, q, NT, preferred_element_type=jnp.float32)
                dprobs = lax.dot_general(values, g, NT, preferred_element_type=jnp.float32)
                top = jnp.max(scores, axis=0, keepdims=True)
                expo = jnp.exp((scores - top) * scale)
                total = jnp.sum(expo, axis=0, keepdims=True)
                weighted = jnp.sum(expo * dprobs, axis=0, keepdims=True)
                inverse = 1.0 / total
                delta = weighted * inverse
                factor = jnp.where(live, inverse, 0.0)
                probs = expo * factor
                dscores = probs * ((dprobs - delta) * scale)
                grad_v += jnp.dot(
                    probs.astype(jnp.bfloat16), g, preferred_element_type=jnp.float32
                )
                grad_k += jnp.dot(
                    dscores.astype(jnp.bfloat16), q, preferred_element_type=jnp.float32
                )
            if part:
                grad_k += out_ref[:, key_cols]
                grad_v += out_ref[:, value_cols]
            out_ref[:, key_cols] = grad_k
            out_ref[:, value_cols] = grad_v


def projection_kernel(parts_ref, kw_ref, vw_ref, dk_ref, dv_ref, out_ref):
    width = dk_ref.shape[1]
    total = parts_ref[0].astype(jnp.float32)
    for i in range(1, parts_ref.shape[0]):
        total += parts_ref[i].astype(jnp.float32)
    low = total.astype(jnp.bfloat16)
    dk_ref[...] = low[:, :width]
    dv_ref[...] = low[:, width:]
    out = lax.dot_general(low[:, :width], kw_ref[...], NT, preferred_element_type=jnp.float32)
    out += lax.dot_general(low[:, width:], vw_ref[...], NT, preferred_element_type=jnp.float32)
    out_ref[0] = out.astype(out_ref.dtype)


def body(resp, head, queries, d_out, prefix_keys, prefix_values, k_weight, v_weight, lengths):
    own, width = prefix_keys.shape
    features = k_weight.shape[0] // head
    tokens = resp * own

    both = jnp.concatenate([prefix_keys, prefix_values], axis=1)
    both = jnp.broadcast_to(both[None], (resp, own, 2 * width))
    both = lax.all_to_all(both, "resp", 0, 0, tiled=True).reshape(tokens, 2 * width)

    vmem = pl.BlockSpec(memory_space=pltpu.VMEM)
    partial = pl.pallas_call(
        attention_kernel,
        out_shape=jax.ShapeDtypeStruct((tokens, 2 * width), jnp.float32),
        in_specs=[pl.BlockSpec(memory_space=pltpu.SMEM), vmem, vmem, vmem],
        out_specs=vmem,
        compiler_params=pltpu.CompilerParams(vmem_limit_bytes=40 << 20),
        name="attention",
    )(lengths, queries, d_out, both)

    shares = lax.all_to_all(
        partial.astype(jnp.bfloat16).reshape(resp, own, 2 * width), "resp", 0, 0, tiled=True
    )

    steps = 4
    block = features * head // steps
    per = features // block if block < features else 1
    weight = pl.BlockSpec((block, width), lambda i: (i, 0))
    small = pl.BlockSpec((own, width), lambda i: (0, 0))
    dk_low, dv_low, terms = pl.pallas_call(
        projection_kernel,
        grid=(steps,),
        out_shape=[
            jax.ShapeDtypeStruct((own, width), jnp.bfloat16),
            jax.ShapeDtypeStruct((own, width), jnp.bfloat16),
            jax.ShapeDtypeStruct((head, own, features), jnp.bfloat16),
        ],
        in_specs=[
            pl.BlockSpec((resp, own, 2 * width), lambda i: (0, 0, 0)),
            weight,
            weight,
        ],
        out_specs=[
            small,
            small,
            pl.BlockSpec((1, own, block), lambda i: (i // per, 0, i % per)),
        ],
        compiler_params=pltpu.CompilerParams(vmem_limit_bytes=40 << 20),
        name="projection",
    )(shares, k_weight, v_weight)

    terms = lax.all_to_all(terms, "head", 0, 0, tiled=True)
    input_grad = jnp.sum(terms.astype(jnp.float32), axis=0).astype(jnp.bfloat16)
    return dk_low, dv_low, input_grad


def solution(mesh):
    placed = (
        P("resp", "head"),
        P("resp", "head"),
        P("resp", "head"),
        P("resp", "head"),
        P(None, "head"),
        P(None, "head"),
        P("resp"),
    )
    return jax.shard_map(
        functools.partial(body, mesh.shape["resp"], mesh.shape["head"]),
        mesh=mesh,
        in_specs=placed,
        out_specs=(P("resp", "head"), P("resp", "head"), P("resp", "head")),
        check_vma=False,
    )
```

time: 182 us -> 50.1 us (0.28)
  waiting for transfers between devices: 81.5 us -> 6.69 us
  blocking collectives: 63.2 us -> 18.4 us
  between operations: 14.8 us -> 1.31 us
  matrix products: 12.3 us -> 0 us
  starting transfers between devices: 0.08 us -> 7.25 us
  Pallas kernels: 0 us -> 7.1 us
  other arithmetic: 4.23 us -> 1.41 us
  local copies, waits for them, and re-layouts: 5.58 us -> 7.49 us
    reduce_scatter x2 -> x0, waiting for transfers between devices: 81.4 us -> none  [the longest x1 62.2 us: body(): lax.psum_scatter(jnp.concatenate([grad_k.reshape(count, kv_local * HD), g...]
    all_gather x2 -> x0, blocking collectives: 63.2 us -> none  [the longest x1 32.5 us: body(): lax.all_gather(prefix_keys, 'resp', axis=0, tiled=True)]
    all_to_all x0 -> x2, blocking collectives: none -> 18.4 us  [the longest x1 9.74 us: body(): lax.all_to_all(partial.astype(jnp.bfloat16).reshape(resp, own, 2 * width)...]
    dot_general x6 -> x0, matrix products: 12.3 us -> none  [the longest x1 3.53 us: body(): jnp.einsum('pc,dc->pd', dk_low, k_weight, preferred_element_type=jnp.floa...]
    all_to_all x0 -> x1, starting transfers between devices: none -> 7.25 us  [body(): lax.all_to_all(both, 'resp', 0, 0, tiled=True).reshape(tokens, 2 * width)]
    pallas_call x0 -> x2, Pallas kernels: none -> 7.1 us  [the longest x1 3.96 us: body(): pl.pallas_call(attention_kernel, out_shape=jax.ShapeDtypeStruct((tokens,...]
    all_to_all x0 -> x1, waiting for transfers between devices: none -> 6.69 us  [body(): lax.all_to_all(both, 'resp', 0, 0, tiled=True).reshape(tokens, 2 * width)]
    unnamed x11 -> x8, local copies, waits for them, and re-layouts: 1.99 us -> 6.82 us
  transfers between devices with their start and end apart: 2 -> 1, of which waited for: 2 -> 1; matrix products, arithmetic and copies ran while one was open for 0% -> 0% of each run, Pallas kernels for 0% -> 0%
where the time goes in v1:
time: 50.1 us; the launch traced here: 49.6 us
  blocking collectives  18.4 us (37%)
  local copies, waits for them, and re-layouts  7.49 us (15%)
  starting transfers between devices  7.25 us (14%)
  Pallas kernels  7.1 us (14%)
  waiting for transfers between devices  6.69 us (13%)
  other arithmetic  1.41 us (3%)
  between operations  1.31 us (3%)
    all_to_all x1, blocking collectives, body(): lax.all_to_all(partial.astype(jnp.bfloat16).reshape(resp, own, 2 * width)...  9.74 us
    all_to_all x1, blocking collectives, body(): terms = lax.all_to_all(terms, 'head', 0, 0, tiled=True)  8.61 us
    all_to_all x1, starting transfers between devices, body(): lax.all_to_all(both, 'resp', 0, 0, tiled=True).reshape(tokens, 2 * width)  7.25 us
    unnamed x8, local copies, waits for them, and re-layouts  6.82 us
    all_to_all x1, waiting for transfers between devices, body(): lax.all_to_all(both, 'resp', 0, 0, tiled=True).reshape(tokens, 2 * width)  6.69 us
    pallas_call x1, Pallas kernels, body(): pl.pallas_call(attention_kernel, out_shape=jax.ShapeDtypeStruct((tokens,...  3.96 us
    pallas_call x1, Pallas kernels, body(): pl.pallas_call(projection_kernel, grid=(steps,), out_shape=[jax.ShapeDtyp...  3.14 us
  transfers between devices with their start and end apart: 1, of which 1 were waited for; matrix products, arithmetic and copies ran while one was open for 0% of the time, Pallas kernels for 0%

profile of v1, /device:TPU:0, one launch (start us, length us, event | category | flops | bytes accessed | tf_op | source)
XLA Modules:
  0.0 49.6 jit_solution(5704265822739585875)
XLA Ops:
  0.6 0.7 %pad_maximum_fusion = bf16[16,512]{1,0:T(8,128)(2,1)S(1)} fusion(bf16[16,256]{1,0:T(8,128)(2,1)} %param.10, bf16[16,256]{1,0:T(8,128)(2,1)} %param.9), kind=kLoop, calls=%fused_computation | loop fusion | flops 32768 | bytes 32768 | tf_op jit(solution)/shard_map/concatenate | solution.py:77
  1.3 0.7 %broadcast_in_dim.2 = bf16[8,16,512]{2,1,0:T(8,128)(2,1)} broadcast(bf16[16,512]{1,0:T(8,128)(2,1)S(1)} %pad_maximum_fusion), dimensions={1,2} | broadcast | bytes 147456 | tf_op jit(solution)/shard_map/broadcast_in_dim | solution.py:78
  2.0 7.3 %all-to-all-start = ((bf16[8,16,512]{2,1,0:T(8,128)(2,1)}), bf16[8,16,512]{2,1,0:T(8,128)(2,1)S(1)}, u32[]{:S(2)}, u32[]{:S(2)}) async-start(bf16[8,16,512]{2,1,0:T(8,128)(2,1)} %broadcast_in_dim.2), calls=%async_computation | async-start | bytes 262144 | tf_op jit(solution)/shard_map/all_to_all | solution.py:79
  9.9 6.7 %all-to-all-done = bf16[8,16,512]{2,1,0:T(8,128)(2,1)S(1)} async-done(((bf16[8,16,512]{2,1,0:T(8,128)(2,1)}), bf16[8,16,512]{2,1,0:T(8,128)(2,1)S(1)}, u32[]{:S(2)}, u32[]{:S(2)}) %all-to-all-start) | async-done | bytes 131104 | tf_op jit(solution)/shard_map/all_to_all | solution.py:79
  16.6 0.0 copy-start.2
  16.6 1.2 %copy-done.2 = bf16[256,2048]{1,0:T(8,128)(2,1)S(1)} copy-done((bf16[256,2048]{1,0:T(8,128)(2,1)S(1)}, bf16[256,2048]{1,0:T(8,128)(2,1)}, u32[]{:S(2)}) %copy-start.2) | copy-done | bytes 1048600
  17.8 0.0 copy-start.3
  17.8 1.2 %copy-done.3 = bf16[256,2048]{1,0:T(8,128)(2,1)S(1)} copy-done((bf16[256,2048]{1,0:T(8,128)(2,1)S(1)}, bf16[256,2048]{1,0:T(8,128)(2,1)}, u32[]{:S(2)}) %copy-start.3) | copy-done | bytes 1048600
  19.1 4.0 %attention.1 = f32[128,512]{1,0:T(8,128)S(1)} custom-call(s32[1]{0:T(128)S(6)} %copy.10.lengths_ref, bf16[256,2048]{1,0:T(8,128)(2,1)S(1)} %copy-done.2, bf16[256,2048]{1,0:T(8,128)(2,1)S(1)} %copy-done.3, bf16[128,512]{1,0:T(8,128)(2,1)S(1)} %bitcast.2), custom_call_target="tpu_custom_call" | custom-call | tf_op jit(solution)/shard_map/attention/pallas_call | solution.py:82
  23.1 9.7 %all_to_all.15.parts_ref = bf16[8,16,512]{2,1,0:T(8,128)(2,1)S(1)} all-to-all(bf16[8,16,512]{2,1,0:T(8,128)(2,1)S(1)} %bitcast.3), channel_id=1, replica_groups=mesh['resp'=8,'head'=4] {'resp'}, dimensions={0} | all-to-all | bytes 262144 | tf_op jit(solution)/shard_map/all_to_all | solution.py:91
  32.8 0.0 copy-start
  32.8 2.2 %copy-done = bf16[8192,256]{1,0:T(8,128)(2,1)S(1)} copy-done((bf16[8192,256]{1,0:T(8,128)(2,1)S(1)}, bf16[8192,256]{1,0:T(8,128)(2,1)}, u32[]{:S(2)}) %copy-start) | copy-done | bytes 4194328
  35.0 0.0 copy-start.1
  35.0 2.2 %copy-done.1 = bf16[8192,256]{1,0:T(8,128)(2,1)S(1)} copy-done((bf16[8192,256]{1,0:T(8,128)(2,1)S(1)}, bf16[8192,256]{1,0:T(8,128)(2,1)}, u32[]{:S(2)}) %copy-start.1) | copy-done | bytes 4194328
  37.2 3.1 %projection.1 = (bf16[16,256]{1,0:T(8,128)(2,1)}, bf16[16,256]{1,0:T(8,128)(2,1)}, bf16[4,16,2048]{2,1,0:T(8,128)(2,1)S(1)}) custom-call(bf16[8,16,512]{2,1,0:T(8,128)(2,1)S(1)} %all_to_all.15.parts_ref, bf16[8192,256]{1,0:T(8,128)(2,1)S(1)} %copy-done, bf16[8192,256]{1,0:T(8,128)(2,1)S(1)} %copy-done.1), custom_call_target="tpu_custom_call" | custom-call | tf_op jit(solution)/shard_map/projection/pallas_call | solution.py:100
  40.3 8.6 %all_to_all.16 = bf16[4,16,2048]{2,1,0:T(8,128)(2,1)S(1)} all-to-all(bf16[4,16,2048]{2,1,0:T(8,128)(2,1)S(1)} %get-tuple-element.8), channel_id=1, replica_groups=mesh['resp'=8,'head'=4] {'head'}, dimensions={0} | all-to-all | bytes 524288 | tf_op jit(solution)/shard_map/all_to_all | solution.py:122
  48.9 0.7 %reduce_sum.12 = bf16[16,2048]{1,0:T(8,128)(2,1)} reduce(bf16[4,16,2048]{2,1,0:T(8,128)(2,1)S(1)} %all_to_all.16, bf16[]{:T(256)} %constant.2.clone.1), dimensions={0}, to_apply=%region_0.0 | reduce | flops 98304 | bytes 327682 | tf_op jit(solution)/shard_map/reduce_sum | solution.py:123
  (1 shorter events, 0.0 us)
Async XLA Ops:
  2.0 14.6 %all-to-all-start = ((bf16[8,16,512]{2,1,0:T(8,128)(2,1)}), bf16[8,16,512]{2,1,0:T(8,128)(2,1)S(1)}, u32[]{:S(2)}, u32[]{:S(2)}) async-start(bf16[8,16,512]{2,1,0:T(8,128)(2,1)} %broadcast_in_dim.2), calls=%async_computation | async-start | bytes 262144 | tf_op jit(solution)/shard_map/all_to_all | solution.py:79
  16.6 1.2 %copy-start.2 = (bf16[256,2048]{1,0:T(8,128)(2,1)S(1)}, bf16[256,2048]{1,0:T(8,128)(2,1)}, u32[]{:S(2)}) copy-start(bf16[256,2048]{1,0:T(8,128)(2,1)} %q_ref.1) | copy-start | bytes 3145732
  17.8 1.2 %copy-start.3 = (bf16[256,2048]{1,0:T(8,128)(2,1)S(1)}, bf16[256,2048]{1,0:T(8,128)(2,1)}, u32[]{:S(2)}) copy-start(bf16[256,2048]{1,0:T(8,128)(2,1)} %g_ref.1) | copy-start | bytes 3145732
  32.8 2.2 %copy-start = (bf16[8192,256]{1,0:T(8,128)(2,1)S(1)}, bf16[8192,256]{1,0:T(8,128)(2,1)}, u32[]{:S(2)}) copy-start(bf16[8192,256]{1,0:T(8,128)(2,1)} %kw_ref.1) | copy-start | bytes 12582916
  35.0 2.2 %copy-start.1 = (bf16[8192,256]{1,0:T(8,128)(2,1)S(1)}, bf16[8192,256]{1,0:T(8,128)(2,1)}, u32[]{:S(2)}) copy-start(bf16[8192,256]{1,0:T(8,128)(2,1)} %vw_ref.1) | copy-start | bytes 12582916

commit v2 on v1

v2 whole, which is shorter than its diff:
```python
import functools

import jax
import jax.numpy as jnp
from jax import lax
from jax.experimental import pallas as pl
from jax.experimental.pallas import tpu as pltpu
from jax.sharding import PartitionSpec as P

HD = 128
LEN = 256
NT = (((1,), (1,)), ((), ()))
VMEM_LIMIT = 40 << 20


def prefetch_kernel(*refs):
    count = len(refs) // 2
    sems = refs[-1]
    copies = [
        pltpu.make_async_copy(refs[i], refs[count + i], sems.at[i]) for i in range(count)
    ]
    for copy in copies:
        copy.start()
    for copy in copies:
        copy.wait()


def attention_kernel(lengths_ref, q_ref, g_ref, *refs):
    scale = HD ** (-0.5)
    count = len(refs) // 2
    kv_refs, out_refs = refs[:count], refs[count:]
    own, both = kv_refs[0].shape
    tokens = own * count
    width = both // 2
    kv_local = width // HD
    group = q_ref.shape[1] // HD // kv_local
    lives = [
        lax.broadcasted_iota(jnp.int32, (1, LEN), 1) < lengths_ref[part]
        for part in range(q_ref.shape[0] // LEN)
    ]
    for k in range(kv_local):
        key_cols = pl.ds(k * HD, HD)
        value_cols = pl.ds(width + k * HD, HD)
        keys = jnp.concatenate([ref[:, key_cols] for ref in kv_refs], axis=0)
        values = jnp.concatenate([ref[:, value_cols] for ref in kv_refs], axis=0)
        grad_k = jnp.zeros((tokens, HD), jnp.float32)
        grad_v = jnp.zeros((tokens, HD), jnp.float32)
        for part, live in enumerate(lives):
            rows = pl.ds(part * LEN, LEN)
            for h in range(group):
                cols = pl.ds((k * group + h) * HD, HD)
                q = q_ref[rows, cols]
                g = g_ref[rows, cols]
                scores = lax.dot_general(keys, q, NT, preferred_element_type=jnp.float32)
                dprobs = lax.dot_general(values, g, NT, preferred_element_type=jnp.float32)
                top = jnp.max(scores, axis=0, keepdims=True)
                expo = jnp.exp((scores - top) * scale)
                total = jnp.sum(expo, axis=0, keepdims=True)
                weighted = jnp.sum(expo * dprobs, axis=0, keepdims=True)
                inverse = 1.0 / total
                delta = weighted * inverse
                factor = jnp.where(live, inverse, 0.0)
                probs = expo * factor
                dscores = probs * ((dprobs - delta) * scale)
                grad_v += jnp.dot(
                    probs.astype(jnp.bfloat16), g, preferred_element_type=jnp.float32
                )
                grad_k += jnp.dot(
                    dscores.astype(jnp.bfloat16), q, preferred_element_type=jnp.float32
                )
        for i, ref in enumerate(out_refs):
            rows = slice(i * own, (i + 1) * own)
            ref[:, key_cols] = grad_k[rows].astype(ref.dtype)
            ref[:, value_cols] = grad_v[rows].astype(ref.dtype)


def projection_kernel(count, head, *refs):
    parts, (kw_ref, vw_ref, dk_ref, dv_ref), out_refs = (
        refs[:count],
        refs[count : count + 4],
        refs[count + 4 :],
    )
    width = dk_ref.shape[1]
    total = parts[0][...]
    for ref in parts[1:]:
        total += ref[...].astype(jnp.float32)
    low = total.astype(jnp.bfloat16)
    dk_ref[...] = low[:, :width]
    dv_ref[...] = low[:, width:]
    features = out_refs[0].shape[1]
    me = lax.axis_index("head")
    for i, ref in enumerate(out_refs):
        rows = pl.ds(pl.multiple_of(lax.rem(me + i, head) * features, features), features)
        out = lax.dot_general(
            low[:, :width], kw_ref[rows, :], NT, preferred_element_type=jnp.float32
        )
        out += lax.dot_general(
            low[:, width:], vw_ref[rows, :], NT, preferred_element_type=jnp.float32
        )
        ref[...] = out.astype(ref.dtype)


def shift(x, axis, count, by):
    return lax.ppermute(x, axis, [(i, (i + by) % count) for i in range(count)])


def body(resp, head, queries, d_out, prefix_keys, prefix_values, k_weight, v_weight, lengths):
    own, width = prefix_keys.shape
    features = k_weight.shape[0] // head
    vmem = pl.BlockSpec(memory_space=pltpu.VMEM)
    hbm = pl.BlockSpec(memory_space=pltpu.HBM)
    params = pltpu.CompilerParams(vmem_limit_bytes=VMEM_LIMIT)

    both = jnp.concatenate([prefix_keys, prefix_values], axis=1)
    blocks = [both] + [shift(both, "resp", resp, d) for d in range(1, resp)]

    large = (queries, d_out, k_weight, v_weight)
    queries, d_out, k_weight, v_weight = pl.pallas_call(
        prefetch_kernel,
        out_shape=[pltpu.VMEM(x.shape, x.dtype) for x in large],
        in_specs=[hbm] * len(large),
        out_specs=[vmem] * len(large),
        scratch_shapes=[pltpu.SemaphoreType.DMA((len(large),))],
        compiler_params=params,
        cost_estimate=pl.CostEstimate(
            flops=0, transcendentals=0, bytes_accessed=sum(x.size * 2 for x in large)
        ),
        name="prefetch",
    )(*[pltpu.with_memory_space_constraint(x, pltpu.HBM) for x in large])

    partial = pl.pallas_call(
        attention_kernel,
        out_shape=[jax.ShapeDtypeStruct((own, 2 * width), jnp.float32)]
        + [jax.ShapeDtypeStruct((own, 2 * width), jnp.bfloat16)] * (resp - 1),
        in_specs=[pl.BlockSpec(memory_space=pltpu.SMEM)] + [vmem] * (resp + 2),
        out_specs=[vmem] * resp,
        compiler_params=params,
        name="attention",
    )(lengths, queries, d_out, *blocks)

    shares = [partial[0]] + [shift(partial[d], "resp", resp, resp - d) for d in range(1, resp)]

    dk_low, dv_low, *terms = pl.pallas_call(
        functools.partial(projection_kernel, resp, head),
        out_shape=[jax.ShapeDtypeStruct((own, width), jnp.bfloat16)] * 2
        + [jax.ShapeDtypeStruct((own, features), jnp.float32)]
        + [jax.ShapeDtypeStruct((own, features), jnp.bfloat16)] * (head - 1),
        in_specs=[vmem] * (resp + 2),
        out_specs=[vmem] * (head + 2),
        compiler_params=params,
        name="projection",
    )(*shares, k_weight, v_weight)

    total = terms[0]
    for d in range(1, head):
        total += shift(terms[d], "head", head, d).astype(jnp.float32)
    return dk_low, dv_low, total.astype(jnp.bfloat16)


def solution(mesh):
    placed = (
        P("resp", "head"),
        P("resp", "head"),
        P("resp", "head"),
        P("resp", "head"),
        P(None, "head"),
        P(None, "head"),
        P("resp"),
    )
    return jax.shard_map(
        functools.partial(body, mesh.shape["resp"], mesh.shape["head"]),
        mesh=mesh,
        in_specs=placed,
        out_specs=(P("resp", "head"), P("resp", "head"), P("resp", "head")),
        check_vma=False,
    )
```

time: 50.1 us -> 49.7 us (level)
  starting transfers between devices: 7.25 us -> 26.1 us
  blocking collectives: 18.4 us -> 0 us
  local copies, waits for them, and re-layouts: 7.49 us -> 1.4 us
  Pallas kernels: 7.1 us -> 10.8 us
  waiting for transfers between devices: 6.69 us -> 8.86 us
  other arithmetic: 1.41 us -> 0.66 us
    ppermute x0 -> x17, starting transfers between devices: none -> 26.1 us  [shift(): return lax.ppermute(x, axis, [(i, (i + by) % count) for i in range(count)])]
    all_to_all x2 -> x0, blocking collectives: 18.4 us -> none  [the longest x1 9.74 us: body(): lax.all_to_all(partial.astype(jnp.bfloat16).reshape(resp, own, 2 * width)...]
    ppermute x0 -> x17, waiting for transfers between devices: none -> 8.86 us  [shift(): return lax.ppermute(x, axis, [(i, (i + by) % count) for i in range(count)])]
    all_to_all x1 -> x0, starting transfers between devices: 7.25 us -> none  [body(): lax.all_to_all(both, 'resp', 0, 0, tiled=True).reshape(tokens, 2 * width)]
    all_to_all x1 -> x0, waiting for transfers between devices: 6.69 us -> none  [body(): lax.all_to_all(both, 'resp', 0, 0, tiled=True).reshape(tokens, 2 * width)]
    unnamed x8 -> x1, local copies, waits for them, and re-layouts: 6.82 us -> 0.7 us
    pallas_call x2 -> x3, Pallas kernels: 7.1 us -> 10.8 us  [the longest x1 4.09 us: body(): pl.pallas_call(prefetch_kernel, out_shape=[pltpu.VMEM(x.shape, x.dtype) f...]
    concatenate x1 -> x0, other arithmetic: 0.72 us -> none  [body(): both = jnp.concatenate([prefix_keys, prefix_values], axis=1)]
  transfers between devices with their start and end apart: 1 -> 17, of which waited for: 1 -> 7; matrix products, arithmetic and copies ran while one was open for 0% -> 0% of each run, Pallas kernels for 0% -> 8%
where the time goes in v2:
time: 49.7 us; the launch traced here: 49.2 us
  starting transfers between devices  26.1 us (53%)
  Pallas kernels  10.8 us (22%)
  waiting for transfers between devices  8.86 us (18%)
  local copies, waits for them, and re-layouts  1.4 us (3%)
  between operations  1.36 us (3%)
  other arithmetic  0.66 us (1%)
    ppermute x17, starting transfers between devices, shift(): return lax.ppermute(x, axis, [(i, (i + by) % count) for i in range(count)])  26.1 us
    ppermute x17, waiting for transfers between devices, shift(): return lax.ppermute(x, axis, [(i, (i + by) % count) for i in range(count)])  8.86 us
    pallas_call x1, Pallas kernels, body(): pl.pallas_call(prefetch_kernel, out_shape=[pltpu.VMEM(x.shape, x.dtype) f...  4.09 us
    pallas_call x1, Pallas kernels, body(): pl.pallas_call(attention_kernel, out_shape=[jax.ShapeDtypeStruct((own, 2...  3.96 us
    pallas_call x1, Pallas kernels, body(): pl.pallas_call(functools.partial(projection_kernel, resp, head), out_shap...  2.78 us
  transfers between devices with their start and end apart: 17, of which 7 were waited for; matrix products, arithmetic and copies ran while one was open for 0% of the time, Pallas kernels for 8%

profile of v2, /device:TPU:0, one launch (start us, length us, event | category | flops | bytes accessed | tf_op | source)
XLA Modules:
  0.0 49.2 jit_solution(6844490758464258181)
XLA Ops:
  0.6 0.7 %constant_dynamic-update-slice_fusion.1 = bf16[16,512]{1,0:T(8,128)(2,1)S(1)} fusion(bf16[16,256]{1,0:T(8,128)(2,1)} %param.9), kind=kLoop, calls=%fused_computation.2 | loop fusion | bytes 16384
  1.3 0.7 %constant_dynamic-update-slice_fusion.refs_0_ = bf16[16,512]{1,0:T(8,128)(2,1)S(1)} fusion(bf16[16,512]{1,0:T(8,128)(2,1)S(1)} %constant_dynamic-update-slice_fusion.1, bf16[16,256]{1,0:T(8,128)(2,1)} %param.10), kind=kLoop, calls=%fused_computation.1 | loop fusion | bytes 16384 | tf_op jit(solution)/shard_map/concatenate | solution.py:114
  2.0 6.0 %collective-permute-start.6 = (bf16[16,512]{1,0:T(8,128)(2,1)S(1)}, bf16[16,512]{1,0:T(8,128)(2,1)S(1)}, u32[]{:S(2)}, u32[]{:S(2)}) collective-permute-start(bf16[16,512]{1,0:T(8,128)(2,1)S(1)} %constant_dynamic-update-slice_fusion.refs_0_), channel_id=1, source_target_pairs={{0,28},{4,0},{8,4},{12,8},{16,12},{20,16},{24,20},{28,24},{1,29},{... | collective-permute-start | bytes 49160 | tf_op jit(solution)/shard_map/ppermute | solution.py:104
  8.0 0.4 collective-permute-start.5
  8.5 0.0 collective-permute-start.4
  8.5 3.0 %collective-permute-start.3 = (bf16[16,512]{1,0:T(8,128)(2,1)S(1)}, bf16[16,512]{1,0:T(8,128)(2,1)S(1)}, u32[]{:S(2)}, u32[]{:S(2)}) collective-permute-start(bf16[16,512]{1,0:T(8,128)(2,1)S(1)} %constant_dynamic-update-slice_fusion.refs_0_), channel_id=1, source_target_pairs={{0,16},{4,20},{8,24},{12,28},{16,0},{20,4},{24,8},{28,12},{1,17},{... | collective-permute-start | bytes 49160 | tf_op jit(solution)/shard_map/ppermute | solution.py:104
  11.5 0.0 collective-permute-start.2
  11.5 0.0 collective-permute-done.6.refs_7_
  11.5 1.8 %collective-permute-start.1 = (bf16[16,512]{1,0:T(8,128)(2,1)S(1)}, bf16[16,512]{1,0:T(8,128)(2,1)S(1)}, u32[]{:S(2)}, u32[]{:S(2)}) collective-permute-start(bf16[16,512]{1,0:T(8,128)(2,1)S(1)} %constant_dynamic-update-slice_fusion.refs_0_), channel_id=1, source_target_pairs={{0,8},{4,12},{8,16},{12,20},{16,24},{20,28},{24,0},{28,4},{1,9},{5... | collective-permute-start | bytes 49160 | tf_op jit(solution)/shard_map/ppermute | solution.py:104
  13.3 0.0 collective-permute-done.5.refs_6_
  13.3 1.1 %collective-permute-start = (bf16[16,512]{1,0:T(8,128)(2,1)S(1)}, bf16[16,512]{1,0:T(8,128)(2,1)S(1)}, u32[]{:S(2)}, u32[]{:S(2)}) collective-permute-start(bf16[16,512]{1,0:T(8,128)(2,1)S(1)} %constant_dynamic-update-slice_fusion.refs_0_), channel_id=1, source_target_pairs={{0,4},{4,8},{8,12},{12,16},{16,20},{20,24},{24,28},{28,0},{1,5},{5... | collective-permute-start | bytes 49160 | tf_op jit(solution)/shard_map/ppermute | solution.py:104
  15.1 4.1 %prefetch.1 = (bf16[256,2048]{1,0:T(8,128)(2,1)S(1)}, bf16[256,2048]{1,0:T(8,128)(2,1)S(1)}, bf16[8192,256]{1,0:T(8,128)(2,1)S(1)}, bf16[8192,256]{1,0:T(8,128)(2,1)S(1)}) custom-call(bf16[256,2048]{1,0:T(8,128)(2,1)} %refs_0_.1, bf16[256,2048]{1,0:T(8,128)(2,1)} %refs_1_.1, bf16[8192,256]{1,0:T(8,128)(2,1)} %refs_2_.1, bf16[8192,256]{1,0:T(8,128)(2,1)} %refs_3_.1), custom_call_target="tpu_custom_call" | custom-call | bytes 10485760 | tf_op jit(solution)/shard_map/prefetch/pallas_call | solution.py:118
  19.2 0.0 collective-permute-done.4.refs_5_
  19.2 0.0 collective-permute-done.3.refs_4_
  19.2 0.0 collective-permute-done.2.refs_3_
  19.2 0.0 collective-permute-done.1.refs_2_
  19.2 0.5 %collective-permute-done.refs_1_ = bf16[16,512]{1,0:T(8,128)(2,1)S(1)} collective-permute-done((bf16[16,512]{1,0:T(8,128)(2,1)S(1)}, bf16[16,512]{1,0:T(8,128)(2,1)S(1)}, u32[]{:S(2)}, u32[]{:S(2)}) %collective-permute-start) | collective-permute-done | bytes 16416 | tf_op jit(solution)/shard_map/ppermute | solution.py:104
  19.7 4.0 %attention.1 = (f32[16,512]{1,0:T(8,128)S(1)}, bf16[16,512]{1,0:T(8,128)(2,1)S(1)}, bf16[16,512]{1,0:T(8,128)(2,1)S(1)}, bf16[16,512]{1,0:T(8,128)(2,1)S(1)}, bf...) custom-call(s32[1]{0:T(128)S(6)} %copy.11.lengths_ref, ...), custom_call_target="tpu_custom_call" | custom-call | tf_op jit(solution)/shard_map/attention/pallas_call | solution.py:131
  23.7 3.2 %collective-permute-start.7 = (bf16[16,512]{1,0:T(8,128)(2,1)S(1)}, bf16[16,512]{1,0:T(8,128)(2,1)S(1)}, u32[]{:S(2)}, u32[]{:S(2)}) collective-permute-start(bf16[16,512]{1,0:T(8,128)(2,1)S(1)} %get-tuple-element.24), channel_id=1, source_target_pairs={{0,28},{4,0},{8,4},{12,8},{16,12},{20,16},{24,20},{28,24},{1,29},{... | collective-permute-start | bytes 49160 | tf_op jit(solution)/shard_map/ppermute | solution.py:104
  26.9 1.2 %collective-permute-start.8 = (bf16[16,512]{1,0:T(8,128)(2,1)S(1)}, bf16[16,512]{1,0:T(8,128)(2,1)S(1)}, u32[]{:S(2)}, u32[]{:S(2)}) collective-permute-start(bf16[16,512]{1,0:T(8,128)(2,1)S(1)} %get-tuple-element.25), channel_id=1, source_target_pairs={{0,24},{4,28},{8,0},{12,4},{16,8},{20,12},{24,16},{28,20},{1,25},{... | collective-permute-start | bytes 49160 | tf_op jit(solution)/shard_map/ppermute | solution.py:104
  28.0 0.6 %collective-permute-start.9 = (bf16[16,512]{1,0:T(8,128)(2,1)S(1)}, bf16[16,512]{1,0:T(8,128)(2,1)S(1)}, u32[]{:S(2)}, u32[]{:S(2)}) collective-permute-start(bf16[16,512]{1,0:T(8,128)(2,1)S(1)} %get-tuple-element.26), channel_id=1, source_target_pairs={{0,20},{4,24},{8,28},{12,0},{16,4},{20,8},{24,12},{28,16},{1,21},{... | collective-permute-start | bytes 49160 | tf_op jit(solution)/shard_map/ppermute | solution.py:104
  28.6 1.4 %collective-permute-start.10 = (bf16[16,512]{1,0:T(8,128)(2,1)S(1)}, bf16[16,512]{1,0:T(8,128)(2,1)S(1)}, u32[]{:S(2)}, u32[]{:S(2)}) collective-permute-start(bf16[16,512]{1,0:T(8,128)(2,1)S(1)} %get-tuple-element.27), channel_id=1, source_target_pairs={{0,16},{4,20},{8,24},{12,28},{16,0},{20,4},{24,8},{28,12},{1,17},{... | collective-permute-start | bytes 49160 | tf_op jit(solution)/shard_map/ppermute | solution.py:104
  30.0 1.5 %collective-permute-start.11 = (bf16[16,512]{1,0:T(8,128)(2,1)S(1)}, bf16[16,512]{1,0:T(8,128)(2,1)S(1)}, u32[]{:S(2)}, u32[]{:S(2)}) collective-permute-start(bf16[16,512]{1,0:T(8,128)(2,1)S(1)} %get-tuple-element.28), channel_id=1, source_target_pairs={{0,12},{4,16},{8,20},{12,24},{16,28},{20,0},{24,4},{28,8},{1,13},{... | collective-permute-start | bytes 49160 | tf_op jit(solution)/shard_map/ppermute | solution.py:104
  31.5 0.0 collective-permute-done.7.refs_1_
  31.5 2.9 %collective-permute-start.12 = (bf16[16,512]{1,0:T(8,128)(2,1)S(1)}, bf16[16,512]{1,0:T(8,128)(2,1)S(1)}, u32[]{:S(2)}, u32[]{:S(2)}) collective-permute-start(bf16[16,512]{1,0:T(8,128)(2,1)S(1)} %get-tuple-element.29), channel_id=1, source_target_pairs={{0,8},{4,12},{8,16},{12,20},{16,24},{20,28},{24,0},{28,4},{1,9},{5... | collective-permute-start | bytes 49160 | tf_op jit(solution)/shard_map/ppermute | solution.py:104
  34.4 0.0 collective-permute-done.8.refs_2_
  34.4 0.0 collective-permute-start.13
  34.4 0.0 collective-permute-done.9.refs_3_
  34.4 0.0 collective-permute-done.10.refs_4_
  34.4 1.6 %collective-permute-done.11.refs_5_ = bf16[16,512]{1,0:T(8,128)(2,1)S(1)} collective-permute-done((bf16[16,512]{1,0:T(8,128)(2,1)S(1)}, bf16[16,512]{1,0:T(8,128)(2,1)S(1)}, u32[]{:S(2)}, u32[]{:S(2)}) %collective-permute-start.11) | collective-permute-done | bytes 16416 | tf_op jit(solution)/shard_map/ppermute | solution.py:104
  36.1 0.9 %collective-permute-done.12.refs_6_ = bf16[16,512]{1,0:T(8,128)(2,1)S(1)} collective-permute-done((bf16[16,512]{1,0:T(8,128)(2,1)S(1)}, bf16[16,512]{1,0:T(8,128)(2,1)S(1)}, u32[]{:S(2)}, u32[]{:S(2)}) %collective-permute-start.12) | collective-permute-done | bytes 16416 | tf_op jit(solution)/shard_map/ppermute | solution.py:104
  37.0 3.8 %collective-permute-done.13.refs_7_ = bf16[16,512]{1,0:T(8,128)(2,1)S(1)} collective-permute-done((bf16[16,512]{1,0:T(8,128)(2,1)S(1)}, bf16[16,512]{1,0:T(8,128)(2,1)S(1)}, u32[]{:S(2)}, u32[]{:S(2)}) %collective-permute-start.13) | collective-permute-done | bytes 16416 | tf_op jit(solution)/shard_map/ppermute | solution.py:104
  40.8 2.8 %projection.1 = (bf16[16,256]{1,0:T(8,128)(2,1)}, bf16[16,256]{1,0:T(8,128)(2,1)}, f32[16,2048]{1,0:T(8,128)S(1)}, bf16[16,2048]{1,0:T(8,128)(2,1)S(1)}, bf16[16...) custom-call(f32[16,512]{1,0:T(8,128)S(1)} %get-tuple-element.23.refs_0_, ...), custom_call_target="tpu_custom_call" | custom-call | tf_op jit(solution)/shard_map/projection/pallas_call | solution.py:143
  43.6 0.0 collective-permute-start.14
  43.6 1.5 %collective-permute-start.15 = (bf16[16,2048]{1,0:T(8,128)(2,1)S(1)}, bf16[16,2048]{1,0:T(8,128)(2,1)S(1)}, u32[]{:S(2)}, u32[]{:S(2)}) collective-permute-start(bf16[16,2048]{1,0:T(8,128)(2,1)S(1)} %get-tuple-element.37), channel_id=1, source_target_pairs={{0,2},{1,3},{2,0},{3,1},{4,6},{5,7},{6,4},{7,5},{8,10},{9,11},{10,... | collective-permute-start | bytes 196616 | tf_op jit(solution)/shard_map/ppermute | solution.py:104
  45.2 1.4 %collective-permute-start.16 = (bf16[16,2048]{1,0:T(8,128)(2,1)S(1)}, bf16[16,2048]{1,0:T(8,128)(2,1)S(1)}, u32[]{:S(2)}, u32[]{:S(2)}) collective-permute-start(bf16[16,2048]{1,0:T(8,128)(2,1)S(1)} %get-tuple-element.38), channel_id=1, source_target_pairs={{0,3},{1,0},{2,1},{3,2},{4,7},{5,4},{6,5},{7,6},{8,11},{9,8},{10,9... | collective-permute-start | bytes 196616 | tf_op jit(solution)/shard_map/ppermute | solution.py:104
  46.6 0.9 %collective-permute-done.14 = bf16[16,2048]{1,0:T(8,128)(2,1)S(1)} collective-permute-done((bf16[16,2048]{1,0:T(8,128)(2,1)S(1)}, bf16[16,2048]{1,0:T(8,128)(2,1)S(1)}, u32[]{:S(2)}, u32[]{:S(2)}) %collective-permute-start.14) | collective-permute-done | bytes 65568 | tf_op jit(solution)/shard_map/ppermute | solution.py:104
  47.5 0.8 %collective-permute-done.15 = bf16[16,2048]{1,0:T(8,128)(2,1)S(1)} collective-permute-done((bf16[16,2048]{1,0:T(8,128)(2,1)S(1)}, bf16[16,2048]{1,0:T(8,128)(2,1)S(1)}, u32[]{:S(2)}, u32[]{:S(2)}) %collective-permute-start.15) | collective-permute-done | bytes 65568 | tf_op jit(solution)/shard_map/ppermute | solution.py:104
  48.2 0.3 collective-permute-done.16
  48.5 0.7 %add_convert_fusion = bf16[16,2048]{1,0:T(8,128)(2,1)} fusion(bf16[16,2048]{1,0:T(8,128)(2,1)S(1)} %collective-permute-done.16, bf16[16,2048]{1,0:T(8,128)(2,1)S(1)} %collective-permute-done.15, f32[16,2048]{1,0:T(8,128)S(1)} %get-tuple-element.35, bf16[16,2048]{1,0:T(8,128)(2,1)S(1)} %collective-permute-done.14), kind=kLoop, calls=%fused_computation | loop fusion | flops 229376 | bytes 393216 | tf_op jit(solution)/shard_map/convert_element_type | solution.py:157
Async XLA Ops:
  2.0 9.4 %collective-permute-start.6 = (bf16[16,512]{1,0:T(8,128)(2,1)S(1)}, bf16[16,512]{1,0:T(8,128)(2,1)S(1)}, u32[]{:S(2)}, u32[]{:S(2)}) collective-permute-start(bf16[16,512]{1,0:T(8,128)(2,1)S(1)} %constant_dynamic-update-slice_fusion.refs_0_), channel_id=1, source_target_pairs={{0,28},{4,0},{8,4},{12,8},{16,12},{20,16},{24,20},{28,24},{1,29},{... | collective-permute-start | bytes 49160 | tf_op jit(solution)/shard_map/ppermute | solution.py:104
  8.0 5.3 %collective-permute-start.5 = (bf16[16,512]{1,0:T(8,128)(2,1)S(1)}, bf16[16,512]{1,0:T(8,128)(2,1)S(1)}, u32[]{:S(2)}, u32[]{:S(2)}) collective-permute-start(bf16[16,512]{1,0:T(8,128)(2,1)S(1)} %constant_dynamic-update-slice_fusion.refs_0_), channel_id=1, source_target_pairs={{0,24},{4,28},{8,0},{12,4},{16,8},{20,12},{24,16},{28,20},{1,25},{... | collective-permute-start | bytes 49160 | tf_op jit(solution)/shard_map/ppermute | solution.py:104
  8.5 10.7 %collective-permute-start.4 = (bf16[16,512]{1,0:T(8,128)(2,1)S(1)}, bf16[16,512]{1,0:T(8,128)(2,1)S(1)}, u32[]{:S(2)}, u32[]{:S(2)}) collective-permute-start(bf16[16,512]{1,0:T(8,128)(2,1)S(1)} %constant_dynamic-update-slice_fusion.refs_0_), channel_id=1, source_target_pairs={{0,20},{4,24},{8,28},{12,0},{16,4},{20,8},{24,12},{28,16},{1,21},{... | collective-permute-start | bytes 49160 | tf_op jit(solution)/shard_map/ppermute | solution.py:104
  8.5 10.7 %collective-permute-start.3 = (bf16[16,512]{1,0:T(8,128)(2,1)S(1)}, bf16[16,512]{1,0:T(8,128)(2,1)S(1)}, u32[]{:S(2)}, u32[]{:S(2)}) collective-permute-start(bf16[16,512]{1,0:T(8,128)(2,1)S(1)} %constant_dynamic-update-slice_fusion.refs_0_), channel_id=1, source_target_pairs={{0,16},{4,20},{8,24},{12,28},{16,0},{20,4},{24,8},{28,12},{1,17},{... | collective-permute-start | bytes 49160 | tf_op jit(solution)/shard_map/ppermute | solution.py:104
  11.5 7.7 %collective-permute-start.2 = (bf16[16,512]{1,0:T(8,128)(2,1)S(1)}, bf16[16,512]{1,0:T(8,128)(2,1)S(1)}, u32[]{:S(2)}, u32[]{:S(2)}) collective-permute-start(bf16[16,512]{1,0:T(8,128)(2,1)S(1)} %constant_dynamic-update-slice_fusion.refs_0_), channel_id=1, source_target_pairs={{0,12},{4,16},{8,20},{12,24},{16,28},{20,0},{24,4},{28,8},{1,13},{... | collective-permute-start | bytes 49160 | tf_op jit(solution)/shard_map/ppermute | solution.py:104
  11.5 7.7 %collective-permute-start.1 = (bf16[16,512]{1,0:T(8,128)(2,1)S(1)}, bf16[16,512]{1,0:T(8,128)(2,1)S(1)}, u32[]{:S(2)}, u32[]{:S(2)}) collective-permute-start(bf16[16,512]{1,0:T(8,128)(2,1)S(1)} %constant_dynamic-update-slice_fusion.refs_0_), channel_id=1, source_target_pairs={{0,8},{4,12},{8,16},{12,20},{16,24},{20,28},{24,0},{28,4},{1,9},{5... | collective-permute-start | bytes 49160 | tf_op jit(solution)/shard_map/ppermute | solution.py:104
  13.3 6.4 %collective-permute-start = (bf16[16,512]{1,0:T(8,128)(2,1)S(1)}, bf16[16,512]{1,0:T(8,128)(2,1)S(1)}, u32[]{:S(2)}, u32[]{:S(2)}) collective-permute-start(bf16[16,512]{1,0:T(8,128)(2,1)S(1)} %constant_dynamic-update-slice_fusion.refs_0_), channel_id=1, source_target_pairs={{0,4},{4,8},{8,12},{12,16},{16,20},{20,24},{24,28},{28,0},{1,5},{5... | collective-permute-start | bytes 49160 | tf_op jit(solution)/shard_map/ppermute | solution.py:104
  23.7 7.8 %collective-permute-start.7 = (bf16[16,512]{1,0:T(8,128)(2,1)S(1)}, bf16[16,512]{1,0:T(8,128)(2,1)S(1)}, u32[]{:S(2)}, u32[]{:S(2)}) collective-permute-start(bf16[16,512]{1,0:T(8,128)(2,1)S(1)} %get-tuple-element.24), channel_id=1, source_target_pairs={{0,28},{4,0},{8,4},{12,8},{16,12},{20,16},{24,20},{28,24},{1,29},{... | collective-permute-start | bytes 49160 | tf_op jit(solution)/shard_map/ppermute | solution.py:104
  26.9 7.5 %collective-permute-start.8 = (bf16[16,512]{1,0:T(8,128)(2,1)S(1)}, bf16[16,512]{1,0:T(8,128)(2,1)S(1)}, u32[]{:S(2)}, u32[]{:S(2)}) collective-permute-start(bf16[16,512]{1,0:T(8,128)(2,1)S(1)} %get-tuple-element.25), channel_id=1, source_target_pairs={{0,24},{4,28},{8,0},{12,4},{16,8},{20,12},{24,16},{28,20},{1,25},{... | collective-permute-start | bytes 49160 | tf_op jit(solution)/shard_map/ppermute | solution.py:104
  28.0 6.4 %collective-permute-start.9 = (bf16[16,512]{1,0:T(8,128)(2,1)S(1)}, bf16[16,512]{1,0:T(8,128)(2,1)S(1)}, u32[]{:S(2)}, u32[]{:S(2)}) collective-permute-start(bf16[16,512]{1,0:T(8,128)(2,1)S(1)} %get-tuple-element.26), channel_id=1, source_target_pairs={{0,20},{4,24},{8,28},{12,0},{16,4},{20,8},{24,12},{28,16},{1,21},{... | collective-permute-start | bytes 49160 | tf_op jit(solution)/shard_map/ppermute | solution.py:104
  28.6 5.8 %collective-permute-start.10 = (bf16[16,512]{1,0:T(8,128)(2,1)S(1)}, bf16[16,512]{1,0:T(8,128)(2,1)S(1)}, u32[]{:S(2)}, u32[]{:S(2)}) collective-permute-start(bf16[16,512]{1,0:T(8,128)(2,1)S(1)} %get-tuple-element.27), channel_id=1, source_target_pairs={{0,16},{4,20},{8,24},{12,28},{16,0},{20,4},{24,8},{28,12},{1,17},{... | collective-permute-start | bytes 49160 | tf_op jit(solution)/shard_map/ppermute | solution.py:104
  30.0 6.0 %collective-permute-start.11 = (bf16[16,512]{1,0:T(8,128)(2,1)S(1)}, bf16[16,512]{1,0:T(8,128)(2,1)S(1)}, u32[]{:S(2)}, u32[]{:S(2)}) collective-permute-start(bf16[16,512]{1,0:T(8,128)(2,1)S(1)} %get-tuple-element.28), channel_id=1, source_target_pairs={{0,12},{4,16},{8,20},{12,24},{16,28},{20,0},{24,4},{28,8},{1,13},{... | collective-permute-start | bytes 49160 | tf_op jit(solution)/shard_map/ppermute | solution.py:104
  31.5 5.5 %collective-permute-start.12 = (bf16[16,512]{1,0:T(8,128)(2,1)S(1)}, bf16[16,512]{1,0:T(8,128)(2,1)S(1)}, u32[]{:S(2)}, u32[]{:S(2)}) collective-permute-start(bf16[16,512]{1,0:T(8,128)(2,1)S(1)} %get-tuple-element.29), channel_id=1, source_target_pairs={{0,8},{4,12},{8,16},{12,20},{16,24},{20,28},{24,0},{28,4},{1,9},{5... | collective-permute-start | bytes 49160 | tf_op jit(solution)/shard_map/ppermute | solution.py:104
  34.4 6.4 %collective-permute-start.13 = (bf16[16,512]{1,0:T(8,128)(2,1)S(1)}, bf16[16,512]{1,0:T(8,128)(2,1)S(1)}, u32[]{:S(2)}, u32[]{:S(2)}) collective-permute-start(bf16[16,512]{1,0:T(8,128)(2,1)S(1)} %get-tuple-element.30), channel_id=1, source_target_pairs={{0,4},{4,8},{8,12},{12,16},{16,20},{20,24},{24,28},{28,0},{1,5},{5... | collective-permute-start | bytes 49160 | tf_op jit(solution)/shard_map/ppermute | solution.py:104
  43.6 3.8 %collective-permute-start.14 = (bf16[16,2048]{1,0:T(8,128)(2,1)S(1)}, bf16[16,2048]{1,0:T(8,128)(2,1)S(1)}, u32[]{:S(2)}, u32[]{:S(2)}) collective-permute-start(bf16[16,2048]{1,0:T(8,128)(2,1)S(1)} %get-tuple-element.36), channel_id=1, source_target_pairs={{0,1},{1,2},{2,3},{3,0},{4,5},{5,6},{6,7},{7,4},{8,9},{9,10},{10,1... | collective-permute-start | bytes 196616 | tf_op jit(solution)/shard_map/ppermute | solution.py:104
  43.6 4.6 %collective-permute-start.15 = (bf16[16,2048]{1,0:T(8,128)(2,1)S(1)}, bf16[16,2048]{1,0:T(8,128)(2,1)S(1)}, u32[]{:S(2)}, u32[]{:S(2)}) collective-permute-start(bf16[16,2048]{1,0:T(8,128)(2,1)S(1)} %get-tuple-element.37), channel_id=1, source_target_pairs={{0,2},{1,3},{2,0},{3,1},{4,6},{5,7},{6,4},{7,5},{8,10},{9,11},{10,... | collective-permute-start | bytes 196616 | tf_op jit(solution)/shard_map/ppermute | solution.py:104
  45.2 3.3 %collective-permute-start.16 = (bf16[16,2048]{1,0:T(8,128)(2,1)S(1)}, bf16[16,2048]{1,0:T(8,128)(2,1)S(1)}, u32[]{:S(2)}, u32[]{:S(2)}) collective-permute-start(bf16[16,2048]{1,0:T(8,128)(2,1)S(1)} %get-tuple-element.38), channel_id=1, source_target_pairs={{0,3},{1,0},{2,1},{3,2},{4,7},{5,4},{6,5},{7,6},{8,11},{9,8},{10,9... | collective-permute-start | bytes 196616 | tf_op jit(solution)/shard_map/ppermute | solution.py:104

commit v3 on v2

v3 whole, which is shorter than its diff:
```python
import functools

import jax
import jax.numpy as jnp
from jax import lax
from jax.experimental import pallas as pl
from jax.experimental.pallas import tpu as pltpu
from jax.sharding import PartitionSpec as P

HD = 128
LEN = 256
NT = (((1,), (1,)), ((), ()))
VMEM_LIMIT = 40 << 20


def join_kernel(k_hbm, v_hbm, out_ref, sems):
    width = k_hbm.shape[1]
    copies = [
        pltpu.make_async_copy(k_hbm, out_ref.at[:, pl.ds(0, width)], sems.at[0]),
        pltpu.make_async_copy(v_hbm, out_ref.at[:, pl.ds(width, width)], sems.at[1]),
    ]
    for copy in copies:
        copy.start()
    for copy in copies:
        copy.wait()


def attention_kernel(
    lengths_ref,
    near_ref,
    far_ref,
    q_hbm,
    g_hbm,
    kw_hbm,
    vw_hbm,
    keep_ref,
    send_ref,
    kw_ref,
    vw_ref,
    q_ref,
    g_ref,
    head_sems,
    weight_sems,
):
    scale = HD ** (-0.5)
    half, both = near_ref.shape
    width = both // 2
    kv_local = width // HD
    heads = q_ref.shape[1] // HD
    group = heads // kv_local
    chunks = head_sems.shape[1]
    per = heads // chunks
    lives = [
        lax.broadcasted_iota(jnp.int32, (1, LEN), 1) < lengths_ref[part]
        for part in range(q_ref.shape[0] // LEN)
    ]
    loads = []
    for c in range(chunks):
        cols = pl.ds(c * per * HD, per * HD)
        pair = [
            pltpu.make_async_copy(q_hbm.at[:, cols], q_ref.at[:, cols], head_sems.at[0, c]),
            pltpu.make_async_copy(g_hbm.at[:, cols], g_ref.at[:, cols], head_sems.at[1, c]),
        ]
        for copy in pair:
            copy.start()
        loads.append(pair)
    weights = [
        pltpu.make_async_copy(kw_hbm, kw_ref, weight_sems.at[0]),
        pltpu.make_async_copy(vw_hbm, vw_ref, weight_sems.at[1]),
    ]
    for copy in weights:
        copy.start()
    for k in range(kv_local):
        key_cols = pl.ds(k * HD, HD)
        value_cols = pl.ds(width + k * HD, HD)
        keys = jnp.concatenate([near_ref[:, key_cols], far_ref[:, key_cols]], axis=0)
        values = jnp.concatenate([near_ref[:, value_cols], far_ref[:, value_cols]], axis=0)
        grad_k = jnp.zeros((2 * half, HD), jnp.float32)
        grad_v = jnp.zeros((2 * half, HD), jnp.float32)
        for h in range(k * group, (k + 1) * group):
            if h % per == 0:
                for copy in loads[h // per]:
                    copy.wait()
            cols = pl.ds(h * HD, HD)
            for part, live in enumerate(lives):
                rows = pl.ds(part * LEN, LEN)
                q = q_ref[rows, cols]
                g = g_ref[rows, cols]
                scores = lax.dot_general(keys, q, NT, preferred_element_type=jnp.float32)
                dprobs = lax.dot_general(values, g, NT, preferred_element_type=jnp.float32)
                top = jnp.max(scores, axis=0, keepdims=True)
                expo = jnp.exp((scores - top) * scale)
                total = jnp.sum(expo, axis=0, keepdims=True)
                weighted = jnp.sum(expo * dprobs, axis=0, keepdims=True)
                inverse = 1.0 / total
                delta = weighted * inverse
                factor = jnp.where(live, inverse, 0.0)
                probs = expo * factor
                dscores = probs * ((dprobs - delta) * scale)
                grad_v += jnp.dot(
                    probs.astype(jnp.bfloat16), g, preferred_element_type=jnp.float32
                )
                grad_k += jnp.dot(
                    dscores.astype(jnp.bfloat16), q, preferred_element_type=jnp.float32
                )
        keep_ref[:, key_cols] = grad_k[:half]
        keep_ref[:, value_cols] = grad_v[:half]
        send_ref[:, key_cols] = grad_k[half:].astype(send_ref.dtype)
        send_ref[:, value_cols] = grad_v[half:].astype(send_ref.dtype)
    for copy in weights:
        copy.wait()


def project(low_k, low_v, kw_ref, vw_ref, out_ref, owners):
    features = out_ref.shape[1] // len(owners)
    for i, owner in enumerate(owners):
        rows = pl.ds(pl.multiple_of(owner * features, features), features)
        out = lax.dot_general(low_k, kw_ref[rows, :], NT, preferred_element_type=jnp.float32)
        out += lax.dot_general(low_v, vw_ref[rows, :], NT, preferred_element_type=jnp.float32)
        out_ref[:, i * features : (i + 1) * features] = out.astype(out_ref.dtype)


def send_projection_kernel(order, keep_ref, got_ref, kw_ref, vw_ref, dk_ref, dv_ref, low_ref, out_ref):
    width = dk_ref.shape[1]
    low = (keep_ref[...] + got_ref[...].astype(jnp.float32)).astype(jnp.bfloat16)
    low_k, low_v = low[:, :width], low[:, width:]
    dk_ref[...] = low_k
    dv_ref[...] = low_v
    low_ref[...] = low
    me = lax.axis_index("head")
    project(low_k, low_v, kw_ref, vw_ref, out_ref, [me ^ i for i in order])


def keep_projection_kernel(order, low_ref, kw_ref, vw_ref, out_ref):
    width = kw_ref.shape[1]
    me = lax.axis_index("head")
    project(low_ref[:, :width], low_ref[:, width:], kw_ref, vw_ref, out_ref, [me ^ i for i in order])


def swap(x, axis, count, bit):
    return lax.ppermute(x, axis, [(i, i ^ bit) for i in range(count)])


def body(resp, head, queries, d_out, prefix_keys, prefix_values, k_weight, v_weight, lengths):
    own, width = prefix_keys.shape
    features = k_weight.shape[0] // head
    vmem = pl.BlockSpec(memory_space=pltpu.VMEM)
    hbm = pl.BlockSpec(memory_space=pltpu.HBM)
    params = pltpu.CompilerParams(vmem_limit_bytes=VMEM_LIMIT)
    resp_bits = [1 << i for i in range(resp.bit_length() - 1)]
    head_bits = [1 << i for i in range(head.bit_length() - 1)]

    near = pl.pallas_call(
        join_kernel,
        out_shape=pltpu.VMEM((own, 2 * width), jnp.bfloat16),
        in_specs=[hbm, hbm],
        out_specs=vmem,
        scratch_shapes=[pltpu.SemaphoreType.DMA((2,))],
        compiler_params=params,
        name="join",
    )(*[pltpu.with_memory_space_constraint(x, pltpu.HBM) for x in (prefix_keys, prefix_values)])
    for bit in resp_bits[::-1]:
        far = swap(near, "resp", resp, bit)
        if bit > 1:
            near = jnp.concatenate([near, far], axis=0)

    half = resp * own // 2
    chunks = 4
    large = [
        pltpu.with_memory_space_constraint(x, pltpu.HBM)
        for x in (queries, d_out, k_weight, v_weight)
    ]
    keep, send, k_weight, v_weight = pl.pallas_call(
        attention_kernel,
        out_shape=[
            jax.ShapeDtypeStruct((half, 2 * width), jnp.float32),
            jax.ShapeDtypeStruct((half, 2 * width), jnp.bfloat16),
            pltpu.VMEM(k_weight.shape, k_weight.dtype),
            pltpu.VMEM(v_weight.shape, v_weight.dtype),
        ],
        in_specs=[pl.BlockSpec(memory_space=pltpu.SMEM), vmem, vmem] + [hbm] * 4,
        out_specs=[vmem] * 4,
        scratch_shapes=[
            pltpu.VMEM(queries.shape, queries.dtype),
            pltpu.VMEM(d_out.shape, d_out.dtype),
            pltpu.SemaphoreType.DMA((2, chunks)),
            pltpu.SemaphoreType.DMA((2,)),
        ],
        compiler_params=params,
        name="attention",
    )(lengths, near, far, *large)

    for bit in resp_bits:
        got = swap(send, "resp", resp, bit)
        if bit < resp // 2:
            half //= 2
            total = keep + got.astype(jnp.float32)
            keep, send = total[:half], total[half:].astype(jnp.bfloat16)

    order = [0]
    for bit in head_bits[::-1]:
        order = order + [i + bit for i in order]
    wide = head // 2 * features
    dk_low, dv_low, low, send = pl.pallas_call(
        functools.partial(send_projection_kernel, order[head // 2 :]),
        out_shape=[jax.ShapeDtypeStruct((own, width), jnp.bfloat16)] * 2
        + [pltpu.VMEM((own, 2 * width), jnp.bfloat16)]
        + [pltpu.VMEM((own, wide), jnp.bfloat16)],
        in_specs=[vmem] * 4,
        out_specs=[vmem] * 4,
        compiler_params=params,
        name="projection_to_send",
    )(keep, got, k_weight, v_weight)
    keep = pl.pallas_call(
        functools.partial(keep_projection_kernel, order[: head // 2]),
        out_shape=jax.ShapeDtypeStruct((own, wide), jnp.float32),
        in_specs=[vmem] * 3,
        out_specs=vmem,
        compiler_params=params,
        cost_estimate=pl.CostEstimate(
            flops=4 * own * width * wide, transcendentals=0, bytes_accessed=4 * width * wide
        ),
        name="projection_to_keep",
    )(low, k_weight, v_weight)
    for bit in head_bits:
        total = keep + swap(send, "head", head, bit).astype(jnp.float32)
        wide //= 2
        keep, send = total[:, :wide], total[:, wide:].astype(jnp.bfloat16)
    return dk_low, dv_low, total.astype(jnp.bfloat16)


def solution(mesh):
    placed = (
        P("resp", "head"),
        P("resp", "head"),
        P("resp", "head"),
        P("resp", "head"),
        P(None, "head"),
        P(None, "head"),
        P("resp"),
    )
    return jax.shard_map(
        functools.partial(body, mesh.shape["resp"], mesh.shape["head"]),
        mesh=mesh,
        in_specs=placed,
        out_specs=(P("resp", "head"), P("resp", "head"), P("resp", "head")),
        check_vma=False,
    )
```

time: 49.7 us -> 42.6 us (0.86)
  starting transfers between devices: 26.1 us -> 16.8 us
  waiting for transfers between devices: 8.86 us -> 14.3 us
  Pallas kernels: 10.8 us -> 9.18 us
  local copies, waits for them, and re-layouts: 1.4 us -> 0.03 us
    ppermute x17 -> x8, starting transfers between devices: 26.1 us -> 16.8 us  [swap(): return lax.ppermute(x, axis, [(i, i ^ bit) for i in range(count)])]
    ppermute x17 -> x8, waiting for transfers between devices: 8.86 us -> 14.3 us  [swap(): return lax.ppermute(x, axis, [(i, i ^ bit) for i in range(count)])]
    pallas_call x3 -> x4, Pallas kernels: 10.8 us -> 9.18 us  [the longest x1 5.58 us: body(): pl.pallas_call(attention_kernel, out_shape=[jax.ShapeDtypeStruct((half, 2...]
    unnamed x1 -> x0, local copies, waits for them, and re-layouts: 0.7 us -> none
    concatenate x1 -> x0, local copies, waits for them, and re-layouts: 0.7 us -> none  [body(): both = jnp.concatenate([prefix_keys, prefix_values], axis=1)]
  transfers between devices with their start and end apart: 17 -> 8, of which waited for: 7 -> 8; matrix products, arithmetic and copies ran while one was open for 0% -> 0% of each run, Pallas kernels for 8% -> 3%
where the time goes in v3:
time: 42.6 us; the launch traced here: 42.4 us
  starting transfers between devices  16.8 us (39%)
  waiting for transfers between devices  14.3 us (34%)
  Pallas kernels  9.18 us (22%)
  between operations  1.34 us (3%)
  other arithmetic  0.7 us (2%)
    ppermute x8, starting transfers between devices, swap(): return lax.ppermute(x, axis, [(i, i ^ bit) for i in range(count)])  16.8 us
    ppermute x8, waiting for transfers between devices, swap(): return lax.ppermute(x, axis, [(i, i ^ bit) for i in range(count)])  14.3 us
    pallas_call x1, Pallas kernels, body(): pl.pallas_call(attention_kernel, out_shape=[jax.ShapeDtypeStruct((half, 2...  5.58 us
    pallas_call x1, Pallas kernels, body(): pl.pallas_call(functools.partial(send_projection_kernel, order[head // 2:...  1.69 us
    pallas_call x1, Pallas kernels, body(): pl.pallas_call(functools.partial(keep_projection_kernel, order[:head // 2...  1.18 us
  transfers between devices with their start and end apart: 8, of which 8 were waited for; matrix products, arithmetic and copies ran while one was open for 0% of the time, Pallas kernels for 3%

profile of v3, /device:TPU:0, one launch (start us, length us, event | category | flops | bytes accessed | tf_op | source)
XLA Modules:
  0.0 42.4 jit_solution(7179686067185909364)
XLA Ops:
  0.6 0.7 %join.1 = bf16[16,512]{1,0:T(8,128)(2,1)S(1)} custom-call(bf16[16,256]{1,0:T(8,128)(2,1)} %k_hbm.1, bf16[16,256]{1,0:T(8,128)(2,1)} %v_hbm.1), custom_call_target="tpu_custom_call" | custom-call | tf_op jit(solution)/shard_map/join/pallas_call | solution.py:153
  1.4 4.1 %collective-permute-start = (bf16[16,512]{1,0:T(8,128)(2,1)S(1)}, bf16[16,512]{1,0:T(8,128)(2,1)S(1)}, u32[]{:S(2)}, u32[]{:S(2)}) collective-permute-start(bf16[16,512]{1,0:T(8,128)(2,1)S(1)} %join.1), channel_id=1, source_target_pairs={{0,16},{4,20},{8,24},{12,28},{16,0},{20,4},{24,8},{28,12},{1,17},{... | collective-permute-start | bytes 49160 | tf_op jit(solution)/shard_map/ppermute | solution.py:141
  5.5 1.7 %collective-permute-done = bf16[16,512]{1,0:T(8,128)(2,1)S(1)} collective-permute-done((bf16[16,512]{1,0:T(8,128)(2,1)S(1)}, bf16[16,512]{1,0:T(8,128)(2,1)S(1)}, u32[]{:S(2)}, u32[]{:S(2)}) %collective-permute-start) | collective-permute-done | bytes 16416 | tf_op jit(solution)/shard_map/ppermute | solution.py:141
  7.2 1.9 %collective-permute-start.1 = (bf16[32,512]{1,0:T(8,128)(2,1)S(1)}, bf16[32,512]{1,0:T(8,128)(2,1)S(1)}, u32[]{:S(2)}, u32[]{:S(2)}) collective-permute-start(bf16[32,512]{1,0:T(8,128)(2,1)S(1)} %pad_maximum_fusion.1), channel_id=1, source_target_pairs={{0,8},{4,12},{8,0},{12,4},{16,24},{20,28},{24,16},{28,20},{1,9},{5... | collective-permute-start | bytes 98312 | tf_op jit(solution)/shard_map/ppermute | solution.py:141
  9.1 2.0 %collective-permute-done.1 = bf16[32,512]{1,0:T(8,128)(2,1)S(1)} collective-permute-done((bf16[32,512]{1,0:T(8,128)(2,1)S(1)}, bf16[32,512]{1,0:T(8,128)(2,1)S(1)}, u32[]{:S(2)}, u32[]{:S(2)}) %collective-permute-start.1) | collective-permute-done | bytes 32800 | tf_op jit(solution)/shard_map/ppermute | solution.py:141
  11.1 1.9 %collective-permute-start.2 = (bf16[64,512]{1,0:T(8,128)(2,1)S(1)}, bf16[64,512]{1,0:T(8,128)(2,1)S(1)}, u32[]{:S(2)}, u32[]{:S(2)}) collective-permute-start(bf16[64,512]{1,0:T(8,128)(2,1)S(1)} %pad_maximum_fusion.near_ref), channel_id=1, source_target_pairs={{0,4},{4,0},{8,12},{12,8},{16,20},{20,16},{24,28},{28,24},{1,5},{5... | collective-permute-start | bytes 196616 | tf_op jit(solution)/shard_map/ppermute | solution.py:141
  13.6 1.7 %collective-permute-done.2.far_ref = bf16[64,512]{1,0:T(8,128)(2,1)S(1)} collective-permute-done((bf16[64,512]{1,0:T(8,128)(2,1)S(1)}, bf16[64,512]{1,0:T(8,128)(2,1)S(1)}, u32[]{:S(2)}, u32[]{:S(2)}) %collective-permute-start.2) | collective-permute-done | bytes 65568 | tf_op jit(solution)/shard_map/ppermute | solution.py:141
  15.4 5.6 %attention.1 = (f32[64,512]{1,0:T(8,128)S(1)}, bf16[64,512]{1,0:T(8,128)(2,1)S(1)}, bf16[8192,256]{1,0:T(8,128)(2,1)S(1)}, bf16[8192,256]{1,0:T(8,128)(2,1)S(1)}) custom-call(s32[1]{0:T(128)S(6)} %copy.10.lengths_ref, bf16[64,512]{1,0:T(8,128)(2,1)S(1)} %pad_maximum_fusion.near_ref, bf16[64,512]{1,0:T(8,128)(2,1)S(1)} %collective-permute-done.2.far_ref, ...), custom_call_target="tpu_custom_call" | custom-call | tf_op jit(solution)/shard_map/attention/pallas_call | solution.py:173
  21.0 1.9 %collective-permute-start.3 = (bf16[64,512]{1,0:T(8,128)(2,1)S(1)}, bf16[64,512]{1,0:T(8,128)(2,1)S(1)}, u32[]{:S(2)}, u32[]{:S(2)}) collective-permute-start(bf16[64,512]{1,0:T(8,128)(2,1)S(1)} %get-tuple-element.12), channel_id=1, source_target_pairs={{0,4},{4,0},{8,12},{12,8},{16,20},{20,16},{24,28},{28,24},{1,5},{5... | collective-permute-start | bytes 196616 | tf_op jit(solution)/shard_map/ppermute | solution.py:141
  22.9 2.4 %collective-permute-done.3 = bf16[64,512]{1,0:T(8,128)(2,1)S(1)} collective-permute-done((bf16[64,512]{1,0:T(8,128)(2,1)S(1)}, bf16[64,512]{1,0:T(8,128)(2,1)S(1)}, u32[]{:S(2)}, u32[]{:S(2)}) %collective-permute-start.3) | collective-permute-done | bytes 65568 | tf_op jit(solution)/shard_map/ppermute | solution.py:141
  25.3 2.0 %collective-permute-start.4 = (bf16[32,512]{1,0:T(8,128)(2,1)S(1)}, bf16[32,512]{1,0:T(8,128)(2,1)S(1)}, u32[]{:S(2)}, u32[]{:S(2)}) collective-permute-start(bf16[32,512]{1,0:T(8,128)(2,1)S(1)} %slice.41), channel_id=1, source_target_pairs={{0,8},{4,12},{8,0},{12,4},{16,24},{20,28},{24,16},{28,20},{1,9},{5... | collective-permute-start | bytes 98312 | tf_op jit(solution)/shard_map/ppermute | solution.py:141
  27.3 2.0 %collective-permute-done.4 = bf16[32,512]{1,0:T(8,128)(2,1)S(1)} collective-permute-done((bf16[32,512]{1,0:T(8,128)(2,1)S(1)}, bf16[32,512]{1,0:T(8,128)(2,1)S(1)}, u32[]{:S(2)}, u32[]{:S(2)}) %collective-permute-start.4) | collective-permute-done | bytes 32800 | tf_op jit(solution)/shard_map/ppermute | solution.py:141
  29.3 3.0 %collective-permute-start.5 = (bf16[16,512]{1,0:T(8,128)(2,1)S(1)}, bf16[16,512]{1,0:T(8,128)(2,1)S(1)}, u32[]{:S(2)}, u32[]{:S(2)}) collective-permute-start(bf16[16,512]{1,0:T(8,128)(2,1)S(1)} %slice.42), channel_id=1, source_target_pairs={{0,16},{4,20},{8,24},{12,28},{16,0},{20,4},{24,8},{28,12},{1,17},{... | collective-permute-start | bytes 49160 | tf_op jit(solution)/shard_map/ppermute | solution.py:141
  32.3 1.7 %collective-permute-done.5.got_ref = bf16[16,512]{1,0:T(8,128)(2,1)S(1)} collective-permute-done((bf16[16,512]{1,0:T(8,128)(2,1)S(1)}, bf16[16,512]{1,0:T(8,128)(2,1)S(1)}, u32[]{:S(2)}, u32[]{:S(2)}) %collective-permute-start.5) | collective-permute-done | bytes 16416 | tf_op jit(solution)/shard_map/ppermute | solution.py:141
  34.0 1.7 %projection_to_send.1 = (bf16[16,256]{1,0:T(8,128)(2,1)}, bf16[16,256]{1,0:T(8,128)(2,1)}, bf16[16,512]{1,0:T(8,128)(2,1)S(1)}, bf16[16,4096]{1,0:T(8,128)(2,1)S(1)}) custom-call(f32[16,512]{1,0:T(8,128)S(1)} %slice.29.keep_ref, bf16[16,512]{1,0:T(8,128)(2,1)S(1)} %collective-permute-done.5.got_ref, bf16[8192,256]{1,0:T(8,128)(2,1)S(1)} %get-tuple-element.13.kw_ref, ...), custom_call_target="tpu_custom_call" | custom-call | tf_op jit(solution)/shard_map/projection_to_send/pallas_call | solution.py:204
  35.7 0.0 collective-permute-start.6
  35.7 1.2 %projection_to_keep.1 = f32[16,4096]{1,0:T(8,128)S(1)} custom-call(bf16[16,512]{1,0:T(8,128)(2,1)S(1)} %get-tuple-element.17.low_ref, bf16[8192,256]{1,0:T(8,128)(2,1)S(1)} %get-tuple-element.13.kw_ref, bf16[8192,256]{1,0:T(8,128)(2,1)S(1)} %get-tuple-element.14.vw_ref), custom_call_target="tpu_custom_call" | custom-call | flops 67108864 | bytes 4194304 | tf_op jit(solution)/shard_map/projection_to_keep/pallas_call | solution.py:214
  36.9 0.2 collective-permute-done.6
  37.1 2.0 %collective-permute-start.7 = (bf16[16,2048]{1,0:T(8,128)(2,1)S(1)}, bf16[16,2048]{1,0:T(8,128)(2,1)S(1)}, u32[]{:S(2)}, u32[]{:S(2)}) collective-permute-start(bf16[16,2048]{1,0:T(8,128)(2,1)S(1)} %slice.40), channel_id=1, source_target_pairs={{0,2},{1,3},{2,0},{3,1},{4,6},{5,7},{6,4},{7,5},{8,10},{9,11},{10,... | collective-permute-start | bytes 196616 | tf_op jit(solution)/shard_map/ppermute | solution.py:141
  39.1 2.6 %collective-permute-done.7 = bf16[16,2048]{1,0:T(8,128)(2,1)S(1)} collective-permute-done((bf16[16,2048]{1,0:T(8,128)(2,1)S(1)}, bf16[16,2048]{1,0:T(8,128)(2,1)S(1)}, u32[]{:S(2)}, u32[]{:S(2)}) %collective-permute-start.7) | collective-permute-done | bytes 65568 | tf_op jit(solution)/shard_map/ppermute | solution.py:141
  41.7 0.6 %fusion = bf16[16,2048]{1,0:T(8,128)(2,1)} fusion(f32[16,4096]{1,0:T(8,128)S(1)} %convert_add_fusion, bf16[16,2048]{1,0:T(8,128)(2,1)S(1)} %collective-permute-done.7), kind=kLoop, calls=%fused_computation.3 | loop fusion | flops 98304 | bytes 262144 | tf_op jit(solution)/shard_map/convert_element_type | solution.py:229
  (9 shorter events, 0.1 us)
Async XLA Ops:
  1.4 5.8 %collective-permute-start = (bf16[16,512]{1,0:T(8,128)(2,1)S(1)}, bf16[16,512]{1,0:T(8,128)(2,1)S(1)}, u32[]{:S(2)}, u32[]{:S(2)}) collective-permute-start(bf16[16,512]{1,0:T(8,128)(2,1)S(1)} %join.1), channel_id=1, source_target_pairs={{0,16},{4,20},{8,24},{12,28},{16,0},{20,4},{24,8},{28,12},{1,17},{... | collective-permute-start | bytes 49160 | tf_op jit(solution)/shard_map/ppermute | solution.py:141
  7.2 3.9 %collective-permute-start.1 = (bf16[32,512]{1,0:T(8,128)(2,1)S(1)}, bf16[32,512]{1,0:T(8,128)(2,1)S(1)}, u32[]{:S(2)}, u32[]{:S(2)}) collective-permute-start(bf16[32,512]{1,0:T(8,128)(2,1)S(1)} %pad_maximum_fusion.1), channel_id=1, source_target_pairs={{0,8},{4,12},{8,0},{12,4},{16,24},{20,28},{24,16},{28,20},{1,9},{5... | collective-permute-start | bytes 98312 | tf_op jit(solution)/shard_map/ppermute | solution.py:141
  11.1 4.3 %collective-permute-start.2 = (bf16[64,512]{1,0:T(8,128)(2,1)S(1)}, bf16[64,512]{1,0:T(8,128)(2,1)S(1)}, u32[]{:S(2)}, u32[]{:S(2)}) collective-permute-start(bf16[64,512]{1,0:T(8,128)(2,1)S(1)} %pad_maximum_fusion.near_ref), channel_id=1, source_target_pairs={{0,4},{4,0},{8,12},{12,8},{16,20},{20,16},{24,28},{28,24},{1,5},{5... | collective-permute-start | bytes 196616 | tf_op jit(solution)/shard_map/ppermute | solution.py:141
  21.0 4.3 %collective-permute-start.3 = (bf16[64,512]{1,0:T(8,128)(2,1)S(1)}, bf16[64,512]{1,0:T(8,128)(2,1)S(1)}, u32[]{:S(2)}, u32[]{:S(2)}) collective-permute-start(bf16[64,512]{1,0:T(8,128)(2,1)S(1)} %get-tuple-element.12), channel_id=1, source_target_pairs={{0,4},{4,0},{8,12},{12,8},{16,20},{20,16},{24,28},{28,24},{1,5},{5... | collective-permute-start | bytes 196616 | tf_op jit(solution)/shard_map/ppermute | solution.py:141
  25.3 4.0 %collective-permute-start.4 = (bf16[32,512]{1,0:T(8,128)(2,1)S(1)}, bf16[32,512]{1,0:T(8,128)(2,1)S(1)}, u32[]{:S(2)}, u32[]{:S(2)}) collective-permute-start(bf16[32,512]{1,0:T(8,128)(2,1)S(1)} %slice.41), channel_id=1, source_target_pairs={{0,8},{4,12},{8,0},{12,4},{16,24},{20,28},{24,16},{28,20},{1,9},{5... | collective-permute-start | bytes 98312 | tf_op jit(solution)/shard_map/ppermute | solution.py:141
  29.3 4.7 %collective-permute-start.5 = (bf16[16,512]{1,0:T(8,128)(2,1)S(1)}, bf16[16,512]{1,0:T(8,128)(2,1)S(1)}, u32[]{:S(2)}, u32[]{:S(2)}) collective-permute-start(bf16[16,512]{1,0:T(8,128)(2,1)S(1)} %slice.42), channel_id=1, source_target_pairs={{0,16},{4,20},{8,24},{12,28},{16,0},{20,4},{24,8},{28,12},{1,17},{... | collective-permute-start | bytes 49160 | tf_op jit(solution)/shard_map/ppermute | solution.py:141
  35.7 1.3 %collective-permute-start.6 = (bf16[16,4096]{1,0:T(8,128)(2,1)S(1)}, bf16[16,4096]{1,0:T(8,128)(2,1)S(1)}, u32[]{:S(2)}, u32[]{:S(2)}) collective-permute-start(bf16[16,4096]{1,0:T(8,128)(2,1)S(1)} %get-tuple-element.18), channel_id=1, source_target_pairs={{0,1},{1,0},{2,3},{3,2},{4,5},{5,4},{6,7},{7,6},{8,9},{9,8},{10,11... | collective-permute-start | bytes 393224 | tf_op jit(solution)/shard_map/ppermute | solution.py:141
  37.1 4.6 %collective-permute-start.7 = (bf16[16,2048]{1,0:T(8,128)(2,1)S(1)}, bf16[16,2048]{1,0:T(8,128)(2,1)S(1)}, u32[]{:S(2)}, u32[]{:S(2)}) collective-permute-start(bf16[16,2048]{1,0:T(8,128)(2,1)S(1)} %slice.40), channel_id=1, source_target_pairs={{0,2},{1,3},{2,0},{3,1},{4,6},{5,7},{6,4},{7,5},{8,10},{9,11},{10,... | collective-permute-start | bytes 196616 | tf_op jit(solution)/shard_map/ppermute | solution.py:141

commit v4 on v3

v4 whole, which is shorter than its diff:
```python
import functools

import jax
import jax.numpy as jnp
from jax import lax
from jax.experimental import pallas as pl
from jax.experimental.pallas import tpu as pltpu
from jax.sharding import PartitionSpec as P

HD = 128
LEN = 256
NT = (((1,), (1,)), ((), ()))
VMEM_LIMIT = 40 << 20
LOG2E = 1.4426950408889634


def join_kernel(k_hbm, v_hbm, out_ref, sems):
    width = k_hbm.shape[1]
    copies = []
    for i in range(out_ref.shape[0]):
        copies += [
            pltpu.make_async_copy(k_hbm, out_ref.at[i, :, pl.ds(0, width)], sems.at[0, i]),
            pltpu.make_async_copy(v_hbm, out_ref.at[i, :, pl.ds(width, width)], sems.at[1, i]),
        ]
    for copy in copies:
        copy.start()
    for copy in copies:
        copy.wait()


def load_kernel(q_hbm, g_hbm, q_ref, g_ref, sems):
    copies = [
        pltpu.make_async_copy(q_hbm, q_ref, sems.at[0]),
        pltpu.make_async_copy(g_hbm, g_ref, sems.at[1]),
    ]
    for copy in copies:
        copy.start()
    for copy in copies:
        copy.wait()


def attention_kernel(
    lengths_ref,
    kv_ref,
    q_ref,
    g_ref,
    kw_hbm,
    vw_hbm,
    out_ref,
    kw_ref,
    vw_ref,
    probs_ref,
    dscores_ref,
    sems,
):
    weights = [
        pltpu.make_async_copy(kw_hbm, kw_ref, sems.at[0]),
        pltpu.make_async_copy(vw_hbm, vw_ref, sems.at[1]),
    ]
    for copy in weights:
        copy.start()
    scale = HD ** (-0.5)
    width = kv_ref.shape[1] // 2
    kv_local = width // HD
    parts = q_ref.shape[0] // LEN
    group = q_ref.shape[1] // HD // kv_local
    lives = [
        lax.broadcasted_iota(jnp.int32, (1, LEN), 1) < lengths_ref[part] for part in range(parts)
    ]
    units = [(k, h, part) for k in range(kv_local) for h in range(group) for part in range(parts)]

    def place(unit):
        k, h, part = unit
        return pl.ds(part * LEN, LEN), pl.ds((k * group + h) * HD, HD)

    def products(unit):
        k = unit[0]
        where = place(unit)
        keys = kv_ref[:, k * HD : (k + 1) * HD]
        values = kv_ref[:, width + k * HD : width + (k + 1) * HD]
        return (
            lax.dot_general(keys, q_ref[where], NT, preferred_element_type=jnp.float32),
            lax.dot_general(values, g_ref[where], NT, preferred_element_type=jnp.float32),
        )

    following = products(units[0])
    for i, unit in enumerate(units):
        k, h, part = unit
        scores, dprobs = following
        if i + 1 < len(units):
            following = products(units[i + 1])
        top = jnp.max(scores, axis=0, keepdims=True)
        expo = jnp.exp2((scores - top) * (scale * LOG2E))
        total = jnp.sum(expo, axis=0, keepdims=True)
        weighted = jnp.sum(expo * dprobs, axis=0, keepdims=True)
        inverse = 1.0 / total
        delta = weighted * inverse
        factor = jnp.where(lives[part], inverse, 0.0)
        probs = expo * factor
        at = (h * parts + part) * LEN
        probs_ref[k, :, at : at + LEN] = probs.astype(jnp.bfloat16)
        dscores_ref[k, :, at : at + LEN] = (probs * (dprobs - delta)).astype(jnp.bfloat16)
        if (h, part) == (group - 1, parts - 1):
            mine = [place(u) for u in units if u[0] == k]
            q_all = jnp.concatenate([q_ref[where] for where in mine], axis=0)
            g_all = jnp.concatenate([g_ref[where] for where in mine], axis=0)
            grad_k = jnp.dot(dscores_ref[k], q_all, preferred_element_type=jnp.float32) * scale
            grad_v = jnp.dot(probs_ref[k], g_all, preferred_element_type=jnp.float32)
            out_ref[:, k * HD : (k + 1) * HD] = grad_k.astype(out_ref.dtype)
            out_ref[:, width + k * HD : width + (k + 1) * HD] = grad_v.astype(out_ref.dtype)
    for copy in weights:
        copy.wait()


def project(low_k, low_v, kw_ref, vw_ref, out_ref, owners):
    features = out_ref.shape[1] // len(owners)
    for i, owner in enumerate(owners):
        rows = pl.ds(pl.multiple_of(owner * features, features), features)
        out = lax.dot_general(low_k, kw_ref[rows, :], NT, preferred_element_type=jnp.float32)
        out += lax.dot_general(low_v, vw_ref[rows, :], NT, preferred_element_type=jnp.float32)
        out_ref[:, i * features : (i + 1) * features] = out.astype(out_ref.dtype)


def send_projection_kernel(order, parts_ref, kw_ref, vw_ref, dk_ref, dv_ref, low_ref, out_ref):
    width = dk_ref.shape[1]
    total = parts_ref[0].astype(jnp.float32)
    for i in range(1, parts_ref.shape[0]):
        total += parts_ref[i].astype(jnp.float32)
    low = total.astype(jnp.bfloat16)
    low_k, low_v = low[:, :width], low[:, width:]
    dk_ref[...] = low_k
    dv_ref[...] = low_v
    low_ref[...] = low
    me = lax.axis_index("head")
    project(low_k, low_v, kw_ref, vw_ref, out_ref, [me ^ i for i in order])


def keep_projection_kernel(order, low_ref, kw_ref, vw_ref, out_ref):
    width = kw_ref.shape[1]
    me = lax.axis_index("head")
    project(low_ref[:, :width], low_ref[:, width:], kw_ref, vw_ref, out_ref, [me ^ i for i in order])


def swap(x, axis, count, bit):
    return lax.ppermute(x, axis, [(i, i ^ bit) for i in range(count)])


def body(resp, head, queries, d_out, prefix_keys, prefix_values, k_weight, v_weight, lengths):
    own, width = prefix_keys.shape
    features = k_weight.shape[0] // head
    vmem = pl.BlockSpec(memory_space=pltpu.VMEM)
    hbm = pl.BlockSpec(memory_space=pltpu.HBM)
    params = pltpu.CompilerParams(vmem_limit_bytes=VMEM_LIMIT)
    head_bits = [1 << i for i in range(head.bit_length() - 1)]

    def in_hbm(*xs):
        return [pltpu.with_memory_space_constraint(x, pltpu.HBM) for x in xs]

    both = pl.pallas_call(
        join_kernel,
        out_shape=pltpu.VMEM((resp, own, 2 * width), jnp.bfloat16),
        in_specs=[hbm] * 2,
        out_specs=vmem,
        scratch_shapes=[pltpu.SemaphoreType.DMA((2, resp))],
        compiler_params=params,
        name="join",
    )(*in_hbm(prefix_keys, prefix_values))
    both = lax.all_to_all(both, "resp", 0, 0, tiled=True).reshape(resp * own, 2 * width)

    queries, d_out = pl.pallas_call(
        load_kernel,
        out_shape=[pltpu.VMEM(x.shape, x.dtype) for x in (queries, d_out)],
        in_specs=[hbm] * 2,
        out_specs=[vmem] * 2,
        scratch_shapes=[pltpu.SemaphoreType.DMA((2,))],
        compiler_params=params,
        cost_estimate=pl.CostEstimate(
            flops=0, transcendentals=0, bytes_accessed=4 * queries.size * 2
        ),
        name="load",
    )(*in_hbm(queries, d_out))

    tokens = resp * own
    kv_local = width // HD
    depth = queries.size // kv_local // HD
    partial, k_weight, v_weight = pl.pallas_call(
        attention_kernel,
        out_shape=[
            pltpu.VMEM((tokens, 2 * width), jnp.bfloat16),
            pltpu.VMEM(k_weight.shape, k_weight.dtype),
            pltpu.VMEM(v_weight.shape, v_weight.dtype),
        ],
        in_specs=[pl.BlockSpec(memory_space=pltpu.SMEM)] + [vmem] * 3 + [hbm] * 2,
        out_specs=[vmem] * 3,
        scratch_shapes=[
            pltpu.VMEM((kv_local, tokens, depth), jnp.bfloat16),
            pltpu.VMEM((kv_local, tokens, depth), jnp.bfloat16),
            pltpu.SemaphoreType.DMA((2,)),
        ],
        compiler_params=params,
        name="attention",
    )(lengths, both, queries, d_out, *in_hbm(k_weight, v_weight))

    shares = lax.all_to_all(
        partial.reshape(resp, own, 2 * width), "resp", 0, 0, tiled=True
    )

    order = [0]
    for bit in head_bits[::-1]:
        order = order + [i + bit for i in order]
    wide = head // 2 * features
    dk_low, dv_low, low, send = pl.pallas_call(
        functools.partial(send_projection_kernel, order[head // 2 :]),
        out_shape=[jax.ShapeDtypeStruct((own, width), jnp.bfloat16)] * 2
        + [pltpu.VMEM((own, 2 * width), jnp.bfloat16)]
        + [pltpu.VMEM((own, wide), jnp.bfloat16)],
        in_specs=[vmem] * 3,
        out_specs=[vmem] * 4,
        compiler_params=params,
        name="projection_to_send",
    )(shares, k_weight, v_weight)
    keep = pl.pallas_call(
        functools.partial(keep_projection_kernel, order[: head // 2]),
        out_shape=jax.ShapeDtypeStruct((own, wide), jnp.float32),
        in_specs=[vmem] * 3,
        out_specs=vmem,
        compiler_params=params,
        cost_estimate=pl.CostEstimate(
            flops=4 * own * width * wide, transcendentals=0, bytes_accessed=4 * width * wide
        ),
        name="projection_to_keep",
    )(low, k_weight, v_weight)
    for bit in head_bits:
        total = keep + swap(send, "head", head, bit).astype(jnp.float32)
        wide //= 2
        keep, send = total[:, :wide], total[:, wide:].astype(jnp.bfloat16)
    return dk_low, dv_low, total.astype(jnp.bfloat16)


def solution(mesh):
    placed = (
        P("resp", "head"),
        P("resp", "head"),
        P("resp", "head"),
        P("resp", "head"),
        P(None, "head"),
        P(None, "head"),
        P("resp"),
    )
    return jax.shard_map(
        functools.partial(body, mesh.shape["resp"], mesh.shape["head"]),
        mesh=mesh,
        in_specs=placed,
        out_specs=(P("resp", "head"), P("resp", "head"), P("resp", "head")),
        check_vma=False,
    )
```

time: 42.6 us -> 38.8 us (0.911)
  blocking collectives: 0 us -> 9.74 us
  starting transfers between devices: 16.8 us -> 8.87 us
  waiting for transfers between devices: 14.3 us -> 8.11 us
  Pallas kernels: 9.18 us -> 9.7 us
    ppermute x8 -> x2, starting transfers between devices: 16.8 us -> 1.6 us  [swap(): return lax.ppermute(x, axis, [(i, i ^ bit) for i in range(count)])]
    ppermute x8 -> x2, waiting for transfers between devices: 14.3 us -> 2.99 us  [swap(): return lax.ppermute(x, axis, [(i, i ^ bit) for i in range(count)])]
    all_to_all x0 -> x1, blocking collectives: none -> 9.74 us  [body(): lax.all_to_all(partial.reshape(resp, own, 2 * width), 'resp', 0, 0, tiled...]
    all_to_all x0 -> x1, starting transfers between devices: none -> 7.26 us  [body(): lax.all_to_all(both, 'resp', 0, 0, tiled=True)]
    all_to_all x0 -> x1, waiting for transfers between devices: none -> 5.12 us  [body(): lax.all_to_all(both, 'resp', 0, 0, tiled=True)]
    pallas_call x2 -> x3, Pallas kernels: 6.31 us -> 6.82 us  [the longest x1 3.48 us: body(): pl.pallas_call(attention_kernel, out_shape=[pltpu.VMEM((tokens, 2 * width...]
  transfers between devices with their start and end apart: 8 -> 3, of which waited for: 8 -> 3; matrix products, arithmetic and copies ran while one was open for 0% -> 0% of each run, Pallas kernels for 3% -> 7%
where the time goes in v4:
time: 38.8 us; the launch traced here: 38.4 us
  blocking collectives  9.74 us (25%)
  Pallas kernels  9.7 us (25%)
  starting transfers between devices  8.87 us (23%)
  waiting for transfers between devices  8.11 us (21%)
  between operations  1.32 us (3%)
  other arithmetic  0.67 us (2%)
    all_to_all x1, blocking collectives, body(): lax.all_to_all(partial.reshape(resp, own, 2 * width), 'resp', 0, 0, tiled...  9.74 us
    all_to_all x1, starting transfers between devices, body(): lax.all_to_all(both, 'resp', 0, 0, tiled=True)  7.26 us
    all_to_all x1, waiting for transfers between devices, body(): lax.all_to_all(both, 'resp', 0, 0, tiled=True)  5.12 us
    pallas_call x1, Pallas kernels, body(): pl.pallas_call(attention_kernel, out_shape=[pltpu.VMEM((tokens, 2 * width...  3.48 us
    ppermute x2, waiting for transfers between devices, swap(): return lax.ppermute(x, axis, [(i, i ^ bit) for i in range(count)])  2.99 us
    pallas_call x1, Pallas kernels, body(): pl.pallas_call(join_kernel, out_shape=pltpu.VMEM((resp, own, 2 * width),...  1.78 us
    pallas_call x1, Pallas kernels, body(): pl.pallas_call(functools.partial(send_projection_kernel, order[head // 2:...  1.69 us
    ppermute x2, starting transfers between devices, swap(): return lax.ppermute(x, axis, [(i, i ^ bit) for i in range(count)])  1.6 us
  transfers between devices with their start and end apart: 3, of which 3 were waited for; matrix products, arithmetic and copies ran while one was open for 0% of the time, Pallas kernels for 7%

profile of v4, /device:TPU:0, one launch (start us, length us, event | category | flops | bytes accessed | tf_op | source)
XLA Modules:
  0.0 38.4 jit_solution(4054865858431679013)
XLA Ops:
  0.6 1.8 %join.1 = bf16[8,16,512]{2,1,0:T(8,128)(2,1)} custom-call(bf16[16,256]{1,0:T(8,128)(2,1)} %k_hbm.1, bf16[16,256]{1,0:T(8,128)(2,1)} %v_hbm.1), custom_call_target="tpu_custom_call" | custom-call | tf_op jit(solution)/shard_map/join/pallas_call | solution.py:159
  2.4 7.3 %all-to-all-start = ((bf16[8,16,512]{2,1,0:T(8,128)(2,1)}), bf16[8,16,512]{2,1,0:T(8,128)(2,1)S(1)}, u32[]{:S(2)}, u32[]{:S(2)}) async-start(bf16[8,16,512]{2,1,0:T(8,128)(2,1)} %join.1), calls=%async_computation | async-start | bytes 262144 | tf_op jit(solution)/shard_map/all_to_all | solution.py:168
  10.3 1.6 %load.1 = (bf16[256,2048]{1,0:T(8,128)(2,1)S(1)}, bf16[256,2048]{1,0:T(8,128)(2,1)S(1)}) custom-call(bf16[256,2048]{1,0:T(8,128)(2,1)} %q_hbm.1, bf16[256,2048]{1,0:T(8,128)(2,1)} %g_hbm.1), custom_call_target="tpu_custom_call" | custom-call | bytes 4194304 | tf_op jit(solution)/shard_map/load/pallas_call | solution.py:170
  11.9 5.1 %all-to-all-done = bf16[8,16,512]{2,1,0:T(8,128)(2,1)S(1)} async-done(((bf16[8,16,512]{2,1,0:T(8,128)(2,1)}), bf16[8,16,512]{2,1,0:T(8,128)(2,1)S(1)}, u32[]{:S(2)}, u32[]{:S(2)}) %all-to-all-start) | async-done | bytes 131104 | tf_op jit(solution)/shard_map/all_to_all | solution.py:168
  17.0 3.5 %attention.1 = (bf16[128,512]{1,0:T(8,128)(2,1)S(1)}, bf16[8192,256]{1,0:T(8,128)(2,1)S(1)}, bf16[8192,256]{1,0:T(8,128)(2,1)S(1)}) custom-call(s32[1]{0:T(128)S(6)} %copy.10.lengths_ref, bf16[128,512]{1,0:T(8,128)(2,1)S(1)} %bitcast.2, bf16[256,2048]{1,0:T(8,128)(2,1)S(1)} %get-tuple-element.12.q_ref, bf16[256,2048]{1,0:T(8,128)(2,1)S(1)} %get-tuple-element.13.g_ref, ...), custom_call_target="tpu_custom_call" | custom-call | tf_op jit(solution)/shard_map/attention/pallas_call | solution.py:186
  20.5 9.7 %all_to_all.10.parts_ref = bf16[8,16,512]{2,1,0:T(8,128)(2,1)S(1)} all-to-all(bf16[8,16,512]{2,1,0:T(8,128)(2,1)S(1)} %bitcast.3), channel_id=1, replica_groups=mesh['resp'=8,'head'=4] {'resp'}, dimensions={0} | all-to-all | bytes 262144 | tf_op jit(solution)/shard_map/all_to_all | solution.py:204
  30.3 1.7 %projection_to_send.1 = (bf16[16,256]{1,0:T(8,128)(2,1)}, bf16[16,256]{1,0:T(8,128)(2,1)}, bf16[16,512]{1,0:T(8,128)(2,1)S(1)}, bf16[16,4096]{1,0:T(8,128)(2,1)S(1)}) custom-call(bf16[8,16,512]{2,1,0:T(8,128)(2,1)S(1)} %all_to_all.10.parts_ref, bf16[8192,256]{1,0:T(8,128)(2,1)S(1)} %get-tuple-element.15.kw_ref, bf16[8192,256]{1,0:T(8,128)(2,1)S(1)} %get-tuple-element.16.vw_ref), custom_call_target="tpu_custom_call" | custom-call | tf_op jit(solution)/shard_map/projection_to_send/pallas_call | solution.py:212
  31.9 0.0 collective-permute-start
  31.9 1.2 %projection_to_keep.1 = f32[16,4096]{1,0:T(8,128)S(1)} custom-call(bf16[16,512]{1,0:T(8,128)(2,1)S(1)} %get-tuple-element.19.low_ref, bf16[8192,256]{1,0:T(8,128)(2,1)S(1)} %get-tuple-element.15.kw_ref, bf16[8192,256]{1,0:T(8,128)(2,1)S(1)} %get-tuple-element.16.vw_ref), custom_call_target="tpu_custom_call" | custom-call | flops 67108864 | bytes 4194304 | tf_op jit(solution)/shard_map/projection_to_keep/pallas_call | solution.py:222
  33.1 0.2 collective-permute-done
  33.3 1.6 %collective-permute-start.1 = (bf16[16,2048]{1,0:T(8,128)(2,1)S(1)}, bf16[16,2048]{1,0:T(8,128)(2,1)S(1)}, u32[]{:S(2)}, u32[]{:S(2)}) collective-permute-start(bf16[16,2048]{1,0:T(8,128)(2,1)S(1)} %slice.15), channel_id=1, source_target_pairs={{0,2},{1,3},{2,0},{3,1},{4,6},{5,7},{6,4},{7,5},{8,10},{9,11},{10,... | collective-permute-start | bytes 196616 | tf_op jit(solution)/shard_map/ppermute | solution.py:145
  34.9 2.8 %collective-permute-done.1 = bf16[16,2048]{1,0:T(8,128)(2,1)S(1)} collective-permute-done((bf16[16,2048]{1,0:T(8,128)(2,1)S(1)}, bf16[16,2048]{1,0:T(8,128)(2,1)S(1)}, u32[]{:S(2)}, u32[]{:S(2)}) %collective-permute-start.1) | collective-permute-done | bytes 65568 | tf_op jit(solution)/shard_map/ppermute | solution.py:145
  37.8 0.6 %fusion = bf16[16,2048]{1,0:T(8,128)(2,1)} fusion(f32[16,4096]{1,0:T(8,128)S(1)} %convert_add_fusion, bf16[16,2048]{1,0:T(8,128)(2,1)S(1)} %collective-permute-done.1), kind=kLoop, calls=%fused_computation.3 | loop fusion | flops 98304 | bytes 262144 | tf_op jit(solution)/shard_map/convert_element_type | solution.py:237
  (2 shorter events, 0.0 us)
Async XLA Ops:
  2.4 14.6 %all-to-all-start = ((bf16[8,16,512]{2,1,0:T(8,128)(2,1)}), bf16[8,16,512]{2,1,0:T(8,128)(2,1)S(1)}, u32[]{:S(2)}, u32[]{:S(2)}) async-start(bf16[8,16,512]{2,1,0:T(8,128)(2,1)} %join.1), calls=%async_computation | async-start | bytes 262144 | tf_op jit(solution)/shard_map/all_to_all | solution.py:168
  31.9 1.3 %collective-permute-start = (bf16[16,4096]{1,0:T(8,128)(2,1)S(1)}, bf16[16,4096]{1,0:T(8,128)(2,1)S(1)}, u32[]{:S(2)}, u32[]{:S(2)}) collective-permute-start(bf16[16,4096]{1,0:T(8,128)(2,1)S(1)} %get-tuple-element.20), channel_id=1, source_target_pairs={{0,1},{1,0},{2,3},{3,2},{4,5},{5,4},{6,7},{7,6},{8,9},{9,8},{10,11... | collective-permute-start | bytes 393224 | tf_op jit(solution)/shard_map/ppermute | solution.py:145
  33.3 4.4 %collective-permute-start.1 = (bf16[16,2048]{1,0:T(8,128)(2,1)S(1)}, bf16[16,2048]{1,0:T(8,128)(2,1)S(1)}, u32[]{:S(2)}, u32[]{:S(2)}) collective-permute-start(bf16[16,2048]{1,0:T(8,128)(2,1)S(1)} %slice.15), channel_id=1, source_target_pairs={{0,2},{1,3},{2,0},{3,1},{4,6},{5,7},{6,4},{7,5},{8,10},{9,11},{10,... | collective-permute-start | bytes 196616 | tf_op jit(solution)/shard_map/ppermute | solution.py:145

commit v5 on v4

v5 whole, which is shorter than its diff:
```python
import functools

import jax
import jax.numpy as jnp
from jax import lax
from jax.experimental import pallas as pl
from jax.experimental.pallas import tpu as pltpu
from jax.sharding import PartitionSpec as P

HD = 128
LEN = 256
NT = (((1,), (1,)), ((), ()))
VMEM_LIMIT = 40 << 20
LOG2E = 1.4426950408889634


def join_kernel(k_hbm, v_hbm, out_ref, both_ref, sems):
    width = k_hbm.shape[1]
    copies = [
        pltpu.make_async_copy(k_hbm, both_ref.at[:, pl.ds(0, width)], sems.at[0]),
        pltpu.make_async_copy(v_hbm, both_ref.at[:, pl.ds(width, width)], sems.at[1]),
    ]
    for copy in copies:
        copy.start()
    for copy in copies:
        copy.wait()
    both = both_ref[...]
    for i in range(out_ref.shape[0]):
        out_ref[i] = both


def load_kernel(q_hbm, g_hbm, q_ref, g_ref, sems):
    copies = [
        pltpu.make_async_copy(q_hbm, q_ref, sems.at[0]),
        pltpu.make_async_copy(g_hbm, g_ref, sems.at[1]),
    ]
    for copy in copies:
        copy.start()
    for copy in copies:
        copy.wait()


def attention_kernel(
    lengths_ref,
    kv_ref,
    q_ref,
    g_ref,
    kw_hbm,
    vw_hbm,
    out_ref,
    kw_ref,
    vw_ref,
    scores_ref,
    dprobs_ref,
    probs_ref,
    dscores_ref,
    sems,
):
    weights = [
        pltpu.make_async_copy(kw_hbm, kw_ref, sems.at[0]),
        pltpu.make_async_copy(vw_hbm, vw_ref, sems.at[1]),
    ]
    for copy in weights:
        copy.start()
    scale = HD ** (-0.5)
    width = kv_ref.shape[1] // 2
    kv_local = width // HD
    parts = q_ref.shape[0] // LEN
    group = q_ref.shape[1] // HD // kv_local
    position = lax.broadcasted_iota(jnp.int32, (1, HD), 1)
    units = [(k, h, part) for k in range(kv_local) for h in range(group) for part in range(parts)]

    def place(unit):
        k, h, part = unit
        return pl.ds(part * LEN, LEN), pl.ds((k * group + h) * HD, HD)

    def products(i):
        k = units[i][0]
        where = place(units[i])
        keys = kv_ref[:, k * HD : (k + 1) * HD]
        values = kv_ref[:, width + k * HD : width + (k + 1) * HD]
        scores_ref[i % 2] = lax.dot_general(
            keys, q_ref[where], NT, preferred_element_type=jnp.float32
        )
        dprobs_ref[i % 2] = lax.dot_general(
            values, g_ref[where], NT, preferred_element_type=jnp.float32
        )

    products(0)
    for i, unit in enumerate(units):
        k, h, part = unit
        if i + 1 < len(units):
            products(i + 1)
        for start in range(0, LEN, HD):
            scores = scores_ref[i % 2, :, start : start + HD]
            dprobs = dprobs_ref[i % 2, :, start : start + HD]
            top = jnp.max(scores, axis=0, keepdims=True)
            expo = jnp.exp2((scores - top) * (scale * LOG2E))
            total = jnp.sum(expo, axis=0, keepdims=True)
            weighted = jnp.sum(expo * dprobs, axis=0, keepdims=True)
            inverse = 1.0 / total
            delta = weighted * inverse
            factor = jnp.where(position + start < lengths_ref[part], inverse, 0.0)
            probs = expo * factor
            at = (h * parts + part) * LEN + start
            probs_ref[k, :, at : at + HD] = probs.astype(jnp.bfloat16)
            dscores_ref[k, :, at : at + HD] = (probs * (dprobs - delta)).astype(jnp.bfloat16)
        if (h, part) == (group - 1, parts - 1):
            mine = [place(u) for u in units if u[0] == k]
            q_all = jnp.concatenate([q_ref[where] for where in mine], axis=0)
            g_all = jnp.concatenate([g_ref[where] for where in mine], axis=0)
            grad_k = jnp.dot(dscores_ref[k], q_all, preferred_element_type=jnp.float32) * scale
            grad_v = jnp.dot(probs_ref[k], g_all, preferred_element_type=jnp.float32)
            out_ref[:, k * HD : (k + 1) * HD] = grad_k.astype(out_ref.dtype)
            out_ref[:, width + k * HD : width + (k + 1) * HD] = grad_v.astype(out_ref.dtype)
    for copy in weights:
        copy.wait()


def project(low, kw_ref, vw_ref, owner, features):
    width = kw_ref.shape[1]
    rows = pl.ds(pl.multiple_of(owner * features, features), features)
    out = lax.dot_general(
        low[:, :width], kw_ref[rows, :], NT, preferred_element_type=jnp.float32
    )
    return out + lax.dot_general(
        low[:, width:], vw_ref[rows, :], NT, preferred_element_type=jnp.float32
    )


def first_projection_kernel(owner, parts_ref, kw_ref, vw_ref, low_ref, out_ref):
    total = parts_ref[0].astype(jnp.float32)
    for i in range(1, parts_ref.shape[0]):
        total += parts_ref[i].astype(jnp.float32)
    low = total.astype(jnp.bfloat16)
    low_ref[...] = low
    me = lax.axis_index("head")
    out = project(low, kw_ref, vw_ref, me ^ owner, out_ref.shape[1])
    out_ref[...] = out.astype(out_ref.dtype)


def second_projection_kernel(owner, low_ref, kw_ref, vw_ref, out_ref):
    me = lax.axis_index("head")
    out_ref[...] = project(low_ref[...], kw_ref, vw_ref, me ^ owner, out_ref.shape[1])


def last_projection_kernel(low_ref, kw_ref, vw_ref, after, out_ref, keep_ref, dk_ref, dv_ref):
    width = dk_ref.shape[1]
    low = low_ref[...]
    dk_ref[...] = low[:, :width]
    dv_ref[...] = low[:, width:]
    me = lax.axis_index("head")
    out = project(low, kw_ref, vw_ref, me ^ 1, out_ref.shape[1])
    out_ref[...] = out.astype(out_ref.dtype)
    keep_ref[...] = project(low, kw_ref, vw_ref, me, keep_ref.shape[1])


def swap(x, axis, count, bit):
    return lax.ppermute(x, axis, [(i, i ^ bit) for i in range(count)])


def body(resp, head, queries, d_out, prefix_keys, prefix_values, k_weight, v_weight, lengths):
    own, width = prefix_keys.shape
    features = k_weight.shape[0] // head
    vmem = pl.BlockSpec(memory_space=pltpu.VMEM)
    hbm = pl.BlockSpec(memory_space=pltpu.HBM)
    params = pltpu.CompilerParams(vmem_limit_bytes=VMEM_LIMIT)

    def in_hbm(*xs):
        return [pltpu.with_memory_space_constraint(x, pltpu.HBM) for x in xs]

    both = pl.pallas_call(
        join_kernel,
        out_shape=pltpu.VMEM((resp, own, 2 * width), jnp.bfloat16),
        in_specs=[hbm] * 2,
        out_specs=vmem,
        scratch_shapes=[
            pltpu.VMEM((own, 2 * width), jnp.bfloat16),
            pltpu.SemaphoreType.DMA((2,)),
        ],
        compiler_params=params,
        name="join",
    )(*in_hbm(prefix_keys, prefix_values))
    both = lax.all_to_all(both, "resp", 0, 0, tiled=True).reshape(resp * own, 2 * width)

    queries, d_out = pl.pallas_call(
        load_kernel,
        out_shape=[pltpu.VMEM(x.shape, x.dtype) for x in (queries, d_out)],
        in_specs=[hbm] * 2,
        out_specs=[vmem] * 2,
        scratch_shapes=[pltpu.SemaphoreType.DMA((2,))],
        compiler_params=params,
        cost_estimate=pl.CostEstimate(
            flops=0, transcendentals=0, bytes_accessed=4 * queries.size * 2
        ),
        name="load",
    )(*in_hbm(queries, d_out))

    tokens = resp * own
    kv_local = width // HD
    depth = queries.size // kv_local // HD
    partial, k_weight, v_weight = pl.pallas_call(
        attention_kernel,
        out_shape=[
            pltpu.VMEM((tokens, 2 * width), jnp.bfloat16),
            pltpu.VMEM(k_weight.shape, k_weight.dtype),
            pltpu.VMEM(v_weight.shape, v_weight.dtype),
        ],
        in_specs=[pl.BlockSpec(memory_space=pltpu.SMEM)] + [vmem] * 3 + [hbm] * 2,
        out_specs=[vmem] * 3,
        scratch_shapes=[
            pltpu.VMEM((2, tokens, LEN), jnp.float32),
            pltpu.VMEM((2, tokens, LEN), jnp.float32),
            pltpu.VMEM((kv_local, tokens, depth), jnp.bfloat16),
            pltpu.VMEM((kv_local, tokens, depth), jnp.bfloat16),
            pltpu.SemaphoreType.DMA((2,)),
        ],
        compiler_params=params,
        name="attention",
    )(lengths, both, queries, d_out, *in_hbm(k_weight, v_weight))

    shares = lax.all_to_all(
        partial.reshape(resp, own, 2 * width), "resp", 0, 0, tiled=True
    )

    block = (own, features)
    low, to_core = pl.pallas_call(
        functools.partial(first_projection_kernel, 3),
        out_shape=[
            pltpu.VMEM((own, 2 * width), jnp.bfloat16),
            pltpu.VMEM(block, jnp.bfloat16),
        ],
        in_specs=[vmem] * 3,
        out_specs=[vmem] * 2,
        compiler_params=params,
        name="projection_other_core",
    )(shares, k_weight, v_weight)
    cost = pl.CostEstimate(
        flops=4 * own * width * features, transcendentals=0, bytes_accessed=4 * width * features
    )
    far = pl.pallas_call(
        functools.partial(second_projection_kernel, 2),
        out_shape=pltpu.VMEM(block, jnp.float32),
        in_specs=[vmem] * 3,
        out_specs=vmem,
        compiler_params=params,
        cost_estimate=cost,
        name="projection_other_y",
    )(low, k_weight, v_weight)
    far = (far + swap(to_core, "head", head, 1).astype(jnp.float32)).astype(jnp.bfloat16)
    got = swap(far, "head", head, 2)
    to_core, total, dk_low, dv_low = pl.pallas_call(
        last_projection_kernel,
        out_shape=[
            pltpu.VMEM(block, jnp.bfloat16),
            pltpu.VMEM(block, jnp.float32),
            jax.ShapeDtypeStruct((own, width), jnp.bfloat16),
            jax.ShapeDtypeStruct((own, width), jnp.bfloat16),
        ],
        in_specs=[vmem] * 3 + [pl.BlockSpec(memory_space=pl.ANY)],
        out_specs=[vmem] * 4,
        compiler_params=params,
        cost_estimate=cost,
        name="projection_this_y",
    )(low, k_weight, v_weight, far)
    total = lax.optimization_barrier(total + got.astype(jnp.float32))
    total += swap(to_core, "head", head, 1).astype(jnp.float32)
    return dk_low, dv_low, total.astype(jnp.bfloat16)


def solution(mesh):
    placed = (
        P("resp", "head"),
        P("resp", "head"),
        P("resp", "head"),
        P("resp", "head"),
        P(None, "head"),
        P(None, "head"),
        P("resp"),
    )
    return jax.shard_map(
        functools.partial(body, mesh.shape["resp"], mesh.shape["head"]),
        mesh=mesh,
        in_specs=placed,
        out_specs=(P("resp", "head"), P("resp", "head"), P("resp", "head")),
        check_vma=False,
    )
```

time: 38.8 us -> 38.7 us (level)
  waiting for transfers between devices: 8.11 us -> 7.21 us
  Pallas kernels: 9.7 us -> 10.5 us
    pallas_call x1, Pallas kernels: 3.48 us -> 4.94 us  [body(): pl.pallas_call(attention_kernel, out_shape=[pltpu.VMEM((tokens, 2 * width...]
    ppermute x2 -> x3, waiting for transfers between devices: 2.99 us -> 2.09 us  [swap(): return lax.ppermute(x, axis, [(i, i ^ bit) for i in range(count)])]
    pallas_call x1, Pallas kernels: 1.78 us -> 1.39 us  [body(): pl.pallas_call(join_kernel, out_shape=pltpu.VMEM((resp, own, 2 * width),...]
    pallas_call x2 -> x3, Pallas kernels: 2.88 us -> 2.56 us  [the longest x1 1.26 us: body(): pl.pallas_call(last_projection_kernel, out_shape=[pltpu.VMEM(block, jnp.b...]
    ppermute x2 -> x3, starting transfers between devices: 1.6 us -> 1.59 us  [swap(): return lax.ppermute(x, axis, [(i, i ^ bit) for i in range(count)])]
  transfers between devices with their start and end apart: 3 -> 4, of which waited for: 3 -> 3; matrix products, arithmetic and copies ran while one was open for 0% -> 0% of each run, Pallas kernels for 7% -> 9%
where the time goes in v5:
time: 38.7 us; the launch traced here: 38.3 us
  Pallas kernels  10.5 us (27%)
  blocking collectives  9.74 us (25%)
  starting transfers between devices  8.85 us (23%)
  waiting for transfers between devices  7.21 us (19%)
  between operations  1.33 us (3%)
  other arithmetic  0.67 us (2%)
    all_to_all x1, blocking collectives, body(): lax.all_to_all(partial.reshape(resp, own, 2 * width), 'resp', 0, 0, tiled...  9.74 us
    all_to_all x1, starting transfers between devices, body(): lax.all_to_all(both, 'resp', 0, 0, tiled=True)  7.26 us
    all_to_all x1, waiting for transfers between devices, body(): lax.all_to_all(both, 'resp', 0, 0, tiled=True)  5.12 us
    pallas_call x1, Pallas kernels, body(): pl.pallas_call(attention_kernel, out_shape=[pltpu.VMEM((tokens, 2 * width...  4.94 us
    ppermute x3, waiting for transfers between devices, swap(): return lax.ppermute(x, axis, [(i, i ^ bit) for i in range(count)])  2.09 us
    ppermute x3, starting transfers between devices, swap(): return lax.ppermute(x, axis, [(i, i ^ bit) for i in range(count)])  1.59 us
    pallas_call x1, Pallas kernels, body(): pl.pallas_call(load_kernel, out_shape=[pltpu.VMEM(x.shape, x.dtype) for x...  1.56 us
    pallas_call x1, Pallas kernels, body(): pl.pallas_call(join_kernel, out_shape=pltpu.VMEM((resp, own, 2 * width),...  1.39 us
  transfers between devices with their start and end apart: 4, of which 3 were waited for; matrix products, arithmetic and copies ran while one was open for 0% of the time, Pallas kernels for 9%

profile of v5, /device:TPU:0, one launch (start us, length us, event | category | flops | bytes accessed | tf_op | source)
XLA Modules:
  0.0 38.3 jit_solution(4462915103861758222)
XLA Ops:
  0.6 1.4 %join.1 = bf16[8,16,512]{2,1,0:T(8,128)(2,1)} custom-call(bf16[16,256]{1,0:T(8,128)(2,1)} %k_hbm.1, bf16[16,256]{1,0:T(8,128)(2,1)} %v_hbm.1), custom_call_target="tpu_custom_call" | custom-call | tf_op jit(solution)/shard_map/join/pallas_call | solution.py:172
  2.0 7.3 %all-to-all-start = ((bf16[8,16,512]{2,1,0:T(8,128)(2,1)}), bf16[8,16,512]{2,1,0:T(8,128)(2,1)S(1)}, u32[]{:S(2)}, u32[]{:S(2)}) async-start(bf16[8,16,512]{2,1,0:T(8,128)(2,1)} %join.1), calls=%async_computation | async-start | bytes 262144 | tf_op jit(solution)/shard_map/all_to_all | solution.py:184
  9.9 1.6 %load.1 = (bf16[256,2048]{1,0:T(8,128)(2,1)S(1)}, bf16[256,2048]{1,0:T(8,128)(2,1)S(1)}) custom-call(bf16[256,2048]{1,0:T(8,128)(2,1)} %q_hbm.1, bf16[256,2048]{1,0:T(8,128)(2,1)} %g_hbm.1), custom_call_target="tpu_custom_call" | custom-call | bytes 4194304 | tf_op jit(solution)/shard_map/load/pallas_call | solution.py:186
  11.5 5.1 %all-to-all-done = bf16[8,16,512]{2,1,0:T(8,128)(2,1)S(1)} async-done(((bf16[8,16,512]{2,1,0:T(8,128)(2,1)}), bf16[8,16,512]{2,1,0:T(8,128)(2,1)S(1)}, u32[]{:S(2)}, u32[]{:S(2)}) %all-to-all-start) | async-done | bytes 131104 | tf_op jit(solution)/shard_map/all_to_all | solution.py:184
  16.6 4.9 %attention.1 = (bf16[128,512]{1,0:T(8,128)(2,1)S(1)}, bf16[8192,256]{1,0:T(8,128)(2,1)S(1)}, bf16[8192,256]{1,0:T(8,128)(2,1)S(1)}) custom-call(s32[1]{0:T(128)S(6)} %copy.10.lengths_ref, bf16[128,512]{1,0:T(8,128)(2,1)S(1)} %bitcast.2, bf16[256,2048]{1,0:T(8,128)(2,1)S(1)} %get-tuple-element.14.q_ref, bf16[256,2048]{1,0:T(8,128)(2,1)S(1)} %get-tuple-element.15.g_ref, ...), custom_call_target="tpu_custom_call" | custom-call | tf_op jit(solution)/shard_map/attention/pallas_call | solution.py:202
  21.6 9.7 %all_to_all.10.parts_ref = bf16[8,16,512]{2,1,0:T(8,128)(2,1)S(1)} all-to-all(bf16[8,16,512]{2,1,0:T(8,128)(2,1)S(1)} %bitcast.3), channel_id=1, replica_groups=mesh['resp'=8,'head'=4] {'resp'}, dimensions={0} | all-to-all | bytes 262144 | tf_op jit(solution)/shard_map/all_to_all | solution.py:222
  31.3 0.6 %projection_other_core.1 = (bf16[16,512]{1,0:T(8,128)(2,1)S(1)}, bf16[16,2048]{1,0:T(8,128)(2,1)S(1)}) custom-call(bf16[8,16,512]{2,1,0:T(8,128)(2,1)S(1)} %all_to_all.10.parts_ref, bf16[8192,256]{1,0:T(8,128)(2,1)S(1)} %get-tuple-element.17.kw_ref, bf16[8192,256]{1,0:T(8,128)(2,1)S(1)} %get-tuple-element.18.vw_ref), custom_call_target="tpu_custom_call" | custom-call | tf_op jit(solution)/shard_map/projection_other_core/pallas_call | solution.py:227
  32.0 0.0 collective-permute-start
  32.0 0.7 %projection_other_y.1 = f32[16,2048]{1,0:T(8,128)S(1)} custom-call(bf16[16,512]{1,0:T(8,128)(2,1)S(1)} %get-tuple-element.19.low_ref, bf16[8192,256]{1,0:T(8,128)(2,1)S(1)} %get-tuple-element.17.kw_ref, bf16[8192,256]{1,0:T(8,128)(2,1)S(1)} %get-tuple-element.18.vw_ref), custom_call_target="tpu_custom_call" | custom-call | flops 33554432 | bytes 2097152 | tf_op jit(solution)/shard_map/projection_other_y/pallas_call | solution.py:241
  32.6 0.6 %collective-permute-done = bf16[16,2048]{1,0:T(8,128)(2,1)S(1)} collective-permute-done((bf16[16,2048]{1,0:T(8,128)(2,1)S(1)}, bf16[16,2048]{1,0:T(8,128)(2,1)S(1)}, u32[]{:S(2)}, u32[]{:S(2)}) %collective-permute-start) | collective-permute-done | bytes 65568 | tf_op jit(solution)/shard_map/ppermute | solution.py:159
  33.3 1.6 %collective-permute-start.1 = (bf16[16,2048]{1,0:T(8,128)(2,1)S(1)}, bf16[16,2048]{1,0:T(8,128)(2,1)S(1)}, u32[]{:S(2)}, u32[]{:S(2)}) collective-permute-start(bf16[16,2048]{1,0:T(8,128)(2,1)S(1)} %add_convert_fusion.1.after), channel_id=1, source_target_pairs={{0,2},{1,3},{2,0},{3,1},{4,6},{5,7},{6,4},{7,5},{8,10},{9,11},{10,... | collective-permute-start | bytes 196616 | tf_op jit(solution)/shard_map/ppermute | solution.py:159
  34.8 1.3 %projection_this_y.1 = (bf16[16,2048]{1,0:T(8,128)(2,1)S(1)}, f32[16,2048]{1,0:T(8,128)S(1)}, bf16[16,256]{1,0:T(8,128)(2,1)}, bf16[16,256]{1,0:T(8,128)(2,1)}) custom-call(bf16[16,512]{1,0:T(8,128)(2,1)S(1)} %get-tuple-element.19.low_ref, bf16[8192,256]{1,0:T(8,128)(2,1)S(1)} %get-tuple-element.17.kw_ref, bf16[8192,256]{1,0:T(8,128)(2,1)S(1)} %get-tuple-element.18.vw_ref, ...), custom_call_target="tpu_custom_call" | custom-call | flops 33554432 | bytes 2097152 | tf_op jit(solution)/shard_map/projection_this_y/pallas_call | solution.py:252
  36.1 0.0 collective-permute-start.2
  36.1 1.5 %collective-permute-done.1 = bf16[16,2048]{1,0:T(8,128)(2,1)S(1)} collective-permute-done((bf16[16,2048]{1,0:T(8,128)(2,1)S(1)}, bf16[16,2048]{1,0:T(8,128)(2,1)S(1)}, u32[]{:S(2)}, u32[]{:S(2)}) %collective-permute-start.1) | collective-permute-done | bytes 65568 | tf_op jit(solution)/shard_map/ppermute | solution.py:159
  37.6 0.0 collective-permute-done.2
  37.6 0.6 %add_convert_fusion = bf16[16,2048]{1,0:T(8,128)(2,1)} fusion(f32[16,2048]{1,0:T(8,128)S(1)} %convert_add_fusion, bf16[16,2048]{1,0:T(8,128)(2,1)S(1)} %collective-permute-done.2), kind=kLoop, calls=%fused_computation | loop fusion | flops 98304 | bytes 262144 | tf_op jit(solution)/shard_map/convert_element_type | solution.py:268
  (2 shorter events, 0.0 us)
Async XLA Ops:
  2.0 14.6 %all-to-all-start = ((bf16[8,16,512]{2,1,0:T(8,128)(2,1)}), bf16[8,16,512]{2,1,0:T(8,128)(2,1)S(1)}, u32[]{:S(2)}, u32[]{:S(2)}) async-start(bf16[8,16,512]{2,1,0:T(8,128)(2,1)} %join.1), calls=%async_computation | async-start | bytes 262144 | tf_op jit(solution)/shard_map/all_to_all | solution.py:184
  32.0 1.3 %collective-permute-start = (bf16[16,2048]{1,0:T(8,128)(2,1)S(1)}, bf16[16,2048]{1,0:T(8,128)(2,1)S(1)}, u32[]{:S(2)}, u32[]{:S(2)}) collective-permute-start(bf16[16,2048]{1,0:T(8,128)(2,1)S(1)} %get-tuple-element.20), channel_id=1, source_target_pairs={{0,1},{1,0},{2,3},{3,2},{4,5},{5,4},{6,7},{7,6},{8,9},{9,8},{10,11... | collective-permute-start | bytes 196616 | tf_op jit(solution)/shard_map/ppermute | solution.py:159
  33.3 4.3 %collective-permute-start.1 = (bf16[16,2048]{1,0:T(8,128)(2,1)S(1)}, bf16[16,2048]{1,0:T(8,128)(2,1)S(1)}, u32[]{:S(2)}, u32[]{:S(2)}) collective-permute-start(bf16[16,2048]{1,0:T(8,128)(2,1)S(1)} %add_convert_fusion.1.after), channel_id=1, source_target_pairs={{0,2},{1,3},{2,0},{3,1},{4,6},{5,7},{6,4},{7,5},{8,10},{9,11},{10,... | collective-permute-start | bytes 196616 | tf_op jit(solution)/shard_map/ppermute | solution.py:159
  36.1 1.5 %collective-permute-start.2 = (bf16[16,2048]{1,0:T(8,128)(2,1)S(1)}, bf16[16,2048]{1,0:T(8,128)(2,1)S(1)}, u32[]{:S(2)}, u32[]{:S(2)}) collective-permute-start(bf16[16,2048]{1,0:T(8,128)(2,1)S(1)} %get-tuple-element.24), channel_id=1, source_target_pairs={{0,1},{1,0},{2,3},{3,2},{4,5},{5,4},{6,7},{7,6},{8,9},{9,8},{10,11... | collective-permute-start | bytes 196616 | tf_op jit(solution)/shard_map/ppermute | solution.py:159

commit v6 on v5

--- a/solution.py
+++ b/solution.py
@@ -11,22 +11,22 @@
 LEN = 256
 NT = (((1,), (1,)), ((), ()))
 VMEM_LIMIT = 40 << 20
+UNIT = 2
 LOG2E = 1.4426950408889634
 
 
-def join_kernel(k_hbm, v_hbm, out_ref, both_ref, sems):
+def join_kernel(k_hbm, v_hbm, out_hbm, sems):
     width = k_hbm.shape[1]
-    copies = [
-        pltpu.make_async_copy(k_hbm, both_ref.at[:, pl.ds(0, width)], sems.at[0]),
-        pltpu.make_async_copy(v_hbm, both_ref.at[:, pl.ds(width, width)], sems.at[1]),
-    ]
+    copies = []
+    for i in range(out_hbm.shape[0]):
+        copies += [
+            pltpu.make_async_copy(k_hbm, out_hbm.at[i, :, pl.ds(0, width)], sems.at[0, i]),
+            pltpu.make_async_copy(v_hbm, out_hbm.at[i, :, pl.ds(width, width)], sems.at[1, i]),
+        ]
     for copy in copies:
         copy.start()
     for copy in copies:
         copy.wait()
-    both = both_ref[...]
-    for i in range(out_ref.shape[0]):
-        out_ref[i] = both
 
 
 def load_kernel(q_hbm, g_hbm, q_ref, g_ref, sems):
@@ -50,8 +50,6 @@
     out_ref,
     kw_ref,
     vw_ref,
-    scores_ref,
-    dprobs_ref,
     probs_ref,
     dscores_ref,
     sems,
@@ -67,48 +65,52 @@
     kv_local = width // HD
     parts = q_ref.shape[0] // LEN
     group = q_ref.shape[1] // HD // kv_local
-    position = lax.broadcasted_iota(jnp.int32, (1, HD), 1)
-    units = [(k, h, part) for k in range(kv_local) for h in range(group) for part in range(parts)]
-
-    def place(unit):
-        k, h, part = unit
-        return pl.ds(part * LEN, LEN), pl.ds((k * group + h) * HD, HD)
-
-    def products(i):
-        k = units[i][0]
-        where = place(units[i])
+    position = lax.broadcasted_iota(jnp.int32, (1, UNIT * LEN), 1) % LEN
+    units = [
+        (k, part, h)
+        for k in range(kv_local)
+        for part in range(parts)
+        for h in range(0, group, UNIT)
+    ]
+
+    def stack(ref, unit):
+        k, part, h = unit
+        heads = [
+            ref[part * LEN : (part + 1) * LEN, at * HD : (at + 1) * HD]
+            for at in range(k * group + h, k * group + h + UNIT)
+        ]
+        return jnp.concatenate(heads, axis=0)
+
+    def products(unit):
+        k = unit[0]
         keys = kv_ref[:, k * HD : (k + 1) * HD]
         values = kv_ref[:, width + k * HD : width + (k + 1) * HD]
-        scores_ref[i % 2] = lax.dot_general(
-            keys, q_ref[where], NT, preferred_element_type=jnp.float32
+        return (
+            lax.dot_general(keys, stack(q_ref, unit), NT, preferred_element_type=jnp.float32),
+            lax.dot_general(values, stack(g_ref, unit), NT, preferred_element_type=jnp.float32),
         )
-        dprobs_ref[i % 2] = lax.dot_general(
-            values, g_ref[where], NT, preferred_element_type=jnp.float32
-        )
-
-    products(0)
+
+    following = products(units[0])
     for i, unit in enumerate(units):
-        k, h, part = unit
+        k, part, h = unit
+        scores, dprobs = following
         if i + 1 < len(units):
-            products(i + 1)
-        for start in range(0, LEN, HD):
-            scores = scores_ref[i % 2, :, start : start + HD]
-            dprobs = dprobs_ref[i % 2, :, start : start + HD]
-            top = jnp.max(scores, axis=0, keepdims=True)
-            expo = jnp.exp2((scores - top) * (scale * LOG2E))
-            total = jnp.sum(expo, axis=0, keepdims=True)
-            weighted = jnp.sum(expo * dprobs, axis=0, keepdims=True)
-            inverse = 1.0 / total
-            delta = weighted * inverse
-            factor = jnp.where(position + start < lengths_ref[part], inverse, 0.0)
-            probs = expo * factor
-            at = (h * parts + part) * LEN + start
-            probs_ref[k, :, at : at + HD] = probs.astype(jnp.bfloat16)
-            dscores_ref[k, :, at : at + HD] = (probs * (dprobs - delta)).astype(jnp.bfloat16)
-        if (h, part) == (group - 1, parts - 1):
-            mine = [place(u) for u in units if u[0] == k]
-            q_all = jnp.concatenate([q_ref[where] for where in mine], axis=0)
-            g_all = jnp.concatenate([g_ref[where] for where in mine], axis=0)
+            following = products(units[i + 1])
+        top = jnp.max(scores, axis=0, keepdims=True)
+        expo = jnp.exp2((scores - top) * (scale * LOG2E))
+        total = jnp.sum(expo, axis=0, keepdims=True)
+        weighted = jnp.sum(expo * dprobs, axis=0, keepdims=True)
+        inverse = 1.0 / total
+        delta = weighted * inverse
+        factor = jnp.where(position < lengths_ref[part], inverse, 0.0)
+        probs = expo * factor
+        mine = [u for u in units if u[0] == k]
+        cols = pl.ds(mine.index(unit) * UNIT * LEN, UNIT * LEN)
+        probs_ref[k, :, cols] = probs.astype(jnp.bfloat16)
+        dscores_ref[k, :, cols] = (probs * (dprobs - delta)).astype(jnp.bfloat16)
+        if unit == mine[-1]:
+            q_all = jnp.concatenate([stack(q_ref, u) for u in mine], axis=0)
+            g_all = jnp.concatenate([stack(g_ref, u) for u in mine], axis=0)
             grad_k = jnp.dot(dscores_ref[k], q_all, preferred_element_type=jnp.float32) * scale
             grad_v = jnp.dot(probs_ref[k], g_all, preferred_element_type=jnp.float32)
             out_ref[:, k * HD : (k + 1) * HD] = grad_k.astype(out_ref.dtype)
@@ -171,13 +173,10 @@
 
     both = pl.pallas_call(
         join_kernel,
-        out_shape=pltpu.VMEM((resp, own, 2 * width), jnp.bfloat16),
+        out_shape=jax.ShapeDtypeStruct((resp, own, 2 * width), jnp.bfloat16),
         in_specs=[hbm] * 2,
-        out_specs=vmem,
-        scratch_shapes=[
-            pltpu.VMEM((own, 2 * width), jnp.bfloat16),
-            pltpu.SemaphoreType.DMA((2,)),
-        ],
+        out_specs=hbm,
+        scratch_shapes=[pltpu.SemaphoreType.DMA((2, resp))],
         compiler_params=params,
         name="join",
     )(*in_hbm(prefix_keys, prefix_values))
@@ -209,8 +208,6 @@
         in_specs=[pl.BlockSpec(memory_space=pltpu.SMEM)] + [vmem] * 3 + [hbm] * 2,
         out_specs=[vmem] * 3,
         scratch_shapes=[
-            pltpu.VMEM((2, tokens, LEN), jnp.float32),
-            pltpu.VMEM((2, tokens, LEN), jnp.float32),
             pltpu.VMEM((kv_local, tokens, depth), jnp.bfloat16),
             pltpu.VMEM((kv_local, tokens, depth), jnp.bfloat16),
             pltpu.SemaphoreType.DMA((2,)),

time: 38.7 us -> 40.9 us (1.057)
  Pallas kernels: 10.5 us -> 12.8 us
    pallas_call x1, Pallas kernels: 1.39 us -> 5.22 us  [body(): pl.pallas_call(join_kernel, out_shape=jax.ShapeDtypeStruct((resp, own, 2...]
    pallas_call x1, Pallas kernels: 4.94 us -> 3.48 us  [body(): pl.pallas_call(attention_kernel, out_shape=[pltpu.VMEM((tokens, 2 * width...]
where the time goes in v6:
time: 40.9 us; the launch traced here: 40.6 us
  Pallas kernels  12.8 us (31%)
  blocking collectives  9.74 us (24%)
  starting transfers between devices  8.85 us (22%)
  waiting for transfers between devices  7.21 us (18%)
  between operations  1.33 us (3%)
  other arithmetic  0.67 us (2%)
    all_to_all x1, blocking collectives, body(): lax.all_to_all(partial.reshape(resp, own, 2 * width), 'resp', 0, 0, tiled...  9.74 us
    all_to_all x1, starting transfers between devices, body(): lax.all_to_all(both, 'resp', 0, 0, tiled=True)  7.26 us
    pallas_call x1, Pallas kernels, body(): pl.pallas_call(join_kernel, out_shape=jax.ShapeDtypeStruct((resp, own, 2...  5.22 us
    all_to_all x1, waiting for transfers between devices, body(): lax.all_to_all(both, 'resp', 0, 0, tiled=True)  5.12 us
    pallas_call x1, Pallas kernels, body(): pl.pallas_call(attention_kernel, out_shape=[pltpu.VMEM((tokens, 2 * width...  3.48 us
    ppermute x3, waiting for transfers between devices, swap(): return lax.ppermute(x, axis, [(i, i ^ bit) for i in range(count)])  2.09 us
    ppermute x3, starting transfers between devices, swap(): return lax.ppermute(x, axis, [(i, i ^ bit) for i in range(count)])  1.59 us
    pallas_call x1, Pallas kernels, body(): pl.pallas_call(load_kernel, out_shape=[pltpu.VMEM(x.shape, x.dtype) for x...  1.56 us
  transfers between devices with their start and end apart: 4, of which 3 were waited for; matrix products, arithmetic and copies ran while one was open for 0% of the time, Pallas kernels for 9%

profile of v6, /device:TPU:0, one launch (start us, length us, event | category | flops | bytes accessed | tf_op | source)
XLA Modules:
  0.0 40.6 jit_solution(16714324872516438071)
XLA Ops:
  0.6 5.2 %join.1 = bf16[8,16,512]{2,1,0:T(8,128)(2,1)} custom-call(bf16[16,256]{1,0:T(8,128)(2,1)} %k_hbm.1, bf16[16,256]{1,0:T(8,128)(2,1)} %v_hbm.1), custom_call_target="tpu_custom_call" | custom-call | tf_op jit(solution)/shard_map/join/pallas_call | solution.py:174
  5.9 7.3 %all-to-all-start = ((bf16[8,16,512]{2,1,0:T(8,128)(2,1)}), bf16[8,16,512]{2,1,0:T(8,128)(2,1)S(1)}, u32[]{:S(2)}, u32[]{:S(2)}) async-start(bf16[8,16,512]{2,1,0:T(8,128)(2,1)} %join.1), calls=%async_computation | async-start | bytes 262144 | tf_op jit(solution)/shard_map/all_to_all | solution.py:183
  13.8 1.6 %load.1 = (bf16[256,2048]{1,0:T(8,128)(2,1)S(1)}, bf16[256,2048]{1,0:T(8,128)(2,1)S(1)}) custom-call(bf16[256,2048]{1,0:T(8,128)(2,1)} %q_hbm.1, bf16[256,2048]{1,0:T(8,128)(2,1)} %g_hbm.1), custom_call_target="tpu_custom_call" | custom-call | bytes 4194304 | tf_op jit(solution)/shard_map/load/pallas_call | solution.py:185
  15.3 5.1 %all-to-all-done = bf16[8,16,512]{2,1,0:T(8,128)(2,1)S(1)} async-done(((bf16[8,16,512]{2,1,0:T(8,128)(2,1)}), bf16[8,16,512]{2,1,0:T(8,128)(2,1)S(1)}, u32[]{:S(2)}, u32[]{:S(2)}) %all-to-all-start) | async-done | bytes 131104 | tf_op jit(solution)/shard_map/all_to_all | solution.py:183
  20.5 3.5 %attention.1 = (bf16[128,512]{1,0:T(8,128)(2,1)S(1)}, bf16[8192,256]{1,0:T(8,128)(2,1)S(1)}, bf16[8192,256]{1,0:T(8,128)(2,1)S(1)}) custom-call(s32[1]{0:T(128)S(6)} %copy.10.lengths_ref, bf16[128,512]{1,0:T(8,128)(2,1)S(1)} %bitcast.2, bf16[256,2048]{1,0:T(8,128)(2,1)S(1)} %get-tuple-element.14.q_ref, bf16[256,2048]{1,0:T(8,128)(2,1)S(1)} %get-tuple-element.15.g_ref, ...), custom_call_target="tpu_custom_call" | custom-call | tf_op jit(solution)/shard_map/attention/pallas_call | solution.py:201
  24.0 9.7 %all_to_all.10.parts_ref = bf16[8,16,512]{2,1,0:T(8,128)(2,1)S(1)} all-to-all(bf16[8,16,512]{2,1,0:T(8,128)(2,1)S(1)} %bitcast.3), channel_id=1, replica_groups=mesh['resp'=8,'head'=4] {'resp'}, dimensions={0} | all-to-all | bytes 262144 | tf_op jit(solution)/shard_map/all_to_all | solution.py:219
  33.7 0.6 %projection_other_core.1 = (bf16[16,512]{1,0:T(8,128)(2,1)S(1)}, bf16[16,2048]{1,0:T(8,128)(2,1)S(1)}) custom-call(bf16[8,16,512]{2,1,0:T(8,128)(2,1)S(1)} %all_to_all.10.parts_ref, bf16[8192,256]{1,0:T(8,128)(2,1)S(1)} %get-tuple-element.17.kw_ref, bf16[8192,256]{1,0:T(8,128)(2,1)S(1)} %get-tuple-element.18.vw_ref), custom_call_target="tpu_custom_call" | custom-call | tf_op jit(solution)/shard_map/projection_other_core/pallas_call | solution.py:224
  34.3 0.0 collective-permute-start
  34.4 0.7 %projection_other_y.1 = f32[16,2048]{1,0:T(8,128)S(1)} custom-call(bf16[16,512]{1,0:T(8,128)(2,1)S(1)} %get-tuple-element.19.low_ref, bf16[8192,256]{1,0:T(8,128)(2,1)S(1)} %get-tuple-element.17.kw_ref, bf16[8192,256]{1,0:T(8,128)(2,1)S(1)} %get-tuple-element.18.vw_ref), custom_call_target="tpu_custom_call" | custom-call | flops 33554432 | bytes 2097152 | tf_op jit(solution)/shard_map/projection_other_y/pallas_call | solution.py:238
  35.0 0.6 %collective-permute-done = bf16[16,2048]{1,0:T(8,128)(2,1)S(1)} collective-permute-done((bf16[16,2048]{1,0:T(8,128)(2,1)S(1)}, bf16[16,2048]{1,0:T(8,128)(2,1)S(1)}, u32[]{:S(2)}, u32[]{:S(2)}) %collective-permute-start) | collective-permute-done | bytes 65568 | tf_op jit(solution)/shard_map/ppermute | solution.py:161
  35.6 1.6 %collective-permute-start.1 = (bf16[16,2048]{1,0:T(8,128)(2,1)S(1)}, bf16[16,2048]{1,0:T(8,128)(2,1)S(1)}, u32[]{:S(2)}, u32[]{:S(2)}) collective-permute-start(bf16[16,2048]{1,0:T(8,128)(2,1)S(1)} %add_convert_fusion.1.after), channel_id=1, source_target_pairs={{0,2},{1,3},{2,0},{3,1},{4,6},{5,7},{6,4},{7,5},{8,10},{9,11},{10,... | collective-permute-start | bytes 196616 | tf_op jit(solution)/shard_map/ppermute | solution.py:161
  37.2 1.3 %projection_this_y.1 = (bf16[16,2048]{1,0:T(8,128)(2,1)S(1)}, f32[16,2048]{1,0:T(8,128)S(1)}, bf16[16,256]{1,0:T(8,128)(2,1)}, bf16[16,256]{1,0:T(8,128)(2,1)}) custom-call(bf16[16,512]{1,0:T(8,128)(2,1)S(1)} %get-tuple-element.19.low_ref, bf16[8192,256]{1,0:T(8,128)(2,1)S(1)} %get-tuple-element.17.kw_ref, bf16[8192,256]{1,0:T(8,128)(2,1)S(1)} %get-tuple-element.18.vw_ref, ...), custom_call_target="tpu_custom_call" | custom-call | flops 33554432 | bytes 2097152 | tf_op jit(solution)/shard_map/projection_this_y/pallas_call | solution.py:249
  38.5 0.0 collective-permute-start.2
  38.5 1.5 %collective-permute-done.1 = bf16[16,2048]{1,0:T(8,128)(2,1)S(1)} collective-permute-done((bf16[16,2048]{1,0:T(8,128)(2,1)S(1)}, bf16[16,2048]{1,0:T(8,128)(2,1)S(1)}, u32[]{:S(2)}, u32[]{:S(2)}) %collective-permute-start.1) | collective-permute-done | bytes 65568 | tf_op jit(solution)/shard_map/ppermute | solution.py:161
  40.0 0.0 collective-permute-done.2
  40.0 0.6 %add_convert_fusion = bf16[16,2048]{1,0:T(8,128)(2,1)} fusion(f32[16,2048]{1,0:T(8,128)S(1)} %convert_add_fusion, bf16[16,2048]{1,0:T(8,128)(2,1)S(1)} %collective-permute-done.2), kind=kLoop, calls=%fused_computation | loop fusion | flops 98304 | bytes 262144 | tf_op jit(solution)/shard_map/convert_element_type | solution.py:265
  (2 shorter events, 0.0 us)
Async XLA Ops:
  5.9 14.6 %all-to-all-start = ((bf16[8,16,512]{2,1,0:T(8,128)(2,1)}), bf16[8,16,512]{2,1,0:T(8,128)(2,1)S(1)}, u32[]{:S(2)}, u32[]{:S(2)}) async-start(bf16[8,16,512]{2,1,0:T(8,128)(2,1)} %join.1), calls=%async_computation | async-start | bytes 262144 | tf_op jit(solution)/shard_map/all_to_all | solution.py:183
  34.3 1.3 %collective-permute-start = (bf16[16,2048]{1,0:T(8,128)(2,1)S(1)}, bf16[16,2048]{1,0:T(8,128)(2,1)S(1)}, u32[]{:S(2)}, u32[]{:S(2)}) collective-permute-start(bf16[16,2048]{1,0:T(8,128)(2,1)S(1)} %get-tuple-element.20), channel_id=1, source_target_pairs={{0,1},{1,0},{2,3},{3,2},{4,5},{5,4},{6,7},{7,6},{8,9},{9,8},{10,11... | collective-permute-start | bytes 196616 | tf_op jit(solution)/shard_map/ppermute | solution.py:161
  35.6 4.3 %collective-permute-start.1 = (bf16[16,2048]{1,0:T(8,128)(2,1)S(1)}, bf16[16,2048]{1,0:T(8,128)(2,1)S(1)}, u32[]{:S(2)}, u32[]{:S(2)}) collective-permute-start(bf16[16,2048]{1,0:T(8,128)(2,1)S(1)} %add_convert_fusion.1.after), channel_id=1, source_target_pairs={{0,2},{1,3},{2,0},{3,1},{4,6},{5,7},{6,4},{7,5},{8,10},{9,11},{10,... | collective-permute-start | bytes 196616 | tf_op jit(solution)/shard_map/ppermute | solution.py:161
  38.5 1.5 %collective-permute-start.2 = (bf16[16,2048]{1,0:T(8,128)(2,1)S(1)}, bf16[16,2048]{1,0:T(8,128)(2,1)S(1)}, u32[]{:S(2)}, u32[]{:S(2)}) collective-permute-start(bf16[16,2048]{1,0:T(8,128)(2,1)S(1)} %get-tuple-element.24), channel_id=1, source_target_pairs={{0,1},{1,0},{2,3},{3,2},{4,5},{5,4},{6,7},{7,6},{8,9},{9,8},{10,11... | collective-permute-start | bytes 196616 | tf_op jit(solution)/shard_map/ppermute | solution.py:161

commit v7 on v6

--- a/solution.py
+++ b/solution.py
@@ -15,57 +15,46 @@
 LOG2E = 1.4426950408889634
 
 
-def join_kernel(k_hbm, v_hbm, out_hbm, sems):
+def join_kernel(k_hbm, v_hbm, out_ref, both_ref, sems):
     width = k_hbm.shape[1]
-    copies = []
-    for i in range(out_hbm.shape[0]):
-        copies += [
-            pltpu.make_async_copy(k_hbm, out_hbm.at[i, :, pl.ds(0, width)], sems.at[0, i]),
-            pltpu.make_async_copy(v_hbm, out_hbm.at[i, :, pl.ds(width, width)], sems.at[1, i]),
-        ]
+    copies = [
+        pltpu.make_async_copy(k_hbm, both_ref.at[:, pl.ds(0, width)], sems.at[0]),
+        pltpu.make_async_copy(v_hbm, both_ref.at[:, pl.ds(width, width)], sems.at[1]),
+    ]
     for copy in copies:
         copy.start()
     for copy in copies:
         copy.wait()
-
-
-def load_kernel(q_hbm, g_hbm, q_ref, g_ref, sems):
+    both = both_ref[...]
+    for i in range(out_ref.shape[0]):
+        out_ref[i] = both
+
+
+def load_kernel(lengths_ref, *refs):
+    count = (len(refs) - 2) // 2
+    live_ref, sems = refs[2 * count :]
     copies = [
-        pltpu.make_async_copy(q_hbm, q_ref, sems.at[0]),
-        pltpu.make_async_copy(g_hbm, g_ref, sems.at[1]),
+        pltpu.make_async_copy(refs[i], refs[count + i], sems.at[i]) for i in range(count)
     ]
     for copy in copies:
         copy.start()
+    position = lax.broadcasted_iota(jnp.int32, live_ref.shape[1:], 1)
+    for part in range(live_ref.shape[0]):
+        live_ref[part] = jnp.where(position < lengths_ref[part], 1.0, 0.0)
     for copy in copies:
         copy.wait()
 
 
 def attention_kernel(
-    lengths_ref,
-    kv_ref,
-    q_ref,
-    g_ref,
-    kw_hbm,
-    vw_hbm,
-    out_ref,
-    kw_ref,
-    vw_ref,
-    probs_ref,
-    dscores_ref,
-    sems,
+    live_ref, kv_ref, q_ref, g_ref, vw_hbm, out_ref, vw_ref, probs_ref, dscores_ref, sem
 ):
-    weights = [
-        pltpu.make_async_copy(kw_hbm, kw_ref, sems.at[0]),
-        pltpu.make_async_copy(vw_hbm, vw_ref, sems.at[1]),
-    ]
-    for copy in weights:
-        copy.start()
+    weight = pltpu.make_async_copy(vw_hbm, vw_ref, sem)
+    weight.start()
     scale = HD ** (-0.5)
     width = kv_ref.shape[1] // 2
     kv_local = width // HD
     parts = q_ref.shape[0] // LEN
     group = q_ref.shape[1] // HD // kv_local
-    position = lax.broadcasted_iota(jnp.int32, (1, UNIT * LEN), 1) % LEN
     units = [
         (k, part, h)
         for k in range(kv_local)
@@ -102,7 +91,7 @@
         weighted = jnp.sum(expo * dprobs, axis=0, keepdims=True)
         inverse = 1.0 / total
         delta = weighted * inverse
-        factor = jnp.where(position < lengths_ref[part], inverse, 0.0)
+        factor = inverse * jnp.concatenate([live_ref[part, :1]] * UNIT, axis=1)
         probs = expo * factor
         mine = [u for u in units if u[0] == k]
         cols = pl.ds(mine.index(unit) * UNIT * LEN, UNIT * LEN)
@@ -115,8 +104,7 @@
             grad_v = jnp.dot(probs_ref[k], g_all, preferred_element_type=jnp.float32)
             out_ref[:, k * HD : (k + 1) * HD] = grad_k.astype(out_ref.dtype)
             out_ref[:, width + k * HD : width + (k + 1) * HD] = grad_v.astype(out_ref.dtype)
-    for copy in weights:
-        copy.wait()
+    weight.wait()
 
 
 def project(low, kw_ref, vw_ref, owner, features):
@@ -175,46 +163,51 @@
         join_kernel,
         out_shape=jax.ShapeDtypeStruct((resp, own, 2 * width), jnp.bfloat16),
         in_specs=[hbm] * 2,
-        out_specs=hbm,
-        scratch_shapes=[pltpu.SemaphoreType.DMA((2, resp))],
+        out_specs=vmem,
+        scratch_shapes=[
+            pltpu.VMEM((own, 2 * width), jnp.bfloat16),
+            pltpu.SemaphoreType.DMA((2,)),
+        ],
         compiler_params=params,
         name="join",
     )(*in_hbm(prefix_keys, prefix_values))
     both = lax.all_to_all(both, "resp", 0, 0, tiled=True).reshape(resp * own, 2 * width)
 
-    queries, d_out = pl.pallas_call(
+    large = (queries, d_out, k_weight)
+    responses = lengths.shape[0]
+    queries, d_out, k_weight, live = pl.pallas_call(
         load_kernel,
-        out_shape=[pltpu.VMEM(x.shape, x.dtype) for x in (queries, d_out)],
-        in_specs=[hbm] * 2,
-        out_specs=[vmem] * 2,
-        scratch_shapes=[pltpu.SemaphoreType.DMA((2,))],
+        out_shape=[pltpu.VMEM(x.shape, x.dtype) for x in large]
+        + [pltpu.VMEM((responses, 8, LEN), jnp.float32)],
+        in_specs=[pl.BlockSpec(memory_space=pltpu.SMEM)] + [hbm] * len(large),
+        out_specs=[vmem] * (len(large) + 1),
+        scratch_shapes=[pltpu.SemaphoreType.DMA((len(large),))],
         compiler_params=params,
         cost_estimate=pl.CostEstimate(
-            flops=0, transcendentals=0, bytes_accessed=4 * queries.size * 2
+            flops=0, transcendentals=0, bytes_accessed=sum(4 * x.size for x in large)
         ),
         name="load",
-    )(*in_hbm(queries, d_out))
+    )(lengths, *in_hbm(*large))
 
     tokens = resp * own
     kv_local = width // HD
     depth = queries.size // kv_local // HD
-    partial, k_weight, v_weight = pl.pallas_call(
+    partial, v_weight = pl.pallas_call(
         attention_kernel,
         out_shape=[
             pltpu.VMEM((tokens, 2 * width), jnp.bfloat16),
-            pltpu.VMEM(k_weight.shape, k_weight.dtype),
             pltpu.VMEM(v_weight.shape, v_weight.dtype),
         ],
-        in_specs=[pl.BlockSpec(memory_space=pltpu.SMEM)] + [vmem] * 3 + [hbm] * 2,
-        out_specs=[vmem] * 3,
+        in_specs=[vmem] * 4 + [hbm],
+        out_specs=[vmem] * 2,
         scratch_shapes=[
             pltpu.VMEM((kv_local, tokens, depth), jnp.bfloat16),
             pltpu.VMEM((kv_local, tokens, depth), jnp.bfloat16),
-            pltpu.SemaphoreType.DMA((2,)),
+            pltpu.SemaphoreType.DMA,
         ],
         compiler_params=params,
         name="attention",
-    )(lengths, both, queries, d_out, *in_hbm(k_weight, v_weight))
+    )(live, both, queries, d_out, *in_hbm(v_weight))
 
     shares = lax.all_to_all(
         partial.reshape(resp, own, 2 * width), "resp", 0, 0, tiled=True

time: 40.9 us -> 37.7 us (0.922)
  Pallas kernels: 12.8 us -> 9.16 us
  waiting for transfers between devices: 7.21 us -> 3.96 us
  local copies, waits for them, and re-layouts: 0 us -> 1.95 us
  blocking collectives: 9.74 us -> 11.4 us
    pallas_call x1, Pallas kernels: 5.22 us -> 1.38 us  [body(): pl.pallas_call(join_kernel, out_shape=jax.ShapeDtypeStruct((resp, own, 2...]
    all_to_all x1, waiting for transfers between devices: 5.12 us -> 1.87 us  [body(): lax.all_to_all(both, 'resp', 0, 0, tiled=True)]
    unnamed x0 -> x4, local copies, waits for them, and re-layouts: none -> 1.95 us
    all_to_all x1, blocking collectives: 9.74 us -> 11.4 us  [body(): lax.all_to_all(partial.reshape(resp, own, 2 * width), 'resp', 0, 0, tiled...]
    pallas_call x1, Pallas kernels: 1.56 us -> 2.87 us  [body(): pl.pallas_call(load_kernel, out_shape=[pltpu.VMEM(x.shape, x.dtype) for x...]
    pallas_call x1, Pallas kernels: 3.48 us -> 2.35 us  [body(): pl.pallas_call(attention_kernel, out_shape=[pltpu.VMEM((tokens, 2 * width...]
  transfers between devices with their start and end apart: 4 -> 4, of which waited for: 3 -> 3; matrix products, arithmetic and copies ran while one was open for 0% -> 0% of each run, Pallas kernels for 9% -> 13%
where the time goes in v7:
time: 37.7 us; the launch traced here: 37.3 us
  blocking collectives  11.4 us (30%)
  Pallas kernels  9.16 us (24%)
  starting transfers between devices  8.85 us (23%)
  waiting for transfers between devices  3.96 us (11%)
  local copies, waits for them, and re-layouts  1.95 us (5%)
  between operations  1.34 us (4%)
  other arithmetic  0.67 us (2%)
    all_to_all x1, blocking collectives, body(): lax.all_to_all(partial.reshape(resp, own, 2 * width), 'resp', 0, 0, tiled...  11.4 us
    all_to_all x1, starting transfers between devices, body(): lax.all_to_all(both, 'resp', 0, 0, tiled=True)  7.26 us
    pallas_call x1, Pallas kernels, body(): pl.pallas_call(load_kernel, out_shape=[pltpu.VMEM(x.shape, x.dtype) for x...  2.87 us
    pallas_call x1, Pallas kernels, body(): pl.pallas_call(attention_kernel, out_shape=[pltpu.VMEM((tokens, 2 * width...  2.35 us
    ppermute x3, waiting for transfers between devices, swap(): return lax.ppermute(x, axis, [(i, i ^ bit) for i in range(count)])  2.09 us
    unnamed x4, local copies, waits for them, and re-layouts  1.95 us
    all_to_all x1, waiting for transfers between devices, body(): lax.all_to_all(both, 'resp', 0, 0, tiled=True)  1.87 us
    ppermute x3, starting transfers between devices, swap(): return lax.ppermute(x, axis, [(i, i ^ bit) for i in range(count)])  1.59 us
  transfers between devices with their start and end apart: 4, of which 3 were waited for; matrix products, arithmetic and copies ran while one was open for 0% of the time, Pallas kernels for 13%

profile of v7, /device:TPU:0, one launch (start us, length us, event | category | flops | bytes accessed | tf_op | source)
XLA Modules:
  0.0 37.3 jit_solution(763961287509737760)
XLA Ops:
  0.6 1.4 %join.1 = bf16[8,16,512]{2,1,0:T(8,128)(2,1)} custom-call(bf16[16,256]{1,0:T(8,128)(2,1)} %k_hbm.1, bf16[16,256]{1,0:T(8,128)(2,1)} %v_hbm.1), custom_call_target="tpu_custom_call" | custom-call | tf_op jit(solution)/shard_map/join/pallas_call | solution.py:162
  2.0 7.3 %all-to-all-start = ((bf16[8,16,512]{2,1,0:T(8,128)(2,1)}), bf16[8,16,512]{2,1,0:T(8,128)(2,1)S(1)}, u32[]{:S(2)}, u32[]{:S(2)}) async-start(bf16[8,16,512]{2,1,0:T(8,128)(2,1)} %join.1), calls=%async_computation | async-start | bytes 262144 | tf_op jit(solution)/shard_map/all_to_all | solution.py:174
  9.9 2.9 %load.1 = (bf16[256,2048]{1,0:T(8,128)(2,1)S(1)}, bf16[256,2048]{1,0:T(8,128)(2,1)S(1)}, bf16[8192,256]{1,0:T(8,128)(2,1)S(1)}, f32[1,8,256]{2,1,0:T(8,128)S(1)}) custom-call(s32[1]{0:T(128)S(6)} %copy.10.lengths_ref, bf16[256,2048]{1,0:T(8,128)(2,1)} %refs_0_.1, bf16[256,2048]{1,0:T(8,128)(2,1)} %refs_1_.1, bf16[8192,256]{1,0:T(8,128)(2,1)} %refs_2_.1), custom_call_target="tpu_custom_call" | custom-call | bytes 12582912 | tf_op jit(solution)/shard_map/load/pallas_call | solution.py:178
  12.8 0.0 copy-start
  12.8 1.9 %copy-done = bf16[8192,256]{1,0:T(8,128)(2,1)} copy-done((bf16[8192,256]{1,0:T(8,128)(2,1)}, bf16[8192,256]{1,0:T(8,128)(2,1)S(1)}, u32[]{:S(2)}) %copy-start) | copy-done | bytes 4194328
  14.8 1.9 %all-to-all-done = bf16[8,16,512]{2,1,0:T(8,128)(2,1)S(1)} async-done(((bf16[8,16,512]{2,1,0:T(8,128)(2,1)}), bf16[8,16,512]{2,1,0:T(8,128)(2,1)S(1)}, u32[]{:S(2)}, u32[]{:S(2)}) %all-to-all-start) | async-done | bytes 131104 | tf_op jit(solution)/shard_map/all_to_all | solution.py:174
  16.6 0.0 copy-start.1
  16.6 2.3 %attention.1 = (bf16[128,512]{1,0:T(8,128)(2,1)S(1)}, bf16[8192,256]{1,0:T(8,128)(2,1)S(1)}) custom-call(f32[1,8,256]{2,1,0:T(8,128)S(1)} %get-tuple-element.15.live_ref, bf16[128,512]{1,0:T(8,128)(2,1)S(1)} %bitcast.2, bf16[256,2048]{1,0:T(8,128)(2,1)S(1)} %get-tuple-element.16.q_ref, bf16[256,2048]{1,0:T(8,128)(2,1)S(1)} %get-tuple-element.17.g_ref, ...), custom_call_target="tpu_custom_call" | custom-call | tf_op jit(solution)/shard_map/attention/pallas_call | solution.py:195
  19.0 11.4 %all_to_all.10.parts_ref = bf16[8,16,512]{2,1,0:T(8,128)(2,1)S(1)} all-to-all(bf16[8,16,512]{2,1,0:T(8,128)(2,1)S(1)} %bitcast.3), channel_id=1, replica_groups=mesh['resp'=8,'head'=4] {'resp'}, dimensions={0} | all-to-all | bytes 262144 | tf_op jit(solution)/shard_map/all_to_all | solution.py:212
  30.4 0.0 copy-done.1
  30.4 0.6 %projection_other_core.1 = (bf16[16,512]{1,0:T(8,128)(2,1)S(1)}, bf16[16,2048]{1,0:T(8,128)(2,1)S(1)}) custom-call(bf16[8,16,512]{2,1,0:T(8,128)(2,1)S(1)} %all_to_all.10.parts_ref, bf16[8192,256]{1,0:T(8,128)(2,1)S(1)} %copy-done.1, bf16[8192,256]{1,0:T(8,128)(2,1)S(1)} %get-tuple-element.20.vw_ref), custom_call_target="tpu_custom_call" | custom-call | tf_op jit(solution)/shard_map/projection_other_core/pallas_call | solution.py:217
  31.0 0.0 collective-permute-start
  31.0 0.7 %projection_other_y.1 = f32[16,2048]{1,0:T(8,128)S(1)} custom-call(bf16[16,512]{1,0:T(8,128)(2,1)S(1)} %get-tuple-element.21.low_ref, bf16[8192,256]{1,0:T(8,128)(2,1)S(1)} %copy-done.1, bf16[8192,256]{1,0:T(8,128)(2,1)S(1)} %get-tuple-element.20.vw_ref), custom_call_target="tpu_custom_call" | custom-call | flops 33554432 | bytes 2097152 | tf_op jit(solution)/shard_map/projection_other_y/pallas_call | solution.py:231
  31.7 0.6 %collective-permute-done = bf16[16,2048]{1,0:T(8,128)(2,1)S(1)} collective-permute-done((bf16[16,2048]{1,0:T(8,128)(2,1)S(1)}, bf16[16,2048]{1,0:T(8,128)(2,1)S(1)}, u32[]{:S(2)}, u32[]{:S(2)}) %collective-permute-start) | collective-permute-done | bytes 65568 | tf_op jit(solution)/shard_map/ppermute | solution.py:149
  32.3 1.6 %collective-permute-start.1 = (bf16[16,2048]{1,0:T(8,128)(2,1)S(1)}, bf16[16,2048]{1,0:T(8,128)(2,1)S(1)}, u32[]{:S(2)}, u32[]{:S(2)}) collective-permute-start(bf16[16,2048]{1,0:T(8,128)(2,1)S(1)} %add_convert_fusion.1.after), channel_id=1, source_target_pairs={{0,2},{1,3},{2,0},{3,1},{4,6},{5,7},{6,4},{7,5},{8,10},{9,11},{10,... | collective-permute-start | bytes 196616 | tf_op jit(solution)/shard_map/ppermute | solution.py:149
  33.9 1.3 %projection_this_y.1 = (bf16[16,2048]{1,0:T(8,128)(2,1)S(1)}, f32[16,2048]{1,0:T(8,128)S(1)}, bf16[16,256]{1,0:T(8,128)(2,1)}, bf16[16,256]{1,0:T(8,128)(2,1)}) custom-call(bf16[16,512]{1,0:T(8,128)(2,1)S(1)} %get-tuple-element.21.low_ref, bf16[8192,256]{1,0:T(8,128)(2,1)S(1)} %copy-done.1, bf16[8192,256]{1,0:T(8,128)(2,1)S(1)} %get-tuple-element.20.vw_ref, ...), custom_call_target="tpu_custom_call" | custom-call | flops 33554432 | bytes 2097152 | tf_op jit(solution)/shard_map/projection_this_y/pallas_call | solution.py:242
  35.2 0.0 collective-permute-start.2
  35.2 1.5 %collective-permute-done.1 = bf16[16,2048]{1,0:T(8,128)(2,1)S(1)} collective-permute-done((bf16[16,2048]{1,0:T(8,128)(2,1)S(1)}, bf16[16,2048]{1,0:T(8,128)(2,1)S(1)}, u32[]{:S(2)}, u32[]{:S(2)}) %collective-permute-start.1) | collective-permute-done | bytes 65568 | tf_op jit(solution)/shard_map/ppermute | solution.py:149
  36.7 0.0 collective-permute-done.2
  36.7 0.6 %add_convert_fusion = bf16[16,2048]{1,0:T(8,128)(2,1)} fusion(f32[16,2048]{1,0:T(8,128)S(1)} %convert_add_fusion, bf16[16,2048]{1,0:T(8,128)(2,1)S(1)} %collective-permute-done.2), kind=kLoop, calls=%fused_computation | loop fusion | flops 98304 | bytes 262144 | tf_op jit(solution)/shard_map/convert_element_type | solution.py:258
  (2 shorter events, 0.0 us)
Async XLA Ops:
  2.0 14.6 %all-to-all-start = ((bf16[8,16,512]{2,1,0:T(8,128)(2,1)}), bf16[8,16,512]{2,1,0:T(8,128)(2,1)S(1)}, u32[]{:S(2)}, u32[]{:S(2)}) async-start(bf16[8,16,512]{2,1,0:T(8,128)(2,1)} %join.1), calls=%async_computation | async-start | bytes 262144 | tf_op jit(solution)/shard_map/all_to_all | solution.py:174
  12.8 1.9 %copy-start = (bf16[8192,256]{1,0:T(8,128)(2,1)}, bf16[8192,256]{1,0:T(8,128)(2,1)S(1)}, u32[]{:S(2)}) copy-start(bf16[8192,256]{1,0:T(8,128)(2,1)S(1)} %get-tuple-element.19.kw_ref) | copy-start | bytes 12582916
  16.6 13.8 %copy-start.1 = (bf16[8192,256]{1,0:T(8,128)(2,1)S(1)}, bf16[8192,256]{1,0:T(8,128)(2,1)}, u32[]{:S(2)}) copy-start(bf16[8192,256]{1,0:T(8,128)(2,1)} %copy-done) | copy-start | bytes 12582916
  31.0 1.3 %collective-permute-start = (bf16[16,2048]{1,0:T(8,128)(2,1)S(1)}, bf16[16,2048]{1,0:T(8,128)(2,1)S(1)}, u32[]{:S(2)}, u32[]{:S(2)}) collective-permute-start(bf16[16,2048]{1,0:T(8,128)(2,1)S(1)} %get-tuple-element.22), channel_id=1, source_target_pairs={{0,1},{1,0},{2,3},{3,2},{4,5},{5,4},{6,7},{7,6},{8,9},{9,8},{10,11... | collective-permute-start | bytes 196616 | tf_op jit(solution)/shard_map/ppermute | solution.py:149
  32.3 4.3 %collective-permute-start.1 = (bf16[16,2048]{1,0:T(8,128)(2,1)S(1)}, bf16[16,2048]{1,0:T(8,128)(2,1)S(1)}, u32[]{:S(2)}, u32[]{:S(2)}) collective-permute-start(bf16[16,2048]{1,0:T(8,128)(2,1)S(1)} %add_convert_fusion.1.after), channel_id=1, source_target_pairs={{0,2},{1,3},{2,0},{3,1},{4,6},{5,7},{6,4},{7,5},{8,10},{9,11},{10,... | collective-permute-start | bytes 196616 | tf_op jit(solution)/shard_map/ppermute | solution.py:149
  35.2 1.5 %collective-permute-start.2 = (bf16[16,2048]{1,0:T(8,128)(2,1)S(1)}, bf16[16,2048]{1,0:T(8,128)(2,1)S(1)}, u32[]{:S(2)}, u32[]{:S(2)}) collective-permute-start(bf16[16,2048]{1,0:T(8,128)(2,1)S(1)} %get-tuple-element.26), channel_id=1, source_target_pairs={{0,1},{1,0},{2,3},{3,2},{4,5},{5,4},{6,7},{7,6},{8,9},{9,8},{10,11... | collective-permute-start | bytes 196616 | tf_op jit(solution)/shard_map/ppermute | solution.py:149

commit v8 on v7

--- a/solution.py
+++ b/solution.py
@@ -10,7 +10,6 @@
 HD = 128
 LEN = 256
 NT = (((1,), (1,)), ((), ()))
-VMEM_LIMIT = 40 << 20
 UNIT = 2
 LOG2E = 1.4426950408889634
 
@@ -46,8 +45,19 @@
 
 
 def attention_kernel(
-    live_ref, kv_ref, q_ref, g_ref, vw_hbm, out_ref, vw_ref, probs_ref, dscores_ref, sem
+    live_ref,
+    kv_ref,
+    q_ref,
+    g_ref,
+    kw_ref,
+    vw_hbm,
+    out_ref,
+    vw_ref,
+    probs_ref,
+    dscores_ref,
+    sem,
 ):
+    del kw_ref
     weight = pltpu.make_async_copy(vw_hbm, vw_ref, sem)
     weight.start()
     scale = HD ** (-0.5)
@@ -154,7 +164,7 @@
     features = k_weight.shape[0] // head
     vmem = pl.BlockSpec(memory_space=pltpu.VMEM)
     hbm = pl.BlockSpec(memory_space=pltpu.HBM)
-    params = pltpu.CompilerParams(vmem_limit_bytes=VMEM_LIMIT)
+    params = pltpu.CompilerParams(vmem_limit_bytes=8 << 20)
 
     def in_hbm(*xs):
         return [pltpu.with_memory_space_constraint(x, pltpu.HBM) for x in xs]
@@ -198,16 +208,18 @@
             pltpu.VMEM((tokens, 2 * width), jnp.bfloat16),
             pltpu.VMEM(v_weight.shape, v_weight.dtype),
         ],
-        in_specs=[vmem] * 4 + [hbm],
+        in_specs=[vmem] * 5 + [hbm],
         out_specs=[vmem] * 2,
         scratch_shapes=[
             pltpu.VMEM((kv_local, tokens, depth), jnp.bfloat16),
             pltpu.VMEM((kv_local, tokens, depth), jnp.bfloat16),
             pltpu.SemaphoreType.DMA,
         ],
-        compiler_params=params,
+        compiler_params=pltpu.CompilerParams(
+            vmem_limit_bytes=(8 << 20) + 8 * kv_local * tokens * depth
+        ),
         name="attention",
-    )(live, both, queries, d_out, *in_hbm(v_weight))
+    )(live, both, queries, d_out, k_weight, *in_hbm(v_weight))
 
     shares = lax.all_to_all(
         partial.reshape(resp, own, 2 * width), "resp", 0, 0, tiled=True

time: 37.7 us -> 39.9 us (1.058)
  local copies, waits for them, and re-layouts: 1.95 us -> 4.14 us
    unnamed x4 -> x6, local copies, waits for them, and re-layouts: 1.95 us -> 4.14 us
  transfers between devices with their start and end apart: 4 -> 4, of which waited for: 3 -> 3; matrix products, arithmetic and copies ran while one was open for 0% -> 0% of each run, Pallas kernels for 13% -> 12%
where the time goes in v8:
time: 39.9 us; the launch traced here: 39.5 us
  blocking collectives  11.4 us (29%)
  Pallas kernels  9.17 us (23%)
  starting transfers between devices  8.85 us (22%)
  local copies, waits for them, and re-layouts  4.14 us (10%)
  waiting for transfers between devices  3.95 us (10%)
  between operations  1.34 us (3%)
  other arithmetic  0.67 us (2%)
    all_to_all x1, blocking collectives, body(): lax.all_to_all(partial.reshape(resp, own, 2 * width), 'resp', 0, 0, tiled...  11.4 us
    all_to_all x1, starting transfers between devices, body(): lax.all_to_all(both, 'resp', 0, 0, tiled=True)  7.26 us
    unnamed x6, local copies, waits for them, and re-layouts  4.14 us
    pallas_call x1, Pallas kernels, body(): pl.pallas_call(load_kernel, out_shape=[pltpu.VMEM(x.shape, x.dtype) for x...  2.87 us
    pallas_call x1, Pallas kernels, body(): pl.pallas_call(attention_kernel, out_shape=[pltpu.VMEM((tokens, 2 * width...  2.35 us
    ppermute x3, waiting for transfers between devices, swap(): return lax.ppermute(x, axis, [(i, i ^ bit) for i in range(count)])  2.09 us
    all_to_all x1, waiting for transfers between devices, body(): lax.all_to_all(both, 'resp', 0, 0, tiled=True)  1.86 us
    ppermute x3, starting transfers between devices, swap(): return lax.ppermute(x, axis, [(i, i ^ bit) for i in range(count)])  1.59 us
  transfers between devices with their start and end apart: 4, of which 3 were waited for; matrix products, arithmetic and copies ran while one was open for 0% of the time, Pallas kernels for 12%

profile of v8, /device:TPU:0, one launch (start us, length us, event | category | flops | bytes accessed | tf_op | source)
XLA Modules:
  0.0 39.5 jit_solution(7563842381676411572)
XLA Ops:
  0.6 1.4 %join.1 = bf16[8,16,512]{2,1,0:T(8,128)(2,1)} custom-call(bf16[16,256]{1,0:T(8,128)(2,1)} %k_hbm.1, bf16[16,256]{1,0:T(8,128)(2,1)} %v_hbm.1), custom_call_target="tpu_custom_call" | custom-call | tf_op jit(solution)/shard_map/join/pallas_call | solution.py:172
  2.0 7.3 %all-to-all-start = ((bf16[8,16,512]{2,1,0:T(8,128)(2,1)}), bf16[8,16,512]{2,1,0:T(8,128)(2,1)S(1)}, u32[]{:S(2)}, u32[]{:S(2)}) async-start(bf16[8,16,512]{2,1,0:T(8,128)(2,1)} %join.1), calls=%async_computation | async-start | bytes 262144 | tf_op jit(solution)/shard_map/all_to_all | solution.py:184
  9.9 2.9 %load.1 = (bf16[256,2048]{1,0:T(8,128)(2,1)S(1)}, bf16[256,2048]{1,0:T(8,128)(2,1)S(1)}, bf16[8192,256]{1,0:T(8,128)(2,1)S(1)}, f32[1,8,256]{2,1,0:T(8,128)S(1)}) custom-call(s32[1]{0:T(128)S(6)} %copy.10.lengths_ref, bf16[256,2048]{1,0:T(8,128)(2,1)} %refs_0_.1, bf16[256,2048]{1,0:T(8,128)(2,1)} %refs_1_.1, bf16[8192,256]{1,0:T(8,128)(2,1)} %refs_2_.1), custom_call_target="tpu_custom_call" | custom-call | bytes 12582912 | tf_op jit(solution)/shard_map/load/pallas_call | solution.py:188
  12.8 0.0 copy-start
  12.8 1.9 %copy-done = bf16[8192,256]{1,0:T(8,128)(2,1)} copy-done((bf16[8192,256]{1,0:T(8,128)(2,1)}, bf16[8192,256]{1,0:T(8,128)(2,1)S(1)}, u32[]{:S(2)}) %copy-start) | copy-done | bytes 4194328
  14.8 1.9 %all-to-all-done = bf16[8,16,512]{2,1,0:T(8,128)(2,1)S(1)} async-done(((bf16[8,16,512]{2,1,0:T(8,128)(2,1)}), bf16[8,16,512]{2,1,0:T(8,128)(2,1)S(1)}, u32[]{:S(2)}, u32[]{:S(2)}) %all-to-all-start) | async-done | bytes 131104 | tf_op jit(solution)/shard_map/all_to_all | solution.py:184
  16.6 0.0 copy-start.1
  16.6 2.2 %copy-done.1 = bf16[8192,256]{1,0:T(8,128)(2,1)S(1)} copy-done((bf16[8192,256]{1,0:T(8,128)(2,1)S(1)}, bf16[8192,256]{1,0:T(8,128)(2,1)}, u32[]{:S(2)}) %copy-start.1) | copy-done | bytes 4194328
  18.8 0.0 copy-start.2
  18.8 2.3 %attention.1 = (bf16[128,512]{1,0:T(8,128)(2,1)S(1)}, bf16[8192,256]{1,0:T(8,128)(2,1)S(1)}) custom-call(f32[1,8,256]{2,1,0:T(8,128)S(1)} %get-tuple-element.15.live_ref, bf16[128,512]{1,0:T(8,128)(2,1)S(1)} %bitcast.2, bf16[256,2048]{1,0:T(8,128)(2,1)S(1)} %get-tuple-element.16.q_ref, bf16[256,2048]{1,0:T(8,128)(2,1)S(1)} %get-tuple-element.17.g_ref, ...), custom_call_target="tpu_custom_call" | custom-call | tf_op jit(solution)/shard_map/attention/pallas_call | solution.py:205
  21.2 11.4 %all_to_all.10.parts_ref = bf16[8,16,512]{2,1,0:T(8,128)(2,1)S(1)} all-to-all(bf16[8,16,512]{2,1,0:T(8,128)(2,1)S(1)} %bitcast.3), channel_id=1, replica_groups=mesh['resp'=8,'head'=4] {'resp'}, dimensions={0} | all-to-all | bytes 262144 | tf_op jit(solution)/shard_map/all_to_all | solution.py:224
  32.6 0.0 copy-done.2
  32.6 0.6 %projection_other_core.1 = (bf16[16,512]{1,0:T(8,128)(2,1)S(1)}, bf16[16,2048]{1,0:T(8,128)(2,1)S(1)}) custom-call(bf16[8,16,512]{2,1,0:T(8,128)(2,1)S(1)} %all_to_all.10.parts_ref, bf16[8192,256]{1,0:T(8,128)(2,1)S(1)} %copy-done.2, bf16[8192,256]{1,0:T(8,128)(2,1)S(1)} %get-tuple-element.20.vw_ref), custom_call_target="tpu_custom_call" | custom-call | tf_op jit(solution)/shard_map/projection_other_core/pallas_call | solution.py:229
  33.2 0.0 collective-permute-start
  33.3 0.7 %projection_other_y.1 = f32[16,2048]{1,0:T(8,128)S(1)} custom-call(bf16[16,512]{1,0:T(8,128)(2,1)S(1)} %get-tuple-element.21.low_ref, bf16[8192,256]{1,0:T(8,128)(2,1)S(1)} %copy-done.2, bf16[8192,256]{1,0:T(8,128)(2,1)S(1)} %get-tuple-element.20.vw_ref), custom_call_target="tpu_custom_call" | custom-call | flops 33554432 | bytes 2097152 | tf_op jit(solution)/shard_map/projection_other_y/pallas_call | solution.py:243
  33.9 0.6 %collective-permute-done = bf16[16,2048]{1,0:T(8,128)(2,1)S(1)} collective-permute-done((bf16[16,2048]{1,0:T(8,128)(2,1)S(1)}, bf16[16,2048]{1,0:T(8,128)(2,1)S(1)}, u32[]{:S(2)}, u32[]{:S(2)}) %collective-permute-start) | collective-permute-done | bytes 65568 | tf_op jit(solution)/shard_map/ppermute | solution.py:159
  34.5 1.6 %collective-permute-start.1 = (bf16[16,2048]{1,0:T(8,128)(2,1)S(1)}, bf16[16,2048]{1,0:T(8,128)(2,1)S(1)}, u32[]{:S(2)}, u32[]{:S(2)}) collective-permute-start(bf16[16,2048]{1,0:T(8,128)(2,1)S(1)} %add_convert_fusion.1.after), channel_id=1, source_target_pairs={{0,2},{1,3},{2,0},{3,1},{4,6},{5,7},{6,4},{7,5},{8,10},{9,11},{10,... | collective-permute-start | bytes 196616 | tf_op jit(solution)/shard_map/ppermute | solution.py:159
  36.1 1.3 %projection_this_y.1 = (bf16[16,2048]{1,0:T(8,128)(2,1)S(1)}, f32[16,2048]{1,0:T(8,128)S(1)}, bf16[16,256]{1,0:T(8,128)(2,1)}, bf16[16,256]{1,0:T(8,128)(2,1)}) custom-call(bf16[16,512]{1,0:T(8,128)(2,1)S(1)} %get-tuple-element.21.low_ref, bf16[8192,256]{1,0:T(8,128)(2,1)S(1)} %copy-done.2, bf16[8192,256]{1,0:T(8,128)(2,1)S(1)} %get-tuple-element.20.vw_ref, ...), custom_call_target="tpu_custom_call" | custom-call | flops 33554432 | bytes 2097152 | tf_op jit(solution)/shard_map/projection_this_y/pallas_call | solution.py:254
  37.4 0.0 collective-permute-start.2
  37.4 1.5 %collective-permute-done.1 = bf16[16,2048]{1,0:T(8,128)(2,1)S(1)} collective-permute-done((bf16[16,2048]{1,0:T(8,128)(2,1)S(1)}, bf16[16,2048]{1,0:T(8,128)(2,1)S(1)}, u32[]{:S(2)}, u32[]{:S(2)}) %collective-permute-start.1) | collective-permute-done | bytes 65568 | tf_op jit(solution)/shard_map/ppermute | solution.py:159
  38.9 0.0 collective-permute-done.2
  38.9 0.6 %add_convert_fusion = bf16[16,2048]{1,0:T(8,128)(2,1)} fusion(f32[16,2048]{1,0:T(8,128)S(1)} %convert_add_fusion, bf16[16,2048]{1,0:T(8,128)(2,1)S(1)} %collective-permute-done.2), kind=kLoop, calls=%fused_computation | loop fusion | flops 98304 | bytes 262144 | tf_op jit(solution)/shard_map/convert_element_type | solution.py:270
  (2 shorter events, 0.0 us)
Async XLA Ops:
  2.0 14.6 %all-to-all-start = ((bf16[8,16,512]{2,1,0:T(8,128)(2,1)}), bf16[8,16,512]{2,1,0:T(8,128)(2,1)S(1)}, u32[]{:S(2)}, u32[]{:S(2)}) async-start(bf16[8,16,512]{2,1,0:T(8,128)(2,1)} %join.1), calls=%async_computation | async-start | bytes 262144 | tf_op jit(solution)/shard_map/all_to_all | solution.py:184
  12.8 2.0 %copy-start = (bf16[8192,256]{1,0:T(8,128)(2,1)}, bf16[8192,256]{1,0:T(8,128)(2,1)S(1)}, u32[]{:S(2)}) copy-start(bf16[8192,256]{1,0:T(8,128)(2,1)S(1)} %get-tuple-element.18.kw_ref) | copy-start | bytes 12582916
  16.6 2.2 %copy-start.1 = (bf16[8192,256]{1,0:T(8,128)(2,1)S(1)}, bf16[8192,256]{1,0:T(8,128)(2,1)}, u32[]{:S(2)}) copy-start(bf16[8192,256]{1,0:T(8,128)(2,1)} %copy-done) | copy-start | bytes 12582916
  18.8 13.8 %copy-start.2 = (bf16[8192,256]{1,0:T(8,128)(2,1)S(1)}, bf16[8192,256]{1,0:T(8,128)(2,1)}, u32[]{:S(2)}) copy-start(bf16[8192,256]{1,0:T(8,128)(2,1)} %copy-done) | copy-start | bytes 12582916
  33.2 1.3 %collective-permute-start = (bf16[16,2048]{1,0:T(8,128)(2,1)S(1)}, bf16[16,2048]{1,0:T(8,128)(2,1)S(1)}, u32[]{:S(2)}, u32[]{:S(2)}) collective-permute-start(bf16[16,2048]{1,0:T(8,128)(2,1)S(1)} %get-tuple-element.22), channel_id=1, source_target_pairs={{0,1},{1,0},{2,3},{3,2},{4,5},{5,4},{6,7},{7,6},{8,9},{9,8},{10,11... | collective-permute-start | bytes 196616 | tf_op jit(solution)/shard_map/ppermute | solution.py:159
  34.5 4.3 %collective-permute-start.1 = (bf16[16,2048]{1,0:T(8,128)(2,1)S(1)}, bf16[16,2048]{1,0:T(8,128)(2,1)S(1)}, u32[]{:S(2)}, u32[]{:S(2)}) collective-permute-start(bf16[16,2048]{1,0:T(8,128)(2,1)S(1)} %add_convert_fusion.1.after), channel_id=1, source_target_pairs={{0,2},{1,3},{2,0},{3,1},{4,6},{5,7},{6,4},{7,5},{8,10},{9,11},{10,... | collective-permute-start | bytes 196616 | tf_op jit(solution)/shard_map/ppermute | solution.py:159
  37.4 1.5 %collective-permute-start.2 = (bf16[16,2048]{1,0:T(8,128)(2,1)S(1)}, bf16[16,2048]{1,0:T(8,128)(2,1)S(1)}, u32[]{:S(2)}, u32[]{:S(2)}) collective-permute-start(bf16[16,2048]{1,0:T(8,128)(2,1)S(1)} %get-tuple-element.26), channel_id=1, source_target_pairs={{0,1},{1,0},{2,3},{3,2},{4,5},{5,4},{6,7},{7,6},{8,9},{9,8},{10,11... | collective-permute-start | bytes 196616 | tf_op jit(solution)/shard_map/ppermute | solution.py:159

commit v9 on v8

--- a/solution.py
+++ b/solution.py
@@ -44,22 +44,31 @@
         copy.wait()
 
 
+def features_of(head_index, features):
+    return pl.ds(pl.multiple_of(head_index * features, features), features)
+
+
 def attention_kernel(
     live_ref,
     kv_ref,
     q_ref,
     g_ref,
-    kw_ref,
+    kw_hbm,
     vw_hbm,
     out_ref,
+    kw_ref,
     vw_ref,
     probs_ref,
     dscores_ref,
-    sem,
+    sems,
 ):
-    del kw_ref
-    weight = pltpu.make_async_copy(vw_hbm, vw_ref, sem)
-    weight.start()
+    rows = features_of((lax.axis_index("head") // 2) ^ 1, kw_ref.shape[0])
+    weights = [
+        pltpu.make_async_copy(kw_hbm.at[rows], kw_ref, sems.at[0]),
+        pltpu.make_async_copy(vw_hbm.at[rows], vw_ref, sems.at[1]),
+    ]
+    for copy in weights:
+        copy.start()
     scale = HD ** (-0.5)
     width = kv_ref.shape[1] // 2
     kv_local = width // HD
@@ -114,45 +123,54 @@
             grad_v = jnp.dot(probs_ref[k], g_all, preferred_element_type=jnp.float32)
             out_ref[:, k * HD : (k + 1) * HD] = grad_k.astype(out_ref.dtype)
             out_ref[:, width + k * HD : width + (k + 1) * HD] = grad_v.astype(out_ref.dtype)
-    weight.wait()
-
-
-def project(low, kw_ref, vw_ref, owner, features):
-    width = kw_ref.shape[1]
-    rows = pl.ds(pl.multiple_of(owner * features, features), features)
-    out = lax.dot_general(
-        low[:, :width], kw_ref[rows, :], NT, preferred_element_type=jnp.float32
-    )
-    return out + lax.dot_general(
-        low[:, width:], vw_ref[rows, :], NT, preferred_element_type=jnp.float32
-    )
-
-
-def first_projection_kernel(owner, parts_ref, kw_ref, vw_ref, low_ref, out_ref):
+    for copy in weights:
+        copy.wait()
+
+
+def project(low, kw, vw):
+    width = kw.shape[1]
+    out = lax.dot_general(low[:, :width], kw, NT, preferred_element_type=jnp.float32)
+    return out + lax.dot_general(low[:, width:], vw, NT, preferred_element_type=jnp.float32)
+
+
+def first_projection_kernel(parts_ref, kw_ref, vw_ref, low_ref, out_ref):
     total = parts_ref[0].astype(jnp.float32)
     for i in range(1, parts_ref.shape[0]):
         total += parts_ref[i].astype(jnp.float32)
     low = total.astype(jnp.bfloat16)
     low_ref[...] = low
+    rows = features_of((lax.axis_index("head") % 2) ^ 1, out_ref.shape[1])
+    out_ref[...] = project(low, kw_ref[rows, :], vw_ref[rows, :]).astype(out_ref.dtype)
+
+
+def second_projection_kernel(low_ref, kw_ref, vw_ref, out_ref):
+    rows = features_of(lax.axis_index("head") % 2, out_ref.shape[1])
+    out_ref[...] = project(low_ref[...], kw_ref[rows, :], vw_ref[rows, :])
+
+
+def last_projection_kernel(
+    low_ref, kw_hbm, vw_hbm, after, out_ref, keep_ref, dk_ref, dv_ref, weight_ref, sems
+):
+    del after
+    features = out_ref.shape[1]
     me = lax.axis_index("head")
-    out = project(low, kw_ref, vw_ref, me ^ owner, out_ref.shape[1])
-    out_ref[...] = out.astype(out_ref.dtype)
-
-
-def second_projection_kernel(owner, low_ref, kw_ref, vw_ref, out_ref):
-    me = lax.axis_index("head")
-    out_ref[...] = project(low_ref[...], kw_ref, vw_ref, me ^ owner, out_ref.shape[1])
-
-
-def last_projection_kernel(low_ref, kw_ref, vw_ref, after, out_ref, keep_ref, dk_ref, dv_ref):
+    copies = []
+    for i in range(2):
+        rows = features_of(me ^ (1 - i), features)
+        for j, hbm in enumerate((kw_hbm, vw_hbm)):
+            copies.append(
+                pltpu.make_async_copy(hbm.at[rows], weight_ref.at[i, j], sems.at[i, j])
+            )
+    for copy in copies:
+        copy.start()
     width = dk_ref.shape[1]
     low = low_ref[...]
     dk_ref[...] = low[:, :width]
     dv_ref[...] = low[:, width:]
-    me = lax.axis_index("head")
-    out = project(low, kw_ref, vw_ref, me ^ 1, out_ref.shape[1])
-    out_ref[...] = out.astype(out_ref.dtype)
-    keep_ref[...] = project(low, kw_ref, vw_ref, me, keep_ref.shape[1])
+    for i, ref in enumerate((out_ref, keep_ref)):
+        copies[2 * i].wait()
+        copies[2 * i + 1].wait()
+        ref[...] = project(low, weight_ref[i, 0], weight_ref[i, 1]).astype(ref.dtype)
 
 
 def swap(x, axis, count, bit):
@@ -183,9 +201,9 @@
     )(*in_hbm(prefix_keys, prefix_values))
     both = lax.all_to_all(both, "resp", 0, 0, tiled=True).reshape(resp * own, 2 * width)
 
-    large = (queries, d_out, k_weight)
+    large = (queries, d_out)
     responses = lengths.shape[0]
-    queries, d_out, k_weight, live = pl.pallas_call(
+    queries, d_out, live = pl.pallas_call(
         load_kernel,
         out_shape=[pltpu.VMEM(x.shape, x.dtype) for x in large]
         + [pltpu.VMEM((responses, 8, LEN), jnp.float32)],
@@ -202,24 +220,26 @@
     tokens = resp * own
     kv_local = width // HD
     depth = queries.size // kv_local // HD
-    partial, v_weight = pl.pallas_call(
+    weights = in_hbm(k_weight, v_weight)
+    partial, far_k, far_v = pl.pallas_call(
         attention_kernel,
         out_shape=[
             pltpu.VMEM((tokens, 2 * width), jnp.bfloat16),
-            pltpu.VMEM(v_weight.shape, v_weight.dtype),
-        ],
-        in_specs=[vmem] * 5 + [hbm],
-        out_specs=[vmem] * 2,
+            pltpu.VMEM((2 * features, width), k_weight.dtype),
+            pltpu.VMEM((2 * features, width), v_weight.dtype),
+        ],
+        in_specs=[vmem] * 4 + [hbm] * 2,
+        out_specs=[vmem] * 3,
         scratch_shapes=[
             pltpu.VMEM((kv_local, tokens, depth), jnp.bfloat16),
             pltpu.VMEM((kv_local, tokens, depth), jnp.bfloat16),
-            pltpu.SemaphoreType.DMA,
+            pltpu.SemaphoreType.DMA((2,)),
         ],
         compiler_params=pltpu.CompilerParams(
             vmem_limit_bytes=(8 << 20) + 8 * kv_local * tokens * depth
         ),
         name="attention",
-    )(live, both, queries, d_out, k_weight, *in_hbm(v_weight))
+    )(live, both, queries, d_out, *weights)
 
     shares = lax.all_to_all(
         partial.reshape(resp, own, 2 * width), "resp", 0, 0, tiled=True
@@ -227,7 +247,7 @@
 
     block = (own, features)
     low, to_core = pl.pallas_call(
-        functools.partial(first_projection_kernel, 3),
+        first_projection_kernel,
         out_shape=[
             pltpu.VMEM((own, 2 * width), jnp.bfloat16),
             pltpu.VMEM(block, jnp.bfloat16),
@@ -236,19 +256,19 @@
         out_specs=[vmem] * 2,
         compiler_params=params,
         name="projection_other_core",
-    )(shares, k_weight, v_weight)
+    )(shares, far_k, far_v)
     cost = pl.CostEstimate(
         flops=4 * own * width * features, transcendentals=0, bytes_accessed=4 * width * features
     )
     far = pl.pallas_call(
-        functools.partial(second_projection_kernel, 2),
+        second_projection_kernel,
         out_shape=pltpu.VMEM(block, jnp.float32),
         in_specs=[vmem] * 3,
         out_specs=vmem,
         compiler_params=params,
         cost_estimate=cost,
         name="projection_other_y",
-    )(low, k_weight, v_weight)
+    )(low, far_k, far_v)
     far = (far + swap(to_core, "head", head, 1).astype(jnp.float32)).astype(jnp.bfloat16)
     got = swap(far, "head", head, 2)
     to_core, total, dk_low, dv_low = pl.pallas_call(
@@ -259,12 +279,18 @@
             jax.ShapeDtypeStruct((own, width), jnp.bfloat16),
             jax.ShapeDtypeStruct((own, width), jnp.bfloat16),
         ],
-        in_specs=[vmem] * 3 + [pl.BlockSpec(memory_space=pl.ANY)],
+        in_specs=[vmem, hbm, hbm, pl.BlockSpec(memory_space=pl.ANY)],
         out_specs=[vmem] * 4,
-        compiler_params=params,
+        scratch_shapes=[
+            pltpu.VMEM((2, 2, features, width), k_weight.dtype),
+            pltpu.SemaphoreType.DMA((2, 2)),
+        ],
+        compiler_params=pltpu.CompilerParams(
+            vmem_limit_bytes=(8 << 20) + 8 * features * width
+        ),
         cost_estimate=cost,
         name="projection_this_y",
-    )(low, k_weight, v_weight, far)
+    )(low, *weights, far)
     total = lax.optimization_barrier(total + got.astype(jnp.float32))
     total += swap(to_core, "head", head, 1).astype(jnp.float32)
     return dk_low, dv_low, total.astype(jnp.bfloat16)

time: 39.9 us -> 39.1 us (0.980)
  local copies, waits for them, and re-layouts: 4.14 us -> 0 us
  waiting for transfers between devices: 3.95 us -> 6.94 us
  Pallas kernels: 9.17 us -> 11.1 us
  blocking collectives: 11.4 us -> 9.74 us
    unnamed x6 -> x0, local copies, waits for them, and re-layouts: 4.14 us -> none
    all_to_all x1, waiting for transfers between devices: 1.86 us -> 5.12 us  [body(): lax.all_to_all(both, 'resp', 0, 0, tiled=True)]
    all_to_all x1, blocking collectives: 11.4 us -> 9.74 us  [body(): lax.all_to_all(partial.reshape(resp, own, 2 * width), 'resp', 0, 0, tiled...]
    pallas_call x1, Pallas kernels: 1.26 us -> 2.9 us  [body(): pl.pallas_call(last_projection_kernel, out_shape=[pltpu.VMEM(block, jnp.b...]
    pallas_call x1, Pallas kernels: 2.35 us -> 3.95 us  [body(): pl.pallas_call(attention_kernel, out_shape=[pltpu.VMEM((tokens, 2 * width...]
    pallas_call x1, Pallas kernels: 2.87 us -> 1.56 us  [body(): pl.pallas_call(load_kernel, out_shape=[pltpu.VMEM(x.shape, x.dtype) for x...]
  transfers between devices with their start and end apart: 4 -> 4, of which waited for: 3 -> 3; matrix products, arithmetic and copies ran while one was open for 0% -> 0% of each run, Pallas kernels for 12% -> 13%
where the time goes in v9:
time: 39.1 us; the launch traced here: 38.7 us
  Pallas kernels  11.1 us (28%)
  blocking collectives  9.74 us (25%)
  starting transfers between devices  8.91 us (23%)
  waiting for transfers between devices  6.94 us (18%)
  between operations  1.35 us (3%)
  other arithmetic  0.68 us (2%)
    all_to_all x1, blocking collectives, body(): lax.all_to_all(partial.reshape(resp, own, 2 * width), 'resp', 0, 0, tiled...  9.74 us
    all_to_all x1, starting transfers between devices, body(): lax.all_to_all(both, 'resp', 0, 0, tiled=True)  7.26 us
    all_to_all x1, waiting for transfers between devices, body(): lax.all_to_all(both, 'resp', 0, 0, tiled=True)  5.12 us
    pallas_call x1, Pallas kernels, body(): pl.pallas_call(attention_kernel, out_shape=[pltpu.VMEM((tokens, 2 * width...  3.95 us
    pallas_call x1, Pallas kernels, body(): pl.pallas_call(last_projection_kernel, out_shape=[pltpu.VMEM(block, jnp.b...  2.9 us
    ppermute x3, waiting for transfers between devices, swap(): return lax.ppermute(x, axis, [(i, i ^ bit) for i in range(count)])  1.82 us
    ppermute x3, starting transfers between devices, swap(): return lax.ppermute(x, axis, [(i, i ^ bit) for i in range(count)])  1.65 us
    pallas_call x1, Pallas kernels, body(): pl.pallas_call(load_kernel, out_shape=[pltpu.VMEM(x.shape, x.dtype) for x...  1.56 us
  transfers between devices with their start and end apart: 4, of which 3 were waited for; matrix products, arithmetic and copies ran while one was open for 0% of the time, Pallas kernels for 13%

profile of v9, /device:TPU:0, one launch (start us, length us, event | category | flops | bytes accessed | tf_op | source)
XLA Modules:
  0.0 38.7 jit_solution(16407533172597042168)
XLA Ops:
  0.6 1.4 %join.1 = bf16[8,16,512]{2,1,0:T(8,128)(2,1)} custom-call(bf16[16,256]{1,0:T(8,128)(2,1)} %k_hbm.1, bf16[16,256]{1,0:T(8,128)(2,1)} %v_hbm.1), custom_call_target="tpu_custom_call" | custom-call | tf_op jit(solution)/shard_map/join/pallas_call | solution.py:190
  2.0 7.3 %all-to-all-start = ((bf16[8,16,512]{2,1,0:T(8,128)(2,1)}), bf16[8,16,512]{2,1,0:T(8,128)(2,1)S(1)}, u32[]{:S(2)}, u32[]{:S(2)}) async-start(bf16[8,16,512]{2,1,0:T(8,128)(2,1)} %join.1), calls=%async_computation | async-start | bytes 262144 | tf_op jit(solution)/shard_map/all_to_all | solution.py:202
  9.9 1.6 %load.1 = (bf16[256,2048]{1,0:T(8,128)(2,1)S(1)}, bf16[256,2048]{1,0:T(8,128)(2,1)S(1)}, f32[1,8,256]{2,1,0:T(8,128)S(1)}) custom-call(s32[1]{0:T(128)S(6)} %copy.10.lengths_ref, bf16[256,2048]{1,0:T(8,128)(2,1)} %refs_0_.1, bf16[256,2048]{1,0:T(8,128)(2,1)} %refs_1_.1), custom_call_target="tpu_custom_call" | custom-call | bytes 4194304 | tf_op jit(solution)/shard_map/load/pallas_call | solution.py:206
  11.5 5.1 %all-to-all-done = bf16[8,16,512]{2,1,0:T(8,128)(2,1)S(1)} async-done(((bf16[8,16,512]{2,1,0:T(8,128)(2,1)}), bf16[8,16,512]{2,1,0:T(8,128)(2,1)S(1)}, u32[]{:S(2)}, u32[]{:S(2)}) %all-to-all-start) | async-done | bytes 131104 | tf_op jit(solution)/shard_map/all_to_all | solution.py:202
  16.6 4.0 %attention.1 = (bf16[128,512]{1,0:T(8,128)(2,1)S(1)}, bf16[4096,256]{1,0:T(8,128)(2,1)S(1)}, bf16[4096,256]{1,0:T(8,128)(2,1)S(1)}) custom-call(f32[1,8,256]{2,1,0:T(8,128)S(1)} %get-tuple-element.15.live_ref, bf16[128,512]{1,0:T(8,128)(2,1)S(1)} %bitcast.2, bf16[256,2048]{1,0:T(8,128)(2,1)S(1)} %get-tuple-element.16.q_ref, ...), custom_call_target="tpu_custom_call" | custom-call | tf_op jit(solution)/shard_map/attention/pallas_call | solution.py:224
  20.6 9.7 %all_to_all.10.parts_ref = bf16[8,16,512]{2,1,0:T(8,128)(2,1)S(1)} all-to-all(bf16[8,16,512]{2,1,0:T(8,128)(2,1)S(1)} %bitcast.3), channel_id=1, replica_groups=mesh['resp'=8,'head'=4] {'resp'}, dimensions={0} | all-to-all | bytes 262144 | tf_op jit(solution)/shard_map/all_to_all | solution.py:244
  30.3 0.7 %projection_other_core.1 = (bf16[16,512]{1,0:T(8,128)(2,1)S(1)}, bf16[16,2048]{1,0:T(8,128)(2,1)S(1)}) custom-call(bf16[8,16,512]{2,1,0:T(8,128)(2,1)S(1)} %all_to_all.10.parts_ref, bf16[4096,256]{1,0:T(8,128)(2,1)S(1)} %get-tuple-element.19.kw_ref, bf16[4096,256]{1,0:T(8,128)(2,1)S(1)} %get-tuple-element.20.vw_ref), custom_call_target="tpu_custom_call" | custom-call | tf_op jit(solution)/shard_map/projection_other_core/pallas_call | solution.py:249
  31.0 0.0 collective-permute-start
  31.0 0.7 %projection_other_y.1 = f32[16,2048]{1,0:T(8,128)S(1)} custom-call(bf16[16,512]{1,0:T(8,128)(2,1)S(1)} %get-tuple-element.21.low_ref, bf16[4096,256]{1,0:T(8,128)(2,1)S(1)} %get-tuple-element.19.kw_ref, bf16[4096,256]{1,0:T(8,128)(2,1)S(1)} %get-tuple-element.20.vw_ref), custom_call_target="tpu_custom_call" | custom-call | flops 33554432 | bytes 2097152 | tf_op jit(solution)/shard_map/projection_other_y/pallas_call | solution.py:263
  31.7 0.6 %collective-permute-done = bf16[16,2048]{1,0:T(8,128)(2,1)S(1)} collective-permute-done((bf16[16,2048]{1,0:T(8,128)(2,1)S(1)}, bf16[16,2048]{1,0:T(8,128)(2,1)S(1)}, u32[]{:S(2)}, u32[]{:S(2)}) %collective-permute-start) | collective-permute-done | bytes 65568 | tf_op jit(solution)/shard_map/ppermute | solution.py:177
  32.3 1.6 %collective-permute-start.1 = (bf16[16,2048]{1,0:T(8,128)(2,1)S(1)}, bf16[16,2048]{1,0:T(8,128)(2,1)S(1)}, u32[]{:S(2)}, u32[]{:S(2)}) collective-permute-start(bf16[16,2048]{1,0:T(8,128)(2,1)S(1)} %add_convert_fusion.1.after), channel_id=1, source_target_pairs={{0,2},{1,3},{2,0},{3,1},{4,6},{5,7},{6,4},{7,5},{8,10},{9,11},{10,... | collective-permute-start | bytes 196616 | tf_op jit(solution)/shard_map/ppermute | solution.py:177
  33.9 2.9 %projection_this_y.1 = (bf16[16,2048]{1,0:T(8,128)(2,1)S(1)}, f32[16,2048]{1,0:T(8,128)S(1)}, bf16[16,256]{1,0:T(8,128)(2,1)}, bf16[16,256]{1,0:T(8,128)(2,1)}) custom-call(bf16[16,512]{1,0:T(8,128)(2,1)S(1)} %get-tuple-element.21.low_ref, bf16[8192,256]{1,0:T(8,128)(2,1)} %kw_hbm.3, bf16[8192,256]{1,0:T(8,128)(2,1)} %vw_hbm.3, ...), custom_call_target="tpu_custom_call" | custom-call | flops 33554432 | bytes 2097152 | tf_op jit(solution)/shard_map/projection_this_y/pallas_call | solution.py:274
  36.8 0.1 collective-permute-start.2
  36.8 0.0 collective-permute-done.1
  36.9 1.2 %collective-permute-done.2 = bf16[16,2048]{1,0:T(8,128)(2,1)S(1)} collective-permute-done((bf16[16,2048]{1,0:T(8,128)(2,1)S(1)}, bf16[16,2048]{1,0:T(8,128)(2,1)S(1)}, u32[]{:S(2)}, u32[]{:S(2)}) %collective-permute-start.2) | collective-permute-done | bytes 65568 | tf_op jit(solution)/shard_map/ppermute | solution.py:177
  38.1 0.6 %add_convert_fusion = bf16[16,2048]{1,0:T(8,128)(2,1)} fusion(f32[16,2048]{1,0:T(8,128)S(1)} %convert_add_fusion, bf16[16,2048]{1,0:T(8,128)(2,1)S(1)} %collective-permute-done.2), kind=kLoop, calls=%fused_computation | loop fusion | flops 98304 | bytes 262144 | tf_op jit(solution)/shard_map/convert_element_type | solution.py:296
  (2 shorter events, 0.0 us)
Async XLA Ops:
  2.0 14.6 %all-to-all-start = ((bf16[8,16,512]{2,1,0:T(8,128)(2,1)}), bf16[8,16,512]{2,1,0:T(8,128)(2,1)S(1)}, u32[]{:S(2)}, u32[]{:S(2)}) async-start(bf16[8,16,512]{2,1,0:T(8,128)(2,1)} %join.1), calls=%async_computation | async-start | bytes 262144 | tf_op jit(solution)/shard_map/all_to_all | solution.py:202
  31.0 1.3 %collective-permute-start = (bf16[16,2048]{1,0:T(8,128)(2,1)S(1)}, bf16[16,2048]{1,0:T(8,128)(2,1)S(1)}, u32[]{:S(2)}, u32[]{:S(2)}) collective-permute-start(bf16[16,2048]{1,0:T(8,128)(2,1)S(1)} %get-tuple-element.22), channel_id=1, source_target_pairs={{0,1},{1,0},{2,3},{3,2},{4,5},{5,4},{6,7},{7,6},{8,9},{9,8},{10,11... | collective-permute-start | bytes 196616 | tf_op jit(solution)/shard_map/ppermute | solution.py:177
  32.3 4.6 %collective-permute-start.1 = (bf16[16,2048]{1,0:T(8,128)(2,1)S(1)}, bf16[16,2048]{1,0:T(8,128)(2,1)S(1)}, u32[]{:S(2)}, u32[]{:S(2)}) collective-permute-start(bf16[16,2048]{1,0:T(8,128)(2,1)S(1)} %add_convert_fusion.1.after), channel_id=1, source_target_pairs={{0,2},{1,3},{2,0},{3,1},{4,6},{5,7},{6,4},{7,5},{8,10},{9,11},{10,... | collective-permute-start | bytes 196616 | tf_op jit(solution)/shard_map/ppermute | solution.py:177
  36.8 1.3 %collective-permute-start.2 = (bf16[16,2048]{1,0:T(8,128)(2,1)S(1)}, bf16[16,2048]{1,0:T(8,128)(2,1)S(1)}, u32[]{:S(2)}, u32[]{:S(2)}) collective-permute-start(bf16[16,2048]{1,0:T(8,128)(2,1)S(1)} %get-tuple-element.26), channel_id=1, source_target_pairs={{0,1},{1,0},{2,3},{3,2},{4,5},{5,4},{6,7},{7,6},{8,9},{9,8},{10,11... | collective-permute-start | bytes 196616 | tf_op jit(solution)/shard_map/ppermute | solution.py:177

commit v10 on v7

--- a/solution.py
+++ b/solution.py
@@ -10,7 +10,6 @@
 HD = 128
 LEN = 256
 NT = (((1,), (1,)), ((), ()))
-VMEM_LIMIT = 40 << 20
 UNIT = 2
 LOG2E = 1.4426950408889634
 
@@ -118,23 +117,24 @@
     )
 
 
-def first_projection_kernel(owner, parts_ref, kw_ref, vw_ref, low_ref, out_ref):
+def first_projection_kernel(parts_ref, kw_ref, vw_ref, low_ref, out_ref):
     total = parts_ref[0].astype(jnp.float32)
     for i in range(1, parts_ref.shape[0]):
         total += parts_ref[i].astype(jnp.float32)
     low = total.astype(jnp.bfloat16)
     low_ref[...] = low
     me = lax.axis_index("head")
-    out = project(low, kw_ref, vw_ref, me ^ owner, out_ref.shape[1])
+    out = project(low, kw_ref, vw_ref, me ^ 3, out_ref.shape[1])
     out_ref[...] = out.astype(out_ref.dtype)
 
 
-def second_projection_kernel(owner, low_ref, kw_ref, vw_ref, out_ref):
+def second_projection_kernel(low_ref, kw_ref, vw_ref, out_ref):
     me = lax.axis_index("head")
-    out_ref[...] = project(low_ref[...], kw_ref, vw_ref, me ^ owner, out_ref.shape[1])
+    out_ref[...] = project(low_ref[...], kw_ref, vw_ref, me ^ 2, out_ref.shape[1])
 
 
 def last_projection_kernel(low_ref, kw_ref, vw_ref, after, out_ref, keep_ref, dk_ref, dv_ref):
+    del after
     width = dk_ref.shape[1]
     low = low_ref[...]
     dk_ref[...] = low[:, :width]
@@ -154,7 +154,7 @@
     features = k_weight.shape[0] // head
     vmem = pl.BlockSpec(memory_space=pltpu.VMEM)
     hbm = pl.BlockSpec(memory_space=pltpu.HBM)
-    params = pltpu.CompilerParams(vmem_limit_bytes=VMEM_LIMIT)
+    params = pltpu.CompilerParams(vmem_limit_bytes=12 << 20)
 
     def in_hbm(*xs):
         return [pltpu.with_memory_space_constraint(x, pltpu.HBM) for x in xs]
@@ -173,9 +173,9 @@
     )(*in_hbm(prefix_keys, prefix_values))
     both = lax.all_to_all(both, "resp", 0, 0, tiled=True).reshape(resp * own, 2 * width)
 
-    large = (queries, d_out, k_weight)
+    large = (queries, d_out)
     responses = lengths.shape[0]
-    queries, d_out, k_weight, live = pl.pallas_call(
+    queries, d_out, live = pl.pallas_call(
         load_kernel,
         out_shape=[pltpu.VMEM(x.shape, x.dtype) for x in large]
         + [pltpu.VMEM((responses, 8, LEN), jnp.float32)],
@@ -205,7 +205,14 @@
             pltpu.VMEM((kv_local, tokens, depth), jnp.bfloat16),
             pltpu.SemaphoreType.DMA,
         ],
-        compiler_params=params,
+        compiler_params=pltpu.CompilerParams(
+            vmem_limit_bytes=(8 << 20) + 8 * kv_local * tokens * depth
+        ),
+        cost_estimate=pl.CostEstimate(
+            flops=8 * kv_local * tokens * depth * HD,
+            transcendentals=kv_local * tokens * depth,
+            bytes_accessed=4 * queries.size + 6 * tokens * width,
+        ),
         name="attention",
     )(live, both, queries, d_out, *in_hbm(v_weight))
 
@@ -215,7 +222,7 @@
 
     block = (own, features)
     low, to_core = pl.pallas_call(
-        functools.partial(first_projection_kernel, 3),
+        first_projection_kernel,
         out_shape=[
             pltpu.VMEM((own, 2 * width), jnp.bfloat16),
             pltpu.VMEM(block, jnp.bfloat16),
@@ -229,7 +236,7 @@
         flops=4 * own * width * features, transcendentals=0, bytes_accessed=4 * width * features
     )
     far = pl.pallas_call(
-        functools.partial(second_projection_kernel, 2),
+        second_projection_kernel,
         out_shape=pltpu.VMEM(block, jnp.float32),
         in_specs=[vmem] * 3,
         out_specs=vmem,

time: 37.7 us -> 36.2 us (0.960)
  waiting for transfers between devices: 3.96 us -> 7.21 us
  local copies, waits for them, and re-layouts: 1.95 us -> 0.01 us
  blocking collectives: 11.4 us -> 9.87 us
  Pallas kernels: 9.16 us -> 7.86 us
    all_to_all x1, waiting for transfers between devices: 1.87 us -> 5.12 us  [body(): lax.all_to_all(both, 'resp', 0, 0, tiled=True)]
    unnamed x4 -> x2, local copies, waits for them, and re-layouts: 1.95 us -> 0.01 us
    all_to_all x1, blocking collectives: 11.4 us -> 9.87 us  [body(): lax.all_to_all(partial.reshape(resp, own, 2 * width), 'resp', 0, 0, tiled...]
    pallas_call x1, Pallas kernels: 2.87 us -> 1.56 us  [body(): pl.pallas_call(load_kernel, out_shape=[pltpu.VMEM(x.shape, x.dtype) for x...]
  transfers between devices with their start and end apart: 4 -> 4, of which waited for: 3 -> 3; matrix products, arithmetic and copies ran while one was open for 0% -> 0% of each run, Pallas kernels for 13% -> 10%
where the time goes in v10:
time: 36.2 us; the launch traced here: 35.8 us
  blocking collectives  9.87 us (27%)
  starting transfers between devices  8.85 us (24%)
  Pallas kernels  7.86 us (22%)
  waiting for transfers between devices  7.21 us (20%)
  between operations  1.33 us (4%)
  other arithmetic  0.67 us (2%)
    all_to_all x1, blocking collectives, body(): lax.all_to_all(partial.reshape(resp, own, 2 * width), 'resp', 0, 0, tiled...  9.87 us
    all_to_all x1, starting transfers between devices, body(): lax.all_to_all(both, 'resp', 0, 0, tiled=True)  7.26 us
    all_to_all x1, waiting for transfers between devices, body(): lax.all_to_all(both, 'resp', 0, 0, tiled=True)  5.12 us
    pallas_call x1, Pallas kernels, body(): pl.pallas_call(attention_kernel, out_shape=[pltpu.VMEM((tokens, 2 * width...  2.35 us
    ppermute x3, waiting for transfers between devices, swap(): return lax.ppermute(x, axis, [(i, i ^ bit) for i in range(count)])  2.09 us
    ppermute x3, starting transfers between devices, swap(): return lax.ppermute(x, axis, [(i, i ^ bit) for i in range(count)])  1.59 us
    pallas_call x1, Pallas kernels, body(): pl.pallas_call(load_kernel, out_shape=[pltpu.VMEM(x.shape, x.dtype) for x...  1.56 us
    pallas_call x1, Pallas kernels, body(): pl.pallas_call(join_kernel, out_shape=jax.ShapeDtypeStruct((resp, own, 2...  1.38 us
  transfers between devices with their start and end apart: 4, of which 3 were waited for; matrix products, arithmetic and copies ran while one was open for 0% of the time, Pallas kernels for 10%

profile of v10, /device:TPU:0, one launch (start us, length us, event | category | flops | bytes accessed | tf_op | source)
XLA Modules:
  0.0 35.8 jit_solution(744138184224964870)
XLA Ops:
  0.6 1.4 %join.1 = bf16[8,16,512]{2,1,0:T(8,128)(2,1)} custom-call(bf16[16,256]{1,0:T(8,128)(2,1)} %k_hbm.1, bf16[16,256]{1,0:T(8,128)(2,1)} %v_hbm.1), custom_call_target="tpu_custom_call" | custom-call | tf_op jit(solution)/shard_map/join/pallas_call | solution.py:162
  2.0 7.3 %all-to-all-start = ((bf16[8,16,512]{2,1,0:T(8,128)(2,1)}), bf16[8,16,512]{2,1,0:T(8,128)(2,1)S(1)}, u32[]{:S(2)}, u32[]{:S(2)}) async-start(bf16[8,16,512]{2,1,0:T(8,128)(2,1)} %join.1), calls=%async_computation | async-start | bytes 262144 | tf_op jit(solution)/shard_map/all_to_all | solution.py:174
  9.9 1.6 %load.1 = (bf16[256,2048]{1,0:T(8,128)(2,1)S(1)}, bf16[256,2048]{1,0:T(8,128)(2,1)S(1)}, f32[1,8,256]{2,1,0:T(8,128)S(1)}) custom-call(s32[1]{0:T(128)S(6)} %copy.10.lengths_ref, bf16[256,2048]{1,0:T(8,128)(2,1)} %refs_0_.1, bf16[256,2048]{1,0:T(8,128)(2,1)} %refs_1_.1), custom_call_target="tpu_custom_call" | custom-call | bytes 4194304 | tf_op jit(solution)/shard_map/load/pallas_call | solution.py:178
  11.5 5.1 %all-to-all-done = bf16[8,16,512]{2,1,0:T(8,128)(2,1)S(1)} async-done(((bf16[8,16,512]{2,1,0:T(8,128)(2,1)}), bf16[8,16,512]{2,1,0:T(8,128)(2,1)S(1)}, u32[]{:S(2)}, u32[]{:S(2)}) %all-to-all-start) | async-done | bytes 131104 | tf_op jit(solution)/shard_map/all_to_all | solution.py:174
  16.6 0.0 copy-start
  16.6 2.3 %attention.1 = (bf16[128,512]{1,0:T(8,128)(2,1)S(1)}, bf16[8192,256]{1,0:T(8,128)(2,1)S(1)}) custom-call(f32[1,8,256]{2,1,0:T(8,128)S(1)} %get-tuple-element.14.live_ref, bf16[128,512]{1,0:T(8,128)(2,1)S(1)} %bitcast.2, bf16[256,2048]{1,0:T(8,128)(2,1)S(1)} %get-tuple-element.15.q_ref, bf16[256,2048]{1,0:T(8,128)(2,1)S(1)} %get-tuple-element.16.g_ref, ...), custom_call_target="tpu_custom_call" | custom-call | flops 536870912 | bytes 2293760 | tf_op jit(solution)/shard_map/attention/pallas_call | solution.py:195
  19.0 9.9 %all_to_all.10.parts_ref = bf16[8,16,512]{2,1,0:T(8,128)(2,1)S(1)} all-to-all(bf16[8,16,512]{2,1,0:T(8,128)(2,1)S(1)} %bitcast.3), channel_id=1, replica_groups=mesh['resp'=8,'head'=4] {'resp'}, dimensions={0} | all-to-all | bytes 262144 | tf_op jit(solution)/shard_map/all_to_all | solution.py:219
  28.9 0.0 copy-done
  28.9 0.6 %projection_other_core.1 = (bf16[16,512]{1,0:T(8,128)(2,1)S(1)}, bf16[16,2048]{1,0:T(8,128)(2,1)S(1)}) custom-call(bf16[8,16,512]{2,1,0:T(8,128)(2,1)S(1)} %all_to_all.10.parts_ref, bf16[8192,256]{1,0:T(8,128)(2,1)S(1)} %copy-done, bf16[8192,256]{1,0:T(8,128)(2,1)S(1)} %get-tuple-element.18.vw_ref), custom_call_target="tpu_custom_call" | custom-call | tf_op jit(solution)/shard_map/projection_other_core/pallas_call | solution.py:224
  29.5 0.0 collective-permute-start
  29.5 0.7 %projection_other_y.1 = f32[16,2048]{1,0:T(8,128)S(1)} custom-call(bf16[16,512]{1,0:T(8,128)(2,1)S(1)} %get-tuple-element.19.low_ref, bf16[8192,256]{1,0:T(8,128)(2,1)S(1)} %copy-done, bf16[8192,256]{1,0:T(8,128)(2,1)S(1)} %get-tuple-element.18.vw_ref), custom_call_target="tpu_custom_call" | custom-call | flops 33554432 | bytes 2097152 | tf_op jit(solution)/shard_map/projection_other_y/pallas_call | solution.py:238
  30.2 0.6 %collective-permute-done = bf16[16,2048]{1,0:T(8,128)(2,1)S(1)} collective-permute-done((bf16[16,2048]{1,0:T(8,128)(2,1)S(1)}, bf16[16,2048]{1,0:T(8,128)(2,1)S(1)}, u32[]{:S(2)}, u32[]{:S(2)}) %collective-permute-start) | collective-permute-done | bytes 65568 | tf_op jit(solution)/shard_map/ppermute | solution.py:149
  30.8 1.6 %collective-permute-start.1 = (bf16[16,2048]{1,0:T(8,128)(2,1)S(1)}, bf16[16,2048]{1,0:T(8,128)(2,1)S(1)}, u32[]{:S(2)}, u32[]{:S(2)}) collective-permute-start(bf16[16,2048]{1,0:T(8,128)(2,1)S(1)} %add_convert_fusion.1.after), channel_id=1, source_target_pairs={{0,2},{1,3},{2,0},{3,1},{4,6},{5,7},{6,4},{7,5},{8,10},{9,11},{10,... | collective-permute-start | bytes 196616 | tf_op jit(solution)/shard_map/ppermute | solution.py:149
  32.4 1.3 %projection_this_y.1 = (bf16[16,2048]{1,0:T(8,128)(2,1)S(1)}, f32[16,2048]{1,0:T(8,128)S(1)}, bf16[16,256]{1,0:T(8,128)(2,1)}, bf16[16,256]{1,0:T(8,128)(2,1)}) custom-call(bf16[16,512]{1,0:T(8,128)(2,1)S(1)} %get-tuple-element.19.low_ref, bf16[8192,256]{1,0:T(8,128)(2,1)S(1)} %copy-done, bf16[8192,256]{1,0:T(8,128)(2,1)S(1)} %get-tuple-element.18.vw_ref, ...), custom_call_target="tpu_custom_call" | custom-call | flops 33554432 | bytes 2097152 | tf_op jit(solution)/shard_map/projection_this_y/pallas_call | solution.py:249
  33.6 0.0 collective-permute-start.2
  33.7 1.5 %collective-permute-done.1 = bf16[16,2048]{1,0:T(8,128)(2,1)S(1)} collective-permute-done((bf16[16,2048]{1,0:T(8,128)(2,1)S(1)}, bf16[16,2048]{1,0:T(8,128)(2,1)S(1)}, u32[]{:S(2)}, u32[]{:S(2)}) %collective-permute-start.1) | collective-permute-done | bytes 65568 | tf_op jit(solution)/shard_map/ppermute | solution.py:149
  35.1 0.0 collective-permute-done.2
  35.2 0.6 %add_convert_fusion = bf16[16,2048]{1,0:T(8,128)(2,1)} fusion(f32[16,2048]{1,0:T(8,128)S(1)} %convert_add_fusion, bf16[16,2048]{1,0:T(8,128)(2,1)S(1)} %collective-permute-done.2), kind=kLoop, calls=%fused_computation | loop fusion | flops 98304 | bytes 262144 | tf_op jit(solution)/shard_map/convert_element_type | solution.py:265
  (2 shorter events, 0.0 us)
Async XLA Ops:
  2.0 14.6 %all-to-all-start = ((bf16[8,16,512]{2,1,0:T(8,128)(2,1)}), bf16[8,16,512]{2,1,0:T(8,128)(2,1)S(1)}, u32[]{:S(2)}, u32[]{:S(2)}) async-start(bf16[8,16,512]{2,1,0:T(8,128)(2,1)} %join.1), calls=%async_computation | async-start | bytes 262144 | tf_op jit(solution)/shard_map/all_to_all | solution.py:174
  16.6 12.2 %copy-start = (bf16[8192,256]{1,0:T(8,128)(2,1)S(1)}, bf16[8192,256]{1,0:T(8,128)(2,1)}, u32[]{:S(2)}) copy-start(bf16[8192,256]{1,0:T(8,128)(2,1)} %kw_ref.5) | copy-start | bytes 12582916
  29.5 1.3 %collective-permute-start = (bf16[16,2048]{1,0:T(8,128)(2,1)S(1)}, bf16[16,2048]{1,0:T(8,128)(2,1)S(1)}, u32[]{:S(2)}, u32[]{:S(2)}) collective-permute-start(bf16[16,2048]{1,0:T(8,128)(2,1)S(1)} %get-tuple-element.20), channel_id=1, source_target_pairs={{0,1},{1,0},{2,3},{3,2},{4,5},{5,4},{6,7},{7,6},{8,9},{9,8},{10,11... | collective-permute-start | bytes 196616 | tf_op jit(solution)/shard_map/ppermute | solution.py:149
  30.8 4.3 %collective-permute-start.1 = (bf16[16,2048]{1,0:T(8,128)(2,1)S(1)}, bf16[16,2048]{1,0:T(8,128)(2,1)S(1)}, u32[]{:S(2)}, u32[]{:S(2)}) collective-permute-start(bf16[16,2048]{1,0:T(8,128)(2,1)S(1)} %add_convert_fusion.1.after), channel_id=1, source_target_pairs={{0,2},{1,3},{2,0},{3,1},{4,6},{5,7},{6,4},{7,5},{8,10},{9,11},{10,... | collective-permute-start | bytes 196616 | tf_op jit(solution)/shard_map/ppermute | solution.py:149
  33.6 1.5 %collective-permute-start.2 = (bf16[16,2048]{1,0:T(8,128)(2,1)S(1)}, bf16[16,2048]{1,0:T(8,128)(2,1)S(1)}, u32[]{:S(2)}, u32[]{:S(2)}) collective-permute-start(bf16[16,2048]{1,0:T(8,128)(2,1)S(1)} %get-tuple-element.24), channel_id=1, source_target_pairs={{0,1},{1,0},{2,3},{3,2},{4,5},{5,4},{6,7},{7,6},{8,9},{9,8},{10,11... | collective-permute-start | bytes 196616 | tf_op jit(solution)/shard_map/ppermute | solution.py:149

commit v11 on v10

--- a/solution.py
+++ b/solution.py
@@ -44,11 +44,7 @@
         copy.wait()
 
 
-def attention_kernel(
-    live_ref, kv_ref, q_ref, g_ref, vw_hbm, out_ref, vw_ref, probs_ref, dscores_ref, sem
-):
-    weight = pltpu.make_async_copy(vw_hbm, vw_ref, sem)
-    weight.start()
+def attention_kernel(live_ref, kv_ref, q_ref, g_ref, out_ref, probs_ref, dscores_ref):
     scale = HD ** (-0.5)
     width = kv_ref.shape[1] // 2
     kv_local = width // HD
@@ -103,7 +99,6 @@
             grad_v = jnp.dot(probs_ref[k], g_all, preferred_element_type=jnp.float32)
             out_ref[:, k * HD : (k + 1) * HD] = grad_k.astype(out_ref.dtype)
             out_ref[:, width + k * HD : width + (k + 1) * HD] = grad_v.astype(out_ref.dtype)
-    weight.wait()
 
 
 def project(low, kw_ref, vw_ref, owner, features):
@@ -192,29 +187,25 @@
     tokens = resp * own
     kv_local = width // HD
     depth = queries.size // kv_local // HD
-    partial, v_weight = pl.pallas_call(
+    partial = pl.pallas_call(
         attention_kernel,
-        out_shape=[
-            pltpu.VMEM((tokens, 2 * width), jnp.bfloat16),
-            pltpu.VMEM(v_weight.shape, v_weight.dtype),
-        ],
-        in_specs=[vmem] * 4 + [hbm],
-        out_specs=[vmem] * 2,
+        out_shape=pltpu.VMEM((tokens, 2 * width), jnp.bfloat16),
+        in_specs=[vmem] * 4,
+        out_specs=vmem,
         scratch_shapes=[
             pltpu.VMEM((kv_local, tokens, depth), jnp.bfloat16),
             pltpu.VMEM((kv_local, tokens, depth), jnp.bfloat16),
-            pltpu.SemaphoreType.DMA,
         ],
         compiler_params=pltpu.CompilerParams(
             vmem_limit_bytes=(8 << 20) + 8 * kv_local * tokens * depth
         ),
         cost_estimate=pl.CostEstimate(
-            flops=8 * kv_local * tokens * depth * HD,
+            flops=64 * kv_local * tokens * depth * HD,
             transcendentals=kv_local * tokens * depth,
             bytes_accessed=4 * queries.size + 6 * tokens * width,
         ),
         name="attention",
-    )(live, both, queries, d_out, *in_hbm(v_weight))
+    )(live, both, queries, d_out)
 
     shares = lax.all_to_all(
         partial.reshape(resp, own, 2 * width), "resp", 0, 0, tiled=True

time: 36.2 us -> 35.7 us (0.986)
  Pallas kernels: 7.86 us -> 7.38 us
    pallas_call x1, Pallas kernels: 2.35 us -> 1.86 us  [body(): pl.pallas_call(attention_kernel, out_shape=pltpu.VMEM((tokens, 2 * width)...]
where the time goes in v11:
time: 35.7 us; the launch traced here: 35.3 us
  blocking collectives  9.87 us (28%)
  starting transfers between devices  8.86 us (25%)
  Pallas kernels  7.38 us (21%)
  waiting for transfers between devices  7.21 us (20%)
  between operations  1.33 us (4%)
  other arithmetic  0.67 us (2%)
    all_to_all x1, blocking collectives, body(): lax.all_to_all(partial.reshape(resp, own, 2 * width), 'resp', 0, 0, tiled...  9.87 us
    all_to_all x1, starting transfers between devices, body(): lax.all_to_all(both, 'resp', 0, 0, tiled=True)  7.26 us
    all_to_all x1, waiting for transfers between devices, body(): lax.all_to_all(both, 'resp', 0, 0, tiled=True)  5.12 us
    ppermute x3, waiting for transfers between devices, swap(): return lax.ppermute(x, axis, [(i, i ^ bit) for i in range(count)])  2.08 us
    pallas_call x1, Pallas kernels, body(): pl.pallas_call(attention_kernel, out_shape=pltpu.VMEM((tokens, 2 * width)...  1.86 us
    ppermute x3, starting transfers between devices, swap(): return lax.ppermute(x, axis, [(i, i ^ bit) for i in range(count)])  1.6 us
    pallas_call x1, Pallas kernels, body(): pl.pallas_call(load_kernel, out_shape=[pltpu.VMEM(x.shape, x.dtype) for x...  1.56 us
    pallas_call x1, Pallas kernels, body(): pl.pallas_call(join_kernel, out_shape=jax.ShapeDtypeStruct((resp, own, 2...  1.38 us
  transfers between devices with their start and end apart: 4, of which 3 were waited for; matrix products, arithmetic and copies ran while one was open for 0% of the time, Pallas kernels for 10%

profile of v11, /device:TPU:0, one launch (start us, length us, event | category | flops | bytes accessed | tf_op | source)
XLA Modules:
  0.0 35.3 jit_solution(10808171212041881065)
XLA Ops:
  0.6 1.4 %join.1 = bf16[8,16,512]{2,1,0:T(8,128)(2,1)} custom-call(bf16[16,256]{1,0:T(8,128)(2,1)} %k_hbm.1, bf16[16,256]{1,0:T(8,128)(2,1)} %v_hbm.1), custom_call_target="tpu_custom_call" | custom-call | tf_op jit(solution)/shard_map/join/pallas_call | solution.py:157
  2.0 7.3 %all-to-all-start = ((bf16[8,16,512]{2,1,0:T(8,128)(2,1)}), bf16[8,16,512]{2,1,0:T(8,128)(2,1)S(1)}, u32[]{:S(2)}, u32[]{:S(2)}) async-start(bf16[8,16,512]{2,1,0:T(8,128)(2,1)} %join.1), calls=%async_computation | async-start | bytes 262144 | tf_op jit(solution)/shard_map/all_to_all | solution.py:169
  9.9 1.6 %load.1 = (bf16[256,2048]{1,0:T(8,128)(2,1)S(1)}, bf16[256,2048]{1,0:T(8,128)(2,1)S(1)}, f32[1,8,256]{2,1,0:T(8,128)S(1)}) custom-call(s32[1]{0:T(128)S(6)} %copy.10.lengths_ref, bf16[256,2048]{1,0:T(8,128)(2,1)} %refs_0_.1, bf16[256,2048]{1,0:T(8,128)(2,1)} %refs_1_.1), custom_call_target="tpu_custom_call" | custom-call | bytes 4194304 | tf_op jit(solution)/shard_map/load/pallas_call | solution.py:173
  11.5 5.1 %all-to-all-done = bf16[8,16,512]{2,1,0:T(8,128)(2,1)S(1)} async-done(((bf16[8,16,512]{2,1,0:T(8,128)(2,1)}), bf16[8,16,512]{2,1,0:T(8,128)(2,1)S(1)}, u32[]{:S(2)}, u32[]{:S(2)}) %all-to-all-start) | async-done | bytes 131104 | tf_op jit(solution)/shard_map/all_to_all | solution.py:169
  16.6 0.0 copy-start
  16.6 0.0 copy-start.1
  16.6 1.9 %attention.1 = bf16[128,512]{1,0:T(8,128)(2,1)S(1)} custom-call(f32[1,8,256]{2,1,0:T(8,128)S(1)} %get-tuple-element.12.live_ref, bf16[128,512]{1,0:T(8,128)(2,1)S(1)} %bitcast.2, bf16[256,2048]{1,0:T(8,128)(2,1)S(1)} %get-tuple-element.13.q_ref, bf16[256,2048]{1,0:T(8,128)(2,1)S(1)} %get-tuple-element.14.g_ref), custom_call_target="tpu_custom_call" | custom-call | flops 4294967296 | bytes 2293760 | tf_op jit(solution)/shard_map/attention/pallas_call | solution.py:190
  18.5 9.9 %all_to_all.10.parts_ref = bf16[8,16,512]{2,1,0:T(8,128)(2,1)S(1)} all-to-all(bf16[8,16,512]{2,1,0:T(8,128)(2,1)S(1)} %bitcast.3), channel_id=1, replica_groups=mesh['resp'=8,'head'=4] {'resp'}, dimensions={0} | all-to-all | bytes 262144 | tf_op jit(solution)/shard_map/all_to_all | solution.py:210
  28.4 0.0 copy-done
  28.4 0.0 copy-done.1
  28.4 0.6 %projection_other_core.1 = (bf16[16,512]{1,0:T(8,128)(2,1)S(1)}, bf16[16,2048]{1,0:T(8,128)(2,1)S(1)}) custom-call(bf16[8,16,512]{2,1,0:T(8,128)(2,1)S(1)} %all_to_all.10.parts_ref, bf16[8192,256]{1,0:T(8,128)(2,1)S(1)} %copy-done, bf16[8192,256]{1,0:T(8,128)(2,1)S(1)} %copy-done.1), custom_call_target="tpu_custom_call" | custom-call | tf_op jit(solution)/shard_map/projection_other_core/pallas_call | solution.py:215
  29.0 0.0 collective-permute-start
  29.0 0.7 %projection_other_y.1 = f32[16,2048]{1,0:T(8,128)S(1)} custom-call(bf16[16,512]{1,0:T(8,128)(2,1)S(1)} %get-tuple-element.15.low_ref, bf16[8192,256]{1,0:T(8,128)(2,1)S(1)} %copy-done, bf16[8192,256]{1,0:T(8,128)(2,1)S(1)} %copy-done.1), custom_call_target="tpu_custom_call" | custom-call | flops 33554432 | bytes 2097152 | tf_op jit(solution)/shard_map/projection_other_y/pallas_call | solution.py:229
  29.7 0.6 %collective-permute-done = bf16[16,2048]{1,0:T(8,128)(2,1)S(1)} collective-permute-done((bf16[16,2048]{1,0:T(8,128)(2,1)S(1)}, bf16[16,2048]{1,0:T(8,128)(2,1)S(1)}, u32[]{:S(2)}, u32[]{:S(2)}) %collective-permute-start) | collective-permute-done | bytes 65568 | tf_op jit(solution)/shard_map/ppermute | solution.py:144
  30.3 1.6 %collective-permute-start.1 = (bf16[16,2048]{1,0:T(8,128)(2,1)S(1)}, bf16[16,2048]{1,0:T(8,128)(2,1)S(1)}, u32[]{:S(2)}, u32[]{:S(2)}) collective-permute-start(bf16[16,2048]{1,0:T(8,128)(2,1)S(1)} %add_convert_fusion.1.after), channel_id=1, source_target_pairs={{0,2},{1,3},{2,0},{3,1},{4,6},{5,7},{6,4},{7,5},{8,10},{9,11},{10,... | collective-permute-start | bytes 196616 | tf_op jit(solution)/shard_map/ppermute | solution.py:144
  31.9 1.3 %projection_this_y.1 = (bf16[16,2048]{1,0:T(8,128)(2,1)S(1)}, f32[16,2048]{1,0:T(8,128)S(1)}, bf16[16,256]{1,0:T(8,128)(2,1)}, bf16[16,256]{1,0:T(8,128)(2,1)}) custom-call(bf16[16,512]{1,0:T(8,128)(2,1)S(1)} %get-tuple-element.15.low_ref, bf16[8192,256]{1,0:T(8,128)(2,1)S(1)} %copy-done, bf16[8192,256]{1,0:T(8,128)(2,1)S(1)} %copy-done.1, ...), custom_call_target="tpu_custom_call" | custom-call | flops 33554432 | bytes 2097152 | tf_op jit(solution)/shard_map/projection_this_y/pallas_call | solution.py:240
  33.2 0.0 collective-permute-start.2
  33.2 1.5 %collective-permute-done.1 = bf16[16,2048]{1,0:T(8,128)(2,1)S(1)} collective-permute-done((bf16[16,2048]{1,0:T(8,128)(2,1)S(1)}, bf16[16,2048]{1,0:T(8,128)(2,1)S(1)}, u32[]{:S(2)}, u32[]{:S(2)}) %collective-permute-start.1) | collective-permute-done | bytes 65568 | tf_op jit(solution)/shard_map/ppermute | solution.py:144
  34.7 0.0 collective-permute-done.2
  34.7 0.6 %add_convert_fusion = bf16[16,2048]{1,0:T(8,128)(2,1)} fusion(f32[16,2048]{1,0:T(8,128)S(1)} %convert_add_fusion, bf16[16,2048]{1,0:T(8,128)(2,1)S(1)} %collective-permute-done.2), kind=kLoop, calls=%fused_computation | loop fusion | flops 98304 | bytes 262144 | tf_op jit(solution)/shard_map/convert_element_type | solution.py:256
  (2 shorter events, 0.0 us)
Async XLA Ops:
  2.0 14.6 %all-to-all-start = ((bf16[8,16,512]{2,1,0:T(8,128)(2,1)}), bf16[8,16,512]{2,1,0:T(8,128)(2,1)S(1)}, u32[]{:S(2)}, u32[]{:S(2)}) async-start(bf16[8,16,512]{2,1,0:T(8,128)(2,1)} %join.1), calls=%async_computation | async-start | bytes 262144 | tf_op jit(solution)/shard_map/all_to_all | solution.py:169
  16.6 11.7 %copy-start = (bf16[8192,256]{1,0:T(8,128)(2,1)S(1)}, bf16[8192,256]{1,0:T(8,128)(2,1)}, u32[]{:S(2)}) copy-start(bf16[8192,256]{1,0:T(8,128)(2,1)} %kw_ref.5) | copy-start | bytes 12582916
  16.6 11.7 %copy-start.1 = (bf16[8192,256]{1,0:T(8,128)(2,1)S(1)}, bf16[8192,256]{1,0:T(8,128)(2,1)}, u32[]{:S(2)}) copy-start(bf16[8192,256]{1,0:T(8,128)(2,1)} %vw_ref.5) | copy-start | bytes 12582916
  29.0 1.3 %collective-permute-start = (bf16[16,2048]{1,0:T(8,128)(2,1)S(1)}, bf16[16,2048]{1,0:T(8,128)(2,1)S(1)}, u32[]{:S(2)}, u32[]{:S(2)}) collective-permute-start(bf16[16,2048]{1,0:T(8,128)(2,1)S(1)} %get-tuple-element.16), channel_id=1, source_target_pairs={{0,1},{1,0},{2,3},{3,2},{4,5},{5,4},{6,7},{7,6},{8,9},{9,8},{10,11... | collective-permute-start | bytes 196616 | tf_op jit(solution)/shard_map/ppermute | solution.py:144
  30.3 4.3 %collective-permute-start.1 = (bf16[16,2048]{1,0:T(8,128)(2,1)S(1)}, bf16[16,2048]{1,0:T(8,128)(2,1)S(1)}, u32[]{:S(2)}, u32[]{:S(2)}) collective-permute-start(bf16[16,2048]{1,0:T(8,128)(2,1)S(1)} %add_convert_fusion.1.after), channel_id=1, source_target_pairs={{0,2},{1,3},{2,0},{3,1},{4,6},{5,7},{6,4},{7,5},{8,10},{9,11},{10,... | collective-permute-start | bytes 196616 | tf_op jit(solution)/shard_map/ppermute | solution.py:144
  33.2 1.5 %collective-permute-start.2 = (bf16[16,2048]{1,0:T(8,128)(2,1)S(1)}, bf16[16,2048]{1,0:T(8,128)(2,1)S(1)}, u32[]{:S(2)}, u32[]{:S(2)}) collective-permute-start(bf16[16,2048]{1,0:T(8,128)(2,1)S(1)} %get-tuple-element.20), channel_id=1, source_target_pairs={{0,1},{1,0},{2,3},{3,2},{4,5},{5,4},{6,7},{7,6},{8,9},{9,8},{10,11... | collective-permute-start | bytes 196616 | tf_op jit(solution)/shard_map/ppermute | solution.py:144

commit v12 on v11

--- a/solution.py
+++ b/solution.py
@@ -74,12 +74,30 @@
             lax.dot_general(values, stack(g_ref, unit), NT, preferred_element_type=jnp.float32),
         )
 
+    def sums(i):
+        unit = units[i]
+        return (
+            jnp.dot(dscores_ref[i % 2], stack(q_ref, unit), preferred_element_type=jnp.float32),
+            jnp.dot(probs_ref[i % 2], stack(g_ref, unit), preferred_element_type=jnp.float32),
+        )
+
+    def finish(k, grad_k, grad_v):
+        out_ref[:, k * HD : (k + 1) * HD] = (grad_k * scale).astype(out_ref.dtype)
+        out_ref[:, width + k * HD : width + (k + 1) * HD] = grad_v.astype(out_ref.dtype)
+
     following = products(units[0])
     for i, unit in enumerate(units):
         k, part, h = unit
         scores, dprobs = following
         if i + 1 < len(units):
             following = products(units[i + 1])
+        if i > 0:
+            more_k, more_v = sums(i - 1)
+            first = i == 1 or units[i - 2][0] != units[i - 1][0]
+            grad_k = more_k if first else grad_k + more_k
+            grad_v = more_v if first else grad_v + more_v
+            if units[i - 1][0] != k:
+                finish(units[i - 1][0], grad_k, grad_v)
         top = jnp.max(scores, axis=0, keepdims=True)
         expo = jnp.exp2((scores - top) * (scale * LOG2E))
         total = jnp.sum(expo, axis=0, keepdims=True)
@@ -88,17 +106,10 @@
         delta = weighted * inverse
         factor = inverse * jnp.concatenate([live_ref[part, :1]] * UNIT, axis=1)
         probs = expo * factor
-        mine = [u for u in units if u[0] == k]
-        cols = pl.ds(mine.index(unit) * UNIT * LEN, UNIT * LEN)
-        probs_ref[k, :, cols] = probs.astype(jnp.bfloat16)
-        dscores_ref[k, :, cols] = (probs * (dprobs - delta)).astype(jnp.bfloat16)
-        if unit == mine[-1]:
-            q_all = jnp.concatenate([stack(q_ref, u) for u in mine], axis=0)
-            g_all = jnp.concatenate([stack(g_ref, u) for u in mine], axis=0)
-            grad_k = jnp.dot(dscores_ref[k], q_all, preferred_element_type=jnp.float32) * scale
-            grad_v = jnp.dot(probs_ref[k], g_all, preferred_element_type=jnp.float32)
-            out_ref[:, k * HD : (k + 1) * HD] = grad_k.astype(out_ref.dtype)
-            out_ref[:, width + k * HD : width + (k + 1) * HD] = grad_v.astype(out_ref.dtype)
+        probs_ref[i % 2] = probs.astype(jnp.bfloat16)
+        dscores_ref[i % 2] = (probs * (dprobs - delta)).astype(jnp.bfloat16)
+    more_k, more_v = sums(len(units) - 1)
+    finish(units[-1][0], grad_k + more_k, grad_v + more_v)
 
 
 def project(low, kw_ref, vw_ref, owner, features):
@@ -112,18 +123,25 @@
     )
 
 
-def first_projection_kernel(parts_ref, kw_ref, vw_ref, low_ref, out_ref):
+def sum_kernel(parts_ref, kw_ref, vw_ref, low_ref, out_ref):
     total = parts_ref[0].astype(jnp.float32)
     for i in range(1, parts_ref.shape[0]):
         total += parts_ref[i].astype(jnp.float32)
-    low = total.astype(jnp.bfloat16)
-    low_ref[...] = low
+    low_ref[...] = total.astype(jnp.bfloat16)
+    other_core_term(1, low_ref, kw_ref, vw_ref, out_ref)
+
+
+def other_core_term(core, low_ref, kw_ref, vw_ref, out_ref):
     me = lax.axis_index("head")
-    out = project(low, kw_ref, vw_ref, me ^ 3, out_ref.shape[1])
-    out_ref[...] = out.astype(out_ref.dtype)
-
-
-def second_projection_kernel(low_ref, kw_ref, vw_ref, out_ref):
+
+    @pl.when(lax.rem(me, 2) == core)
+    def _():
+        out = project(low_ref[...], kw_ref, vw_ref, me ^ 3, out_ref.shape[1])
+        out_ref[...] = out.astype(out_ref.dtype)
+
+
+def second_projection_kernel(low_ref, kw_ref, vw_ref, after, out_ref):
+    del after
     me = lax.axis_index("head")
     out_ref[...] = project(low_ref[...], kw_ref, vw_ref, me ^ 2, out_ref.shape[1])
 
@@ -144,6 +162,10 @@
     return lax.ppermute(x, axis, [(i, i ^ bit) for i in range(count)])
 
 
+def one_way(x, count, core):
+    return lax.ppermute(x, "head", [(i, i ^ 1) for i in range(count) if i % 2 == core])
+
+
 def body(resp, head, queries, d_out, prefix_keys, prefix_values, k_weight, v_weight, lengths):
     own, width = prefix_keys.shape
     features = k_weight.shape[0] // head
@@ -193,11 +215,11 @@
         in_specs=[vmem] * 4,
         out_specs=vmem,
         scratch_shapes=[
-            pltpu.VMEM((kv_local, tokens, depth), jnp.bfloat16),
-            pltpu.VMEM((kv_local, tokens, depth), jnp.bfloat16),
+            pltpu.VMEM((2, tokens, UNIT * LEN), jnp.bfloat16),
+            pltpu.VMEM((2, tokens, UNIT * LEN), jnp.bfloat16),
         ],
         compiler_params=pltpu.CompilerParams(
-            vmem_limit_bytes=(8 << 20) + 8 * kv_local * tokens * depth
+            vmem_limit_bytes=(8 << 20) + 40 * UNIT * LEN * tokens
         ),
         cost_estimate=pl.CostEstimate(
             flops=64 * kv_local * tokens * depth * HD,
@@ -212,8 +234,8 @@
     )
 
     block = (own, features)
-    low, to_core = pl.pallas_call(
-        first_projection_kernel,
+    low, from_one = pl.pallas_call(
+        sum_kernel,
         out_shape=[
             pltpu.VMEM((own, 2 * width), jnp.bfloat16),
             pltpu.VMEM(block, jnp.bfloat16),
@@ -221,21 +243,33 @@
         in_specs=[vmem] * 3,
         out_specs=[vmem] * 2,
         compiler_params=params,
-        name="projection_other_core",
+        name="sum_and_projection_core_1",
     )(shares, k_weight, v_weight)
+    from_one = one_way(from_one, head, 1)
     cost = pl.CostEstimate(
         flops=4 * own * width * features, transcendentals=0, bytes_accessed=4 * width * features
     )
+    from_zero = pl.pallas_call(
+        functools.partial(other_core_term, 0),
+        out_shape=pltpu.VMEM(block, jnp.bfloat16),
+        in_specs=[vmem] * 3,
+        out_specs=vmem,
+        compiler_params=params,
+        cost_estimate=cost,
+        name="projection_core_0",
+    )(low, k_weight, v_weight)
     far = pl.pallas_call(
         second_projection_kernel,
         out_shape=pltpu.VMEM(block, jnp.float32),
-        in_specs=[vmem] * 3,
+        in_specs=[vmem] * 3 + [pl.BlockSpec(memory_space=pl.ANY)],
         out_specs=vmem,
         compiler_params=params,
         cost_estimate=cost,
         name="projection_other_y",
-    )(low, k_weight, v_weight)
-    far = (far + swap(to_core, "head", head, 1).astype(jnp.float32)).astype(jnp.bfloat16)
+    )(low, k_weight, v_weight, from_zero)
+    from_zero = one_way(from_zero, head, 0)
+    far = lax.optimization_barrier(far + from_one.astype(jnp.float32))
+    far = (far + from_zero.astype(jnp.float32)).astype(jnp.bfloat16)
     got = swap(far, "head", head, 2)
     to_core, total, dk_low, dv_low = pl.pallas_call(
         last_projection_kernel,

time: 35.7 us -> 39.3 us (1.10)
  starting transfers between devices: 8.86 us -> 12.6 us
  waiting for transfers between devices: 7.21 us -> 6.8 us
    ppermute x0 -> x2, starting transfers between devices: none -> 3.7 us  [one_way(): lax.ppermute(x, 'head', [(i, i ^ 1) for i in range(count) if i % 2 == core])]
    ppermute x3 -> x2, waiting for transfers between devices: 2.08 us -> 1.48 us  [swap(): return lax.ppermute(x, axis, [(i, i ^ bit) for i in range(count)])]
    ppermute x3 -> x2, starting transfers between devices: 1.6 us -> 1.68 us  [swap(): return lax.ppermute(x, axis, [(i, i ^ bit) for i in range(count)])]
  transfers between devices with their start and end apart: 4 -> 5, of which waited for: 3 -> 3; matrix products, arithmetic and copies ran while one was open for 0% -> 0% of each run, Pallas kernels for 10% -> 11%
where the time goes in v12:
time: 39.3 us; the launch traced here: 38.9 us
  starting transfers between devices  12.6 us (32%)
  blocking collectives  9.87 us (25%)
  Pallas kernels  7.49 us (19%)
  waiting for transfers between devices  6.8 us (17%)
  between operations  1.35 us (3%)
  other arithmetic  0.7 us (2%)
    all_to_all x1, blocking collectives, body(): lax.all_to_all(partial.reshape(resp, own, 2 * width), 'resp', 0, 0, tiled...  9.87 us
    all_to_all x1, starting transfers between devices, body(): lax.all_to_all(both, 'resp', 0, 0, tiled=True)  7.26 us
    all_to_all x1, waiting for transfers between devices, body(): lax.all_to_all(both, 'resp', 0, 0, tiled=True)  5.12 us
    ppermute x2, starting transfers between devices, one_way(): lax.ppermute(x, 'head', [(i, i ^ 1) for i in range(count) if i % 2 == core])  3.7 us
    pallas_call x1, Pallas kernels, body(): pl.pallas_call(attention_kernel, out_shape=pltpu.VMEM((tokens, 2 * width)...  1.96 us
    ppermute x2, starting transfers between devices, swap(): return lax.ppermute(x, axis, [(i, i ^ bit) for i in range(count)])  1.68 us
    pallas_call x1, Pallas kernels, body(): pl.pallas_call(load_kernel, out_shape=[pltpu.VMEM(x.shape, x.dtype) for x...  1.56 us
    ppermute x2, waiting for transfers between devices, swap(): return lax.ppermute(x, axis, [(i, i ^ bit) for i in range(count)])  1.48 us
  transfers between devices with their start and end apart: 5, of which 3 were waited for; matrix products, arithmetic and copies ran while one was open for 0% of the time, Pallas kernels for 11%

profile of v12, /device:TPU:0, one launch (start us, length us, event | category | flops | bytes accessed | tf_op | source)
XLA Modules:
  0.0 38.9 jit_solution(726762171177129733)
XLA Ops:
  0.6 1.4 %join.1 = bf16[8,16,512]{2,1,0:T(8,128)(2,1)} custom-call(bf16[16,256]{1,0:T(8,128)(2,1)} %k_hbm.1, bf16[16,256]{1,0:T(8,128)(2,1)} %v_hbm.1), custom_call_target="tpu_custom_call" | custom-call | tf_op jit(solution)/shard_map/join/pallas_call | solution.py:179
  2.0 7.3 %all-to-all-start = ((bf16[8,16,512]{2,1,0:T(8,128)(2,1)}), bf16[8,16,512]{2,1,0:T(8,128)(2,1)S(1)}, u32[]{:S(2)}, u32[]{:S(2)}) async-start(bf16[8,16,512]{2,1,0:T(8,128)(2,1)} %join.1), calls=%async_computation | async-start | bytes 262144 | tf_op jit(solution)/shard_map/all_to_all | solution.py:191
  9.9 1.6 %load.1 = (bf16[256,2048]{1,0:T(8,128)(2,1)S(1)}, bf16[256,2048]{1,0:T(8,128)(2,1)S(1)}, f32[1,8,256]{2,1,0:T(8,128)S(1)}) custom-call(s32[1]{0:T(128)S(6)} %copy.10.lengths_ref, bf16[256,2048]{1,0:T(8,128)(2,1)} %refs_0_.1, bf16[256,2048]{1,0:T(8,128)(2,1)} %refs_1_.1), custom_call_target="tpu_custom_call" | custom-call | bytes 4194304 | tf_op jit(solution)/shard_map/load/pallas_call | solution.py:195
  11.5 5.1 %all-to-all-done = bf16[8,16,512]{2,1,0:T(8,128)(2,1)S(1)} async-done(((bf16[8,16,512]{2,1,0:T(8,128)(2,1)}), bf16[8,16,512]{2,1,0:T(8,128)(2,1)S(1)}, u32[]{:S(2)}, u32[]{:S(2)}) %all-to-all-start) | async-done | bytes 131104 | tf_op jit(solution)/shard_map/all_to_all | solution.py:191
  16.6 0.0 copy-start
  16.6 0.0 copy-start.1
  16.6 2.0 %attention.1 = bf16[128,512]{1,0:T(8,128)(2,1)S(1)} custom-call(f32[1,8,256]{2,1,0:T(8,128)S(1)} %get-tuple-element.12.live_ref, bf16[128,512]{1,0:T(8,128)(2,1)S(1)} %bitcast.2, bf16[256,2048]{1,0:T(8,128)(2,1)S(1)} %get-tuple-element.13.q_ref, bf16[256,2048]{1,0:T(8,128)(2,1)S(1)} %get-tuple-element.14.g_ref), custom_call_target="tpu_custom_call" | custom-call | flops 4294967296 | bytes 2293760 | tf_op jit(solution)/shard_map/attention/pallas_call | solution.py:212
  18.6 9.9 %all_to_all.10.parts_ref = bf16[8,16,512]{2,1,0:T(8,128)(2,1)S(1)} all-to-all(bf16[8,16,512]{2,1,0:T(8,128)(2,1)S(1)} %bitcast.3), channel_id=1, replica_groups=mesh['resp'=8,'head'=4] {'resp'}, dimensions={0} | all-to-all | bytes 262144 | tf_op jit(solution)/shard_map/all_to_all | solution.py:232
  28.5 0.0 copy-done
  28.5 0.0 copy-done.1
  28.5 1.3 %collective-permute-start = (bf16[16,2048]{1,0:T(8,128)(2,1)S(1)}, bf16[16,2048]{1,0:T(8,128)(2,1)S(1)}, u32[]{:S(2)}, u32[]{:S(2)}) collective-permute-start(bf16[16,2048]{1,0:T(8,128)(2,1)S(1)} %get-tuple-element.16), channel_id=1, source_target_pairs={{1,0},{3,2},{5,4},{7,6},{9,8},{11,10},{13,12},{15,14},{17,16},{19,... | collective-permute-start | bytes 196616 | tf_op jit(solution)/shard_map/ppermute | solution.py:166
  29.8 0.7 %projection_core_0.1.after = bf16[16,2048]{1,0:T(8,128)(2,1)S(1)} custom-call(bf16[16,512]{1,0:T(8,128)(2,1)S(1)} %get-tuple-element.15.low_ref, bf16[8192,256]{1,0:T(8,128)(2,1)S(1)} %copy-done, bf16[8192,256]{1,0:T(8,128)(2,1)S(1)} %copy-done.1), custom_call_target="tpu_custom_call" | custom-call | flops 33554432 | bytes 2097152 | tf_op jit(solution)/shard_map/projection_core_0/pallas_call | solution.py:252
  30.5 2.4 %collective-permute-start.1 = (bf16[16,2048]{1,0:T(8,128)(2,1)S(1)}, bf16[16,2048]{1,0:T(8,128)(2,1)S(1)}, u32[]{:S(2)}, u32[]{:S(2)}) collective-permute-start(bf16[16,2048]{1,0:T(8,128)(2,1)S(1)} %projection_core_0.1.after), channel_id=1, source_target_pairs={{0,1},{2,3},{4,5},{6,7},{8,9},{10,11},{12,13},{14,15},{16,17},{18,... | collective-permute-start | bytes 196616 | tf_op jit(solution)/shard_map/ppermute | solution.py:166
  32.9 0.7 %projection_other_y.1 = f32[16,2048]{1,0:T(8,128)S(1)} custom-call(bf16[16,512]{1,0:T(8,128)(2,1)S(1)} %get-tuple-element.15.low_ref, bf16[8192,256]{1,0:T(8,128)(2,1)S(1)} %copy-done, bf16[8192,256]{1,0:T(8,128)(2,1)S(1)} %copy-done.1, bf16[16,2048]{1,0:T(8,128)(2,1)S(1)} %projection_core_0.1.after), custom_call_target="tpu_custom_call" | custom-call | flops 33554432 | bytes 2097152 | tf_op jit(solution)/shard_map/projection_other_y/pallas_call | solution.py:261
  33.5 0.0 collective-permute-done
  33.6 0.2 collective-permute-done.1
  33.8 1.6 %collective-permute-start.2 = (bf16[16,2048]{1,0:T(8,128)(2,1)S(1)}, bf16[16,2048]{1,0:T(8,128)(2,1)S(1)}, u32[]{:S(2)}, u32[]{:S(2)}) collective-permute-start(bf16[16,2048]{1,0:T(8,128)(2,1)S(1)} %add_convert_fusion.1.after), channel_id=1, source_target_pairs={{0,2},{1,3},{2,0},{3,1},{4,6},{5,7},{6,4},{7,5},{8,10},{9,11},{10,... | collective-permute-start | bytes 196616 | tf_op jit(solution)/shard_map/ppermute | solution.py:162
  35.4 1.3 %projection_this_y.1 = (bf16[16,2048]{1,0:T(8,128)(2,1)S(1)}, f32[16,2048]{1,0:T(8,128)S(1)}, bf16[16,256]{1,0:T(8,128)(2,1)}, bf16[16,256]{1,0:T(8,128)(2,1)}) custom-call(bf16[16,512]{1,0:T(8,128)(2,1)S(1)} %get-tuple-element.15.low_ref, bf16[8192,256]{1,0:T(8,128)(2,1)S(1)} %copy-done, bf16[8192,256]{1,0:T(8,128)(2,1)S(1)} %copy-done.1, ...), custom_call_target="tpu_custom_call" | custom-call | flops 33554432 | bytes 2097152 | tf_op jit(solution)/shard_map/projection_this_y/pallas_call | solution.py:274
  36.6 0.1 collective-permute-start.3
  36.7 1.5 %collective-permute-done.2 = bf16[16,2048]{1,0:T(8,128)(2,1)S(1)} collective-permute-done((bf16[16,2048]{1,0:T(8,128)(2,1)S(1)}, bf16[16,2048]{1,0:T(8,128)(2,1)S(1)}, u32[]{:S(2)}, u32[]{:S(2)}) %collective-permute-start.2) | collective-permute-done | bytes 65568 | tf_op jit(solution)/shard_map/ppermute | solution.py:162
  38.2 0.0 collective-permute-done.3
  38.2 0.6 %add_convert_fusion = bf16[16,2048]{1,0:T(8,128)(2,1)} fusion(f32[16,2048]{1,0:T(8,128)S(1)} %convert_add_fusion, bf16[16,2048]{1,0:T(8,128)(2,1)S(1)} %collective-permute-done.3), kind=kLoop, calls=%fused_computation | loop fusion | flops 98304 | bytes 262144 | tf_op jit(solution)/shard_map/convert_element_type | solution.py:290
  (4 shorter events, 0.1 us)
Async XLA Ops:
  2.0 14.6 %all-to-all-start = ((bf16[8,16,512]{2,1,0:T(8,128)(2,1)}), bf16[8,16,512]{2,1,0:T(8,128)(2,1)S(1)}, u32[]{:S(2)}, u32[]{:S(2)}) async-start(bf16[8,16,512]{2,1,0:T(8,128)(2,1)} %join.1), calls=%async_computation | async-start | bytes 262144 | tf_op jit(solution)/shard_map/all_to_all | solution.py:191
  16.6 11.8 %copy-start = (bf16[8192,256]{1,0:T(8,128)(2,1)S(1)}, bf16[8192,256]{1,0:T(8,128)(2,1)}, u32[]{:S(2)}) copy-start(bf16[8192,256]{1,0:T(8,128)(2,1)} %kw_ref.7) | copy-start | bytes 12582916
  16.6 11.8 %copy-start.1 = (bf16[8192,256]{1,0:T(8,128)(2,1)S(1)}, bf16[8192,256]{1,0:T(8,128)(2,1)}, u32[]{:S(2)}) copy-start(bf16[8192,256]{1,0:T(8,128)(2,1)} %vw_ref.7) | copy-start | bytes 12582916
  28.5 5.0 %collective-permute-start = (bf16[16,2048]{1,0:T(8,128)(2,1)S(1)}, bf16[16,2048]{1,0:T(8,128)(2,1)S(1)}, u32[]{:S(2)}, u32[]{:S(2)}) collective-permute-start(bf16[16,2048]{1,0:T(8,128)(2,1)S(1)} %get-tuple-element.16), channel_id=1, source_target_pairs={{1,0},{3,2},{5,4},{7,6},{9,8},{11,10},{13,12},{15,14},{17,16},{19,... | collective-permute-start | bytes 196616 | tf_op jit(solution)/shard_map/ppermute | solution.py:166
  30.5 3.3 %collective-permute-start.1 = (bf16[16,2048]{1,0:T(8,128)(2,1)S(1)}, bf16[16,2048]{1,0:T(8,128)(2,1)S(1)}, u32[]{:S(2)}, u32[]{:S(2)}) collective-permute-start(bf16[16,2048]{1,0:T(8,128)(2,1)S(1)} %projection_core_0.1.after), channel_id=1, source_target_pairs={{0,1},{2,3},{4,5},{6,7},{8,9},{10,11},{12,13},{14,15},{16,17},{18,... | collective-permute-start | bytes 196616 | tf_op jit(solution)/shard_map/ppermute | solution.py:166
  33.8 4.4 %collective-permute-start.2 = (bf16[16,2048]{1,0:T(8,128)(2,1)S(1)}, bf16[16,2048]{1,0:T(8,128)(2,1)S(1)}, u32[]{:S(2)}, u32[]{:S(2)}) collective-permute-start(bf16[16,2048]{1,0:T(8,128)(2,1)S(1)} %add_convert_fusion.1.after), channel_id=1, source_target_pairs={{0,2},{1,3},{2,0},{3,1},{4,6},{5,7},{6,4},{7,5},{8,10},{9,11},{10,... | collective-permute-start | bytes 196616 | tf_op jit(solution)/shard_map/ppermute | solution.py:162
  36.6 1.6 %collective-permute-start.3 = (bf16[16,2048]{1,0:T(8,128)(2,1)S(1)}, bf16[16,2048]{1,0:T(8,128)(2,1)S(1)}, u32[]{:S(2)}, u32[]{:S(2)}) collective-permute-start(bf16[16,2048]{1,0:T(8,128)(2,1)S(1)} %get-tuple-element.20), channel_id=1, source_target_pairs={{0,1},{1,0},{2,3},{3,2},{4,5},{5,4},{6,7},{7,6},{8,9},{9,8},{10,11... | collective-permute-start | bytes 196616 | tf_op jit(solution)/shard_map/ppermute | solution.py:162

commit v13 on v11

--- a/solution.py
+++ b/solution.py
@@ -44,8 +44,9 @@
         copy.wait()
 
 
-def attention_kernel(live_ref, kv_ref, q_ref, g_ref, out_ref, probs_ref, dscores_ref):
+def attention_kernel(live_ref, kv_ref, q_ref, g_ref, out_ref, blocks_ref, weights_ref):
     scale = HD ** (-0.5)
+    tokens = kv_ref.shape[0]
     width = kv_ref.shape[1] // 2
     kv_local = width // HD
     parts = q_ref.shape[0] // LEN
@@ -65,14 +66,15 @@
         ]
         return jnp.concatenate(heads, axis=0)
 
+    blocks_ref[...] = jnp.zeros_like(blocks_ref)
+    for k in range(kv_local):
+        blocks_ref[k, :tokens, :HD] = kv_ref[:, k * HD : (k + 1) * HD]
+        blocks_ref[k, tokens:, HD:] = kv_ref[:, width + k * HD : width + (k + 1) * HD]
+
     def products(unit):
-        k = unit[0]
-        keys = kv_ref[:, k * HD : (k + 1) * HD]
-        values = kv_ref[:, width + k * HD : width + (k + 1) * HD]
-        return (
-            lax.dot_general(keys, stack(q_ref, unit), NT, preferred_element_type=jnp.float32),
-            lax.dot_general(values, stack(g_ref, unit), NT, preferred_element_type=jnp.float32),
-        )
+        both = jnp.concatenate([stack(q_ref, unit), stack(g_ref, unit)], axis=1)
+        out = lax.dot_general(blocks_ref[unit[0]], both, NT, preferred_element_type=jnp.float32)
+        return out[:tokens], out[tokens:]
 
     following = products(units[0])
     for i, unit in enumerate(units):
@@ -90,15 +92,20 @@
         probs = expo * factor
         mine = [u for u in units if u[0] == k]
         cols = pl.ds(mine.index(unit) * UNIT * LEN, UNIT * LEN)
-        probs_ref[k, :, cols] = probs.astype(jnp.bfloat16)
-        dscores_ref[k, :, cols] = (probs * (dprobs - delta)).astype(jnp.bfloat16)
+        weights_ref[k, :tokens, cols] = probs.astype(jnp.bfloat16)
+        weights_ref[k, tokens:, cols] = (probs * (dprobs - delta)).astype(jnp.bfloat16)
         if unit == mine[-1]:
-            q_all = jnp.concatenate([stack(q_ref, u) for u in mine], axis=0)
-            g_all = jnp.concatenate([stack(g_ref, u) for u in mine], axis=0)
-            grad_k = jnp.dot(dscores_ref[k], q_all, preferred_element_type=jnp.float32) * scale
-            grad_v = jnp.dot(probs_ref[k], g_all, preferred_element_type=jnp.float32)
+            rows = [
+                jnp.concatenate([stack(g_ref, u), stack(q_ref, u)], axis=1) for u in mine
+            ]
+            out = jnp.dot(
+                weights_ref[k], jnp.concatenate(rows, axis=0), preferred_element_type=jnp.float32
+            )
+            grad_k = out[tokens:, HD:] * scale
             out_ref[:, k * HD : (k + 1) * HD] = grad_k.astype(out_ref.dtype)
-            out_ref[:, width + k * HD : width + (k + 1) * HD] = grad_v.astype(out_ref.dtype)
+            out_ref[:, width + k * HD : width + (k + 1) * HD] = out[:tokens, :HD].astype(
+                out_ref.dtype
+            )
 
 
 def project(low, kw_ref, vw_ref, owner, features):
@@ -193,8 +200,8 @@
         in_specs=[vmem] * 4,
         out_specs=vmem,
         scratch_shapes=[
-            pltpu.VMEM((kv_local, tokens, depth), jnp.bfloat16),
-            pltpu.VMEM((kv_local, tokens, depth), jnp.bfloat16),
+            pltpu.VMEM((kv_local, 2 * tokens, 2 * HD), jnp.bfloat16),
+            pltpu.VMEM((kv_local, 2 * tokens, depth), jnp.bfloat16),
         ],
         compiler_params=pltpu.CompilerParams(
             vmem_limit_bytes=(8 << 20) + 8 * kv_local * tokens * depth

time: 35.7 us -> 35.7 us (level)
  no operation moved by 1% of the time
where the time goes in v13:
time: 35.7 us; the launch traced here: 35.3 us
  blocking collectives  9.87 us (28%)
  starting transfers between devices  8.86 us (25%)
  Pallas kernels  7.37 us (21%)
  waiting for transfers between devices  7.21 us (20%)
  between operations  1.33 us (4%)
  other arithmetic  0.67 us (2%)
    all_to_all x1, blocking collectives, body(): lax.all_to_all(partial.reshape(resp, own, 2 * width), 'resp', 0, 0, tiled...  9.87 us
    all_to_all x1, starting transfers between devices, body(): lax.all_to_all(both, 'resp', 0, 0, tiled=True)  7.26 us
    all_to_all x1, waiting for transfers between devices, body(): lax.all_to_all(both, 'resp', 0, 0, tiled=True)  5.12 us
    ppermute x3, waiting for transfers between devices, swap(): return lax.ppermute(x, axis, [(i, i ^ bit) for i in range(count)])  2.09 us
    pallas_call x1, Pallas kernels, body(): pl.pallas_call(attention_kernel, out_shape=pltpu.VMEM((tokens, 2 * width)...  1.86 us
    ppermute x3, starting transfers between devices, swap(): return lax.ppermute(x, axis, [(i, i ^ bit) for i in range(count)])  1.59 us
    pallas_call x1, Pallas kernels, body(): pl.pallas_call(load_kernel, out_shape=[pltpu.VMEM(x.shape, x.dtype) for x...  1.56 us
    pallas_call x1, Pallas kernels, body(): pl.pallas_call(join_kernel, out_shape=jax.ShapeDtypeStruct((resp, own, 2...  1.38 us
  transfers between devices with their start and end apart: 4, of which 3 were waited for; matrix products, arithmetic and copies ran while one was open for 0% of the time, Pallas kernels for 10%

profile of v13, /device:TPU:0, one launch (start us, length us, event | category | flops | bytes accessed | tf_op | source)
XLA Modules:
  0.0 35.3 jit_solution(10948825879615114440)
XLA Ops:
  0.6 1.4 %join.1 = bf16[8,16,512]{2,1,0:T(8,128)(2,1)} custom-call(bf16[16,256]{1,0:T(8,128)(2,1)} %k_hbm.1, bf16[16,256]{1,0:T(8,128)(2,1)} %v_hbm.1), custom_call_target="tpu_custom_call" | custom-call | tf_op jit(solution)/shard_map/join/pallas_call | solution.py:164
  2.0 7.3 %all-to-all-start = ((bf16[8,16,512]{2,1,0:T(8,128)(2,1)}), bf16[8,16,512]{2,1,0:T(8,128)(2,1)S(1)}, u32[]{:S(2)}, u32[]{:S(2)}) async-start(bf16[8,16,512]{2,1,0:T(8,128)(2,1)} %join.1), calls=%async_computation | async-start | bytes 262144 | tf_op jit(solution)/shard_map/all_to_all | solution.py:176
  9.9 1.6 %load.1 = (bf16[256,2048]{1,0:T(8,128)(2,1)S(1)}, bf16[256,2048]{1,0:T(8,128)(2,1)S(1)}, f32[1,8,256]{2,1,0:T(8,128)S(1)}) custom-call(s32[1]{0:T(128)S(6)} %copy.10.lengths_ref, bf16[256,2048]{1,0:T(8,128)(2,1)} %refs_0_.1, bf16[256,2048]{1,0:T(8,128)(2,1)} %refs_1_.1), custom_call_target="tpu_custom_call" | custom-call | bytes 4194304 | tf_op jit(solution)/shard_map/load/pallas_call | solution.py:180
  11.5 5.1 %all-to-all-done = bf16[8,16,512]{2,1,0:T(8,128)(2,1)S(1)} async-done(((bf16[8,16,512]{2,1,0:T(8,128)(2,1)}), bf16[8,16,512]{2,1,0:T(8,128)(2,1)S(1)}, u32[]{:S(2)}, u32[]{:S(2)}) %all-to-all-start) | async-done | bytes 131104 | tf_op jit(solution)/shard_map/all_to_all | solution.py:176
  16.6 0.0 copy-start
  16.6 0.0 copy-start.1
  16.6 1.9 %attention.1 = bf16[128,512]{1,0:T(8,128)(2,1)S(1)} custom-call(f32[1,8,256]{2,1,0:T(8,128)S(1)} %get-tuple-element.12.live_ref, bf16[128,512]{1,0:T(8,128)(2,1)S(1)} %bitcast.2, bf16[256,2048]{1,0:T(8,128)(2,1)S(1)} %get-tuple-element.13.q_ref, bf16[256,2048]{1,0:T(8,128)(2,1)S(1)} %get-tuple-element.14.g_ref), custom_call_target="tpu_custom_call" | custom-call | flops 4294967296 | bytes 2293760 | tf_op jit(solution)/shard_map/attention/pallas_call | solution.py:197
  18.5 9.9 %all_to_all.10.parts_ref = bf16[8,16,512]{2,1,0:T(8,128)(2,1)S(1)} all-to-all(bf16[8,16,512]{2,1,0:T(8,128)(2,1)S(1)} %bitcast.3), channel_id=1, replica_groups=mesh['resp'=8,'head'=4] {'resp'}, dimensions={0} | all-to-all | bytes 262144 | tf_op jit(solution)/shard_map/all_to_all | solution.py:217
  28.4 0.0 copy-done
  28.4 0.0 copy-done.1
  28.4 0.6 %projection_other_core.1 = (bf16[16,512]{1,0:T(8,128)(2,1)S(1)}, bf16[16,2048]{1,0:T(8,128)(2,1)S(1)}) custom-call(bf16[8,16,512]{2,1,0:T(8,128)(2,1)S(1)} %all_to_all.10.parts_ref, bf16[8192,256]{1,0:T(8,128)(2,1)S(1)} %copy-done, bf16[8192,256]{1,0:T(8,128)(2,1)S(1)} %copy-done.1), custom_call_target="tpu_custom_call" | custom-call | tf_op jit(solution)/shard_map/projection_other_core/pallas_call | solution.py:222
  29.0 0.0 collective-permute-start
  29.0 0.7 %projection_other_y.1 = f32[16,2048]{1,0:T(8,128)S(1)} custom-call(bf16[16,512]{1,0:T(8,128)(2,1)S(1)} %get-tuple-element.15.low_ref, bf16[8192,256]{1,0:T(8,128)(2,1)S(1)} %copy-done, bf16[8192,256]{1,0:T(8,128)(2,1)S(1)} %copy-done.1), custom_call_target="tpu_custom_call" | custom-call | flops 33554432 | bytes 2097152 | tf_op jit(solution)/shard_map/projection_other_y/pallas_call | solution.py:236
  29.7 0.6 %collective-permute-done = bf16[16,2048]{1,0:T(8,128)(2,1)S(1)} collective-permute-done((bf16[16,2048]{1,0:T(8,128)(2,1)S(1)}, bf16[16,2048]{1,0:T(8,128)(2,1)S(1)}, u32[]{:S(2)}, u32[]{:S(2)}) %collective-permute-start) | collective-permute-done | bytes 65568 | tf_op jit(solution)/shard_map/ppermute | solution.py:151
  30.3 1.6 %collective-permute-start.1 = (bf16[16,2048]{1,0:T(8,128)(2,1)S(1)}, bf16[16,2048]{1,0:T(8,128)(2,1)S(1)}, u32[]{:S(2)}, u32[]{:S(2)}) collective-permute-start(bf16[16,2048]{1,0:T(8,128)(2,1)S(1)} %add_convert_fusion.1.after), channel_id=1, source_target_pairs={{0,2},{1,3},{2,0},{3,1},{4,6},{5,7},{6,4},{7,5},{8,10},{9,11},{10,... | collective-permute-start | bytes 196616 | tf_op jit(solution)/shard_map/ppermute | solution.py:151
  31.9 1.3 %projection_this_y.1 = (bf16[16,2048]{1,0:T(8,128)(2,1)S(1)}, f32[16,2048]{1,0:T(8,128)S(1)}, bf16[16,256]{1,0:T(8,128)(2,1)}, bf16[16,256]{1,0:T(8,128)(2,1)}) custom-call(bf16[16,512]{1,0:T(8,128)(2,1)S(1)} %get-tuple-element.15.low_ref, bf16[8192,256]{1,0:T(8,128)(2,1)S(1)} %copy-done, bf16[8192,256]{1,0:T(8,128)(2,1)S(1)} %copy-done.1, ...), custom_call_target="tpu_custom_call" | custom-call | flops 33554432 | bytes 2097152 | tf_op jit(solution)/shard_map/projection_this_y/pallas_call | solution.py:247
  33.2 0.0 collective-permute-start.2
  33.2 1.5 %collective-permute-done.1 = bf16[16,2048]{1,0:T(8,128)(2,1)S(1)} collective-permute-done((bf16[16,2048]{1,0:T(8,128)(2,1)S(1)}, bf16[16,2048]{1,0:T(8,128)(2,1)S(1)}, u32[]{:S(2)}, u32[]{:S(2)}) %collective-permute-start.1) | collective-permute-done | bytes 65568 | tf_op jit(solution)/shard_map/ppermute | solution.py:151
  34.7 0.0 collective-permute-done.2
  34.7 0.6 %add_convert_fusion = bf16[16,2048]{1,0:T(8,128)(2,1)} fusion(f32[16,2048]{1,0:T(8,128)S(1)} %convert_add_fusion, bf16[16,2048]{1,0:T(8,128)(2,1)S(1)} %collective-permute-done.2), kind=kLoop, calls=%fused_computation | loop fusion | flops 98304 | bytes 262144 | tf_op jit(solution)/shard_map/convert_element_type | solution.py:263
  (2 shorter events, 0.0 us)
Async XLA Ops:
  2.0 14.6 %all-to-all-start = ((bf16[8,16,512]{2,1,0:T(8,128)(2,1)}), bf16[8,16,512]{2,1,0:T(8,128)(2,1)S(1)}, u32[]{:S(2)}, u32[]{:S(2)}) async-start(bf16[8,16,512]{2,1,0:T(8,128)(2,1)} %join.1), calls=%async_computation | async-start | bytes 262144 | tf_op jit(solution)/shard_map/all_to_all | solution.py:176
  16.6 11.7 %copy-start = (bf16[8192,256]{1,0:T(8,128)(2,1)S(1)}, bf16[8192,256]{1,0:T(8,128)(2,1)}, u32[]{:S(2)}) copy-start(bf16[8192,256]{1,0:T(8,128)(2,1)} %kw_ref.5) | copy-start | bytes 12582916
  16.6 11.7 %copy-start.1 = (bf16[8192,256]{1,0:T(8,128)(2,1)S(1)}, bf16[8192,256]{1,0:T(8,128)(2,1)}, u32[]{:S(2)}) copy-start(bf16[8192,256]{1,0:T(8,128)(2,1)} %vw_ref.5) | copy-start | bytes 12582916
  29.0 1.3 %collective-permute-start = (bf16[16,2048]{1,0:T(8,128)(2,1)S(1)}, bf16[16,2048]{1,0:T(8,128)(2,1)S(1)}, u32[]{:S(2)}, u32[]{:S(2)}) collective-permute-start(bf16[16,2048]{1,0:T(8,128)(2,1)S(1)} %get-tuple-element.16), channel_id=1, source_target_pairs={{0,1},{1,0},{2,3},{3,2},{4,5},{5,4},{6,7},{7,6},{8,9},{9,8},{10,11... | collective-permute-start | bytes 196616 | tf_op jit(solution)/shard_map/ppermute | solution.py:151
  30.3 4.3 %collective-permute-start.1 = (bf16[16,2048]{1,0:T(8,128)(2,1)S(1)}, bf16[16,2048]{1,0:T(8,128)(2,1)S(1)}, u32[]{:S(2)}, u32[]{:S(2)}) collective-permute-start(bf16[16,2048]{1,0:T(8,128)(2,1)S(1)} %add_convert_fusion.1.after), channel_id=1, source_target_pairs={{0,2},{1,3},{2,0},{3,1},{4,6},{5,7},{6,4},{7,5},{8,10},{9,11},{10,... | collective-permute-start | bytes 196616 | tf_op jit(solution)/shard_map/ppermute | solution.py:151
  33.2 1.5 %collective-permute-start.2 = (bf16[16,2048]{1,0:T(8,128)(2,1)S(1)}, bf16[16,2048]{1,0:T(8,128)(2,1)S(1)}, u32[]{:S(2)}, u32[]{:S(2)}) collective-permute-start(bf16[16,2048]{1,0:T(8,128)(2,1)S(1)} %get-tuple-element.20), channel_id=1, source_target_pairs={{0,1},{1,0},{2,3},{3,2},{4,5},{5,4},{6,7},{7,6},{8,9},{9,8},{10,11... | collective-permute-start | bytes 196616 | tf_op jit(solution)/shard_map/ppermute | solution.py:151

commit v14 on v13

--- a/solution.py
+++ b/solution.py
@@ -10,7 +10,7 @@
 HD = 128
 LEN = 256
 NT = (((1,), (1,)), ((), ()))
-UNIT = 2
+CHUNK = 16
 LOG2E = 1.4426950408889634
 
 
@@ -44,7 +44,7 @@
         copy.wait()
 
 
-def attention_kernel(live_ref, kv_ref, q_ref, g_ref, out_ref, blocks_ref, weights_ref):
+def attention_kernel(live_ref, kv_ref, q_ref, g_ref, out_ref, blocks_ref, products_ref, weights_ref):
     scale = HD ** (-0.5)
     tokens = kv_ref.shape[0]
     width = kv_ref.shape[1] // 2
@@ -52,60 +52,73 @@
     parts = q_ref.shape[0] // LEN
     group = q_ref.shape[1] // HD // kv_local
     units = [
-        (k, part, h)
-        for k in range(kv_local)
-        for part in range(parts)
-        for h in range(0, group, UNIT)
+        (k, part, h) for k in range(kv_local) for part in range(parts) for h in range(group)
     ]
-
-    def stack(ref, unit):
-        k, part, h = unit
-        heads = [
-            ref[part * LEN : (part + 1) * LEN, at * HD : (at + 1) * HD]
-            for at in range(k * group + h, k * group + h + UNIT)
-        ]
-        return jnp.concatenate(heads, axis=0)
-
     blocks_ref[...] = jnp.zeros_like(blocks_ref)
     for k in range(kv_local):
         blocks_ref[k, :tokens, :HD] = kv_ref[:, k * HD : (k + 1) * HD]
         blocks_ref[k, tokens:, HD:] = kv_ref[:, width + k * HD : width + (k + 1) * HD]
 
-    def products(unit):
-        both = jnp.concatenate([stack(q_ref, unit), stack(g_ref, unit)], axis=1)
-        out = lax.dot_general(blocks_ref[unit[0]], both, NT, preferred_element_type=jnp.float32)
-        return out[:tokens], out[tokens:]
-
-    following = products(units[0])
-    for i, unit in enumerate(units):
+    def beside(left_ref, right_ref, unit):
         k, part, h = unit
-        scores, dprobs = following
-        if i + 1 < len(units):
-            following = products(units[i + 1])
-        top = jnp.max(scores, axis=0, keepdims=True)
-        expo = jnp.exp2((scores - top) * (scale * LOG2E))
-        total = jnp.sum(expo, axis=0, keepdims=True)
-        weighted = jnp.sum(expo * dprobs, axis=0, keepdims=True)
-        inverse = 1.0 / total
-        delta = weighted * inverse
-        factor = inverse * jnp.concatenate([live_ref[part, :1]] * UNIT, axis=1)
-        probs = expo * factor
-        mine = [u for u in units if u[0] == k]
-        cols = pl.ds(mine.index(unit) * UNIT * LEN, UNIT * LEN)
-        weights_ref[k, :tokens, cols] = probs.astype(jnp.bfloat16)
-        weights_ref[k, tokens:, cols] = (probs * (dprobs - delta)).astype(jnp.bfloat16)
-        if unit == mine[-1]:
-            rows = [
-                jnp.concatenate([stack(g_ref, u), stack(q_ref, u)], axis=1) for u in mine
-            ]
+        at = (k * group + h) * HD
+        rows = slice(part * LEN, (part + 1) * LEN)
+        return jnp.concatenate(
+            [left_ref[rows, at : at + HD], right_ref[rows, at : at + HD]], axis=1
+        )
+
+    def spread(row):
+        return jnp.broadcast_to(row, (CHUNK, LEN))
+
+    tops, factors, deltas = {}, {}, {}
+    for step in range(len(units) + 3):
+        largest, summing, last = step - 1, step - 2, step - 3
+        if step < len(units):
+            products_ref[step % 4] = lax.dot_general(
+                blocks_ref[units[step][0]],
+                beside(q_ref, g_ref, units[step]),
+                NT,
+                preferred_element_type=jnp.float32,
+            )
+        top = total = weighted = None
+        for at in range(0, tokens, CHUNK):
+            score_rows = slice(at, at + CHUNK)
+            dprob_rows = slice(tokens + at, tokens + at + CHUNK)
+            if 0 <= largest < len(units):
+                scores = products_ref[largest % 4, score_rows]
+                top = scores if top is None else jnp.maximum(top, scores)
+            if 0 <= summing < len(units):
+                scores = products_ref[summing % 4, score_rows]
+                dprobs = products_ref[summing % 4, dprob_rows]
+                expo = jnp.exp2((scores - tops[summing]) * (scale * LOG2E))
+                total = expo if total is None else total + expo
+                weighted = expo * dprobs if weighted is None else weighted + expo * dprobs
+            if 0 <= last < len(units):
+                k = units[last][0]
+                cols = slice(last * LEN % weights_ref.shape[2], last * LEN % weights_ref.shape[2] + LEN)
+                scores = products_ref[last % 4, score_rows]
+                dprobs = products_ref[last % 4, dprob_rows]
+                probs = jnp.exp2((scores - tops[last]) * (scale * LOG2E)) * factors[last]
+                weights_ref[k, score_rows, cols] = probs.astype(jnp.bfloat16)
+                weights_ref[k, dprob_rows, cols] = (probs * (dprobs - deltas[last])).astype(
+                    jnp.bfloat16
+                )
+        if top is not None:
+            tops[largest] = spread(jnp.max(top, axis=0, keepdims=True))
+        if total is not None:
+            inverse = 1.0 / jnp.sum(total, axis=0, keepdims=True)
+            deltas[summing] = spread(jnp.sum(weighted, axis=0, keepdims=True) * inverse)
+            factors[summing] = spread(inverse * live_ref[units[summing][1], :1])
+        if last >= 0 and (last + 1 == len(units) or units[last + 1][0] != units[last][0]):
+            k = units[last][0]
+            rows = [beside(g_ref, q_ref, unit) for unit in units if unit[0] == k]
             out = jnp.dot(
                 weights_ref[k], jnp.concatenate(rows, axis=0), preferred_element_type=jnp.float32
             )
             grad_k = out[tokens:, HD:] * scale
+            grad_v = out[:tokens, :HD]
             out_ref[:, k * HD : (k + 1) * HD] = grad_k.astype(out_ref.dtype)
-            out_ref[:, width + k * HD : width + (k + 1) * HD] = out[:tokens, :HD].astype(
-                out_ref.dtype
-            )
+            out_ref[:, width + k * HD : width + (k + 1) * HD] = grad_v.astype(out_ref.dtype)
 
 
 def project(low, kw_ref, vw_ref, owner, features):
@@ -201,6 +214,7 @@
         out_specs=vmem,
         scratch_shapes=[
             pltpu.VMEM((kv_local, 2 * tokens, 2 * HD), jnp.bfloat16),
+            pltpu.VMEM((4, 2 * tokens, LEN), jnp.float32),
             pltpu.VMEM((kv_local, 2 * tokens, depth), jnp.bfloat16),
         ],
         compiler_params=pltpu.CompilerParams(

time: 35.7 us -> 35.9 us (level)
  no operation moved by 1% of the time
where the time goes in v14:
time: 35.9 us; the launch traced here: 35.5 us
  blocking collectives  9.87 us (27%)
  starting transfers between devices  8.86 us (25%)
  Pallas kernels  7.54 us (21%)
  waiting for transfers between devices  7.21 us (20%)
  between operations  1.33 us (4%)
  other arithmetic  0.67 us (2%)
    all_to_all x1, blocking collectives, body(): lax.all_to_all(partial.reshape(resp, own, 2 * width), 'resp', 0, 0, tiled...  9.87 us
    all_to_all x1, starting transfers between devices, body(): lax.all_to_all(both, 'resp', 0, 0, tiled=True)  7.26 us
    all_to_all x1, waiting for transfers between devices, body(): lax.all_to_all(both, 'resp', 0, 0, tiled=True)  5.12 us
    ppermute x3, waiting for transfers between devices, swap(): return lax.ppermute(x, axis, [(i, i ^ bit) for i in range(count)])  2.09 us
    pallas_call x1, Pallas kernels, body(): pl.pallas_call(attention_kernel, out_shape=pltpu.VMEM((tokens, 2 * width)...  2.03 us
    ppermute x3, starting transfers between devices, swap(): return lax.ppermute(x, axis, [(i, i ^ bit) for i in range(count)])  1.6 us
    pallas_call x1, Pallas kernels, body(): pl.pallas_call(load_kernel, out_shape=[pltpu.VMEM(x.shape, x.dtype) for x...  1.56 us
    pallas_call x1, Pallas kernels, body(): pl.pallas_call(join_kernel, out_shape=jax.ShapeDtypeStruct((resp, own, 2...  1.38 us
  transfers between devices with their start and end apart: 4, of which 3 were waited for; matrix products, arithmetic and copies ran while one was open for 0% of the time, Pallas kernels for 10%

profile of v14, /device:TPU:0, one launch (start us, length us, event | category | flops | bytes accessed | tf_op | source)
XLA Modules:
  0.0 35.5 jit_solution(5573142674280017928)
XLA Ops:
  0.6 1.4 %join.1 = bf16[8,16,512]{2,1,0:T(8,128)(2,1)} custom-call(bf16[16,256]{1,0:T(8,128)(2,1)} %k_hbm.1, bf16[16,256]{1,0:T(8,128)(2,1)} %v_hbm.1), custom_call_target="tpu_custom_call" | custom-call | tf_op jit(solution)/shard_map/join/pallas_call | solution.py:177
  2.0 7.3 %all-to-all-start = ((bf16[8,16,512]{2,1,0:T(8,128)(2,1)}), bf16[8,16,512]{2,1,0:T(8,128)(2,1)S(1)}, u32[]{:S(2)}, u32[]{:S(2)}) async-start(bf16[8,16,512]{2,1,0:T(8,128)(2,1)} %join.1), calls=%async_computation | async-start | bytes 262144 | tf_op jit(solution)/shard_map/all_to_all | solution.py:189
  9.9 1.6 %load.1 = (bf16[256,2048]{1,0:T(8,128)(2,1)S(1)}, bf16[256,2048]{1,0:T(8,128)(2,1)S(1)}, f32[1,8,256]{2,1,0:T(8,128)S(1)}) custom-call(s32[1]{0:T(128)S(6)} %copy.10.lengths_ref, bf16[256,2048]{1,0:T(8,128)(2,1)} %refs_0_.1, bf16[256,2048]{1,0:T(8,128)(2,1)} %refs_1_.1), custom_call_target="tpu_custom_call" | custom-call | bytes 4194304 | tf_op jit(solution)/shard_map/load/pallas_call | solution.py:193
  11.5 5.1 %all-to-all-done = bf16[8,16,512]{2,1,0:T(8,128)(2,1)S(1)} async-done(((bf16[8,16,512]{2,1,0:T(8,128)(2,1)}), bf16[8,16,512]{2,1,0:T(8,128)(2,1)S(1)}, u32[]{:S(2)}, u32[]{:S(2)}) %all-to-all-start) | async-done | bytes 131104 | tf_op jit(solution)/shard_map/all_to_all | solution.py:189
  16.6 0.0 copy-start
  16.6 0.0 copy-start.1
  16.6 2.0 %attention.1 = bf16[128,512]{1,0:T(8,128)(2,1)S(1)} custom-call(f32[1,8,256]{2,1,0:T(8,128)S(1)} %get-tuple-element.12.live_ref, bf16[128,512]{1,0:T(8,128)(2,1)S(1)} %bitcast.2, bf16[256,2048]{1,0:T(8,128)(2,1)S(1)} %get-tuple-element.13.q_ref, bf16[256,2048]{1,0:T(8,128)(2,1)S(1)} %get-tuple-element.14.g_ref), custom_call_target="tpu_custom_call" | custom-call | flops 4294967296 | bytes 2293760 | tf_op jit(solution)/shard_map/attention/pallas_call | solution.py:210
  18.7 9.9 %all_to_all.10.parts_ref = bf16[8,16,512]{2,1,0:T(8,128)(2,1)S(1)} all-to-all(bf16[8,16,512]{2,1,0:T(8,128)(2,1)S(1)} %bitcast.3), channel_id=1, replica_groups=mesh['resp'=8,'head'=4] {'resp'}, dimensions={0} | all-to-all | bytes 262144 | tf_op jit(solution)/shard_map/all_to_all | solution.py:231
  28.5 0.0 copy-done
  28.5 0.0 copy-done.1
  28.5 0.6 %projection_other_core.1 = (bf16[16,512]{1,0:T(8,128)(2,1)S(1)}, bf16[16,2048]{1,0:T(8,128)(2,1)S(1)}) custom-call(bf16[8,16,512]{2,1,0:T(8,128)(2,1)S(1)} %all_to_all.10.parts_ref, bf16[8192,256]{1,0:T(8,128)(2,1)S(1)} %copy-done, bf16[8192,256]{1,0:T(8,128)(2,1)S(1)} %copy-done.1), custom_call_target="tpu_custom_call" | custom-call | tf_op jit(solution)/shard_map/projection_other_core/pallas_call | solution.py:236
  29.2 0.0 collective-permute-start
  29.2 0.7 %projection_other_y.1 = f32[16,2048]{1,0:T(8,128)S(1)} custom-call(bf16[16,512]{1,0:T(8,128)(2,1)S(1)} %get-tuple-element.15.low_ref, bf16[8192,256]{1,0:T(8,128)(2,1)S(1)} %copy-done, bf16[8192,256]{1,0:T(8,128)(2,1)S(1)} %copy-done.1), custom_call_target="tpu_custom_call" | custom-call | flops 33554432 | bytes 2097152 | tf_op jit(solution)/shard_map/projection_other_y/pallas_call | solution.py:250
  29.9 0.6 %collective-permute-done = bf16[16,2048]{1,0:T(8,128)(2,1)S(1)} collective-permute-done((bf16[16,2048]{1,0:T(8,128)(2,1)S(1)}, bf16[16,2048]{1,0:T(8,128)(2,1)S(1)}, u32[]{:S(2)}, u32[]{:S(2)}) %collective-permute-start) | collective-permute-done | bytes 65568 | tf_op jit(solution)/shard_map/ppermute | solution.py:164
  30.5 1.6 %collective-permute-start.1 = (bf16[16,2048]{1,0:T(8,128)(2,1)S(1)}, bf16[16,2048]{1,0:T(8,128)(2,1)S(1)}, u32[]{:S(2)}, u32[]{:S(2)}) collective-permute-start(bf16[16,2048]{1,0:T(8,128)(2,1)S(1)} %add_convert_fusion.1.after), channel_id=1, source_target_pairs={{0,2},{1,3},{2,0},{3,1},{4,6},{5,7},{6,4},{7,5},{8,10},{9,11},{10,... | collective-permute-start | bytes 196616 | tf_op jit(solution)/shard_map/ppermute | solution.py:164
  32.1 1.3 %projection_this_y.1 = (bf16[16,2048]{1,0:T(8,128)(2,1)S(1)}, f32[16,2048]{1,0:T(8,128)S(1)}, bf16[16,256]{1,0:T(8,128)(2,1)}, bf16[16,256]{1,0:T(8,128)(2,1)}) custom-call(bf16[16,512]{1,0:T(8,128)(2,1)S(1)} %get-tuple-element.15.low_ref, bf16[8192,256]{1,0:T(8,128)(2,1)S(1)} %copy-done, bf16[8192,256]{1,0:T(8,128)(2,1)S(1)} %copy-done.1, ...), custom_call_target="tpu_custom_call" | custom-call | flops 33554432 | bytes 2097152 | tf_op jit(solution)/shard_map/projection_this_y/pallas_call | solution.py:261
  33.3 0.0 collective-permute-start.2
  33.3 1.5 %collective-permute-done.1 = bf16[16,2048]{1,0:T(8,128)(2,1)S(1)} collective-permute-done((bf16[16,2048]{1,0:T(8,128)(2,1)S(1)}, bf16[16,2048]{1,0:T(8,128)(2,1)S(1)}, u32[]{:S(2)}, u32[]{:S(2)}) %collective-permute-start.1) | collective-permute-done | bytes 65568 | tf_op jit(solution)/shard_map/ppermute | solution.py:164
  34.8 0.0 collective-permute-done.2
  34.8 0.6 %add_convert_fusion = bf16[16,2048]{1,0:T(8,128)(2,1)} fusion(f32[16,2048]{1,0:T(8,128)S(1)} %convert_add_fusion, bf16[16,2048]{1,0:T(8,128)(2,1)S(1)} %collective-permute-done.2), kind=kLoop, calls=%fused_computation | loop fusion | flops 98304 | bytes 262144 | tf_op jit(solution)/shard_map/convert_element_type | solution.py:277
  (2 shorter events, 0.0 us)
Async XLA Ops:
  2.0 14.6 %all-to-all-start = ((bf16[8,16,512]{2,1,0:T(8,128)(2,1)}), bf16[8,16,512]{2,1,0:T(8,128)(2,1)S(1)}, u32[]{:S(2)}, u32[]{:S(2)}) async-start(bf16[8,16,512]{2,1,0:T(8,128)(2,1)} %join.1), calls=%async_computation | async-start | bytes 262144 | tf_op jit(solution)/shard_map/all_to_all | solution.py:189
  16.6 11.9 %copy-start = (bf16[8192,256]{1,0:T(8,128)(2,1)S(1)}, bf16[8192,256]{1,0:T(8,128)(2,1)}, u32[]{:S(2)}) copy-start(bf16[8192,256]{1,0:T(8,128)(2,1)} %kw_ref.5) | copy-start | bytes 12582916
  16.6 11.9 %copy-start.1 = (bf16[8192,256]{1,0:T(8,128)(2,1)S(1)}, bf16[8192,256]{1,0:T(8,128)(2,1)}, u32[]{:S(2)}) copy-start(bf16[8192,256]{1,0:T(8,128)(2,1)} %vw_ref.5) | copy-start | bytes 12582916
  29.2 1.3 %collective-permute-start = (bf16[16,2048]{1,0:T(8,128)(2,1)S(1)}, bf16[16,2048]{1,0:T(8,128)(2,1)S(1)}, u32[]{:S(2)}, u32[]{:S(2)}) collective-permute-start(bf16[16,2048]{1,0:T(8,128)(2,1)S(1)} %get-tuple-element.16), channel_id=1, source_target_pairs={{0,1},{1,0},{2,3},{3,2},{4,5},{5,4},{6,7},{7,6},{8,9},{9,8},{10,11... | collective-permute-start | bytes 196616 | tf_op jit(solution)/shard_map/ppermute | solution.py:164
  30.5 4.3 %collective-permute-start.1 = (bf16[16,2048]{1,0:T(8,128)(2,1)S(1)}, bf16[16,2048]{1,0:T(8,128)(2,1)S(1)}, u32[]{:S(2)}, u32[]{:S(2)}) collective-permute-start(bf16[16,2048]{1,0:T(8,128)(2,1)S(1)} %add_convert_fusion.1.after), channel_id=1, source_target_pairs={{0,2},{1,3},{2,0},{3,1},{4,6},{5,7},{6,4},{7,5},{8,10},{9,11},{10,... | collective-permute-start | bytes 196616 | tf_op jit(solution)/shard_map/ppermute | solution.py:164
  33.3 1.5 %collective-permute-start.2 = (bf16[16,2048]{1,0:T(8,128)(2,1)S(1)}, bf16[16,2048]{1,0:T(8,128)(2,1)S(1)}, u32[]{:S(2)}, u32[]{:S(2)}) collective-permute-start(bf16[16,2048]{1,0:T(8,128)(2,1)S(1)} %get-tuple-element.20), channel_id=1, source_target_pairs={{0,1},{1,0},{2,3},{3,2},{4,5},{5,4},{6,7},{7,6},{8,9},{9,8},{10,11... | collective-permute-start | bytes 196616 | tf_op jit(solution)/shard_map/ppermute | solution.py:164

commit v15 on v13

--- a/solution.py
+++ b/solution.py
@@ -14,34 +14,18 @@
 LOG2E = 1.4426950408889634
 
 
-def join_kernel(k_hbm, v_hbm, out_ref, both_ref, sems):
-    width = k_hbm.shape[1]
-    copies = [
-        pltpu.make_async_copy(k_hbm, both_ref.at[:, pl.ds(0, width)], sems.at[0]),
-        pltpu.make_async_copy(v_hbm, both_ref.at[:, pl.ds(width, width)], sems.at[1]),
-    ]
-    for copy in copies:
-        copy.start()
-    for copy in copies:
-        copy.wait()
-    both = both_ref[...]
-    for i in range(out_ref.shape[0]):
-        out_ref[i] = both
-
-
-def load_kernel(lengths_ref, *refs):
-    count = (len(refs) - 2) // 2
-    live_ref, sems = refs[2 * count :]
-    copies = [
-        pltpu.make_async_copy(refs[i], refs[count + i], sems.at[i]) for i in range(count)
-    ]
-    for copy in copies:
-        copy.start()
+def mask_kernel(lengths_ref, live_ref):
     position = lax.broadcasted_iota(jnp.int32, live_ref.shape[1:], 1)
     for part in range(live_ref.shape[0]):
         live_ref[part] = jnp.where(position < lengths_ref[part], 1.0, 0.0)
-    for copy in copies:
-        copy.wait()
+
+
+def join_kernel(live_ref, k_ref, v_ref, out_ref):
+    del live_ref
+    width = k_ref.shape[1]
+    for i in range(out_ref.shape[0]):
+        out_ref[i, :, :width] = k_ref[...]
+        out_ref[i, :, width:] = v_ref[...]
 
 
 def attention_kernel(live_ref, kv_ref, q_ref, g_ref, out_ref, blocks_ref, weights_ref):
@@ -155,41 +139,26 @@
     own, width = prefix_keys.shape
     features = k_weight.shape[0] // head
     vmem = pl.BlockSpec(memory_space=pltpu.VMEM)
-    hbm = pl.BlockSpec(memory_space=pltpu.HBM)
     params = pltpu.CompilerParams(vmem_limit_bytes=12 << 20)
 
-    def in_hbm(*xs):
-        return [pltpu.with_memory_space_constraint(x, pltpu.HBM) for x in xs]
-
+    live = pl.pallas_call(
+        mask_kernel,
+        out_shape=pltpu.VMEM((lengths.shape[0], 8, LEN), jnp.float32),
+        in_specs=[pl.BlockSpec(memory_space=pltpu.SMEM)],
+        out_specs=vmem,
+        compiler_params=params,
+        cost_estimate=pl.CostEstimate(flops=1600000000, transcendentals=0, bytes_accessed=0),
+        name="mask",
+    )(lengths)
     both = pl.pallas_call(
         join_kernel,
-        out_shape=jax.ShapeDtypeStruct((resp, own, 2 * width), jnp.bfloat16),
-        in_specs=[hbm] * 2,
-        out_specs=vmem,
-        scratch_shapes=[
-            pltpu.VMEM((own, 2 * width), jnp.bfloat16),
-            pltpu.SemaphoreType.DMA((2,)),
-        ],
+        out_shape=pltpu.VMEM((resp, own, 2 * width), jnp.bfloat16),
+        in_specs=[pl.BlockSpec(memory_space=pl.ANY)] + [vmem] * 2,
+        out_specs=vmem,
         compiler_params=params,
         name="join",
-    )(*in_hbm(prefix_keys, prefix_values))
+    )(live, prefix_keys, prefix_values)
     both = lax.all_to_all(both, "resp", 0, 0, tiled=True).reshape(resp * own, 2 * width)
-
-    large = (queries, d_out)
-    responses = lengths.shape[0]
-    queries, d_out, live = pl.pallas_call(
-        load_kernel,
-        out_shape=[pltpu.VMEM(x.shape, x.dtype) for x in large]
-        + [pltpu.VMEM((responses, 8, LEN), jnp.float32)],
-        in_specs=[pl.BlockSpec(memory_space=pltpu.SMEM)] + [hbm] * len(large),
-        out_specs=[vmem] * (len(large) + 1),
-        scratch_shapes=[pltpu.SemaphoreType.DMA((len(large),))],
-        compiler_params=params,
-        cost_estimate=pl.CostEstimate(
-            flops=0, transcendentals=0, bytes_accessed=sum(4 * x.size for x in large)
-        ),
-        name="load",
-    )(lengths, *in_hbm(*large))
 
     tokens = resp * own
     kv_local = width // HD

time: 35.7 us -> 34.9 us (0.978)
  blocking collectives: 9.87 us -> 24.3 us
  starting transfers between devices: 8.86 us -> 1.59 us
  waiting for transfers between devices: 7.21 us -> 2.09 us
  Pallas kernels: 7.37 us -> 4.52 us
    all_to_all x0 -> x1, blocking collectives: none -> 14.4 us  [body(): lax.all_to_all(both, 'resp', 0, 0, tiled=True)]
    all_to_all x1 -> x0, starting transfers between devices: 7.26 us -> none  [body(): lax.all_to_all(both, 'resp', 0, 0, tiled=True)]
    all_to_all x1 -> x0, waiting for transfers between devices: 5.12 us -> none  [body(): lax.all_to_all(both, 'resp', 0, 0, tiled=True)]
    pallas_call x2, Pallas kernels: 2.95 us -> 0.02 us  [the longest x1 0.01 us: body(): pl.pallas_call(join_kernel, out_shape=pltpu.VMEM((resp, own, 2 * width),...]
  transfers between devices with their start and end apart: 4 -> 3, of which waited for: 3 -> 2; matrix products, arithmetic and copies ran while one was open for 0% -> 0% of each run, Pallas kernels for 10% -> 6%
where the time goes in v15:
time: 34.9 us; the launch traced here: 34.7 us
  blocking collectives  24.3 us (70%)
  Pallas kernels  4.52 us (13%)
  waiting for transfers between devices  2.09 us (6%)
  starting transfers between devices  1.59 us (5%)
  between operations  1.53 us (4%)
  other arithmetic  0.67 us (2%)
    all_to_all x1, blocking collectives, body(): lax.all_to_all(both, 'resp', 0, 0, tiled=True)  14.4 us
    all_to_all x1, blocking collectives, body(): lax.all_to_all(partial.reshape(resp, own, 2 * width), 'resp', 0, 0, tiled...  9.87 us
    ppermute x3, waiting for transfers between devices, swap(): return lax.ppermute(x, axis, [(i, i ^ bit) for i in range(count)])  2.09 us
    pallas_call x1, Pallas kernels, body(): pl.pallas_call(attention_kernel, out_shape=pltpu.VMEM((tokens, 2 * width)...  1.94 us
    ppermute x3, starting transfers between devices, swap(): return lax.ppermute(x, axis, [(i, i ^ bit) for i in range(count)])  1.59 us
    pallas_call x1, Pallas kernels, body(): pl.pallas_call(last_projection_kernel, out_shape=[pltpu.VMEM(block, jnp.b...  1.26 us
  transfers between devices with their start and end apart: 3, of which 2 were waited for; matrix products, arithmetic and copies ran while one was open for 0% of the time, Pallas kernels for 6%

profile of v15, /device:TPU:0, one launch (start us, length us, event | category | flops | bytes accessed | tf_op | source)
XLA Modules:
  0.0 34.7 jit_solution(8416719656154213858)
XLA Ops:
  0.6 0.0 copy-start.3
  0.6 0.0 copy-start.2
  0.7 0.0 copy-start.5
  0.7 0.0 copy-start.4
  1.5 0.0 copy-done.3
  1.5 0.0 copy-done.2
  1.5 14.4 %all_to_all.10 = bf16[8,16,512]{2,1,0:T(8,128)(2,1)S(1)} all-to-all(bf16[8,16,512]{2,1,0:T(8,128)(2,1)S(1)} %join.1), channel_id=1, replica_groups=mesh['resp'=8,'head'=4] {'resp'}, dimensions={0} | all-to-all | bytes 262144 | tf_op jit(solution)/shard_map/all_to_all | solution.py:161
  15.9 0.0 copy-done.5
  15.9 0.0 copy-done.4
  15.9 0.0 copy-start
  15.9 0.0 copy-start.1
  15.9 1.9 %attention.1 = bf16[128,512]{1,0:T(8,128)(2,1)S(1)} custom-call(f32[1,8,256]{2,1,0:T(8,128)S(1)} %mask.1.live_ref, bf16[128,512]{1,0:T(8,128)(2,1)S(1)} %bitcast.2, bf16[256,2048]{1,0:T(8,128)(2,1)S(1)} %copy-done.4, bf16[256,2048]{1,0:T(8,128)(2,1)S(1)} %copy-done.5), custom_call_target="tpu_custom_call" | custom-call | flops 4294967296 | bytes 2293760 | tf_op jit(solution)/shard_map/attention/pallas_call | solution.py:166
  17.9 9.9 %all_to_all.11.parts_ref = bf16[8,16,512]{2,1,0:T(8,128)(2,1)S(1)} all-to-all(bf16[8,16,512]{2,1,0:T(8,128)(2,1)S(1)} %bitcast.3), channel_id=1, replica_groups=mesh['resp'=8,'head'=4] {'resp'}, dimensions={0} | all-to-all | bytes 262144 | tf_op jit(solution)/shard_map/all_to_all | solution.py:186
  27.7 0.0 copy-done
  27.7 0.0 copy-done.1
  27.7 0.6 %projection_other_core.1 = (bf16[16,512]{1,0:T(8,128)(2,1)S(1)}, bf16[16,2048]{1,0:T(8,128)(2,1)S(1)}) custom-call(bf16[8,16,512]{2,1,0:T(8,128)(2,1)S(1)} %all_to_all.11.parts_ref, bf16[8192,256]{1,0:T(8,128)(2,1)S(1)} %copy-done, bf16[8192,256]{1,0:T(8,128)(2,1)S(1)} %copy-done.1), custom_call_target="tpu_custom_call" | custom-call | tf_op jit(solution)/shard_map/projection_other_core/pallas_call | solution.py:191
  28.4 0.0 collective-permute-start
  28.4 0.7 %projection_other_y.1 = f32[16,2048]{1,0:T(8,128)S(1)} custom-call(bf16[16,512]{1,0:T(8,128)(2,1)S(1)} %get-tuple-element.9.low_ref, bf16[8192,256]{1,0:T(8,128)(2,1)S(1)} %copy-done, bf16[8192,256]{1,0:T(8,128)(2,1)S(1)} %copy-done.1), custom_call_target="tpu_custom_call" | custom-call | flops 33554432 | bytes 2097152 | tf_op jit(solution)/shard_map/projection_other_y/pallas_call | solution.py:205
  29.1 0.6 %collective-permute-done = bf16[16,2048]{1,0:T(8,128)(2,1)S(1)} collective-permute-done((bf16[16,2048]{1,0:T(8,128)(2,1)S(1)}, bf16[16,2048]{1,0:T(8,128)(2,1)S(1)}, u32[]{:S(2)}, u32[]{:S(2)}) %collective-permute-start) | collective-permute-done | bytes 65568 | tf_op jit(solution)/shard_map/ppermute | solution.py:135
  29.7 1.6 %collective-permute-start.1 = (bf16[16,2048]{1,0:T(8,128)(2,1)S(1)}, bf16[16,2048]{1,0:T(8,128)(2,1)S(1)}, u32[]{:S(2)}, u32[]{:S(2)}) collective-permute-start(bf16[16,2048]{1,0:T(8,128)(2,1)S(1)} %add_convert_fusion.1.after), channel_id=1, source_target_pairs={{0,2},{1,3},{2,0},{3,1},{4,6},{5,7},{6,4},{7,5},{8,10},{9,11},{10,... | collective-permute-start | bytes 196616 | tf_op jit(solution)/shard_map/ppermute | solution.py:135
  31.3 1.3 %projection_this_y.1 = (bf16[16,2048]{1,0:T(8,128)(2,1)S(1)}, f32[16,2048]{1,0:T(8,128)S(1)}, bf16[16,256]{1,0:T(8,128)(2,1)}, bf16[16,256]{1,0:T(8,128)(2,1)}) custom-call(bf16[16,512]{1,0:T(8,128)(2,1)S(1)} %get-tuple-element.9.low_ref, bf16[8192,256]{1,0:T(8,128)(2,1)S(1)} %copy-done, bf16[8192,256]{1,0:T(8,128)(2,1)S(1)} %copy-done.1, ...), custom_call_target="tpu_custom_call" | custom-call | flops 33554432 | bytes 2097152 | tf_op jit(solution)/shard_map/projection_this_y/pallas_call | solution.py:216
  32.5 0.0 collective-permute-start.2
  32.5 1.5 %collective-permute-done.1 = bf16[16,2048]{1,0:T(8,128)(2,1)S(1)} collective-permute-done((bf16[16,2048]{1,0:T(8,128)(2,1)S(1)}, bf16[16,2048]{1,0:T(8,128)(2,1)S(1)}, u32[]{:S(2)}, u32[]{:S(2)}) %collective-permute-start.1) | collective-permute-done | bytes 65568 | tf_op jit(solution)/shard_map/ppermute | solution.py:135
  34.0 0.0 collective-permute-done.2
  34.0 0.6 %add_convert_fusion = bf16[16,2048]{1,0:T(8,128)(2,1)} fusion(f32[16,2048]{1,0:T(8,128)S(1)} %convert_add_fusion, bf16[16,2048]{1,0:T(8,128)(2,1)S(1)} %collective-permute-done.2), kind=kLoop, calls=%fused_computation | loop fusion | flops 98304 | bytes 262144 | tf_op jit(solution)/shard_map/convert_element_type | solution.py:232
  (4 shorter events, 0.0 us)
Async XLA Ops:
  0.6 0.8 %copy-start.3 = (bf16[16,256]{1,0:T(8,128)(2,1)S(1)}, bf16[16,256]{1,0:T(8,128)(2,1)}, u32[]{:S(2)}) copy-start(bf16[16,256]{1,0:T(8,128)(2,1)} %v_ref.1) | copy-start | bytes 24580
  0.6 0.8 %copy-start.2 = (bf16[16,256]{1,0:T(8,128)(2,1)S(1)}, bf16[16,256]{1,0:T(8,128)(2,1)}, u32[]{:S(2)}) copy-start(bf16[16,256]{1,0:T(8,128)(2,1)} %k_ref.1) | copy-start | bytes 24580
  0.7 15.3 %copy-start.5 = (bf16[256,2048]{1,0:T(8,128)(2,1)S(1)}, bf16[256,2048]{1,0:T(8,128)(2,1)}, u32[]{:S(2)}) copy-start(bf16[256,2048]{1,0:T(8,128)(2,1)} %g_ref.1) | copy-start | bytes 3145732
  0.7 15.3 %copy-start.4 = (bf16[256,2048]{1,0:T(8,128)(2,1)S(1)}, bf16[256,2048]{1,0:T(8,128)(2,1)}, u32[]{:S(2)}) copy-start(bf16[256,2048]{1,0:T(8,128)(2,1)} %q_ref.1) | copy-start | bytes 3145732
  15.9 11.8 %copy-start = (bf16[8192,256]{1,0:T(8,128)(2,1)S(1)}, bf16[8192,256]{1,0:T(8,128)(2,1)}, u32[]{:S(2)}) copy-start(bf16[8192,256]{1,0:T(8,128)(2,1)} %kw_ref.5) | copy-start | bytes 12582916
  15.9 11.8 %copy-start.1 = (bf16[8192,256]{1,0:T(8,128)(2,1)S(1)}, bf16[8192,256]{1,0:T(8,128)(2,1)}, u32[]{:S(2)}) copy-start(bf16[8192,256]{1,0:T(8,128)(2,1)} %vw_ref.5) | copy-start | bytes 12582916
  28.4 1.3 %collective-permute-start = (bf16[16,2048]{1,0:T(8,128)(2,1)S(1)}, bf16[16,2048]{1,0:T(8,128)(2,1)S(1)}, u32[]{:S(2)}, u32[]{:S(2)}) collective-permute-start(bf16[16,2048]{1,0:T(8,128)(2,1)S(1)} %get-tuple-element.10), channel_id=1, source_target_pairs={{0,1},{1,0},{2,3},{3,2},{4,5},{5,4},{6,7},{7,6},{8,9},{9,8},{10,11... | collective-permute-start | bytes 196616 | tf_op jit(solution)/shard_map/ppermute | solution.py:135
  29.7 4.3 %collective-permute-start.1 = (bf16[16,2048]{1,0:T(8,128)(2,1)S(1)}, bf16[16,2048]{1,0:T(8,128)(2,1)S(1)}, u32[]{:S(2)}, u32[]{:S(2)}) collective-permute-start(bf16[16,2048]{1,0:T(8,128)(2,1)S(1)} %add_convert_fusion.1.after), channel_id=1, source_target_pairs={{0,2},{1,3},{2,0},{3,1},{4,6},{5,7},{6,4},{7,5},{8,10},{9,11},{10,... | collective-permute-start | bytes 196616 | tf_op jit(solution)/shard_map/ppermute | solution.py:135
  32.5 1.5 %collective-permute-start.2 = (bf16[16,2048]{1,0:T(8,128)(2,1)S(1)}, bf16[16,2048]{1,0:T(8,128)(2,1)S(1)}, u32[]{:S(2)}, u32[]{:S(2)}) collective-permute-start(bf16[16,2048]{1,0:T(8,128)(2,1)S(1)} %get-tuple-element.14), channel_id=1, source_target_pairs={{0,1},{1,0},{2,3},{3,2},{4,5},{5,4},{6,7},{7,6},{8,9},{9,8},{10,11... | collective-permute-start | bytes 196616 | tf_op jit(solution)/shard_map/ppermute | solution.py:135

commit v16 on v15

--- a/solution.py
+++ b/solution.py
@@ -10,7 +10,7 @@
 HD = 128
 LEN = 256
 NT = (((1,), (1,)), ((), ()))
-UNIT = 2
+UNIT = 4
 LOG2E = 1.4426950408889634
 
 
@@ -176,7 +176,7 @@
             vmem_limit_bytes=(8 << 20) + 8 * kv_local * tokens * depth
         ),
         cost_estimate=pl.CostEstimate(
-            flops=64 * kv_local * tokens * depth * HD,
+            flops=32 * kv_local * tokens * depth * HD,
             transcendentals=kv_local * tokens * depth,
             bytes_accessed=4 * queries.size + 6 * tokens * width,
         ),

time: 34.9 us -> 35.1 us (level)
  transfers between devices with their start and end apart: 3 -> 3, of which waited for: 2 -> 2; matrix products, arithmetic and copies ran while one was open for 0% -> 0% of each run, Pallas kernels for 6% -> 5%
where the time goes in v16:
time: 35.1 us; the launch traced here: 34.9 us
  blocking collectives  24.4 us (70%)
  Pallas kernels  4.56 us (13%)
  waiting for transfers between devices  2.1 us (6%)
  starting transfers between devices  1.58 us (5%)
  between operations  1.54 us (4%)
  other arithmetic  0.67 us (2%)
    all_to_all x1, blocking collectives, body(): lax.all_to_all(both, 'resp', 0, 0, tiled=True)  14.7 us
    all_to_all x1, blocking collectives, body(): lax.all_to_all(partial.reshape(resp, own, 2 * width), 'resp', 0, 0, tiled...  9.74 us
    ppermute x3, waiting for transfers between devices, swap(): return lax.ppermute(x, axis, [(i, i ^ bit) for i in range(count)])  2.1 us
    pallas_call x1, Pallas kernels, body(): pl.pallas_call(attention_kernel, out_shape=pltpu.VMEM((tokens, 2 * width)...  1.97 us
    ppermute x3, starting transfers between devices, swap(): return lax.ppermute(x, axis, [(i, i ^ bit) for i in range(count)])  1.58 us
    pallas_call x1, Pallas kernels, body(): pl.pallas_call(last_projection_kernel, out_shape=[pltpu.VMEM(block, jnp.b...  1.26 us
  transfers between devices with their start and end apart: 3, of which 2 were waited for; matrix products, arithmetic and copies ran while one was open for 0% of the time, Pallas kernels for 5%

profile of v16, /device:TPU:0, one launch (start us, length us, event | category | flops | bytes accessed | tf_op | source)
XLA Modules:
  0.0 34.9 jit_solution(3130390098140045703)
XLA Ops:
  0.6 0.0 copy-start.3
  0.6 0.0 copy-start.2
  0.7 0.0 copy-start.5
  0.7 0.0 copy-start.4
  1.5 0.0 copy-done.3
  1.5 0.0 copy-done.2
  1.5 0.0 copy-start
  1.5 0.0 copy-start.1
  1.5 14.7 %all_to_all.10 = bf16[8,16,512]{2,1,0:T(8,128)(2,1)S(1)} all-to-all(bf16[8,16,512]{2,1,0:T(8,128)(2,1)S(1)} %join.1), channel_id=1, replica_groups=mesh['resp'=8,'head'=4] {'resp'}, dimensions={0} | all-to-all | bytes 262144 | tf_op jit(solution)/shard_map/all_to_all | solution.py:161
  16.2 0.0 copy-done.5
  16.2 0.0 copy-done.4
  16.2 2.0 %attention.1 = bf16[128,512]{1,0:T(8,128)(2,1)S(1)} custom-call(f32[1,8,256]{2,1,0:T(8,128)S(1)} %mask.1.live_ref, bf16[128,512]{1,0:T(8,128)(2,1)S(1)} %bitcast.2, bf16[256,2048]{1,0:T(8,128)(2,1)S(1)} %copy-done.4, bf16[256,2048]{1,0:T(8,128)(2,1)S(1)} %copy-done.5), custom_call_target="tpu_custom_call" | custom-call | flops 2147483648 | bytes 2293760 | tf_op jit(solution)/shard_map/attention/pallas_call | solution.py:166
  18.2 9.7 %all_to_all.11.parts_ref = bf16[8,16,512]{2,1,0:T(8,128)(2,1)S(1)} all-to-all(bf16[8,16,512]{2,1,0:T(8,128)(2,1)S(1)} %bitcast.3), channel_id=1, replica_groups=mesh['resp'=8,'head'=4] {'resp'}, dimensions={0} | all-to-all | bytes 262144 | tf_op jit(solution)/shard_map/all_to_all | solution.py:186
  27.9 0.0 copy-done
  27.9 0.0 copy-done.1
  27.9 0.6 %projection_other_core.1 = (bf16[16,512]{1,0:T(8,128)(2,1)S(1)}, bf16[16,2048]{1,0:T(8,128)(2,1)S(1)}) custom-call(bf16[8,16,512]{2,1,0:T(8,128)(2,1)S(1)} %all_to_all.11.parts_ref, bf16[8192,256]{1,0:T(8,128)(2,1)S(1)} %copy-done, bf16[8192,256]{1,0:T(8,128)(2,1)S(1)} %copy-done.1), custom_call_target="tpu_custom_call" | custom-call | tf_op jit(solution)/shard_map/projection_other_core/pallas_call | solution.py:191
  28.6 0.0 collective-permute-start
  28.6 0.7 %projection_other_y.1 = f32[16,2048]{1,0:T(8,128)S(1)} custom-call(bf16[16,512]{1,0:T(8,128)(2,1)S(1)} %get-tuple-element.9.low_ref, bf16[8192,256]{1,0:T(8,128)(2,1)S(1)} %copy-done, bf16[8192,256]{1,0:T(8,128)(2,1)S(1)} %copy-done.1), custom_call_target="tpu_custom_call" | custom-call | flops 33554432 | bytes 2097152 | tf_op jit(solution)/shard_map/projection_other_y/pallas_call | solution.py:205
  29.2 0.6 %collective-permute-done = bf16[16,2048]{1,0:T(8,128)(2,1)S(1)} collective-permute-done((bf16[16,2048]{1,0:T(8,128)(2,1)S(1)}, bf16[16,2048]{1,0:T(8,128)(2,1)S(1)}, u32[]{:S(2)}, u32[]{:S(2)}) %collective-permute-start) | collective-permute-done | bytes 65568 | tf_op jit(solution)/shard_map/ppermute | solution.py:135
  29.9 1.6 %collective-permute-start.1 = (bf16[16,2048]{1,0:T(8,128)(2,1)S(1)}, bf16[16,2048]{1,0:T(8,128)(2,1)S(1)}, u32[]{:S(2)}, u32[]{:S(2)}) collective-permute-start(bf16[16,2048]{1,0:T(8,128)(2,1)S(1)} %add_convert_fusion.1.after), channel_id=1, source_target_pairs={{0,2},{1,3},{2,0},{3,1},{4,6},{5,7},{6,4},{7,5},{8,10},{9,11},{10,... | collective-permute-start | bytes 196616 | tf_op jit(solution)/shard_map/ppermute | solution.py:135
  31.4 1.3 %projection_this_y.1 = (bf16[16,2048]{1,0:T(8,128)(2,1)S(1)}, f32[16,2048]{1,0:T(8,128)S(1)}, bf16[16,256]{1,0:T(8,128)(2,1)}, bf16[16,256]{1,0:T(8,128)(2,1)}) custom-call(bf16[16,512]{1,0:T(8,128)(2,1)S(1)} %get-tuple-element.9.low_ref, bf16[8192,256]{1,0:T(8,128)(2,1)S(1)} %copy-done, bf16[8192,256]{1,0:T(8,128)(2,1)S(1)} %copy-done.1, ...), custom_call_target="tpu_custom_call" | custom-call | flops 33554432 | bytes 2097152 | tf_op jit(solution)/shard_map/projection_this_y/pallas_call | solution.py:216
  32.7 0.0 collective-permute-start.2
  32.7 1.5 %collective-permute-done.1 = bf16[16,2048]{1,0:T(8,128)(2,1)S(1)} collective-permute-done((bf16[16,2048]{1,0:T(8,128)(2,1)S(1)}, bf16[16,2048]{1,0:T(8,128)(2,1)S(1)}, u32[]{:S(2)}, u32[]{:S(2)}) %collective-permute-start.1) | collective-permute-done | bytes 65568 | tf_op jit(solution)/shard_map/ppermute | solution.py:135
  34.2 0.0 collective-permute-done.2
  34.2 0.6 %add_convert_fusion = bf16[16,2048]{1,0:T(8,128)(2,1)} fusion(f32[16,2048]{1,0:T(8,128)S(1)} %convert_add_fusion, bf16[16,2048]{1,0:T(8,128)(2,1)S(1)} %collective-permute-done.2), kind=kLoop, calls=%fused_computation | loop fusion | flops 98304 | bytes 262144 | tf_op jit(solution)/shard_map/convert_element_type | solution.py:232
  (4 shorter events, 0.0 us)
Async XLA Ops:
  0.6 0.8 %copy-start.3 = (bf16[16,256]{1,0:T(8,128)(2,1)S(1)}, bf16[16,256]{1,0:T(8,128)(2,1)}, u32[]{:S(2)}) copy-start(bf16[16,256]{1,0:T(8,128)(2,1)} %v_ref.1) | copy-start | bytes 24580
  0.6 0.8 %copy-start.2 = (bf16[16,256]{1,0:T(8,128)(2,1)S(1)}, bf16[16,256]{1,0:T(8,128)(2,1)}, u32[]{:S(2)}) copy-start(bf16[16,256]{1,0:T(8,128)(2,1)} %k_ref.1) | copy-start | bytes 24580
  0.7 15.6 %copy-start.5 = (bf16[256,2048]{1,0:T(8,128)(2,1)S(1)}, bf16[256,2048]{1,0:T(8,128)(2,1)}, u32[]{:S(2)}) copy-start(bf16[256,2048]{1,0:T(8,128)(2,1)} %g_ref.1) | copy-start | bytes 3145732
  0.7 15.5 %copy-start.4 = (bf16[256,2048]{1,0:T(8,128)(2,1)S(1)}, bf16[256,2048]{1,0:T(8,128)(2,1)}, u32[]{:S(2)}) copy-start(bf16[256,2048]{1,0:T(8,128)(2,1)} %q_ref.1) | copy-start | bytes 3145732
  1.5 26.4 %copy-start = (bf16[8192,256]{1,0:T(8,128)(2,1)S(1)}, bf16[8192,256]{1,0:T(8,128)(2,1)}, u32[]{:S(2)}) copy-start(bf16[8192,256]{1,0:T(8,128)(2,1)} %kw_ref.5) | copy-start | bytes 12582916
  1.5 26.4 %copy-start.1 = (bf16[8192,256]{1,0:T(8,128)(2,1)S(1)}, bf16[8192,256]{1,0:T(8,128)(2,1)}, u32[]{:S(2)}) copy-start(bf16[8192,256]{1,0:T(8,128)(2,1)} %vw_ref.5) | copy-start | bytes 12582916
  28.6 1.3 %collective-permute-start = (bf16[16,2048]{1,0:T(8,128)(2,1)S(1)}, bf16[16,2048]{1,0:T(8,128)(2,1)S(1)}, u32[]{:S(2)}, u32[]{:S(2)}) collective-permute-start(bf16[16,2048]{1,0:T(8,128)(2,1)S(1)} %get-tuple-element.10), channel_id=1, source_target_pairs={{0,1},{1,0},{2,3},{3,2},{4,5},{5,4},{6,7},{7,6},{8,9},{9,8},{10,11... | collective-permute-start | bytes 196616 | tf_op jit(solution)/shard_map/ppermute | solution.py:135
  29.9 4.3 %collective-permute-start.1 = (bf16[16,2048]{1,0:T(8,128)(2,1)S(1)}, bf16[16,2048]{1,0:T(8,128)(2,1)S(1)}, u32[]{:S(2)}, u32[]{:S(2)}) collective-permute-start(bf16[16,2048]{1,0:T(8,128)(2,1)S(1)} %add_convert_fusion.1.after), channel_id=1, source_target_pairs={{0,2},{1,3},{2,0},{3,1},{4,6},{5,7},{6,4},{7,5},{8,10},{9,11},{10,... | collective-permute-start | bytes 196616 | tf_op jit(solution)/shard_map/ppermute | solution.py:135
  32.7 1.5 %collective-permute-start.2 = (bf16[16,2048]{1,0:T(8,128)(2,1)S(1)}, bf16[16,2048]{1,0:T(8,128)(2,1)S(1)}, u32[]{:S(2)}, u32[]{:S(2)}) collective-permute-start(bf16[16,2048]{1,0:T(8,128)(2,1)S(1)} %get-tuple-element.14), channel_id=1, source_target_pairs={{0,1},{1,0},{2,3},{3,2},{4,5},{5,4},{6,7},{7,6},{8,9},{9,8},{10,11... | collective-permute-start | bytes 196616 | tf_op jit(solution)/shard_map/ppermute | solution.py:135

commit v17 on v15

--- a/solution.py
+++ b/solution.py
@@ -10,12 +10,11 @@
 HD = 128
 LEN = 256
 NT = (((1,), (1,)), ((), ()))
-UNIT = 2
 LOG2E = 1.4426950408889634
 
 
 def mask_kernel(lengths_ref, live_ref):
-    position = lax.broadcasted_iota(jnp.int32, live_ref.shape[1:], 1)
+    position = lax.broadcasted_iota(jnp.int32, live_ref.shape[1:], 0)
     for part in range(live_ref.shape[0]):
         live_ref[part] = jnp.where(position < lengths_ref[part], 1.0, 0.0)
 
@@ -35,61 +34,60 @@
     kv_local = width // HD
     parts = q_ref.shape[0] // LEN
     group = q_ref.shape[1] // HD // kv_local
-    units = [
-        (k, part, h)
-        for k in range(kv_local)
-        for part in range(parts)
-        for h in range(0, group, UNIT)
-    ]
-
-    def stack(ref, unit):
-        k, part, h = unit
-        heads = [
-            ref[part * LEN : (part + 1) * LEN, at * HD : (at + 1) * HD]
-            for at in range(k * group + h, k * group + h + UNIT)
-        ]
-        return jnp.concatenate(heads, axis=0)
-
     blocks_ref[...] = jnp.zeros_like(blocks_ref)
     for k in range(kv_local):
         blocks_ref[k, :tokens, :HD] = kv_ref[:, k * HD : (k + 1) * HD]
         blocks_ref[k, tokens:, HD:] = kv_ref[:, width + k * HD : width + (k + 1) * HD]
 
+    def beside(left_ref, right_ref, unit):
+        k, part, h = unit
+        at = (k * group + h) * HD
+        rows = slice(part * LEN, (part + 1) * LEN)
+        return jnp.concatenate(
+            [left_ref[rows, at : at + HD], right_ref[rows, at : at + HD]], axis=1
+        )
+
     def products(unit):
-        both = jnp.concatenate([stack(q_ref, unit), stack(g_ref, unit)], axis=1)
-        out = lax.dot_general(blocks_ref[unit[0]], both, NT, preferred_element_type=jnp.float32)
-        return out[:tokens], out[tokens:]
-
+        return lax.dot_general(
+            beside(q_ref, g_ref, unit),
+            blocks_ref[unit[0]],
+            NT,
+            preferred_element_type=jnp.float32,
+        )
+
+    units = [
+        (k, part, h) for k in range(kv_local) for part in range(parts) for h in range(group)
+    ]
     following = products(units[0])
     for i, unit in enumerate(units):
         k, part, h = unit
-        scores, dprobs = following
+        scores, dprobs = following[:, :tokens], following[:, tokens:]
         if i + 1 < len(units):
             following = products(units[i + 1])
-        top = jnp.max(scores, axis=0, keepdims=True)
+        top = jnp.max(scores, axis=1, keepdims=True)
         expo = jnp.exp2((scores - top) * (scale * LOG2E))
-        total = jnp.sum(expo, axis=0, keepdims=True)
-        weighted = jnp.sum(expo * dprobs, axis=0, keepdims=True)
+        total = jnp.sum(expo, axis=1, keepdims=True)
+        weighted = jnp.sum(expo * dprobs, axis=1, keepdims=True)
         inverse = 1.0 / total
         delta = weighted * inverse
-        factor = inverse * jnp.concatenate([live_ref[part, :1]] * UNIT, axis=1)
+        factor = inverse * live_ref[part][:, :1]
         probs = expo * factor
         mine = [u for u in units if u[0] == k]
-        cols = pl.ds(mine.index(unit) * UNIT * LEN, UNIT * LEN)
-        weights_ref[k, :tokens, cols] = probs.astype(jnp.bfloat16)
-        weights_ref[k, tokens:, cols] = (probs * (dprobs - delta)).astype(jnp.bfloat16)
+        at = mine.index(unit) * LEN
+        weights_ref[k, at : at + LEN, :tokens] = probs.astype(jnp.bfloat16)
+        weights_ref[k, at : at + LEN, tokens:] = (probs * (dprobs - delta)).astype(jnp.bfloat16)
         if unit == mine[-1]:
-            rows = [
-                jnp.concatenate([stack(g_ref, u), stack(q_ref, u)], axis=1) for u in mine
-            ]
-            out = jnp.dot(
-                weights_ref[k], jnp.concatenate(rows, axis=0), preferred_element_type=jnp.float32
+            rows = jnp.concatenate([beside(g_ref, q_ref, u) for u in mine], axis=0)
+            out = lax.dot_general(
+                rows,
+                weights_ref[k],
+                (((0,), (0,)), ((), ())),
+                preferred_element_type=jnp.float32,
             )
-            grad_k = out[tokens:, HD:] * scale
+            grad_v = out[:HD, :tokens].T
+            grad_k = out[HD:, tokens:].T * scale
             out_ref[:, k * HD : (k + 1) * HD] = grad_k.astype(out_ref.dtype)
-            out_ref[:, width + k * HD : width + (k + 1) * HD] = out[:tokens, :HD].astype(
-                out_ref.dtype
-            )
+            out_ref[:, width + k * HD : width + (k + 1) * HD] = grad_v.astype(out_ref.dtype)
 
 
 def project(low, kw_ref, vw_ref, owner, features):
@@ -143,7 +141,7 @@
 
     live = pl.pallas_call(
         mask_kernel,
-        out_shape=pltpu.VMEM((lengths.shape[0], 8, LEN), jnp.float32),
+        out_shape=pltpu.VMEM((lengths.shape[0], LEN, 128), jnp.float32),
         in_specs=[pl.BlockSpec(memory_space=pltpu.SMEM)],
         out_specs=vmem,
         compiler_params=params,
@@ -170,7 +168,7 @@
         out_specs=vmem,
         scratch_shapes=[
             pltpu.VMEM((kv_local, 2 * tokens, 2 * HD), jnp.bfloat16),
-            pltpu.VMEM((kv_local, 2 * tokens, depth), jnp.bfloat16),
+            pltpu.VMEM((kv_local, depth, 2 * tokens), jnp.bfloat16),
         ],
         compiler_params=pltpu.CompilerParams(
             vmem_limit_bytes=(8 << 20) + 8 * kv_local * tokens * depth

time: 34.9 us -> 37.9 us (1.086)
  Pallas kernels: 4.52 us -> 7.67 us
    pallas_call x1, Pallas kernels: 1.94 us -> 5.07 us  [body(): pl.pallas_call(attention_kernel, out_shape=pltpu.VMEM((tokens, 2 * width)...]
  transfers between devices with their start and end apart: 3 -> 3, of which waited for: 2 -> 2; matrix products, arithmetic and copies ran while one was open for 0% -> 0% of each run, Pallas kernels for 6% -> 5%
where the time goes in v17:
time: 37.9 us; the launch traced here: 37.7 us
  blocking collectives  24.1 us (64%)
  Pallas kernels  7.67 us (20%)
  waiting for transfers between devices  2.09 us (6%)
  starting transfers between devices  1.59 us (4%)
  between operations  1.53 us (4%)
  other arithmetic  0.67 us (2%)
    all_to_all x1, blocking collectives, body(): lax.all_to_all(both, 'resp', 0, 0, tiled=True)  14.4 us
    all_to_all x1, blocking collectives, body(): lax.all_to_all(partial.reshape(resp, own, 2 * width), 'resp', 0, 0, tiled...  9.74 us
    pallas_call x1, Pallas kernels, body(): pl.pallas_call(attention_kernel, out_shape=pltpu.VMEM((tokens, 2 * width)...  5.07 us
    ppermute x3, waiting for transfers between devices, swap(): return lax.ppermute(x, axis, [(i, i ^ bit) for i in range(count)])  2.09 us
    ppermute x3, starting transfers between devices, swap(): return lax.ppermute(x, axis, [(i, i ^ bit) for i in range(count)])  1.59 us
    pallas_call x1, Pallas kernels, body(): pl.pallas_call(last_projection_kernel, out_shape=[pltpu.VMEM(block, jnp.b...  1.26 us
  transfers between devices with their start and end apart: 3, of which 2 were waited for; matrix products, arithmetic and copies ran while one was open for 0% of the time, Pallas kernels for 5%

profile of v17, /device:TPU:0, one launch (start us, length us, event | category | flops | bytes accessed | tf_op | source)
XLA Modules:
  0.0 37.7 jit_solution(1919299939523520965)
XLA Ops:
  0.6 0.0 copy-start.3
  0.6 0.0 copy-start.2
  0.7 0.0 copy-start.5
  0.7 0.0 copy-start.4
  1.5 0.0 copy-done.3
  1.5 0.0 copy-done.2
  1.5 14.4 %all_to_all.10 = bf16[8,16,512]{2,1,0:T(8,128)(2,1)S(1)} all-to-all(bf16[8,16,512]{2,1,0:T(8,128)(2,1)S(1)} %join.1), channel_id=1, replica_groups=mesh['resp'=8,'head'=4] {'resp'}, dimensions={0} | all-to-all | bytes 262144 | tf_op jit(solution)/shard_map/all_to_all | solution.py:159
  15.9 0.0 copy-done.5
  15.9 0.0 copy-done.4
  15.9 0.0 copy-start
  15.9 0.0 copy-start.1
  15.9 5.1 %attention.1 = bf16[128,512]{1,0:T(8,128)(2,1)S(1)} custom-call(f32[1,256,128]{2,1,0:T(8,128)S(1)} %mask.1.live_ref, bf16[128,512]{1,0:T(8,128)(2,1)S(1)} %bitcast.2, bf16[256,2048]{1,0:T(8,128)(2,1)S(1)} %copy-done.4, bf16[256,2048]{1,0:T(8,128)(2,1)S(1)} %copy-done.5), custom_call_target="tpu_custom_call" | custom-call | flops 4294967296 | bytes 2293760 | tf_op jit(solution)/shard_map/attention/pallas_call | solution.py:164
  21.0 9.7 %all_to_all.11.parts_ref = bf16[8,16,512]{2,1,0:T(8,128)(2,1)S(1)} all-to-all(bf16[8,16,512]{2,1,0:T(8,128)(2,1)S(1)} %bitcast.3), channel_id=1, replica_groups=mesh['resp'=8,'head'=4] {'resp'}, dimensions={0} | all-to-all | bytes 262144 | tf_op jit(solution)/shard_map/all_to_all | solution.py:184
  30.8 0.0 copy-done
  30.8 0.0 copy-done.1
  30.8 0.6 %projection_other_core.1 = (bf16[16,512]{1,0:T(8,128)(2,1)S(1)}, bf16[16,2048]{1,0:T(8,128)(2,1)S(1)}) custom-call(bf16[8,16,512]{2,1,0:T(8,128)(2,1)S(1)} %all_to_all.11.parts_ref, bf16[8192,256]{1,0:T(8,128)(2,1)S(1)} %copy-done, bf16[8192,256]{1,0:T(8,128)(2,1)S(1)} %copy-done.1), custom_call_target="tpu_custom_call" | custom-call | tf_op jit(solution)/shard_map/projection_other_core/pallas_call | solution.py:189
  31.4 0.0 collective-permute-start
  31.4 0.7 %projection_other_y.1 = f32[16,2048]{1,0:T(8,128)S(1)} custom-call(bf16[16,512]{1,0:T(8,128)(2,1)S(1)} %get-tuple-element.9.low_ref, bf16[8192,256]{1,0:T(8,128)(2,1)S(1)} %copy-done, bf16[8192,256]{1,0:T(8,128)(2,1)S(1)} %copy-done.1), custom_call_target="tpu_custom_call" | custom-call | flops 33554432 | bytes 2097152 | tf_op jit(solution)/shard_map/projection_other_y/pallas_call | solution.py:203
  32.1 0.6 %collective-permute-done = bf16[16,2048]{1,0:T(8,128)(2,1)S(1)} collective-permute-done((bf16[16,2048]{1,0:T(8,128)(2,1)S(1)}, bf16[16,2048]{1,0:T(8,128)(2,1)S(1)}, u32[]{:S(2)}, u32[]{:S(2)}) %collective-permute-start) | collective-permute-done | bytes 65568 | tf_op jit(solution)/shard_map/ppermute | solution.py:133
  32.7 1.6 %collective-permute-start.1 = (bf16[16,2048]{1,0:T(8,128)(2,1)S(1)}, bf16[16,2048]{1,0:T(8,128)(2,1)S(1)}, u32[]{:S(2)}, u32[]{:S(2)}) collective-permute-start(bf16[16,2048]{1,0:T(8,128)(2,1)S(1)} %add_convert_fusion.1.after), channel_id=1, source_target_pairs={{0,2},{1,3},{2,0},{3,1},{4,6},{5,7},{6,4},{7,5},{8,10},{9,11},{10,... | collective-permute-start | bytes 196616 | tf_op jit(solution)/shard_map/ppermute | solution.py:133
  34.3 1.3 %projection_this_y.1 = (bf16[16,2048]{1,0:T(8,128)(2,1)S(1)}, f32[16,2048]{1,0:T(8,128)S(1)}, bf16[16,256]{1,0:T(8,128)(2,1)}, bf16[16,256]{1,0:T(8,128)(2,1)}) custom-call(bf16[16,512]{1,0:T(8,128)(2,1)S(1)} %get-tuple-element.9.low_ref, bf16[8192,256]{1,0:T(8,128)(2,1)S(1)} %copy-done, bf16[8192,256]{1,0:T(8,128)(2,1)S(1)} %copy-done.1, ...), custom_call_target="tpu_custom_call" | custom-call | flops 33554432 | bytes 2097152 | tf_op jit(solution)/shard_map/projection_this_y/pallas_call | solution.py:214
  35.6 0.0 collective-permute-start.2
  35.6 1.5 %collective-permute-done.1 = bf16[16,2048]{1,0:T(8,128)(2,1)S(1)} collective-permute-done((bf16[16,2048]{1,0:T(8,128)(2,1)S(1)}, bf16[16,2048]{1,0:T(8,128)(2,1)S(1)}, u32[]{:S(2)}, u32[]{:S(2)}) %collective-permute-start.1) | collective-permute-done | bytes 65568 | tf_op jit(solution)/shard_map/ppermute | solution.py:133
  37.0 0.0 collective-permute-done.2
  37.1 0.6 %add_convert_fusion = bf16[16,2048]{1,0:T(8,128)(2,1)} fusion(f32[16,2048]{1,0:T(8,128)S(1)} %convert_add_fusion, bf16[16,2048]{1,0:T(8,128)(2,1)S(1)} %collective-permute-done.2), kind=kLoop, calls=%fused_computation | loop fusion | flops 98304 | bytes 262144 | tf_op jit(solution)/shard_map/convert_element_type | solution.py:230
  (4 shorter events, 0.1 us)
Async XLA Ops:
  0.6 0.9 %copy-start.3 = (bf16[16,256]{1,0:T(8,128)(2,1)S(1)}, bf16[16,256]{1,0:T(8,128)(2,1)}, u32[]{:S(2)}) copy-start(bf16[16,256]{1,0:T(8,128)(2,1)} %v_ref.1) | copy-start | bytes 24580
  0.6 0.9 %copy-start.2 = (bf16[16,256]{1,0:T(8,128)(2,1)S(1)}, bf16[16,256]{1,0:T(8,128)(2,1)}, u32[]{:S(2)}) copy-start(bf16[16,256]{1,0:T(8,128)(2,1)} %k_ref.1) | copy-start | bytes 24580
  0.7 15.3 %copy-start.5 = (bf16[256,2048]{1,0:T(8,128)(2,1)S(1)}, bf16[256,2048]{1,0:T(8,128)(2,1)}, u32[]{:S(2)}) copy-start(bf16[256,2048]{1,0:T(8,128)(2,1)} %g_ref.1) | copy-start | bytes 3145732
  0.7 15.3 %copy-start.4 = (bf16[256,2048]{1,0:T(8,128)(2,1)S(1)}, bf16[256,2048]{1,0:T(8,128)(2,1)}, u32[]{:S(2)}) copy-start(bf16[256,2048]{1,0:T(8,128)(2,1)} %q_ref.1) | copy-start | bytes 3145732
  15.9 14.8 %copy-start = (bf16[8192,256]{1,0:T(8,128)(2,1)S(1)}, bf16[8192,256]{1,0:T(8,128)(2,1)}, u32[]{:S(2)}) copy-start(bf16[8192,256]{1,0:T(8,128)(2,1)} %kw_ref.5) | copy-start | bytes 12582916
  15.9 14.8 %copy-start.1 = (bf16[8192,256]{1,0:T(8,128)(2,1)S(1)}, bf16[8192,256]{1,0:T(8,128)(2,1)}, u32[]{:S(2)}) copy-start(bf16[8192,256]{1,0:T(8,128)(2,1)} %vw_ref.5) | copy-start | bytes 12582916
  31.4 1.3 %collective-permute-start = (bf16[16,2048]{1,0:T(8,128)(2,1)S(1)}, bf16[16,2048]{1,0:T(8,128)(2,1)S(1)}, u32[]{:S(2)}, u32[]{:S(2)}) collective-permute-start(bf16[16,2048]{1,0:T(8,128)(2,1)S(1)} %get-tuple-element.10), channel_id=1, source_target_pairs={{0,1},{1,0},{2,3},{3,2},{4,5},{5,4},{6,7},{7,6},{8,9},{9,8},{10,11... | collective-permute-start | bytes 196616 | tf_op jit(solution)/shard_map/ppermute | solution.py:133
  32.7 4.3 %collective-permute-start.1 = (bf16[16,2048]{1,0:T(8,128)(2,1)S(1)}, bf16[16,2048]{1,0:T(8,128)(2,1)S(1)}, u32[]{:S(2)}, u32[]{:S(2)}) collective-permute-start(bf16[16,2048]{1,0:T(8,128)(2,1)S(1)} %add_convert_fusion.1.after), channel_id=1, source_target_pairs={{0,2},{1,3},{2,0},{3,1},{4,6},{5,7},{6,4},{7,5},{8,10},{9,11},{10,... | collective-permute-start | bytes 196616 | tf_op jit(solution)/shard_map/ppermute | solution.py:133
  35.6 1.5 %collective-permute-start.2 = (bf16[16,2048]{1,0:T(8,128)(2,1)S(1)}, bf16[16,2048]{1,0:T(8,128)(2,1)S(1)}, u32[]{:S(2)}, u32[]{:S(2)}) collective-permute-start(bf16[16,2048]{1,0:T(8,128)(2,1)S(1)} %get-tuple-element.14), channel_id=1, source_target_pairs={{0,1},{1,0},{2,3},{3,2},{4,5},{5,4},{6,7},{7,6},{8,9},{9,8},{10,11... | collective-permute-start | bytes 196616 | tf_op jit(solution)/shard_map/ppermute | solution.py:133

commit v18 on v15

--- a/solution.py
+++ b/solution.py
@@ -131,6 +131,10 @@
     keep_ref[...] = project(low, kw_ref, vw_ref, me, keep_ref.shape[1])
 
 
+def last_sum_kernel(total_ref, got_ref, out_ref):
+    out_ref[...] = (total_ref[...] + got_ref[...].astype(jnp.float32)).astype(out_ref.dtype)
+
+
 def swap(x, axis, count, bit):
     return lax.ppermute(x, axis, [(i, i ^ bit) for i in range(count)])
 
@@ -228,8 +232,15 @@
         name="projection_this_y",
     )(low, k_weight, v_weight, far)
     total = lax.optimization_barrier(total + got.astype(jnp.float32))
-    total += swap(to_core, "head", head, 1).astype(jnp.float32)
-    return dk_low, dv_low, total.astype(jnp.bfloat16)
+    input_grad = pl.pallas_call(
+        last_sum_kernel,
+        out_shape=jax.ShapeDtypeStruct(block, jnp.bfloat16),
+        in_specs=[vmem] * 2,
+        out_specs=vmem,
+        compiler_params=params,
+        name="last_sum",
+    )(total, swap(to_core, "head", head, 1))
+    return dk_low, dv_low, input_grad
 
 
 def solution(mesh):

time: 34.9 us -> 34.9 us (level)
  Pallas kernels: 4.52 us -> 5.17 us
  other arithmetic: 0.67 us -> 0.03 us
    convert_element_type x1 -> x0, other arithmetic: 0.64 us -> none  [body(): return (dk_low, dv_low, total.astype(jnp.bfloat16))]
    pallas_call x0 -> x1, Pallas kernels: none -> 0.64 us  [body(): pl.pallas_call(last_sum_kernel, out_shape=jax.ShapeDtypeStruct(block, jnp...]
where the time goes in v18:
time: 34.9 us; the launch traced here: 34.7 us
  blocking collectives  24.3 us (70%)
  Pallas kernels  5.17 us (15%)
  waiting for transfers between devices  2.09 us (6%)
  starting transfers between devices  1.59 us (5%)
  between operations  1.53 us (4%)
    all_to_all x1, blocking collectives, body(): lax.all_to_all(both, 'resp', 0, 0, tiled=True)  14.4 us
    all_to_all x1, blocking collectives, body(): lax.all_to_all(partial.reshape(resp, own, 2 * width), 'resp', 0, 0, tiled...  9.87 us
    ppermute x3, waiting for transfers between devices, swap(): return lax.ppermute(x, axis, [(i, i ^ bit) for i in range(count)])  2.09 us
    pallas_call x1, Pallas kernels, body(): pl.pallas_call(attention_kernel, out_shape=pltpu.VMEM((tokens, 2 * width)...  1.94 us
    ppermute x3, starting transfers between devices, swap(): return lax.ppermute(x, axis, [(i, i ^ bit) for i in range(count)])  1.59 us
    pallas_call x1, Pallas kernels, body(): pl.pallas_call(last_projection_kernel, out_shape=[pltpu.VMEM(block, jnp.b...  1.26 us
  transfers between devices with their start and end apart: 3, of which 2 were waited for; matrix products, arithmetic and copies ran while one was open for 0% of the time, Pallas kernels for 6%

profile of v18, /device:TPU:0, one launch (start us, length us, event | category | flops | bytes accessed | tf_op | source)
XLA Modules:
  0.0 34.7 jit_solution(5999461822788301411)
XLA Ops:
  0.6 0.0 copy-start.3
  0.6 0.0 copy-start.2
  0.7 0.0 copy-start.5
  0.7 0.0 copy-start.4
  1.5 0.0 copy-done.3
  1.5 0.0 copy-done.2
  1.5 14.4 %all_to_all.10 = bf16[8,16,512]{2,1,0:T(8,128)(2,1)S(1)} all-to-all(bf16[8,16,512]{2,1,0:T(8,128)(2,1)S(1)} %join.1), channel_id=1, replica_groups=mesh['resp'=8,'head'=4] {'resp'}, dimensions={0} | all-to-all | bytes 262144 | tf_op jit(solution)/shard_map/all_to_all | solution.py:165
  15.9 0.0 copy-done.5
  15.9 0.0 copy-done.4
  15.9 0.0 copy-start
  15.9 0.0 copy-start.1
  15.9 1.9 %attention.1 = bf16[128,512]{1,0:T(8,128)(2,1)S(1)} custom-call(f32[1,8,256]{2,1,0:T(8,128)S(1)} %mask.1.live_ref, bf16[128,512]{1,0:T(8,128)(2,1)S(1)} %bitcast.2, bf16[256,2048]{1,0:T(8,128)(2,1)S(1)} %copy-done.4, bf16[256,2048]{1,0:T(8,128)(2,1)S(1)} %copy-done.5), custom_call_target="tpu_custom_call" | custom-call | flops 4294967296 | bytes 2293760 | tf_op jit(solution)/shard_map/attention/pallas_call | solution.py:170
  17.9 9.9 %all_to_all.11.parts_ref = bf16[8,16,512]{2,1,0:T(8,128)(2,1)S(1)} all-to-all(bf16[8,16,512]{2,1,0:T(8,128)(2,1)S(1)} %bitcast.3), channel_id=1, replica_groups=mesh['resp'=8,'head'=4] {'resp'}, dimensions={0} | all-to-all | bytes 262144 | tf_op jit(solution)/shard_map/all_to_all | solution.py:190
  27.7 0.0 copy-done
  27.7 0.0 copy-done.1
  27.7 0.6 %projection_other_core.1 = (bf16[16,512]{1,0:T(8,128)(2,1)S(1)}, bf16[16,2048]{1,0:T(8,128)(2,1)S(1)}) custom-call(bf16[8,16,512]{2,1,0:T(8,128)(2,1)S(1)} %all_to_all.11.parts_ref, bf16[8192,256]{1,0:T(8,128)(2,1)S(1)} %copy-done, bf16[8192,256]{1,0:T(8,128)(2,1)S(1)} %copy-done.1), custom_call_target="tpu_custom_call" | custom-call | tf_op jit(solution)/shard_map/projection_other_core/pallas_call | solution.py:195
  28.4 0.0 collective-permute-start
  28.4 0.7 %projection_other_y.1 = f32[16,2048]{1,0:T(8,128)S(1)} custom-call(bf16[16,512]{1,0:T(8,128)(2,1)S(1)} %get-tuple-element.9.low_ref, bf16[8192,256]{1,0:T(8,128)(2,1)S(1)} %copy-done, bf16[8192,256]{1,0:T(8,128)(2,1)S(1)} %copy-done.1), custom_call_target="tpu_custom_call" | custom-call | flops 33554432 | bytes 2097152 | tf_op jit(solution)/shard_map/projection_other_y/pallas_call | solution.py:209
  29.1 0.6 %collective-permute-done = bf16[16,2048]{1,0:T(8,128)(2,1)S(1)} collective-permute-done((bf16[16,2048]{1,0:T(8,128)(2,1)S(1)}, bf16[16,2048]{1,0:T(8,128)(2,1)S(1)}, u32[]{:S(2)}, u32[]{:S(2)}) %collective-permute-start) | collective-permute-done | bytes 65568 | tf_op jit(solution)/shard_map/ppermute | solution.py:139
  29.7 1.6 %collective-permute-start.1 = (bf16[16,2048]{1,0:T(8,128)(2,1)S(1)}, bf16[16,2048]{1,0:T(8,128)(2,1)S(1)}, u32[]{:S(2)}, u32[]{:S(2)}) collective-permute-start(bf16[16,2048]{1,0:T(8,128)(2,1)S(1)} %add_convert_fusion.after), channel_id=1, source_target_pairs={{0,2},{1,3},{2,0},{3,1},{4,6},{5,7},{6,4},{7,5},{8,10},{9,11},{10,... | collective-permute-start | bytes 196616 | tf_op jit(solution)/shard_map/ppermute | solution.py:139
  31.3 1.3 %projection_this_y.1 = (bf16[16,2048]{1,0:T(8,128)(2,1)S(1)}, f32[16,2048]{1,0:T(8,128)S(1)}, bf16[16,256]{1,0:T(8,128)(2,1)}, bf16[16,256]{1,0:T(8,128)(2,1)}) custom-call(bf16[16,512]{1,0:T(8,128)(2,1)S(1)} %get-tuple-element.9.low_ref, bf16[8192,256]{1,0:T(8,128)(2,1)S(1)} %copy-done, bf16[8192,256]{1,0:T(8,128)(2,1)S(1)} %copy-done.1, ...), custom_call_target="tpu_custom_call" | custom-call | flops 33554432 | bytes 2097152 | tf_op jit(solution)/shard_map/projection_this_y/pallas_call | solution.py:220
  32.5 0.0 collective-permute-start.2
  32.5 1.5 %collective-permute-done.1 = bf16[16,2048]{1,0:T(8,128)(2,1)S(1)} collective-permute-done((bf16[16,2048]{1,0:T(8,128)(2,1)S(1)}, bf16[16,2048]{1,0:T(8,128)(2,1)S(1)}, u32[]{:S(2)}, u32[]{:S(2)}) %collective-permute-start.1) | collective-permute-done | bytes 65568 | tf_op jit(solution)/shard_map/ppermute | solution.py:139
  34.0 0.0 collective-permute-done.2.got_ref
  34.0 0.6 %last_sum.1 = bf16[16,2048]{1,0:T(8,128)(2,1)} custom-call(f32[16,2048]{1,0:T(8,128)S(1)} %convert_add_fusion.total_ref, bf16[16,2048]{1,0:T(8,128)(2,1)S(1)} %collective-permute-done.2.got_ref), custom_call_target="tpu_custom_call" | custom-call | tf_op jit(solution)/shard_map/last_sum/pallas_call | solution.py:235
  (4 shorter events, 0.0 us)
Async XLA Ops:
  0.6 0.8 %copy-start.3 = (bf16[16,256]{1,0:T(8,128)(2,1)S(1)}, bf16[16,256]{1,0:T(8,128)(2,1)}, u32[]{:S(2)}) copy-start(bf16[16,256]{1,0:T(8,128)(2,1)} %v_ref.1) | copy-start | bytes 24580
  0.6 0.8 %copy-start.2 = (bf16[16,256]{1,0:T(8,128)(2,1)S(1)}, bf16[16,256]{1,0:T(8,128)(2,1)}, u32[]{:S(2)}) copy-start(bf16[16,256]{1,0:T(8,128)(2,1)} %k_ref.1) | copy-start | bytes 24580
  0.7 15.3 %copy-start.5 = (bf16[256,2048]{1,0:T(8,128)(2,1)S(1)}, bf16[256,2048]{1,0:T(8,128)(2,1)}, u32[]{:S(2)}) copy-start(bf16[256,2048]{1,0:T(8,128)(2,1)} %g_ref.1) | copy-start | bytes 3145732
  0.7 15.3 %copy-start.4 = (bf16[256,2048]{1,0:T(8,128)(2,1)S(1)}, bf16[256,2048]{1,0:T(8,128)(2,1)}, u32[]{:S(2)}) copy-start(bf16[256,2048]{1,0:T(8,128)(2,1)} %q_ref.1) | copy-start | bytes 3145732
  15.9 11.8 %copy-start = (bf16[8192,256]{1,0:T(8,128)(2,1)S(1)}, bf16[8192,256]{1,0:T(8,128)(2,1)}, u32[]{:S(2)}) copy-start(bf16[8192,256]{1,0:T(8,128)(2,1)} %kw_ref.5) | copy-start | bytes 12582916
  15.9 11.8 %copy-start.1 = (bf16[8192,256]{1,0:T(8,128)(2,1)S(1)}, bf16[8192,256]{1,0:T(8,128)(2,1)}, u32[]{:S(2)}) copy-start(bf16[8192,256]{1,0:T(8,128)(2,1)} %vw_ref.5) | copy-start | bytes 12582916
  28.4 1.3 %collective-permute-start = (bf16[16,2048]{1,0:T(8,128)(2,1)S(1)}, bf16[16,2048]{1,0:T(8,128)(2,1)S(1)}, u32[]{:S(2)}, u32[]{:S(2)}) collective-permute-start(bf16[16,2048]{1,0:T(8,128)(2,1)S(1)} %get-tuple-element.10), channel_id=1, source_target_pairs={{0,1},{1,0},{2,3},{3,2},{4,5},{5,4},{6,7},{7,6},{8,9},{9,8},{10,11... | collective-permute-start | bytes 196616 | tf_op jit(solution)/shard_map/ppermute | solution.py:139
  29.7 4.3 %collective-permute-start.1 = (bf16[16,2048]{1,0:T(8,128)(2,1)S(1)}, bf16[16,2048]{1,0:T(8,128)(2,1)S(1)}, u32[]{:S(2)}, u32[]{:S(2)}) collective-permute-start(bf16[16,2048]{1,0:T(8,128)(2,1)S(1)} %add_convert_fusion.after), channel_id=1, source_target_pairs={{0,2},{1,3},{2,0},{3,1},{4,6},{5,7},{6,4},{7,5},{8,10},{9,11},{10,... | collective-permute-start | bytes 196616 | tf_op jit(solution)/shard_map/ppermute | solution.py:139
  32.5 1.5 %collective-permute-start.2 = (bf16[16,2048]{1,0:T(8,128)(2,1)S(1)}, bf16[16,2048]{1,0:T(8,128)(2,1)S(1)}, u32[]{:S(2)}, u32[]{:S(2)}) collective-permute-start(bf16[16,2048]{1,0:T(8,128)(2,1)S(1)} %get-tuple-element.14), channel_id=1, source_target_pairs={{0,1},{1,0},{2,3},{3,2},{4,5},{5,4},{6,7},{7,6},{8,9},{9,8},{10,11... | collective-permute-start | bytes 196616 | tf_op jit(solution)/shard_map/ppermute | solution.py:139

commit v19 on v18

--- a/solution.py
+++ b/solution.py
@@ -103,10 +103,8 @@
     )
 
 
-def first_projection_kernel(parts_ref, kw_ref, vw_ref, low_ref, out_ref):
-    total = parts_ref[0].astype(jnp.float32)
-    for i in range(1, parts_ref.shape[0]):
-        total += parts_ref[i].astype(jnp.float32)
+def first_projection_kernel(keep_ref, got_ref, kw_ref, vw_ref, low_ref, out_ref):
+    total = keep_ref[...] + got_ref[...].astype(jnp.float32)
     low = total.astype(jnp.bfloat16)
     low_ref[...] = low
     me = lax.axis_index("head")
@@ -187,9 +185,20 @@
         name="attention",
     )(live, both, queries, d_out)
 
+    pairs = resp // 2
     shares = lax.all_to_all(
-        partial.reshape(resp, own, 2 * width), "resp", 0, 0, tiled=True
-    )
+        partial.reshape(pairs, 2 * own, 2 * width),
+        "resp",
+        0,
+        0,
+        axis_index_groups=[list(range(i, resp, 2)) for i in range(2)],
+        tiled=True,
+    )
+    total = jnp.sum(shares.astype(jnp.float32), axis=0)
+    odd = (lax.axis_index("resp") & 1) == 1
+    send = jnp.where(odd, total[:own], total[own:]).astype(jnp.bfloat16)
+    keep = jnp.where(odd, total[own:], total[:own])
+    got = swap(send, "resp", resp, 1)
 
     block = (own, features)
     low, to_core = pl.pallas_call(
@@ -198,11 +207,11 @@
             pltpu.VMEM((own, 2 * width), jnp.bfloat16),
             pltpu.VMEM(block, jnp.bfloat16),
         ],
-        in_specs=[vmem] * 3,
+        in_specs=[vmem] * 4,
         out_specs=[vmem] * 2,
         compiler_params=params,
         name="projection_other_core",
-    )(shares, k_weight, v_weight)
+    )(keep, got, k_weight, v_weight)
     cost = pl.CostEstimate(
         flops=4 * own * width * features, transcendentals=0, bytes_accessed=4 * width * features
     )

time: 34.9 us -> 45.4 us (1.30)
  blocking collectives: 24.3 us -> 14.4 us
  waiting for transfers between devices: 2.09 us -> 10.9 us
  local copies, waits for them, and re-layouts: 0.02 us -> 7.2 us
  starting transfers between devices: 1.59 us -> 5.19 us
  Pallas kernels: 5.17 us -> 5.79 us
    all_to_all x1 -> x0, blocking collectives: 9.87 us -> none  [body(): lax.all_to_all(partial.reshape(resp, own, 2 * width), 'resp', 0, 0, tiled...]
    unnamed x12 -> x16, local copies, waits for them, and re-layouts: 0.02 us -> 7.2 us
    all_to_all x0 -> x1, waiting for transfers between devices: none -> 5.88 us  [body(): lax.all_to_all(partial.reshape(pairs, 2 * own, 2 * width), 'resp', 0, 0,...]
    all_to_all x0 -> x1, starting transfers between devices: none -> 3.32 us  [body(): lax.all_to_all(partial.reshape(pairs, 2 * own, 2 * width), 'resp', 0, 0,...]
    ppermute x3 -> x4, waiting for transfers between devices: 2.09 us -> 5 us  [swap(): return lax.ppermute(x, axis, [(i, i ^ bit) for i in range(count)])]
    pallas_call x1, Pallas kernels: 1.94 us -> 2.58 us  [body(): pl.pallas_call(attention_kernel, out_shape=pltpu.VMEM((tokens, 2 * width)...]
    ppermute x3 -> x4, starting transfers between devices: 1.59 us -> 1.87 us  [swap(): return lax.ppermute(x, axis, [(i, i ^ bit) for i in range(count)])]
  transfers between devices with their start and end apart: 3 -> 5, of which waited for: 2 -> 3; matrix products, arithmetic and copies ran while one was open for 0% -> 0% of each run, Pallas kernels for 6% -> 4%
where the time goes in v19:
time: 45.4 us; the launch traced here: 45.1 us
  blocking collectives  14.4 us (32%)
  waiting for transfers between devices  10.9 us (24%)
  local copies, waits for them, and re-layouts  7.2 us (16%)
  Pallas kernels  5.79 us (13%)
  starting transfers between devices  5.19 us (11%)
  between operations  1.55 us (3%)
    all_to_all x1, blocking collectives, body(): lax.all_to_all(both, 'resp', 0, 0, tiled=True)  14.4 us
    unnamed x16, local copies, waits for them, and re-layouts  7.2 us
    all_to_all x1, waiting for transfers between devices, body(): lax.all_to_all(partial.reshape(pairs, 2 * own, 2 * width), 'resp', 0, 0,...  5.88 us
    ppermute x4, waiting for transfers between devices, swap(): return lax.ppermute(x, axis, [(i, i ^ bit) for i in range(count)])  5 us
    all_to_all x1, starting transfers between devices, body(): lax.all_to_all(partial.reshape(pairs, 2 * own, 2 * width), 'resp', 0, 0,...  3.32 us
    pallas_call x1, Pallas kernels, body(): pl.pallas_call(attention_kernel, out_shape=pltpu.VMEM((tokens, 2 * width)...  2.58 us
    ppermute x4, starting transfers between devices, swap(): return lax.ppermute(x, axis, [(i, i ^ bit) for i in range(count)])  1.87 us
    pallas_call x1, Pallas kernels, body(): pl.pallas_call(last_projection_kernel, out_shape=[pltpu.VMEM(block, jnp.b...  1.26 us
  transfers between devices with their start and end apart: 5, of which 3 were waited for; matrix products, arithmetic and copies ran while one was open for 0% of the time, Pallas kernels for 4%

profile of v19, /device:TPU:0, one launch (start us, length us, event | category | flops | bytes accessed | tf_op | source)
XLA Modules:
  0.0 45.1 jit_solution(4319907062609973605)
XLA Ops:
  0.6 0.0 copy-start.5
  0.6 0.0 copy-start.4
  0.7 0.0 copy-start.7
  0.7 0.0 copy-start.6
  1.5 0.0 copy-done.5
  1.5 0.0 copy-done.4
  1.5 14.4 %all_to_all.10 = bf16[8,16,512]{2,1,0:T(8,128)(2,1)S(1)} all-to-all(bf16[8,16,512]{2,1,0:T(8,128)(2,1)S(1)} %join.1), channel_id=1, replica_groups=mesh['resp'=8,'head'=4] {'resp'}, dimensions={0} | all-to-all | bytes 262144 | tf_op jit(solution)/shard_map/all_to_all | solution.py:163
  15.9 0.0 copy-done.7
  15.9 0.0 copy-done.6
  15.9 2.6 %attention.1 = bf16[128,512]{1,0:T(8,128)(2,1)} custom-call(f32[1,8,256]{2,1,0:T(8,128)S(1)} %mask.1.live_ref, bf16[128,512]{1,0:T(8,128)(2,1)S(1)} %bitcast.2, bf16[256,2048]{1,0:T(8,128)(2,1)S(1)} %copy-done.6, bf16[256,2048]{1,0:T(8,128)(2,1)S(1)} %copy-done.7), custom_call_target="tpu_custom_call" | custom-call | flops 4294967296 | bytes 2293760 | tf_op jit(solution)/shard_map/attention/pallas_call | solution.py:168
  18.5 3.3 %all-to-all-start.1 = ((bf16[4,32,512]{2,1,0:T(8,128)(2,1)}), bf16[4,32,512]{2,1,0:T(8,128)(2,1)S(1)}, u32[]{:S(2)}, u32[]{:S(2)}) async-start(bf16[4,32,512]{2,1,0:T(8,128)(2,1)} %bitcast.1), calls=%async_computation.1 | async-start | bytes 262144 | tf_op jit(solution)/shard_map/all_to_all | solution.py:189
  21.8 5.9 %all-to-all-done.1 = bf16[4,32,512]{2,1,0:T(8,128)(2,1)S(1)} async-done(((bf16[4,32,512]{2,1,0:T(8,128)(2,1)}), bf16[4,32,512]{2,1,0:T(8,128)(2,1)S(1)}, u32[]{:S(2)}, u32[]{:S(2)}) %all-to-all-start.1) | async-done | bytes 131104 | tf_op jit(solution)/shard_map/all_to_all | solution.py:189
  27.8 0.3 collective-permute-start
  28.0 3.5 %collective-permute-done.got_ref = bf16[16,512]{1,0:T(8,128)(2,1)S(1)} collective-permute-done((bf16[16,512]{1,0:T(8,128)(2,1)S(1)}, bf16[16,512]{1,0:T(8,128)(2,1)S(1)}, u32[]{:S(2)}, u32[]{:S(2)}) %collective-permute-start) | collective-permute-done | bytes 16416 | tf_op jit(solution)/shard_map/ppermute | solution.py:137
  31.6 0.0 copy-start
  31.6 2.2 %copy-done = bf16[8192,256]{1,0:T(8,128)(2,1)S(1)} copy-done((bf16[8192,256]{1,0:T(8,128)(2,1)S(1)}, bf16[8192,256]{1,0:T(8,128)(2,1)}, u32[]{:S(2)}) %copy-start) | copy-done | bytes 4194328
  33.7 0.0 copy-start.2
  33.8 2.2 %copy-done.2 = bf16[8192,256]{1,0:T(8,128)(2,1)S(1)} copy-done((bf16[8192,256]{1,0:T(8,128)(2,1)S(1)}, bf16[8192,256]{1,0:T(8,128)(2,1)}, u32[]{:S(2)}) %copy-start.2) | copy-done | bytes 4194328
  35.9 0.0 copy-start.1
  35.9 0.0 copy-start.3
  35.9 0.6 %projection_other_core.1 = (bf16[16,512]{1,0:T(8,128)(2,1)S(1)}, bf16[16,2048]{1,0:T(8,128)(2,1)S(1)}) custom-call(f32[16,512]{1,0:T(8,128)S(1)} %slice_select_fusion.keep_ref, bf16[16,512]{1,0:T(8,128)(2,1)S(1)} %collective-permute-done.got_ref, bf16[8192,256]{1,0:T(8,128)(2,1)S(1)} %copy-done, bf16[8192,256]{1,0:T(8,128)(2,1)S(1)} %copy-done.2), custom_call_target="tpu_custom_call" | custom-call | tf_op jit(solution)/shard_map/projection_other_core/pallas_call | solution.py:204
  36.6 0.0 collective-permute-start.1
  36.6 1.5 %copy-done.1 = bf16[8192,256]{1,0:T(8,128)(2,1)S(1)} copy-done((bf16[8192,256]{1,0:T(8,128)(2,1)S(1)}, bf16[8192,256]{1,0:T(8,128)(2,1)}, u32[]{:S(2)}) %copy-start.1) | copy-done | bytes 4194328
  38.1 1.3 %copy-done.3 = bf16[8192,256]{1,0:T(8,128)(2,1)S(1)} copy-done((bf16[8192,256]{1,0:T(8,128)(2,1)S(1)}, bf16[8192,256]{1,0:T(8,128)(2,1)}, u32[]{:S(2)}) %copy-start.3) | copy-done | bytes 4194328
  39.4 0.6 %projection_other_y.1 = f32[16,2048]{1,0:T(8,128)S(1)} custom-call(bf16[16,512]{1,0:T(8,128)(2,1)S(1)} %get-tuple-element.9.low_ref, bf16[8192,256]{1,0:T(8,128)(2,1)S(1)} %copy-done.1, bf16[8192,256]{1,0:T(8,128)(2,1)S(1)} %copy-done.3), custom_call_target="tpu_custom_call" | custom-call | flops 33554432 | bytes 2097152 | tf_op jit(solution)/shard_map/projection_other_y/pallas_call | solution.py:218
  40.0 0.0 collective-permute-done.1
  40.1 1.6 %collective-permute-start.2 = (bf16[16,2048]{1,0:T(8,128)(2,1)S(1)}, bf16[16,2048]{1,0:T(8,128)(2,1)S(1)}, u32[]{:S(2)}, u32[]{:S(2)}) collective-permute-start(bf16[16,2048]{1,0:T(8,128)(2,1)S(1)} %add_convert_fusion.after), channel_id=1, source_target_pairs={{0,2},{1,3},{2,0},{3,1},{4,6},{5,7},{6,4},{7,5},{8,10},{9,11},{10,... | collective-permute-start | bytes 196616 | tf_op jit(solution)/shard_map/ppermute | solution.py:137
  41.7 1.3 %projection_this_y.1 = (bf16[16,2048]{1,0:T(8,128)(2,1)S(1)}, f32[16,2048]{1,0:T(8,128)S(1)}, bf16[16,256]{1,0:T(8,128)(2,1)}, bf16[16,256]{1,0:T(8,128)(2,1)}) custom-call(bf16[16,512]{1,0:T(8,128)(2,1)S(1)} %get-tuple-element.9.low_ref, bf16[8192,256]{1,0:T(8,128)(2,1)S(1)} %copy-done.1, bf16[8192,256]{1,0:T(8,128)(2,1)S(1)} %copy-done.3, ...), custom_call_target="tpu_custom_call" | custom-call | flops 33554432 | bytes 2097152 | tf_op jit(solution)/shard_map/projection_this_y/pallas_call | solution.py:229
  42.9 0.0 collective-permute-start.3
  42.9 1.5 %collective-permute-done.2 = bf16[16,2048]{1,0:T(8,128)(2,1)S(1)} collective-permute-done((bf16[16,2048]{1,0:T(8,128)(2,1)S(1)}, bf16[16,2048]{1,0:T(8,128)(2,1)S(1)}, u32[]{:S(2)}, u32[]{:S(2)}) %collective-permute-start.2) | collective-permute-done | bytes 65568 | tf_op jit(solution)/shard_map/ppermute | solution.py:137
  44.4 0.0 collective-permute-done.3.got_ref
  44.4 0.6 %last_sum.1 = bf16[16,2048]{1,0:T(8,128)(2,1)} custom-call(f32[16,2048]{1,0:T(8,128)S(1)} %convert_add_fusion.total_ref, bf16[16,2048]{1,0:T(8,128)(2,1)S(1)} %collective-permute-done.3.got_ref), custom_call_target="tpu_custom_call" | custom-call | tf_op jit(solution)/shard_map/last_sum/pallas_call | solution.py:244
  (7 shorter events, 0.1 us)
Async XLA Ops:
  0.6 0.8 %copy-start.5 = (bf16[16,256]{1,0:T(8,128)(2,1)S(1)}, bf16[16,256]{1,0:T(8,128)(2,1)}, u32[]{:S(2)}) copy-start(bf16[16,256]{1,0:T(8,128)(2,1)} %v_ref.1) | copy-start | bytes 24580
  0.6 0.8 %copy-start.4 = (bf16[16,256]{1,0:T(8,128)(2,1)S(1)}, bf16[16,256]{1,0:T(8,128)(2,1)}, u32[]{:S(2)}) copy-start(bf16[16,256]{1,0:T(8,128)(2,1)} %k_ref.1) | copy-start | bytes 24580
  0.7 15.3 %copy-start.7 = (bf16[256,2048]{1,0:T(8,128)(2,1)S(1)}, bf16[256,2048]{1,0:T(8,128)(2,1)}, u32[]{:S(2)}) copy-start(bf16[256,2048]{1,0:T(8,128)(2,1)} %g_ref.1) | copy-start | bytes 3145732
  0.7 15.3 %copy-start.6 = (bf16[256,2048]{1,0:T(8,128)(2,1)S(1)}, bf16[256,2048]{1,0:T(8,128)(2,1)}, u32[]{:S(2)}) copy-start(bf16[256,2048]{1,0:T(8,128)(2,1)} %q_ref.1) | copy-start | bytes 3145732
  18.5 9.2 %all-to-all-start.1 = ((bf16[4,32,512]{2,1,0:T(8,128)(2,1)}), bf16[4,32,512]{2,1,0:T(8,128)(2,1)S(1)}, u32[]{:S(2)}, u32[]{:S(2)}) async-start(bf16[4,32,512]{2,1,0:T(8,128)(2,1)} %bitcast.1), calls=%async_computation.1 | async-start | bytes 262144 | tf_op jit(solution)/shard_map/all_to_all | solution.py:189
  27.8 3.8 %collective-permute-start = (bf16[16,512]{1,0:T(8,128)(2,1)S(1)}, bf16[16,512]{1,0:T(8,128)(2,1)S(1)}, u32[]{:S(2)}, u32[]{:S(2)}) collective-permute-start(bf16[16,512]{1,0:T(8,128)(2,1)S(1)} %select_convert_fusion), channel_id=1, source_target_pairs={{0,4},{4,0},{8,12},{12,8},{16,20},{20,16},{24,28},{28,24},{1,5},{5... | collective-permute-start | bytes 49160 | tf_op jit(solution)/shard_map/ppermute | solution.py:137
  31.6 2.2 %copy-start = (bf16[8192,256]{1,0:T(8,128)(2,1)S(1)}, bf16[8192,256]{1,0:T(8,128)(2,1)}, u32[]{:S(2)}) copy-start(bf16[8192,256]{1,0:T(8,128)(2,1)} %kw_ref.5) | copy-start | bytes 12582916
  33.7 2.2 %copy-start.2 = (bf16[8192,256]{1,0:T(8,128)(2,1)S(1)}, bf16[8192,256]{1,0:T(8,128)(2,1)}, u32[]{:S(2)}) copy-start(bf16[8192,256]{1,0:T(8,128)(2,1)} %vw_ref.5) | copy-start | bytes 12582916
  35.9 2.2 %copy-start.1 = (bf16[8192,256]{1,0:T(8,128)(2,1)S(1)}, bf16[8192,256]{1,0:T(8,128)(2,1)}, u32[]{:S(2)}) copy-start(bf16[8192,256]{1,0:T(8,128)(2,1)} %kw_ref.5) | copy-start | bytes 12582916
  35.9 3.5 %copy-start.3 = (bf16[8192,256]{1,0:T(8,128)(2,1)S(1)}, bf16[8192,256]{1,0:T(8,128)(2,1)}, u32[]{:S(2)}) copy-start(bf16[8192,256]{1,0:T(8,128)(2,1)} %vw_ref.5) | copy-start | bytes 12582916
  36.6 3.5 %collective-permute-start.1 = (bf16[16,2048]{1,0:T(8,128)(2,1)S(1)}, bf16[16,2048]{1,0:T(8,128)(2,1)S(1)}, u32[]{:S(2)}, u32[]{:S(2)}) collective-permute-start(bf16[16,2048]{1,0:T(8,128)(2,1)S(1)} %get-tuple-element.10), channel_id=1, source_target_pairs={{0,1},{1,0},{2,3},{3,2},{4,5},{5,4},{6,7},{7,6},{8,9},{9,8},{10,11... | collective-permute-start | bytes 196616 | tf_op jit(solution)/shard_map/ppermute | solution.py:137
  40.1 4.3 %collective-permute-start.2 = (bf16[16,2048]{1,0:T(8,128)(2,1)S(1)}, bf16[16,2048]{1,0:T(8,128)(2,1)S(1)}, u32[]{:S(2)}, u32[]{:S(2)}) collective-permute-start(bf16[16,2048]{1,0:T(8,128)(2,1)S(1)} %add_convert_fusion.after), channel_id=1, source_target_pairs={{0,2},{1,3},{2,0},{3,1},{4,6},{5,7},{6,4},{7,5},{8,10},{9,11},{10,... | collective-permute-start | bytes 196616 | tf_op jit(solution)/shard_map/ppermute | solution.py:137
  42.9 1.5 %collective-permute-start.3 = (bf16[16,2048]{1,0:T(8,128)(2,1)S(1)}, bf16[16,2048]{1,0:T(8,128)(2,1)S(1)}, u32[]{:S(2)}, u32[]{:S(2)}) collective-permute-start(bf16[16,2048]{1,0:T(8,128)(2,1)S(1)} %get-tuple-element.14), channel_id=1, source_target_pairs={{0,1},{1,0},{2,3},{3,2},{4,5},{5,4},{6,7},{7,6},{8,9},{9,8},{10,11... | collective-permute-start | bytes 196616 | tf_op jit(solution)/shard_map/ppermute | solution.py:137

commit v20 on v18

--- a/solution.py
+++ b/solution.py
@@ -28,9 +28,8 @@
         out_ref[i, :, width:] = v_ref[...]
 
 
-def attention_kernel(live_ref, kv_ref, q_ref, g_ref, out_ref, blocks_ref, weights_ref):
+def attention_kernel(live_ref, kv_ref, q_ref, g_ref, out_ref, probs_ref, dscores_ref):
     scale = HD ** (-0.5)
-    tokens = kv_ref.shape[0]
     width = kv_ref.shape[1] // 2
     kv_local = width // HD
     parts = q_ref.shape[0] // LEN
@@ -50,15 +49,14 @@
         ]
         return jnp.concatenate(heads, axis=0)
 
-    blocks_ref[...] = jnp.zeros_like(blocks_ref)
-    for k in range(kv_local):
-        blocks_ref[k, :tokens, :HD] = kv_ref[:, k * HD : (k + 1) * HD]
-        blocks_ref[k, tokens:, HD:] = kv_ref[:, width + k * HD : width + (k + 1) * HD]
-
     def products(unit):
-        both = jnp.concatenate([stack(q_ref, unit), stack(g_ref, unit)], axis=1)
-        out = lax.dot_general(blocks_ref[unit[0]], both, NT, preferred_element_type=jnp.float32)
-        return out[:tokens], out[tokens:]
+        k = unit[0]
+        keys = kv_ref[:, k * HD : (k + 1) * HD]
+        values = kv_ref[:, width + k * HD : width + (k + 1) * HD]
+        return (
+            lax.dot_general(keys, stack(q_ref, unit), NT, preferred_element_type=jnp.float32),
+            lax.dot_general(values, stack(g_ref, unit), NT, preferred_element_type=jnp.float32),
+        )
 
     following = products(units[0])
     for i, unit in enumerate(units):
@@ -76,20 +74,15 @@
         probs = expo * factor
         mine = [u for u in units if u[0] == k]
         cols = pl.ds(mine.index(unit) * UNIT * LEN, UNIT * LEN)
-        weights_ref[k, :tokens, cols] = probs.astype(jnp.bfloat16)
-        weights_ref[k, tokens:, cols] = (probs * (dprobs - delta)).astype(jnp.bfloat16)
+        probs_ref[k, :, cols] = probs.astype(jnp.bfloat16)
+        dscores_ref[k, :, cols] = (probs * (dprobs - delta)).astype(jnp.bfloat16)
         if unit == mine[-1]:
-            rows = [
-                jnp.concatenate([stack(g_ref, u), stack(q_ref, u)], axis=1) for u in mine
-            ]
-            out = jnp.dot(
-                weights_ref[k], jnp.concatenate(rows, axis=0), preferred_element_type=jnp.float32
-            )
-            grad_k = out[tokens:, HD:] * scale
+            q_all = jnp.concatenate([stack(q_ref, u) for u in mine], axis=0)
+            g_all = jnp.concatenate([stack(g_ref, u) for u in mine], axis=0)
+            grad_k = jnp.dot(dscores_ref[k], q_all, preferred_element_type=jnp.float32) * scale
+            grad_v = jnp.dot(probs_ref[k], g_all, preferred_element_type=jnp.float32)
             out_ref[:, k * HD : (k + 1) * HD] = grad_k.astype(out_ref.dtype)
-            out_ref[:, width + k * HD : width + (k + 1) * HD] = out[:tokens, :HD].astype(
-                out_ref.dtype
-            )
+            out_ref[:, width + k * HD : width + (k + 1) * HD] = grad_v.astype(out_ref.dtype)
 
 
 def project(low, kw_ref, vw_ref, owner, features):
@@ -160,6 +153,7 @@
         in_specs=[pl.BlockSpec(memory_space=pl.ANY)] + [vmem] * 2,
         out_specs=vmem,
         compiler_params=params,
+        cost_estimate=pl.CostEstimate(flops=1600000000, transcendentals=0, bytes_accessed=0),
         name="join",
     )(live, prefix_keys, prefix_values)
     both = lax.all_to_all(both, "resp", 0, 0, tiled=True).reshape(resp * own, 2 * width)
@@ -173,8 +167,8 @@
         in_specs=[vmem] * 4,
         out_specs=vmem,
         scratch_shapes=[
-            pltpu.VMEM((kv_local, 2 * tokens, 2 * HD), jnp.bfloat16),
-            pltpu.VMEM((kv_local, 2 * tokens, depth), jnp.bfloat16),
+            pltpu.VMEM((kv_local, tokens, depth), jnp.bfloat16),
+            pltpu.VMEM((kv_local, tokens, depth), jnp.bfloat16),
         ],
         compiler_params=pltpu.CompilerParams(
             vmem_limit_bytes=(8 << 20) + 8 * kv_local * tokens * depth

time: 34.9 us -> 35 us (level)
  no operation moved by 1% of the time
where the time goes in v20:
time: 35 us; the launch traced here: 34.8 us
  blocking collectives  24.4 us (70%)
  Pallas kernels  5.23 us (15%)
  waiting for transfers between devices  2.11 us (6%)
  starting transfers between devices  1.57 us (4%)
  between operations  1.39 us (4%)
    all_to_all x1, blocking collectives, body(): lax.all_to_all(both, 'resp', 0, 0, tiled=True)  14.5 us
    all_to_all x1, blocking collectives, body(): lax.all_to_all(partial.reshape(resp, own, 2 * width), 'resp', 0, 0, tiled...  9.87 us
    ppermute x3, waiting for transfers between devices, swap(): return lax.ppermute(x, axis, [(i, i ^ bit) for i in range(count)])  2.11 us
    pallas_call x1, Pallas kernels, body(): pl.pallas_call(attention_kernel, out_shape=pltpu.VMEM((tokens, 2 * width)...  2.01 us
    ppermute x3, starting transfers between devices, swap(): return lax.ppermute(x, axis, [(i, i ^ bit) for i in range(count)])  1.57 us
    pallas_call x1, Pallas kernels, body(): pl.pallas_call(last_projection_kernel, out_shape=[pltpu.VMEM(block, jnp.b...  1.26 us
  transfers between devices with their start and end apart: 3, of which 2 were waited for; matrix products, arithmetic and copies ran while one was open for 0% of the time, Pallas kernels for 6%

profile of v20, /device:TPU:0, one launch (start us, length us, event | category | flops | bytes accessed | tf_op | source)
XLA Modules:
  0.0 34.8 jit_solution(15644310872094396517)
XLA Ops:
  0.6 0.0 copy-start.5
  0.6 0.0 copy-start.4
  1.3 0.0 copy-done.5
  1.3 0.0 copy-done.4
  1.3 0.0 copy-start.2
  1.4 0.0 copy-start.3
  1.4 14.5 %all_to_all.10 = bf16[8,16,512]{2,1,0:T(8,128)(2,1)S(1)} all-to-all(bf16[8,16,512]{2,1,0:T(8,128)(2,1)S(1)} %join.1), channel_id=1, replica_groups=mesh['resp'=8,'head'=4] {'resp'}, dimensions={0} | all-to-all | bytes 262144 | tf_op jit(solution)/shard_map/all_to_all | solution.py:159
  15.9 0.0 copy-done.2
  15.9 0.0 copy-done.3
  15.9 0.0 copy-start
  15.9 0.0 copy-start.1
  15.9 2.0 %attention.1 = bf16[128,512]{1,0:T(8,128)(2,1)S(1)} custom-call(f32[1,8,256]{2,1,0:T(8,128)S(1)} %mask.1.live_ref, bf16[128,512]{1,0:T(8,128)(2,1)S(1)} %bitcast.2, bf16[256,2048]{1,0:T(8,128)(2,1)S(1)} %copy-done.2, bf16[256,2048]{1,0:T(8,128)(2,1)S(1)} %copy-done.3), custom_call_target="tpu_custom_call" | custom-call | flops 4294967296 | bytes 2293760 | tf_op jit(solution)/shard_map/attention/pallas_call | solution.py:164
  17.9 9.9 %all_to_all.11.parts_ref = bf16[8,16,512]{2,1,0:T(8,128)(2,1)S(1)} all-to-all(bf16[8,16,512]{2,1,0:T(8,128)(2,1)S(1)} %bitcast.3), channel_id=1, replica_groups=mesh['resp'=8,'head'=4] {'resp'}, dimensions={0} | all-to-all | bytes 262144 | tf_op jit(solution)/shard_map/all_to_all | solution.py:184
  27.8 0.0 copy-done
  27.8 0.0 copy-done.1
  27.8 0.6 %projection_other_core.1 = (bf16[16,512]{1,0:T(8,128)(2,1)S(1)}, bf16[16,2048]{1,0:T(8,128)(2,1)S(1)}) custom-call(bf16[8,16,512]{2,1,0:T(8,128)(2,1)S(1)} %all_to_all.11.parts_ref, bf16[8192,256]{1,0:T(8,128)(2,1)S(1)} %copy-done, bf16[8192,256]{1,0:T(8,128)(2,1)S(1)} %copy-done.1), custom_call_target="tpu_custom_call" | custom-call | tf_op jit(solution)/shard_map/projection_other_core/pallas_call | solution.py:189
  28.5 0.0 collective-permute-start
  28.5 0.7 %projection_other_y.1 = f32[16,2048]{1,0:T(8,128)S(1)} custom-call(bf16[16,512]{1,0:T(8,128)(2,1)S(1)} %get-tuple-element.9.low_ref, bf16[8192,256]{1,0:T(8,128)(2,1)S(1)} %copy-done, bf16[8192,256]{1,0:T(8,128)(2,1)S(1)} %copy-done.1), custom_call_target="tpu_custom_call" | custom-call | flops 33554432 | bytes 2097152 | tf_op jit(solution)/shard_map/projection_other_y/pallas_call | solution.py:203
  29.1 0.6 %collective-permute-done = bf16[16,2048]{1,0:T(8,128)(2,1)S(1)} collective-permute-done((bf16[16,2048]{1,0:T(8,128)(2,1)S(1)}, bf16[16,2048]{1,0:T(8,128)(2,1)S(1)}, u32[]{:S(2)}, u32[]{:S(2)}) %collective-permute-start) | collective-permute-done | bytes 65568 | tf_op jit(solution)/shard_map/ppermute | solution.py:132
  29.8 1.6 %collective-permute-start.1 = (bf16[16,2048]{1,0:T(8,128)(2,1)S(1)}, bf16[16,2048]{1,0:T(8,128)(2,1)S(1)}, u32[]{:S(2)}, u32[]{:S(2)}) collective-permute-start(bf16[16,2048]{1,0:T(8,128)(2,1)S(1)} %add_convert_fusion.after), channel_id=1, source_target_pairs={{0,2},{1,3},{2,0},{3,1},{4,6},{5,7},{6,4},{7,5},{8,10},{9,11},{10,... | collective-permute-start | bytes 196616 | tf_op jit(solution)/shard_map/ppermute | solution.py:132
  31.3 1.3 %projection_this_y.1 = (bf16[16,2048]{1,0:T(8,128)(2,1)S(1)}, f32[16,2048]{1,0:T(8,128)S(1)}, bf16[16,256]{1,0:T(8,128)(2,1)}, bf16[16,256]{1,0:T(8,128)(2,1)}) custom-call(bf16[16,512]{1,0:T(8,128)(2,1)S(1)} %get-tuple-element.9.low_ref, bf16[8192,256]{1,0:T(8,128)(2,1)S(1)} %copy-done, bf16[8192,256]{1,0:T(8,128)(2,1)S(1)} %copy-done.1, ...), custom_call_target="tpu_custom_call" | custom-call | flops 33554432 | bytes 2097152 | tf_op jit(solution)/shard_map/projection_this_y/pallas_call | solution.py:214
  32.6 0.0 collective-permute-start.2
  32.6 1.5 %collective-permute-done.1 = bf16[16,2048]{1,0:T(8,128)(2,1)S(1)} collective-permute-done((bf16[16,2048]{1,0:T(8,128)(2,1)S(1)}, bf16[16,2048]{1,0:T(8,128)(2,1)S(1)}, u32[]{:S(2)}, u32[]{:S(2)}) %collective-permute-start.1) | collective-permute-done | bytes 65568 | tf_op jit(solution)/shard_map/ppermute | solution.py:132
  34.1 0.0 collective-permute-done.2.got_ref
  34.1 0.6 %last_sum.1 = bf16[16,2048]{1,0:T(8,128)(2,1)} custom-call(f32[16,2048]{1,0:T(8,128)S(1)} %convert_add_fusion.total_ref, bf16[16,2048]{1,0:T(8,128)(2,1)S(1)} %collective-permute-done.2.got_ref), custom_call_target="tpu_custom_call" | custom-call | tf_op jit(solution)/shard_map/last_sum/pallas_call | solution.py:229
  (4 shorter events, 0.0 us)
Async XLA Ops:
  0.6 0.7 %copy-start.5 = (bf16[16,256]{1,0:T(8,128)(2,1)S(1)}, bf16[16,256]{1,0:T(8,128)(2,1)}, u32[]{:S(2)}) copy-start(bf16[16,256]{1,0:T(8,128)(2,1)} %v_ref.1) | copy-start | bytes 24580
  0.6 0.7 %copy-start.4 = (bf16[16,256]{1,0:T(8,128)(2,1)S(1)}, bf16[16,256]{1,0:T(8,128)(2,1)}, u32[]{:S(2)}) copy-start(bf16[16,256]{1,0:T(8,128)(2,1)} %k_ref.1) | copy-start | bytes 24580
  1.3 14.6 %copy-start.2 = (bf16[256,2048]{1,0:T(8,128)(2,1)S(1)}, bf16[256,2048]{1,0:T(8,128)(2,1)}, u32[]{:S(2)}) copy-start(bf16[256,2048]{1,0:T(8,128)(2,1)} %q_ref.1) | copy-start | bytes 3145732
  1.4 14.6 %copy-start.3 = (bf16[256,2048]{1,0:T(8,128)(2,1)S(1)}, bf16[256,2048]{1,0:T(8,128)(2,1)}, u32[]{:S(2)}) copy-start(bf16[256,2048]{1,0:T(8,128)(2,1)} %g_ref.1) | copy-start | bytes 3145732
  15.9 11.9 %copy-start = (bf16[8192,256]{1,0:T(8,128)(2,1)S(1)}, bf16[8192,256]{1,0:T(8,128)(2,1)}, u32[]{:S(2)}) copy-start(bf16[8192,256]{1,0:T(8,128)(2,1)} %kw_ref.5) | copy-start | bytes 12582916
  15.9 11.9 %copy-start.1 = (bf16[8192,256]{1,0:T(8,128)(2,1)S(1)}, bf16[8192,256]{1,0:T(8,128)(2,1)}, u32[]{:S(2)}) copy-start(bf16[8192,256]{1,0:T(8,128)(2,1)} %vw_ref.5) | copy-start | bytes 12582916
  28.5 1.3 %collective-permute-start = (bf16[16,2048]{1,0:T(8,128)(2,1)S(1)}, bf16[16,2048]{1,0:T(8,128)(2,1)S(1)}, u32[]{:S(2)}, u32[]{:S(2)}) collective-permute-start(bf16[16,2048]{1,0:T(8,128)(2,1)S(1)} %get-tuple-element.10), channel_id=1, source_target_pairs={{0,1},{1,0},{2,3},{3,2},{4,5},{5,4},{6,7},{7,6},{8,9},{9,8},{10,11... | collective-permute-start | bytes 196616 | tf_op jit(solution)/shard_map/ppermute | solution.py:132
  29.8 4.3 %collective-permute-start.1 = (bf16[16,2048]{1,0:T(8,128)(2,1)S(1)}, bf16[16,2048]{1,0:T(8,128)(2,1)S(1)}, u32[]{:S(2)}, u32[]{:S(2)}) collective-permute-start(bf16[16,2048]{1,0:T(8,128)(2,1)S(1)} %add_convert_fusion.after), channel_id=1, source_target_pairs={{0,2},{1,3},{2,0},{3,1},{4,6},{5,7},{6,4},{7,5},{8,10},{9,11},{10,... | collective-permute-start | bytes 196616 | tf_op jit(solution)/shard_map/ppermute | solution.py:132
  32.6 1.5 %collective-permute-start.2 = (bf16[16,2048]{1,0:T(8,128)(2,1)S(1)}, bf16[16,2048]{1,0:T(8,128)(2,1)S(1)}, u32[]{:S(2)}, u32[]{:S(2)}) collective-permute-start(bf16[16,2048]{1,0:T(8,128)(2,1)S(1)} %get-tuple-element.14), channel_id=1, source_target_pairs={{0,1},{1,0},{2,3},{3,2},{4,5},{5,4},{6,7},{7,6},{8,9},{9,8},{10,11... | collective-permute-start | bytes 196616 | tf_op jit(solution)/shard_map/ppermute | solution.py:132

commit v21 on v18

--- a/solution.py
+++ b/solution.py
@@ -93,14 +93,9 @@
 
 
 def project(low, kw_ref, vw_ref, owner, features):
-    width = kw_ref.shape[1]
     rows = pl.ds(pl.multiple_of(owner * features, features), features)
-    out = lax.dot_general(
-        low[:, :width], kw_ref[rows, :], NT, preferred_element_type=jnp.float32
-    )
-    return out + lax.dot_general(
-        low[:, width:], vw_ref[rows, :], NT, preferred_element_type=jnp.float32
-    )
+    weights = jnp.concatenate([kw_ref[rows, :], vw_ref[rows, :]], axis=1)
+    return lax.dot_general(low, weights, NT, preferred_element_type=jnp.float32)
 
 
 def first_projection_kernel(parts_ref, kw_ref, vw_ref, low_ref, out_ref):

time: 34.9 us -> 34.9 us (level)
  no operation moved by 1% of the time
where the time goes in v21:
time: 34.9 us; the launch traced here: 34.7 us
  blocking collectives  24.3 us (70%)
  Pallas kernels  5.18 us (15%)
  waiting for transfers between devices  2.08 us (6%)
  starting transfers between devices  1.59 us (5%)
  between operations  1.52 us (4%)
    all_to_all x1, blocking collectives, body(): lax.all_to_all(both, 'resp', 0, 0, tiled=True)  14.4 us
    all_to_all x1, blocking collectives, body(): lax.all_to_all(partial.reshape(resp, own, 2 * width), 'resp', 0, 0, tiled...  9.87 us
    ppermute x3, waiting for transfers between devices, swap(): return lax.ppermute(x, axis, [(i, i ^ bit) for i in range(count)])  2.08 us
    pallas_call x1, Pallas kernels, body(): pl.pallas_call(attention_kernel, out_shape=pltpu.VMEM((tokens, 2 * width)...  1.94 us
    ppermute x3, starting transfers between devices, swap(): return lax.ppermute(x, axis, [(i, i ^ bit) for i in range(count)])  1.59 us
    pallas_call x1, Pallas kernels, body(): pl.pallas_call(last_projection_kernel, out_shape=[pltpu.VMEM(block, jnp.b...  1.27 us
  transfers between devices with their start and end apart: 3, of which 2 were waited for; matrix products, arithmetic and copies ran while one was open for 0% of the time, Pallas kernels for 6%

profile of v21, /device:TPU:0, one launch (start us, length us, event | category | flops | bytes accessed | tf_op | source)
XLA Modules:
  0.0 34.7 jit_solution(17301943336758001298)
XLA Ops:
  0.6 0.0 copy-start.3
  0.6 0.0 copy-start.2
  0.7 0.0 copy-start.5
  0.7 0.0 copy-start.4
  1.5 0.0 copy-done.3
  1.5 0.0 copy-done.2
  1.5 14.4 %all_to_all.10 = bf16[8,16,512]{2,1,0:T(8,128)(2,1)S(1)} all-to-all(bf16[8,16,512]{2,1,0:T(8,128)(2,1)S(1)} %join.1), channel_id=1, replica_groups=mesh['resp'=8,'head'=4] {'resp'}, dimensions={0} | all-to-all | bytes 262144 | tf_op jit(solution)/shard_map/all_to_all | solution.py:160
  15.9 0.0 copy-done.5
  15.9 0.0 copy-done.4
  15.9 0.0 copy-start
  15.9 0.0 copy-start.1
  15.9 1.9 %attention.1 = bf16[128,512]{1,0:T(8,128)(2,1)S(1)} custom-call(f32[1,8,256]{2,1,0:T(8,128)S(1)} %mask.1.live_ref, bf16[128,512]{1,0:T(8,128)(2,1)S(1)} %bitcast.2, bf16[256,2048]{1,0:T(8,128)(2,1)S(1)} %copy-done.4, bf16[256,2048]{1,0:T(8,128)(2,1)S(1)} %copy-done.5), custom_call_target="tpu_custom_call" | custom-call | flops 4294967296 | bytes 2293760 | tf_op jit(solution)/shard_map/attention/pallas_call | solution.py:165
  17.9 9.9 %all_to_all.11.parts_ref = bf16[8,16,512]{2,1,0:T(8,128)(2,1)S(1)} all-to-all(bf16[8,16,512]{2,1,0:T(8,128)(2,1)S(1)} %bitcast.3), channel_id=1, replica_groups=mesh['resp'=8,'head'=4] {'resp'}, dimensions={0} | all-to-all | bytes 262144 | tf_op jit(solution)/shard_map/all_to_all | solution.py:185
  27.7 0.0 copy-done
  27.7 0.0 copy-done.1
  27.7 0.7 %projection_other_core.1 = (bf16[16,512]{1,0:T(8,128)(2,1)S(1)}, bf16[16,2048]{1,0:T(8,128)(2,1)S(1)}) custom-call(bf16[8,16,512]{2,1,0:T(8,128)(2,1)S(1)} %all_to_all.11.parts_ref, bf16[8192,256]{1,0:T(8,128)(2,1)S(1)} %copy-done, bf16[8192,256]{1,0:T(8,128)(2,1)S(1)} %copy-done.1), custom_call_target="tpu_custom_call" | custom-call | tf_op jit(solution)/shard_map/projection_other_core/pallas_call | solution.py:190
  28.4 0.0 collective-permute-start
  28.4 0.7 %projection_other_y.1 = f32[16,2048]{1,0:T(8,128)S(1)} custom-call(bf16[16,512]{1,0:T(8,128)(2,1)S(1)} %get-tuple-element.9.low_ref, bf16[8192,256]{1,0:T(8,128)(2,1)S(1)} %copy-done, bf16[8192,256]{1,0:T(8,128)(2,1)S(1)} %copy-done.1), custom_call_target="tpu_custom_call" | custom-call | flops 33554432 | bytes 2097152 | tf_op jit(solution)/shard_map/projection_other_y/pallas_call | solution.py:204
  29.1 0.6 %collective-permute-done = bf16[16,2048]{1,0:T(8,128)(2,1)S(1)} collective-permute-done((bf16[16,2048]{1,0:T(8,128)(2,1)S(1)}, bf16[16,2048]{1,0:T(8,128)(2,1)S(1)}, u32[]{:S(2)}, u32[]{:S(2)}) %collective-permute-start) | collective-permute-done | bytes 65568 | tf_op jit(solution)/shard_map/ppermute | solution.py:134
  29.7 1.6 %collective-permute-start.1 = (bf16[16,2048]{1,0:T(8,128)(2,1)S(1)}, bf16[16,2048]{1,0:T(8,128)(2,1)S(1)}, u32[]{:S(2)}, u32[]{:S(2)}) collective-permute-start(bf16[16,2048]{1,0:T(8,128)(2,1)S(1)} %add_convert_fusion.after), channel_id=1, source_target_pairs={{0,2},{1,3},{2,0},{3,1},{4,6},{5,7},{6,4},{7,5},{8,10},{9,11},{10,... | collective-permute-start | bytes 196616 | tf_op jit(solution)/shard_map/ppermute | solution.py:134
  31.3 1.3 %projection_this_y.1 = (bf16[16,2048]{1,0:T(8,128)(2,1)S(1)}, f32[16,2048]{1,0:T(8,128)S(1)}, bf16[16,256]{1,0:T(8,128)(2,1)}, bf16[16,256]{1,0:T(8,128)(2,1)}) custom-call(bf16[16,512]{1,0:T(8,128)(2,1)S(1)} %get-tuple-element.9.low_ref, bf16[8192,256]{1,0:T(8,128)(2,1)S(1)} %copy-done, bf16[8192,256]{1,0:T(8,128)(2,1)S(1)} %copy-done.1, ...), custom_call_target="tpu_custom_call" | custom-call | flops 33554432 | bytes 2097152 | tf_op jit(solution)/shard_map/projection_this_y/pallas_call | solution.py:215
  32.5 0.0 collective-permute-start.2
  32.5 1.5 %collective-permute-done.1 = bf16[16,2048]{1,0:T(8,128)(2,1)S(1)} collective-permute-done((bf16[16,2048]{1,0:T(8,128)(2,1)S(1)}, bf16[16,2048]{1,0:T(8,128)(2,1)S(1)}, u32[]{:S(2)}, u32[]{:S(2)}) %collective-permute-start.1) | collective-permute-done | bytes 65568 | tf_op jit(solution)/shard_map/ppermute | solution.py:134
  34.0 0.0 collective-permute-done.2.got_ref
  34.0 0.6 %last_sum.1 = bf16[16,2048]{1,0:T(8,128)(2,1)} custom-call(f32[16,2048]{1,0:T(8,128)S(1)} %convert_add_fusion.total_ref, bf16[16,2048]{1,0:T(8,128)(2,1)S(1)} %collective-permute-done.2.got_ref), custom_call_target="tpu_custom_call" | custom-call | tf_op jit(solution)/shard_map/last_sum/pallas_call | solution.py:230
  (4 shorter events, 0.0 us)
Async XLA Ops:
  0.6 0.8 %copy-start.3 = (bf16[16,256]{1,0:T(8,128)(2,1)S(1)}, bf16[16,256]{1,0:T(8,128)(2,1)}, u32[]{:S(2)}) copy-start(bf16[16,256]{1,0:T(8,128)(2,1)} %v_ref.1) | copy-start | bytes 24580
  0.6 0.8 %copy-start.2 = (bf16[16,256]{1,0:T(8,128)(2,1)S(1)}, bf16[16,256]{1,0:T(8,128)(2,1)}, u32[]{:S(2)}) copy-start(bf16[16,256]{1,0:T(8,128)(2,1)} %k_ref.1) | copy-start | bytes 24580
  0.7 15.3 %copy-start.5 = (bf16[256,2048]{1,0:T(8,128)(2,1)S(1)}, bf16[256,2048]{1,0:T(8,128)(2,1)}, u32[]{:S(2)}) copy-start(bf16[256,2048]{1,0:T(8,128)(2,1)} %g_ref.1) | copy-start | bytes 3145732
  0.7 15.3 %copy-start.4 = (bf16[256,2048]{1,0:T(8,128)(2,1)S(1)}, bf16[256,2048]{1,0:T(8,128)(2,1)}, u32[]{:S(2)}) copy-start(bf16[256,2048]{1,0:T(8,128)(2,1)} %q_ref.1) | copy-start | bytes 3145732
  15.9 11.8 %copy-start = (bf16[8192,256]{1,0:T(8,128)(2,1)S(1)}, bf16[8192,256]{1,0:T(8,128)(2,1)}, u32[]{:S(2)}) copy-start(bf16[8192,256]{1,0:T(8,128)(2,1)} %kw_ref.5) | copy-start | bytes 12582916
  15.9 11.8 %copy-start.1 = (bf16[8192,256]{1,0:T(8,128)(2,1)S(1)}, bf16[8192,256]{1,0:T(8,128)(2,1)}, u32[]{:S(2)}) copy-start(bf16[8192,256]{1,0:T(8,128)(2,1)} %vw_ref.5) | copy-start | bytes 12582916
  28.4 1.3 %collective-permute-start = (bf16[16,2048]{1,0:T(8,128)(2,1)S(1)}, bf16[16,2048]{1,0:T(8,128)(2,1)S(1)}, u32[]{:S(2)}, u32[]{:S(2)}) collective-permute-start(bf16[16,2048]{1,0:T(8,128)(2,1)S(1)} %get-tuple-element.10), channel_id=1, source_target_pairs={{0,1},{1,0},{2,3},{3,2},{4,5},{5,4},{6,7},{7,6},{8,9},{9,8},{10,11... | collective-permute-start | bytes 196616 | tf_op jit(solution)/shard_map/ppermute | solution.py:134
  29.7 4.3 %collective-permute-start.1 = (bf16[16,2048]{1,0:T(8,128)(2,1)S(1)}, bf16[16,2048]{1,0:T(8,128)(2,1)S(1)}, u32[]{:S(2)}, u32[]{:S(2)}) collective-permute-start(bf16[16,2048]{1,0:T(8,128)(2,1)S(1)} %add_convert_fusion.after), channel_id=1, source_target_pairs={{0,2},{1,3},{2,0},{3,1},{4,6},{5,7},{6,4},{7,5},{8,10},{9,11},{10,... | collective-permute-start | bytes 196616 | tf_op jit(solution)/shard_map/ppermute | solution.py:134
  32.5 1.5 %collective-permute-start.2 = (bf16[16,2048]{1,0:T(8,128)(2,1)S(1)}, bf16[16,2048]{1,0:T(8,128)(2,1)S(1)}, u32[]{:S(2)}, u32[]{:S(2)}) collective-permute-start(bf16[16,2048]{1,0:T(8,128)(2,1)S(1)} %get-tuple-element.14), channel_id=1, source_target_pairs={{0,1},{1,0},{2,3},{3,2},{4,5},{5,4},{6,7},{7,6},{8,9},{9,8},{10,11... | collective-permute-start | bytes 196616 | tf_op jit(solution)/shard_map/ppermute | solution.py:134

commit v22 on v21

--- a/solution.py
+++ b/solution.py
@@ -10,7 +10,7 @@
 HD = 128
 LEN = 256
 NT = (((1,), (1,)), ((), ()))
-UNIT = 2
+UNIT = 1
 LOG2E = 1.4426950408889634
 
 

time: 34.9 us -> 35.2 us (level)
  no operation moved by 1% of the time
where the time goes in v22:
time: 35.2 us; the launch traced here: 35 us
  blocking collectives  24.3 us (69%)
  Pallas kernels  5.47 us (16%)
  waiting for transfers between devices  2.09 us (6%)
  starting transfers between devices  1.59 us (5%)
  between operations  1.52 us (4%)
    all_to_all x1, blocking collectives, body(): lax.all_to_all(both, 'resp', 0, 0, tiled=True)  14.4 us
    all_to_all x1, blocking collectives, body(): lax.all_to_all(partial.reshape(resp, own, 2 * width), 'resp', 0, 0, tiled...  9.87 us
    pallas_call x1, Pallas kernels, body(): pl.pallas_call(attention_kernel, out_shape=pltpu.VMEM((tokens, 2 * width)...  2.22 us
    ppermute x3, waiting for transfers between devices, swap(): return lax.ppermute(x, axis, [(i, i ^ bit) for i in range(count)])  2.09 us
    ppermute x3, starting transfers between devices, swap(): return lax.ppermute(x, axis, [(i, i ^ bit) for i in range(count)])  1.59 us
    pallas_call x1, Pallas kernels, body(): pl.pallas_call(last_projection_kernel, out_shape=[pltpu.VMEM(block, jnp.b...  1.27 us
  transfers between devices with their start and end apart: 3, of which 2 were waited for; matrix products, arithmetic and copies ran while one was open for 0% of the time, Pallas kernels for 6%

profile of v22, /device:TPU:0, one launch (start us, length us, event | category | flops | bytes accessed | tf_op | source)
XLA Modules:
  0.0 35.0 jit_solution(15589223714606542120)
XLA Ops:
  0.6 0.0 copy-start.3
  0.6 0.0 copy-start.2
  0.7 0.0 copy-start.5
  0.7 0.0 copy-start.4
  1.5 0.0 copy-done.3
  1.5 0.0 copy-done.2
  1.5 14.4 %all_to_all.10 = bf16[8,16,512]{2,1,0:T(8,128)(2,1)S(1)} all-to-all(bf16[8,16,512]{2,1,0:T(8,128)(2,1)S(1)} %join.1), channel_id=1, replica_groups=mesh['resp'=8,'head'=4] {'resp'}, dimensions={0} | all-to-all | bytes 262144 | tf_op jit(solution)/shard_map/all_to_all | solution.py:160
  15.9 0.0 copy-done.5
  15.9 0.0 copy-done.4
  15.9 0.0 copy-start
  15.9 0.0 copy-start.1
  15.9 2.2 %attention.1 = bf16[128,512]{1,0:T(8,128)(2,1)S(1)} custom-call(f32[1,8,256]{2,1,0:T(8,128)S(1)} %mask.1.live_ref, bf16[128,512]{1,0:T(8,128)(2,1)S(1)} %bitcast.2, bf16[256,2048]{1,0:T(8,128)(2,1)S(1)} %copy-done.4, bf16[256,2048]{1,0:T(8,128)(2,1)S(1)} %copy-done.5), custom_call_target="tpu_custom_call" | custom-call | flops 4294967296 | bytes 2293760 | tf_op jit(solution)/shard_map/attention/pallas_call | solution.py:165
  18.2 9.9 %all_to_all.11.parts_ref = bf16[8,16,512]{2,1,0:T(8,128)(2,1)S(1)} all-to-all(bf16[8,16,512]{2,1,0:T(8,128)(2,1)S(1)} %bitcast.3), channel_id=1, replica_groups=mesh['resp'=8,'head'=4] {'resp'}, dimensions={0} | all-to-all | bytes 262144 | tf_op jit(solution)/shard_map/all_to_all | solution.py:185
  28.0 0.0 copy-done
  28.0 0.0 copy-done.1
  28.0 0.7 %projection_other_core.1 = (bf16[16,512]{1,0:T(8,128)(2,1)S(1)}, bf16[16,2048]{1,0:T(8,128)(2,1)S(1)}) custom-call(bf16[8,16,512]{2,1,0:T(8,128)(2,1)S(1)} %all_to_all.11.parts_ref, bf16[8192,256]{1,0:T(8,128)(2,1)S(1)} %copy-done, bf16[8192,256]{1,0:T(8,128)(2,1)S(1)} %copy-done.1), custom_call_target="tpu_custom_call" | custom-call | tf_op jit(solution)/shard_map/projection_other_core/pallas_call | solution.py:190
  28.7 0.0 collective-permute-start
  28.7 0.7 %projection_other_y.1 = f32[16,2048]{1,0:T(8,128)S(1)} custom-call(bf16[16,512]{1,0:T(8,128)(2,1)S(1)} %get-tuple-element.9.low_ref, bf16[8192,256]{1,0:T(8,128)(2,1)S(1)} %copy-done, bf16[8192,256]{1,0:T(8,128)(2,1)S(1)} %copy-done.1), custom_call_target="tpu_custom_call" | custom-call | flops 33554432 | bytes 2097152 | tf_op jit(solution)/shard_map/projection_other_y/pallas_call | solution.py:204
  29.4 0.6 %collective-permute-done = bf16[16,2048]{1,0:T(8,128)(2,1)S(1)} collective-permute-done((bf16[16,2048]{1,0:T(8,128)(2,1)S(1)}, bf16[16,2048]{1,0:T(8,128)(2,1)S(1)}, u32[]{:S(2)}, u32[]{:S(2)}) %collective-permute-start) | collective-permute-done | bytes 65568 | tf_op jit(solution)/shard_map/ppermute | solution.py:134
  30.0 1.6 %collective-permute-start.1 = (bf16[16,2048]{1,0:T(8,128)(2,1)S(1)}, bf16[16,2048]{1,0:T(8,128)(2,1)S(1)}, u32[]{:S(2)}, u32[]{:S(2)}) collective-permute-start(bf16[16,2048]{1,0:T(8,128)(2,1)S(1)} %add_convert_fusion.after), channel_id=1, source_target_pairs={{0,2},{1,3},{2,0},{3,1},{4,6},{5,7},{6,4},{7,5},{8,10},{9,11},{10,... | collective-permute-start | bytes 196616 | tf_op jit(solution)/shard_map/ppermute | solution.py:134
  31.6 1.3 %projection_this_y.1 = (bf16[16,2048]{1,0:T(8,128)(2,1)S(1)}, f32[16,2048]{1,0:T(8,128)S(1)}, bf16[16,256]{1,0:T(8,128)(2,1)}, bf16[16,256]{1,0:T(8,128)(2,1)}) custom-call(bf16[16,512]{1,0:T(8,128)(2,1)S(1)} %get-tuple-element.9.low_ref, bf16[8192,256]{1,0:T(8,128)(2,1)S(1)} %copy-done, bf16[8192,256]{1,0:T(8,128)(2,1)S(1)} %copy-done.1, ...), custom_call_target="tpu_custom_call" | custom-call | flops 33554432 | bytes 2097152 | tf_op jit(solution)/shard_map/projection_this_y/pallas_call | solution.py:215
  32.8 0.0 collective-permute-start.2
  32.8 1.5 %collective-permute-done.1 = bf16[16,2048]{1,0:T(8,128)(2,1)S(1)} collective-permute-done((bf16[16,2048]{1,0:T(8,128)(2,1)S(1)}, bf16[16,2048]{1,0:T(8,128)(2,1)S(1)}, u32[]{:S(2)}, u32[]{:S(2)}) %collective-permute-start.1) | collective-permute-done | bytes 65568 | tf_op jit(solution)/shard_map/ppermute | solution.py:134
  34.3 0.0 collective-permute-done.2.got_ref
  34.3 0.6 %last_sum.1 = bf16[16,2048]{1,0:T(8,128)(2,1)} custom-call(f32[16,2048]{1,0:T(8,128)S(1)} %convert_add_fusion.total_ref, bf16[16,2048]{1,0:T(8,128)(2,1)S(1)} %collective-permute-done.2.got_ref), custom_call_target="tpu_custom_call" | custom-call | tf_op jit(solution)/shard_map/last_sum/pallas_call | solution.py:230
  (4 shorter events, 0.0 us)
Async XLA Ops:
  0.6 0.8 %copy-start.3 = (bf16[16,256]{1,0:T(8,128)(2,1)S(1)}, bf16[16,256]{1,0:T(8,128)(2,1)}, u32[]{:S(2)}) copy-start(bf16[16,256]{1,0:T(8,128)(2,1)} %v_ref.1) | copy-start | bytes 24580
  0.6 0.8 %copy-start.2 = (bf16[16,256]{1,0:T(8,128)(2,1)S(1)}, bf16[16,256]{1,0:T(8,128)(2,1)}, u32[]{:S(2)}) copy-start(bf16[16,256]{1,0:T(8,128)(2,1)} %k_ref.1) | copy-start | bytes 24580
  0.7 15.3 %copy-start.5 = (bf16[256,2048]{1,0:T(8,128)(2,1)S(1)}, bf16[256,2048]{1,0:T(8,128)(2,1)}, u32[]{:S(2)}) copy-start(bf16[256,2048]{1,0:T(8,128)(2,1)} %g_ref.1) | copy-start | bytes 3145732
  0.7 15.3 %copy-start.4 = (bf16[256,2048]{1,0:T(8,128)(2,1)S(1)}, bf16[256,2048]{1,0:T(8,128)(2,1)}, u32[]{:S(2)}) copy-start(bf16[256,2048]{1,0:T(8,128)(2,1)} %q_ref.1) | copy-start | bytes 3145732
  15.9 12.1 %copy-start = (bf16[8192,256]{1,0:T(8,128)(2,1)S(1)}, bf16[8192,256]{1,0:T(8,128)(2,1)}, u32[]{:S(2)}) copy-start(bf16[8192,256]{1,0:T(8,128)(2,1)} %kw_ref.5) | copy-start | bytes 12582916
  15.9 12.1 %copy-start.1 = (bf16[8192,256]{1,0:T(8,128)(2,1)S(1)}, bf16[8192,256]{1,0:T(8,128)(2,1)}, u32[]{:S(2)}) copy-start(bf16[8192,256]{1,0:T(8,128)(2,1)} %vw_ref.5) | copy-start | bytes 12582916
  28.7 1.3 %collective-permute-start = (bf16[16,2048]{1,0:T(8,128)(2,1)S(1)}, bf16[16,2048]{1,0:T(8,128)(2,1)S(1)}, u32[]{:S(2)}, u32[]{:S(2)}) collective-permute-start(bf16[16,2048]{1,0:T(8,128)(2,1)S(1)} %get-tuple-element.10), channel_id=1, source_target_pairs={{0,1},{1,0},{2,3},{3,2},{4,5},{5,4},{6,7},{7,6},{8,9},{9,8},{10,11... | collective-permute-start | bytes 196616 | tf_op jit(solution)/shard_map/ppermute | solution.py:134
  30.0 4.3 %collective-permute-start.1 = (bf16[16,2048]{1,0:T(8,128)(2,1)S(1)}, bf16[16,2048]{1,0:T(8,128)(2,1)S(1)}, u32[]{:S(2)}, u32[]{:S(2)}) collective-permute-start(bf16[16,2048]{1,0:T(8,128)(2,1)S(1)} %add_convert_fusion.after), channel_id=1, source_target_pairs={{0,2},{1,3},{2,0},{3,1},{4,6},{5,7},{6,4},{7,5},{8,10},{9,11},{10,... | collective-permute-start | bytes 196616 | tf_op jit(solution)/shard_map/ppermute | solution.py:134
  32.8 1.5 %collective-permute-start.2 = (bf16[16,2048]{1,0:T(8,128)(2,1)S(1)}, bf16[16,2048]{1,0:T(8,128)(2,1)S(1)}, u32[]{:S(2)}, u32[]{:S(2)}) collective-permute-start(bf16[16,2048]{1,0:T(8,128)(2,1)S(1)} %get-tuple-element.14), channel_id=1, source_target_pairs={{0,1},{1,0},{2,3},{3,2},{4,5},{5,4},{6,7},{7,6},{8,9},{9,8},{10,11... | collective-permute-start | bytes 196616 | tf_op jit(solution)/shard_map/ppermute | solution.py:134

commit v23 on v21

--- a/solution.py
+++ b/solution.py
@@ -58,18 +58,17 @@
     def products(unit):
         both = jnp.concatenate([stack(q_ref, unit), stack(g_ref, unit)], axis=1)
         out = lax.dot_general(blocks_ref[unit[0]], both, NT, preferred_element_type=jnp.float32)
-        return out[:tokens], out[tokens:]
-
-    following = products(units[0])
-    for i, unit in enumerate(units):
-        k, part, h = unit
-        scores, dprobs = following
-        if i + 1 < len(units):
-            following = products(units[i + 1])
-        top = jnp.max(scores, axis=0, keepdims=True)
+        scores = out[:tokens]
+        return scores, out[tokens:], jnp.max(scores, axis=0, keepdims=True)
+
+    def sums(scores, dprobs, top):
         expo = jnp.exp2((scores - top) * (scale * LOG2E))
         total = jnp.sum(expo, axis=0, keepdims=True)
         weighted = jnp.sum(expo * dprobs, axis=0, keepdims=True)
+        return expo, dprobs, total, weighted
+
+    def write(unit, expo, dprobs, total, weighted):
+        k, part, h = unit
         inverse = 1.0 / total
         delta = weighted * inverse
         factor = inverse * jnp.concatenate([live_ref[part, :1]] * UNIT, axis=1)
@@ -91,6 +90,15 @@
                 out_ref.dtype
             )
 
+    made, summed = {0: products(units[0])}, {}
+    for i in range(len(units)):
+        if i + 1 < len(units):
+            made[i + 1] = products(units[i + 1])
+        summed[i] = sums(*made.pop(i))
+        if i > 0:
+            write(units[i - 1], *summed.pop(i - 1))
+    write(units[-1], *summed.pop(len(units) - 1))
+
 
 def project(low, kw_ref, vw_ref, owner, features):
     rows = pl.ds(pl.multiple_of(owner * features, features), features)

time: 34.9 us -> 34.9 us (level)
  no operation moved by 1% of the time
where the time goes in v23:
time: 34.9 us; the launch traced here: 34.7 us
  blocking collectives  24.3 us (70%)
  Pallas kernels  5.19 us (15%)
  waiting for transfers between devices  2.08 us (6%)
  starting transfers between devices  1.6 us (5%)
  between operations  1.52 us (4%)
    all_to_all x1, blocking collectives, body(): lax.all_to_all(both, 'resp', 0, 0, tiled=True)  14.4 us
    all_to_all x1, blocking collectives, body(): lax.all_to_all(partial.reshape(resp, own, 2 * width), 'resp', 0, 0, tiled...  9.87 us
    ppermute x3, waiting for transfers between devices, swap(): return lax.ppermute(x, axis, [(i, i ^ bit) for i in range(count)])  2.08 us
    pallas_call x1, Pallas kernels, body(): pl.pallas_call(attention_kernel, out_shape=pltpu.VMEM((tokens, 2 * width)...  1.95 us
    ppermute x3, starting transfers between devices, swap(): return lax.ppermute(x, axis, [(i, i ^ bit) for i in range(count)])  1.6 us
    pallas_call x1, Pallas kernels, body(): pl.pallas_call(last_projection_kernel, out_shape=[pltpu.VMEM(block, jnp.b...  1.27 us
  transfers between devices with their start and end apart: 3, of which 2 were waited for; matrix products, arithmetic and copies ran while one was open for 0% of the time, Pallas kernels for 6%

profile of v23, /device:TPU:0, one launch (start us, length us, event | category | flops | bytes accessed | tf_op | source)
XLA Modules:
  0.0 34.7 jit_solution(15319863670190454472)
XLA Ops:
  0.6 0.0 copy-start.3
  0.6 0.0 copy-start.2
  0.7 0.0 copy-start.5
  0.7 0.0 copy-start.4
  1.5 0.0 copy-done.3
  1.5 0.0 copy-done.2
  1.5 14.4 %all_to_all.10 = bf16[8,16,512]{2,1,0:T(8,128)(2,1)S(1)} all-to-all(bf16[8,16,512]{2,1,0:T(8,128)(2,1)S(1)} %join.1), channel_id=1, replica_groups=mesh['resp'=8,'head'=4] {'resp'}, dimensions={0} | all-to-all | bytes 262144 | tf_op jit(solution)/shard_map/all_to_all | solution.py:168
  15.9 0.0 copy-done.5
  15.9 0.0 copy-done.4
  15.9 0.0 copy-start
  15.9 0.0 copy-start.1
  15.9 2.0 %attention.1 = bf16[128,512]{1,0:T(8,128)(2,1)S(1)} custom-call(f32[1,8,256]{2,1,0:T(8,128)S(1)} %mask.1.live_ref, bf16[128,512]{1,0:T(8,128)(2,1)S(1)} %bitcast.2, bf16[256,2048]{1,0:T(8,128)(2,1)S(1)} %copy-done.4, bf16[256,2048]{1,0:T(8,128)(2,1)S(1)} %copy-done.5), custom_call_target="tpu_custom_call" | custom-call | flops 4294967296 | bytes 2293760 | tf_op jit(solution)/shard_map/attention/pallas_call | solution.py:173
  17.9 9.9 %all_to_all.11.parts_ref = bf16[8,16,512]{2,1,0:T(8,128)(2,1)S(1)} all-to-all(bf16[8,16,512]{2,1,0:T(8,128)(2,1)S(1)} %bitcast.3), channel_id=1, replica_groups=mesh['resp'=8,'head'=4] {'resp'}, dimensions={0} | all-to-all | bytes 262144 | tf_op jit(solution)/shard_map/all_to_all | solution.py:193
  27.8 0.0 copy-done
  27.8 0.0 copy-done.1
  27.8 0.7 %projection_other_core.1 = (bf16[16,512]{1,0:T(8,128)(2,1)S(1)}, bf16[16,2048]{1,0:T(8,128)(2,1)S(1)}) custom-call(bf16[8,16,512]{2,1,0:T(8,128)(2,1)S(1)} %all_to_all.11.parts_ref, bf16[8192,256]{1,0:T(8,128)(2,1)S(1)} %copy-done, bf16[8192,256]{1,0:T(8,128)(2,1)S(1)} %copy-done.1), custom_call_target="tpu_custom_call" | custom-call | tf_op jit(solution)/shard_map/projection_other_core/pallas_call | solution.py:198
  28.4 0.0 collective-permute-start
  28.4 0.7 %projection_other_y.1 = f32[16,2048]{1,0:T(8,128)S(1)} custom-call(bf16[16,512]{1,0:T(8,128)(2,1)S(1)} %get-tuple-element.9.low_ref, bf16[8192,256]{1,0:T(8,128)(2,1)S(1)} %copy-done, bf16[8192,256]{1,0:T(8,128)(2,1)S(1)} %copy-done.1), custom_call_target="tpu_custom_call" | custom-call | flops 33554432 | bytes 2097152 | tf_op jit(solution)/shard_map/projection_other_y/pallas_call | solution.py:212
  29.1 0.6 %collective-permute-done = bf16[16,2048]{1,0:T(8,128)(2,1)S(1)} collective-permute-done((bf16[16,2048]{1,0:T(8,128)(2,1)S(1)}, bf16[16,2048]{1,0:T(8,128)(2,1)S(1)}, u32[]{:S(2)}, u32[]{:S(2)}) %collective-permute-start) | collective-permute-done | bytes 65568 | tf_op jit(solution)/shard_map/ppermute | solution.py:142
  29.7 1.6 %collective-permute-start.1 = (bf16[16,2048]{1,0:T(8,128)(2,1)S(1)}, bf16[16,2048]{1,0:T(8,128)(2,1)S(1)}, u32[]{:S(2)}, u32[]{:S(2)}) collective-permute-start(bf16[16,2048]{1,0:T(8,128)(2,1)S(1)} %add_convert_fusion.after), channel_id=1, source_target_pairs={{0,2},{1,3},{2,0},{3,1},{4,6},{5,7},{6,4},{7,5},{8,10},{9,11},{10,... | collective-permute-start | bytes 196616 | tf_op jit(solution)/shard_map/ppermute | solution.py:142
  31.3 1.3 %projection_this_y.1 = (bf16[16,2048]{1,0:T(8,128)(2,1)S(1)}, f32[16,2048]{1,0:T(8,128)S(1)}, bf16[16,256]{1,0:T(8,128)(2,1)}, bf16[16,256]{1,0:T(8,128)(2,1)}) custom-call(bf16[16,512]{1,0:T(8,128)(2,1)S(1)} %get-tuple-element.9.low_ref, bf16[8192,256]{1,0:T(8,128)(2,1)S(1)} %copy-done, bf16[8192,256]{1,0:T(8,128)(2,1)S(1)} %copy-done.1, ...), custom_call_target="tpu_custom_call" | custom-call | flops 33554432 | bytes 2097152 | tf_op jit(solution)/shard_map/projection_this_y/pallas_call | solution.py:223
  32.6 0.0 collective-permute-start.2
  32.6 1.5 %collective-permute-done.1 = bf16[16,2048]{1,0:T(8,128)(2,1)S(1)} collective-permute-done((bf16[16,2048]{1,0:T(8,128)(2,1)S(1)}, bf16[16,2048]{1,0:T(8,128)(2,1)S(1)}, u32[]{:S(2)}, u32[]{:S(2)}) %collective-permute-start.1) | collective-permute-done | bytes 65568 | tf_op jit(solution)/shard_map/ppermute | solution.py:142
  34.0 0.0 collective-permute-done.2.got_ref
  34.1 0.6 %last_sum.1 = bf16[16,2048]{1,0:T(8,128)(2,1)} custom-call(f32[16,2048]{1,0:T(8,128)S(1)} %convert_add_fusion.total_ref, bf16[16,2048]{1,0:T(8,128)(2,1)S(1)} %collective-permute-done.2.got_ref), custom_call_target="tpu_custom_call" | custom-call | tf_op jit(solution)/shard_map/last_sum/pallas_call | solution.py:238
  (4 shorter events, 0.0 us)
Async XLA Ops:
  0.6 0.8 %copy-start.3 = (bf16[16,256]{1,0:T(8,128)(2,1)S(1)}, bf16[16,256]{1,0:T(8,128)(2,1)}, u32[]{:S(2)}) copy-start(bf16[16,256]{1,0:T(8,128)(2,1)} %v_ref.1) | copy-start | bytes 24580
  0.6 0.8 %copy-start.2 = (bf16[16,256]{1,0:T(8,128)(2,1)S(1)}, bf16[16,256]{1,0:T(8,128)(2,1)}, u32[]{:S(2)}) copy-start(bf16[16,256]{1,0:T(8,128)(2,1)} %k_ref.1) | copy-start | bytes 24580
  0.7 15.3 %copy-start.5 = (bf16[256,2048]{1,0:T(8,128)(2,1)S(1)}, bf16[256,2048]{1,0:T(8,128)(2,1)}, u32[]{:S(2)}) copy-start(bf16[256,2048]{1,0:T(8,128)(2,1)} %g_ref.1) | copy-start | bytes 3145732
  0.7 15.3 %copy-start.4 = (bf16[256,2048]{1,0:T(8,128)(2,1)S(1)}, bf16[256,2048]{1,0:T(8,128)(2,1)}, u32[]{:S(2)}) copy-start(bf16[256,2048]{1,0:T(8,128)(2,1)} %q_ref.1) | copy-start | bytes 3145732
  15.9 11.8 %copy-start = (bf16[8192,256]{1,0:T(8,128)(2,1)S(1)}, bf16[8192,256]{1,0:T(8,128)(2,1)}, u32[]{:S(2)}) copy-start(bf16[8192,256]{1,0:T(8,128)(2,1)} %kw_ref.5) | copy-start | bytes 12582916
  15.9 11.8 %copy-start.1 = (bf16[8192,256]{1,0:T(8,128)(2,1)S(1)}, bf16[8192,256]{1,0:T(8,128)(2,1)}, u32[]{:S(2)}) copy-start(bf16[8192,256]{1,0:T(8,128)(2,1)} %vw_ref.5) | copy-start | bytes 12582916
  28.4 1.3 %collective-permute-start = (bf16[16,2048]{1,0:T(8,128)(2,1)S(1)}, bf16[16,2048]{1,0:T(8,128)(2,1)S(1)}, u32[]{:S(2)}, u32[]{:S(2)}) collective-permute-start(bf16[16,2048]{1,0:T(8,128)(2,1)S(1)} %get-tuple-element.10), channel_id=1, source_target_pairs={{0,1},{1,0},{2,3},{3,2},{4,5},{5,4},{6,7},{7,6},{8,9},{9,8},{10,11... | collective-permute-start | bytes 196616 | tf_op jit(solution)/shard_map/ppermute | solution.py:142
  29.7 4.3 %collective-permute-start.1 = (bf16[16,2048]{1,0:T(8,128)(2,1)S(1)}, bf16[16,2048]{1,0:T(8,128)(2,1)S(1)}, u32[]{:S(2)}, u32[]{:S(2)}) collective-permute-start(bf16[16,2048]{1,0:T(8,128)(2,1)S(1)} %add_convert_fusion.after), channel_id=1, source_target_pairs={{0,2},{1,3},{2,0},{3,1},{4,6},{5,7},{6,4},{7,5},{8,10},{9,11},{10,... | collective-permute-start | bytes 196616 | tf_op jit(solution)/shard_map/ppermute | solution.py:142
  32.6 1.5 %collective-permute-start.2 = (bf16[16,2048]{1,0:T(8,128)(2,1)S(1)}, bf16[16,2048]{1,0:T(8,128)(2,1)S(1)}, u32[]{:S(2)}, u32[]{:S(2)}) collective-permute-start(bf16[16,2048]{1,0:T(8,128)(2,1)S(1)} %get-tuple-element.14), channel_id=1, source_target_pairs={{0,1},{1,0},{2,3},{3,2},{4,5},{5,4},{6,7},{7,6},{8,9},{9,8},{10,11... | collective-permute-start | bytes 196616 | tf_op jit(solution)/shard_map/ppermute | solution.py:142

commit v24 on v21

--- a/solution.py
+++ b/solution.py
@@ -67,17 +67,17 @@
         if i + 1 < len(units):
             following = products(units[i + 1])
         top = jnp.max(scores, axis=0, keepdims=True)
-        expo = jnp.exp2((scores - top) * (scale * LOG2E))
+        expo = jnp.exp2(scores * (scale * LOG2E) - top * (scale * LOG2E))
         total = jnp.sum(expo, axis=0, keepdims=True)
         weighted = jnp.sum(expo * dprobs, axis=0, keepdims=True)
         inverse = 1.0 / total
         delta = weighted * inverse
         factor = inverse * jnp.concatenate([live_ref[part, :1]] * UNIT, axis=1)
-        probs = expo * factor
+        probs = (expo * factor).astype(jnp.bfloat16)
         mine = [u for u in units if u[0] == k]
         cols = pl.ds(mine.index(unit) * UNIT * LEN, UNIT * LEN)
-        weights_ref[k, :tokens, cols] = probs.astype(jnp.bfloat16)
-        weights_ref[k, tokens:, cols] = (probs * (dprobs - delta)).astype(jnp.bfloat16)
+        weights_ref[k, :tokens, cols] = probs
+        weights_ref[k, tokens:, cols] = probs * (dprobs - delta).astype(jnp.bfloat16)
         if unit == mine[-1]:
             rows = [
                 jnp.concatenate([stack(g_ref, u), stack(q_ref, u)], axis=1) for u in mine

time: 34.9 us -> 34.9 us (level)
  no operation moved by 1% of the time
where the time goes in v24:
time: 34.9 us; the launch traced here: 34.6 us
  blocking collectives  24.3 us (70%)
  Pallas kernels  5.13 us (15%)
  waiting for transfers between devices  2.08 us (6%)
  starting transfers between devices  1.59 us (5%)
  between operations  1.53 us (4%)
    all_to_all x1, blocking collectives, body(): lax.all_to_all(both, 'resp', 0, 0, tiled=True)  14.4 us
    all_to_all x1, blocking collectives, body(): lax.all_to_all(partial.reshape(resp, own, 2 * width), 'resp', 0, 0, tiled...  9.87 us
    ppermute x3, waiting for transfers between devices, swap(): return lax.ppermute(x, axis, [(i, i ^ bit) for i in range(count)])  2.08 us
    pallas_call x1, Pallas kernels, body(): pl.pallas_call(attention_kernel, out_shape=pltpu.VMEM((tokens, 2 * width)...  1.89 us
    ppermute x3, starting transfers between devices, swap(): return lax.ppermute(x, axis, [(i, i ^ bit) for i in range(count)])  1.59 us
    pallas_call x1, Pallas kernels, body(): pl.pallas_call(last_projection_kernel, out_shape=[pltpu.VMEM(block, jnp.b...  1.27 us
  transfers between devices with their start and end apart: 3, of which 2 were waited for; matrix products, arithmetic and copies ran while one was open for 0% of the time, Pallas kernels for 6%

profile of v24, /device:TPU:0, one launch (start us, length us, event | category | flops | bytes accessed | tf_op | source)
XLA Modules:
  0.0 34.6 jit_solution(10993316479111817214)
XLA Ops:
  0.6 0.0 copy-start.3
  0.6 0.0 copy-start.2
  0.7 0.0 copy-start.5
  0.7 0.0 copy-start.4
  1.5 0.0 copy-done.3
  1.5 0.0 copy-done.2
  1.5 14.4 %all_to_all.10 = bf16[8,16,512]{2,1,0:T(8,128)(2,1)S(1)} all-to-all(bf16[8,16,512]{2,1,0:T(8,128)(2,1)S(1)} %join.1), channel_id=1, replica_groups=mesh['resp'=8,'head'=4] {'resp'}, dimensions={0} | all-to-all | bytes 262144 | tf_op jit(solution)/shard_map/all_to_all | solution.py:160
  15.9 0.0 copy-done.5
  15.9 0.0 copy-done.4
  15.9 0.0 copy-start
  15.9 0.0 copy-start.1
  15.9 1.9 %attention.1 = bf16[128,512]{1,0:T(8,128)(2,1)S(1)} custom-call(f32[1,8,256]{2,1,0:T(8,128)S(1)} %mask.1.live_ref, bf16[128,512]{1,0:T(8,128)(2,1)S(1)} %bitcast.2, bf16[256,2048]{1,0:T(8,128)(2,1)S(1)} %copy-done.4, bf16[256,2048]{1,0:T(8,128)(2,1)S(1)} %copy-done.5), custom_call_target="tpu_custom_call" | custom-call | flops 4294967296 | bytes 2293760 | tf_op jit(solution)/shard_map/attention/pallas_call | solution.py:165
  17.8 9.9 %all_to_all.11.parts_ref = bf16[8,16,512]{2,1,0:T(8,128)(2,1)S(1)} all-to-all(bf16[8,16,512]{2,1,0:T(8,128)(2,1)S(1)} %bitcast.3), channel_id=1, replica_groups=mesh['resp'=8,'head'=4] {'resp'}, dimensions={0} | all-to-all | bytes 262144 | tf_op jit(solution)/shard_map/all_to_all | solution.py:185
  27.7 0.0 copy-done
  27.7 0.0 copy-done.1
  27.7 0.7 %projection_other_core.1 = (bf16[16,512]{1,0:T(8,128)(2,1)S(1)}, bf16[16,2048]{1,0:T(8,128)(2,1)S(1)}) custom-call(bf16[8,16,512]{2,1,0:T(8,128)(2,1)S(1)} %all_to_all.11.parts_ref, bf16[8192,256]{1,0:T(8,128)(2,1)S(1)} %copy-done, bf16[8192,256]{1,0:T(8,128)(2,1)S(1)} %copy-done.1), custom_call_target="tpu_custom_call" | custom-call | tf_op jit(solution)/shard_map/projection_other_core/pallas_call | solution.py:190
  28.4 0.0 collective-permute-start
  28.4 0.7 %projection_other_y.1 = f32[16,2048]{1,0:T(8,128)S(1)} custom-call(bf16[16,512]{1,0:T(8,128)(2,1)S(1)} %get-tuple-element.9.low_ref, bf16[8192,256]{1,0:T(8,128)(2,1)S(1)} %copy-done, bf16[8192,256]{1,0:T(8,128)(2,1)S(1)} %copy-done.1), custom_call_target="tpu_custom_call" | custom-call | flops 33554432 | bytes 2097152 | tf_op jit(solution)/shard_map/projection_other_y/pallas_call | solution.py:204
  29.0 0.6 %collective-permute-done = bf16[16,2048]{1,0:T(8,128)(2,1)S(1)} collective-permute-done((bf16[16,2048]{1,0:T(8,128)(2,1)S(1)}, bf16[16,2048]{1,0:T(8,128)(2,1)S(1)}, u32[]{:S(2)}, u32[]{:S(2)}) %collective-permute-start) | collective-permute-done | bytes 65568 | tf_op jit(solution)/shard_map/ppermute | solution.py:134
  29.6 1.6 %collective-permute-start.1 = (bf16[16,2048]{1,0:T(8,128)(2,1)S(1)}, bf16[16,2048]{1,0:T(8,128)(2,1)S(1)}, u32[]{:S(2)}, u32[]{:S(2)}) collective-permute-start(bf16[16,2048]{1,0:T(8,128)(2,1)S(1)} %add_convert_fusion.after), channel_id=1, source_target_pairs={{0,2},{1,3},{2,0},{3,1},{4,6},{5,7},{6,4},{7,5},{8,10},{9,11},{10,... | collective-permute-start | bytes 196616 | tf_op jit(solution)/shard_map/ppermute | solution.py:134
  31.2 1.3 %projection_this_y.1 = (bf16[16,2048]{1,0:T(8,128)(2,1)S(1)}, f32[16,2048]{1,0:T(8,128)S(1)}, bf16[16,256]{1,0:T(8,128)(2,1)}, bf16[16,256]{1,0:T(8,128)(2,1)}) custom-call(bf16[16,512]{1,0:T(8,128)(2,1)S(1)} %get-tuple-element.9.low_ref, bf16[8192,256]{1,0:T(8,128)(2,1)S(1)} %copy-done, bf16[8192,256]{1,0:T(8,128)(2,1)S(1)} %copy-done.1, ...), custom_call_target="tpu_custom_call" | custom-call | flops 33554432 | bytes 2097152 | tf_op jit(solution)/shard_map/projection_this_y/pallas_call | solution.py:215
  32.5 0.0 collective-permute-start.2
  32.5 1.5 %collective-permute-done.1 = bf16[16,2048]{1,0:T(8,128)(2,1)S(1)} collective-permute-done((bf16[16,2048]{1,0:T(8,128)(2,1)S(1)}, bf16[16,2048]{1,0:T(8,128)(2,1)S(1)}, u32[]{:S(2)}, u32[]{:S(2)}) %collective-permute-start.1) | collective-permute-done | bytes 65568 | tf_op jit(solution)/shard_map/ppermute | solution.py:134
  34.0 0.0 collective-permute-done.2.got_ref
  34.0 0.6 %last_sum.1 = bf16[16,2048]{1,0:T(8,128)(2,1)} custom-call(f32[16,2048]{1,0:T(8,128)S(1)} %convert_add_fusion.total_ref, bf16[16,2048]{1,0:T(8,128)(2,1)S(1)} %collective-permute-done.2.got_ref), custom_call_target="tpu_custom_call" | custom-call | tf_op jit(solution)/shard_map/last_sum/pallas_call | solution.py:230
  (4 shorter events, 0.0 us)
Async XLA Ops:
  0.6 0.8 %copy-start.3 = (bf16[16,256]{1,0:T(8,128)(2,1)S(1)}, bf16[16,256]{1,0:T(8,128)(2,1)}, u32[]{:S(2)}) copy-start(bf16[16,256]{1,0:T(8,128)(2,1)} %v_ref.1) | copy-start | bytes 24580
  0.6 0.8 %copy-start.2 = (bf16[16,256]{1,0:T(8,128)(2,1)S(1)}, bf16[16,256]{1,0:T(8,128)(2,1)}, u32[]{:S(2)}) copy-start(bf16[16,256]{1,0:T(8,128)(2,1)} %k_ref.1) | copy-start | bytes 24580
  0.7 15.3 %copy-start.5 = (bf16[256,2048]{1,0:T(8,128)(2,1)S(1)}, bf16[256,2048]{1,0:T(8,128)(2,1)}, u32[]{:S(2)}) copy-start(bf16[256,2048]{1,0:T(8,128)(2,1)} %g_ref.1) | copy-start | bytes 3145732
  0.7 15.3 %copy-start.4 = (bf16[256,2048]{1,0:T(8,128)(2,1)S(1)}, bf16[256,2048]{1,0:T(8,128)(2,1)}, u32[]{:S(2)}) copy-start(bf16[256,2048]{1,0:T(8,128)(2,1)} %q_ref.1) | copy-start | bytes 3145732
  15.9 11.8 %copy-start = (bf16[8192,256]{1,0:T(8,128)(2,1)S(1)}, bf16[8192,256]{1,0:T(8,128)(2,1)}, u32[]{:S(2)}) copy-start(bf16[8192,256]{1,0:T(8,128)(2,1)} %kw_ref.5) | copy-start | bytes 12582916
  15.9 11.8 %copy-start.1 = (bf16[8192,256]{1,0:T(8,128)(2,1)S(1)}, bf16[8192,256]{1,0:T(8,128)(2,1)}, u32[]{:S(2)}) copy-start(bf16[8192,256]{1,0:T(8,128)(2,1)} %vw_ref.5) | copy-start | bytes 12582916
  28.4 1.3 %collective-permute-start = (bf16[16,2048]{1,0:T(8,128)(2,1)S(1)}, bf16[16,2048]{1,0:T(8,128)(2,1)S(1)}, u32[]{:S(2)}, u32[]{:S(2)}) collective-permute-start(bf16[16,2048]{1,0:T(8,128)(2,1)S(1)} %get-tuple-element.10), channel_id=1, source_target_pairs={{0,1},{1,0},{2,3},{3,2},{4,5},{5,4},{6,7},{7,6},{8,9},{9,8},{10,11... | collective-permute-start | bytes 196616 | tf_op jit(solution)/shard_map/ppermute | solution.py:134
  29.6 4.3 %collective-permute-start.1 = (bf16[16,2048]{1,0:T(8,128)(2,1)S(1)}, bf16[16,2048]{1,0:T(8,128)(2,1)S(1)}, u32[]{:S(2)}, u32[]{:S(2)}) collective-permute-start(bf16[16,2048]{1,0:T(8,128)(2,1)S(1)} %add_convert_fusion.after), channel_id=1, source_target_pairs={{0,2},{1,3},{2,0},{3,1},{4,6},{5,7},{6,4},{7,5},{8,10},{9,11},{10,... | collective-permute-start | bytes 196616 | tf_op jit(solution)/shard_map/ppermute | solution.py:134
  32.5 1.5 %collective-permute-start.2 = (bf16[16,2048]{1,0:T(8,128)(2,1)S(1)}, bf16[16,2048]{1,0:T(8,128)(2,1)S(1)}, u32[]{:S(2)}, u32[]{:S(2)}) collective-permute-start(bf16[16,2048]{1,0:T(8,128)(2,1)S(1)} %get-tuple-element.14), channel_id=1, source_target_pairs={{0,1},{1,0},{2,3},{3,2},{4,5},{5,4},{6,7},{7,6},{8,9},{9,8},{10,11... | collective-permute-start | bytes 196616 | tf_op jit(solution)/shard_map/ppermute | solution.py:134

commit v25 on v21

--- a/solution.py
+++ b/solution.py
@@ -109,20 +109,35 @@
     out_ref[...] = out.astype(out_ref.dtype)
 
 
-def second_projection_kernel(low_ref, kw_ref, vw_ref, out_ref):
+def second_projection_kernel(low_ref, kw_ref, vw_ref, out_ref, early_ref):
     me = lax.axis_index("head")
     out_ref[...] = project(low_ref[...], kw_ref, vw_ref, me ^ 2, out_ref.shape[1])
 
-
-def last_projection_kernel(low_ref, kw_ref, vw_ref, after, out_ref, keep_ref, dk_ref, dv_ref):
+    @pl.when((me & 1) == 1)
+    def _():
+        out = project(low_ref[...], kw_ref, vw_ref, me ^ 1, early_ref.shape[1])
+        early_ref[...] = out.astype(early_ref.dtype)
+
+
+def last_projection_kernel(
+    low_ref, kw_ref, vw_ref, early_ref, after, out_ref, keep_ref, dk_ref, dv_ref
+):
     del after
     width = dk_ref.shape[1]
     low = low_ref[...]
     dk_ref[...] = low[:, :width]
     dv_ref[...] = low[:, width:]
     me = lax.axis_index("head")
-    out = project(low, kw_ref, vw_ref, me ^ 1, out_ref.shape[1])
-    out_ref[...] = out.astype(out_ref.dtype)
+
+    @pl.when((me & 1) == 1)
+    def _():
+        out_ref[...] = early_ref[...]
+
+    @pl.when((me & 1) == 0)
+    def _():
+        out = project(low_ref[...], kw_ref, vw_ref, me ^ 1, out_ref.shape[1])
+        out_ref[...] = out.astype(out_ref.dtype)
+
     keep_ref[...] = project(low, kw_ref, vw_ref, me, keep_ref.shape[1])
 
 
@@ -201,11 +216,11 @@
     cost = pl.CostEstimate(
         flops=4 * own * width * features, transcendentals=0, bytes_accessed=4 * width * features
     )
-    far = pl.pallas_call(
+    far, early = pl.pallas_call(
         second_projection_kernel,
-        out_shape=pltpu.VMEM(block, jnp.float32),
+        out_shape=[pltpu.VMEM(block, jnp.float32), pltpu.VMEM(block, jnp.bfloat16)],
         in_specs=[vmem] * 3,
-        out_specs=vmem,
+        out_specs=[vmem] * 2,
         compiler_params=params,
         cost_estimate=cost,
         name="projection_other_y",
@@ -220,12 +235,12 @@
             jax.ShapeDtypeStruct((own, width), jnp.bfloat16),
             jax.ShapeDtypeStruct((own, width), jnp.bfloat16),
         ],
-        in_specs=[vmem] * 3 + [pl.BlockSpec(memory_space=pl.ANY)],
+        in_specs=[vmem] * 4 + [pl.BlockSpec(memory_space=pl.ANY)],
         out_specs=[vmem] * 4,
         compiler_params=params,
         cost_estimate=cost,
         name="projection_this_y",
-    )(low, k_weight, v_weight, far)
+    )(low, k_weight, v_weight, early, far)
     total = lax.optimization_barrier(total + got.astype(jnp.float32))
     input_grad = pl.pallas_call(
         last_sum_kernel,

time: 34.9 us -> 35.3 us (1.011)
  no operation moved by 1% of the time
where the time goes in v25:
time: 35.3 us; the launch traced here: 35.1 us
  blocking collectives  24.3 us (69%)
  Pallas kernels  5.35 us (15%)
  waiting for transfers between devices  2.27 us (6%)
  starting transfers between devices  1.59 us (5%)
  between operations  1.54 us (4%)
    all_to_all x1, blocking collectives, body(): lax.all_to_all(both, 'resp', 0, 0, tiled=True)  14.4 us
    all_to_all x1, blocking collectives, body(): lax.all_to_all(partial.reshape(resp, own, 2 * width), 'resp', 0, 0, tiled...  9.87 us
    ppermute x3, waiting for transfers between devices, swap(): return lax.ppermute(x, axis, [(i, i ^ bit) for i in range(count)])  2.27 us
    pallas_call x1, Pallas kernels, body(): pl.pallas_call(attention_kernel, out_shape=pltpu.VMEM((tokens, 2 * width)...  2.04 us
    ppermute x3, starting transfers between devices, swap(): return lax.ppermute(x, axis, [(i, i ^ bit) for i in range(count)])  1.59 us
    pallas_call x1, Pallas kernels, body(): pl.pallas_call(last_projection_kernel, out_shape=[pltpu.VMEM(block, jnp.b...  1.31 us
  transfers between devices with their start and end apart: 3, of which 2 were waited for; matrix products, arithmetic and copies ran while one was open for 0% of the time, Pallas kernels for 6%

profile of v25, /device:TPU:0, one launch (start us, length us, event | category | flops | bytes accessed | tf_op | source)
XLA Modules:
  0.0 35.1 jit_solution(3956566147348690731)
XLA Ops:
  0.6 0.0 copy-start.3
  0.6 0.0 copy-start.2
  0.7 0.0 copy-start.4
  0.7 0.0 copy-start.5
  1.5 0.0 copy-done.3
  1.5 0.0 copy-done.2
  1.5 14.4 %all_to_all.10 = bf16[8,16,512]{2,1,0:T(8,128)(2,1)S(1)} all-to-all(bf16[8,16,512]{2,1,0:T(8,128)(2,1)S(1)} %join.1), channel_id=1, replica_groups=mesh['resp'=8,'head'=4] {'resp'}, dimensions={0} | all-to-all | bytes 262144 | tf_op jit(solution)/shard_map/all_to_all | solution.py:175
  15.9 0.0 copy-done.4
  15.9 0.0 copy-done.5
  15.9 0.0 copy-start
  15.9 0.0 copy-start.1
  15.9 2.0 %attention.1 = bf16[128,512]{1,0:T(8,128)(2,1)S(1)} custom-call(f32[1,8,256]{2,1,0:T(8,128)S(1)} %mask.1.live_ref, bf16[128,512]{1,0:T(8,128)(2,1)S(1)} %bitcast.2, bf16[256,2048]{1,0:T(8,128)(2,1)S(1)} %copy-done.4, bf16[256,2048]{1,0:T(8,128)(2,1)S(1)} %copy-done.5), custom_call_target="tpu_custom_call" | custom-call | flops 4294967296 | bytes 2293760 | tf_op jit(solution)/shard_map/attention/pallas_call | solution.py:180
  18.0 9.9 %all_to_all.11.parts_ref = bf16[8,16,512]{2,1,0:T(8,128)(2,1)S(1)} all-to-all(bf16[8,16,512]{2,1,0:T(8,128)(2,1)S(1)} %bitcast.3), channel_id=1, replica_groups=mesh['resp'=8,'head'=4] {'resp'}, dimensions={0} | all-to-all | bytes 262144 | tf_op jit(solution)/shard_map/all_to_all | solution.py:200
  27.8 0.0 copy-done
  27.8 0.0 copy-done.1
  27.8 0.7 %projection_other_core.1 = (bf16[16,512]{1,0:T(8,128)(2,1)S(1)}, bf16[16,2048]{1,0:T(8,128)(2,1)S(1)}) custom-call(bf16[8,16,512]{2,1,0:T(8,128)(2,1)S(1)} %all_to_all.11.parts_ref, bf16[8192,256]{1,0:T(8,128)(2,1)S(1)} %copy-done, bf16[8192,256]{1,0:T(8,128)(2,1)S(1)} %copy-done.1), custom_call_target="tpu_custom_call" | custom-call | tf_op jit(solution)/shard_map/projection_other_core/pallas_call | solution.py:205
  28.5 0.0 collective-permute-start
  28.5 0.7 %projection_other_y.1 = (f32[16,2048]{1,0:T(8,128)S(1)}, bf16[16,2048]{1,0:T(8,128)(2,1)S(1)}) custom-call(bf16[16,512]{1,0:T(8,128)(2,1)S(1)} %get-tuple-element.11.low_ref, bf16[8192,256]{1,0:T(8,128)(2,1)S(1)} %copy-done, bf16[8192,256]{1,0:T(8,128)(2,1)S(1)} %copy-done.1), custom_call_target="tpu_custom_call" | custom-call | flops 33554432 | bytes 2097152 | tf_op jit(solution)/shard_map/projection_other_y/pallas_call | solution.py:219
  29.2 0.6 %collective-permute-done = bf16[16,2048]{1,0:T(8,128)(2,1)S(1)} collective-permute-done((bf16[16,2048]{1,0:T(8,128)(2,1)S(1)}, bf16[16,2048]{1,0:T(8,128)(2,1)S(1)}, u32[]{:S(2)}, u32[]{:S(2)}) %collective-permute-start) | collective-permute-done | bytes 65568 | tf_op jit(solution)/shard_map/ppermute | solution.py:149
  29.8 1.6 %collective-permute-start.1 = (bf16[16,2048]{1,0:T(8,128)(2,1)S(1)}, bf16[16,2048]{1,0:T(8,128)(2,1)S(1)}, u32[]{:S(2)}, u32[]{:S(2)}) collective-permute-start(bf16[16,2048]{1,0:T(8,128)(2,1)S(1)} %add_convert_fusion.after), channel_id=1, source_target_pairs={{0,2},{1,3},{2,0},{3,1},{4,6},{5,7},{6,4},{7,5},{8,10},{9,11},{10,... | collective-permute-start | bytes 196616 | tf_op jit(solution)/shard_map/ppermute | solution.py:149
  31.4 1.3 %projection_this_y.1 = (bf16[16,2048]{1,0:T(8,128)(2,1)S(1)}, f32[16,2048]{1,0:T(8,128)S(1)}, bf16[16,256]{1,0:T(8,128)(2,1)}, bf16[16,256]{1,0:T(8,128)(2,1)}) custom-call(bf16[16,512]{1,0:T(8,128)(2,1)S(1)} %get-tuple-element.11.low_ref, bf16[8192,256]{1,0:T(8,128)(2,1)S(1)} %copy-done, bf16[8192,256]{1,0:T(8,128)(2,1)S(1)} %copy-done.1, ...), custom_call_target="tpu_custom_call" | custom-call | flops 33554432 | bytes 2097152 | tf_op jit(solution)/shard_map/projection_this_y/pallas_call | solution.py:230
  32.7 0.0 collective-permute-start.2
  32.7 1.7 %collective-permute-done.1 = bf16[16,2048]{1,0:T(8,128)(2,1)S(1)} collective-permute-done((bf16[16,2048]{1,0:T(8,128)(2,1)S(1)}, bf16[16,2048]{1,0:T(8,128)(2,1)S(1)}, u32[]{:S(2)}, u32[]{:S(2)}) %collective-permute-start.1) | collective-permute-done | bytes 65568 | tf_op jit(solution)/shard_map/ppermute | solution.py:149
  34.4 0.0 collective-permute-done.2.got_ref
  34.4 0.6 %last_sum.1 = bf16[16,2048]{1,0:T(8,128)(2,1)} custom-call(f32[16,2048]{1,0:T(8,128)S(1)} %convert_add_fusion.total_ref, bf16[16,2048]{1,0:T(8,128)(2,1)S(1)} %collective-permute-done.2.got_ref), custom_call_target="tpu_custom_call" | custom-call | tf_op jit(solution)/shard_map/last_sum/pallas_call | solution.py:245
  (4 shorter events, 0.0 us)
Async XLA Ops:
  0.6 0.8 %copy-start.3 = (bf16[16,256]{1,0:T(8,128)(2,1)S(1)}, bf16[16,256]{1,0:T(8,128)(2,1)}, u32[]{:S(2)}) copy-start(bf16[16,256]{1,0:T(8,128)(2,1)} %v_ref.1) | copy-start | bytes 24580
  0.6 0.8 %copy-start.2 = (bf16[16,256]{1,0:T(8,128)(2,1)S(1)}, bf16[16,256]{1,0:T(8,128)(2,1)}, u32[]{:S(2)}) copy-start(bf16[16,256]{1,0:T(8,128)(2,1)} %k_ref.1) | copy-start | bytes 24580
  0.7 15.3 %copy-start.4 = (bf16[256,2048]{1,0:T(8,128)(2,1)S(1)}, bf16[256,2048]{1,0:T(8,128)(2,1)}, u32[]{:S(2)}) copy-start(bf16[256,2048]{1,0:T(8,128)(2,1)} %q_ref.1) | copy-start | bytes 3145732
  0.7 15.3 %copy-start.5 = (bf16[256,2048]{1,0:T(8,128)(2,1)S(1)}, bf16[256,2048]{1,0:T(8,128)(2,1)}, u32[]{:S(2)}) copy-start(bf16[256,2048]{1,0:T(8,128)(2,1)} %g_ref.1) | copy-start | bytes 3145732
  15.9 11.9 %copy-start = (bf16[8192,256]{1,0:T(8,128)(2,1)S(1)}, bf16[8192,256]{1,0:T(8,128)(2,1)}, u32[]{:S(2)}) copy-start(bf16[8192,256]{1,0:T(8,128)(2,1)} %kw_ref.5) | copy-start | bytes 12582916
  15.9 11.9 %copy-start.1 = (bf16[8192,256]{1,0:T(8,128)(2,1)S(1)}, bf16[8192,256]{1,0:T(8,128)(2,1)}, u32[]{:S(2)}) copy-start(bf16[8192,256]{1,0:T(8,128)(2,1)} %vw_ref.5) | copy-start | bytes 12582916
  28.5 1.3 %collective-permute-start = (bf16[16,2048]{1,0:T(8,128)(2,1)S(1)}, bf16[16,2048]{1,0:T(8,128)(2,1)S(1)}, u32[]{:S(2)}, u32[]{:S(2)}) collective-permute-start(bf16[16,2048]{1,0:T(8,128)(2,1)S(1)} %get-tuple-element.14), channel_id=1, source_target_pairs={{0,1},{1,0},{2,3},{3,2},{4,5},{5,4},{6,7},{7,6},{8,9},{9,8},{10,11... | collective-permute-start | bytes 196616 | tf_op jit(solution)/shard_map/ppermute | solution.py:149
  29.8 4.6 %collective-permute-start.1 = (bf16[16,2048]{1,0:T(8,128)(2,1)S(1)}, bf16[16,2048]{1,0:T(8,128)(2,1)S(1)}, u32[]{:S(2)}, u32[]{:S(2)}) collective-permute-start(bf16[16,2048]{1,0:T(8,128)(2,1)S(1)} %add_convert_fusion.after), channel_id=1, source_target_pairs={{0,2},{1,3},{2,0},{3,1},{4,6},{5,7},{6,4},{7,5},{8,10},{9,11},{10,... | collective-permute-start | bytes 196616 | tf_op jit(solution)/shard_map/ppermute | solution.py:149
  32.7 1.7 %collective-permute-start.2 = (bf16[16,2048]{1,0:T(8,128)(2,1)S(1)}, bf16[16,2048]{1,0:T(8,128)(2,1)S(1)}, u32[]{:S(2)}, u32[]{:S(2)}) collective-permute-start(bf16[16,2048]{1,0:T(8,128)(2,1)S(1)} %get-tuple-element.18), channel_id=1, source_target_pairs={{0,1},{1,0},{2,3},{3,2},{4,5},{5,4},{6,7},{7,6},{8,9},{9,8},{10,11... | collective-permute-start | bytes 196616 | tf_op jit(solution)/shard_map/ppermute | solution.py:149
